TPU v7x, 32 devices: a whole 2x2x4 slice. The times are simulated.
32 devices in a mesh: ctx: 8 (over y, x, core), tp: 4 (over z).
Axes of the slice: x: 2, y: 2, z: 4, core: 2. Of those that a mesh axis runs over, the one named last changes fastest.
Arguments:
- queries: bfloat16 [2048, 2048], P('ctx', 'tp'), may hold values from -70 to 70
- keys: bfloat16 [2048, 1024], P('ctx', 'tp'), may hold values from -6 to 6
- values: bfloat16 [2048, 1024], P('ctx', 'tp'), may hold values from -6 to 6
- grad_out: bfloat16 [2048, 5376], P(('ctx', 'tp')), may hold values from -24 to 24
- out_weight: bfloat16 [2048, 5376], P('tp'), may hold values from -0.078125 to 0.078125
Outputs:
- grad_queries: float32 [2048, 2048], P('ctx', 'tp')
- grad_keys: float32 [2048, 1024], P('ctx', 'tp')
- grad_values: float32 [2048, 1024], P('ctx', 'tp')
All inputs are finite; a program needn't handle non-finite values.
Results may differ from a plain program's by a relative error of at most 0.014.
Values may be sent and summed in bfloat16 or wider, within the bound.
No kernel may reach another device: no remote copies, remote signals or barrier semaphores. Data moves between devices by JAX's collectives and lax.ppermute only.
A program may use at most 64 MiB of HBM per device.

v0:
```python
import jax
import jax.numpy as jnp
from jax import lax
from jax.sharding import PartitionSpec as P

HD = 128
WIN = 1024


score_scale = 168.0 ** (-0.5)


def passed_along(block, axis, distance):
    devices = range(lax.axis_size(axis))
    route = [(i - distance, i) for i in devices if i - distance in devices]
    return lax.ppermute(block, axis, route)


def band_grads(queries, dout, key_span, value_span, query_pos, key_pos, kv_heads):
    shard_rows = queries.shape[0]
    span_rows = key_span.shape[0]
    group_size = queries.shape[1] // (kv_heads * HD)
    query_heads = queries.reshape(shard_rows, kv_heads, group_size, HD)
    dout_heads = dout.reshape(shard_rows, kv_heads, group_size, HD)
    key_heads = key_span.reshape(span_rows, kv_heads, HD)
    value_heads = value_span.reshape(span_rows, kv_heads, HD)
    scores = (
        jnp.einsum("sgrd,egd->grse", query_heads, key_heads, preferred_element_type=jnp.float32)
        * score_scale
    )
    allowed = (
        (key_pos[None, :] <= query_pos[:, None])
        & (key_pos[None, :] > query_pos[:, None] - WIN)
        & (key_pos[None, :] >= 0)
    )
    scores = jnp.where(allowed, scores, -1e30)
    row_max = jnp.max(scores, axis=-1, keepdims=True)
    weights = jnp.where(allowed, jnp.exp(scores - row_max), 0.0)
    probability = weights / jnp.sum(weights, axis=-1, keepdims=True)
    dprobs = jnp.einsum(
        "sgrd,egd->grse", dout_heads, value_heads, preferred_element_type=jnp.float32
    )
    row_delta = jnp.sum(probability * dprobs, axis=-1, keepdims=True)
    dscores = probability * (dprobs - row_delta)
    probs_low = probability.astype(jnp.bfloat16)
    dscores_low = dscores.astype(jnp.bfloat16)
    grad_value = jnp.einsum(
        "grse,sgrd->egd", probs_low, dout_heads, preferred_element_type=jnp.float32
    )
    grad_query = score_scale * jnp.einsum(
        "grse,egd->sgrd", dscores_low, key_heads, preferred_element_type=jnp.float32
    )
    grad_key = score_scale * jnp.einsum(
        "grse,sgrd->egd", dscores_low, query_heads, preferred_element_type=jnp.float32
    )
    return (
        grad_query.reshape(shard_rows, -1),
        grad_key.reshape(span_rows, -1),
        grad_value.reshape(span_rows, -1),
    )


def on_device(queries, keys, values, grad_out, out_weight):
    shard_rows = queries.shape[0]
    kv_width = keys.shape[1]
    kv_heads = kv_width // HD
    blocks = WIN // shard_rows
    product = lax.dot_general(
        lax.all_gather(grad_out, "tp", axis=0, tiled=True),
        out_weight,
        (((1,), (1,)), ((), ())),
        preferred_element_type=jnp.float32,
    )
    dout = product.astype(jnp.bfloat16)
    key_value = jnp.stack([keys, values])
    shifted = []
    for distance in range(blocks, 0, -1):
        shifted.append(passed_along(key_value, "ctx", distance))
    extended = jnp.concatenate(shifted + [key_value], axis=1)
    shard = lax.axis_index("ctx")
    span_rows = extended.shape[1]
    query_pos = shard * shard_rows + jnp.arange(shard_rows, dtype=jnp.int32)
    key_pos = shard * shard_rows - blocks * shard_rows + jnp.arange(span_rows, dtype=jnp.int32)
    grad_query, grad_key, grad_value = band_grads(
        queries, dout, extended[0], extended[1], query_pos, key_pos, kv_heads
    )
    span_grads = jnp.stack([grad_key, grad_value])
    earlier_low = span_grads[:, : blocks * shard_rows].astype(jnp.bfloat16)
    summed = span_grads[:, blocks * shard_rows :]
    for offset in range(blocks):
        distance = blocks - offset
        block_grads = earlier_low[:, offset * shard_rows : (offset + 1) * shard_rows]
        returned = passed_along(block_grads, "ctx", -distance)
        summed = summed + returned.astype(jnp.float32)
    return (grad_query, summed[0], summed[1])


def solution(mesh):
    in_specs = (
        P("ctx", "tp"),
        P("ctx", "tp"),
        P("ctx", "tp"),
        P(("ctx", "tp"), None),
        P("tp", None),
    )
    out_specs = (P("ctx", "tp"), P("ctx", "tp"), P("ctx", "tp"))
    return jax.shard_map(
        on_device, mesh=mesh, in_specs=in_specs, out_specs=out_specs, check_vma=False
    )
```

profile of v0, /device:TPU:3, one launch (start us, length us, event | category | flops | bytes accessed | tf_op | source)
XLA Modules:
  0.0 127.6 jit_solution(13161022216964679789)
XLA Ops:
  7.2 0.0 all-gather.2.cloned.1.call-start
  7.2 0.7 all-gather.2.cloned.1.call-update
  7.9 1.0 copy.19
  8.9 1.0 copy.20
  10.0 3.2 %collective-permute-start = (bf16[2,256,256]{1,2,0:T(8,128)(2,1)S(1)}, bf16[2,256,256]{1,2,0:T(8,128)(2,1)S(1)}, u32[]{:S(2)}, u32[]{:S(2)}) collective-permute-start(bf16[2,256,256]{1,2,0:T(8,128)(2,1)S(1)} %pad_maximum_fusion.1), channel_id=1, source_target_pairs={{0,16},{4,20},{8,24},{12,28},{1,17},{5,21},{9,25},{13,29},{2,18},{... | collective-permute-start | bytes 786440 | tf_op jit(solution)/shard_map/ppermute | solution.py:16
  13.1 1.9 %collective-permute-start.1 = (bf16[2,256,256]{1,2,0:T(8,128)(2,1)S(1)}, bf16[2,256,256]{1,2,0:T(8,128)(2,1)S(1)}, u32[]{:S(2)}, u32[]{:S(2)}) collective-permute-start(bf16[2,256,256]{1,2,0:T(8,128)(2,1)S(1)} %pad_maximum_fusion.1), channel_id=1, source_target_pairs={{0,12},{4,16},{8,20},{12,24},{16,28},{1,13},{5,17},{9,21},{13,25},... | collective-permute-start | bytes 786440 | tf_op jit(solution)/shard_map/ppermute | solution.py:16
  15.0 1.9 %collective-permute-start.2 = (bf16[2,256,256]{1,2,0:T(8,128)(2,1)S(1)}, bf16[2,256,256]{1,2,0:T(8,128)(2,1)S(1)}, u32[]{:S(2)}, u32[]{:S(2)}) collective-permute-start(bf16[2,256,256]{1,2,0:T(8,128)(2,1)S(1)} %pad_maximum_fusion.1), channel_id=1, source_target_pairs={{0,8},{4,12},{8,16},{12,20},{16,24},{20,28},{1,9},{5,13},{9,17},{1... | collective-permute-start | bytes 786440 | tf_op jit(solution)/shard_map/ppermute | solution.py:16
  17.0 2.7 %collective-permute-start.3 = (bf16[2,256,256]{1,2,0:T(8,128)(2,1)S(1)}, bf16[2,256,256]{1,2,0:T(8,128)(2,1)S(1)}, u32[]{:S(2)}, u32[]{:S(2)}) collective-permute-start(bf16[2,256,256]{1,2,0:T(8,128)(2,1)S(1)} %pad_maximum_fusion.1), channel_id=1, source_target_pairs={{0,4},{4,8},{8,12},{12,16},{16,20},{20,24},{24,28},{1,5},{5,9},{9,... | collective-permute-start | bytes 786440 | tf_op jit(solution)/shard_map/ppermute | solution.py:16
  19.8 1.0 and_and_fusion
  20.7 0.0 copy-start
  20.7 1.2 copy.45
  21.9 0.0 collective-permute-done
  22.0 0.6 collective-permute-done.1
  22.6 2.8 %collective-permute-done.2 = bf16[2,256,256]{1,2,0:T(8,128)(2,1)S(1)} collective-permute-done((bf16[2,256,256]{1,2,0:T(8,128)(2,1)S(1)}, bf16[2,256,256]{1,2,0:T(8,128)(2,1)S(1)}, u32[]{:S(2)}, u32[]{:S(2)}) %collective-permute-start.2) | collective-permute-done | bytes 262176 | tf_op jit(solution)/shard_map/ppermute | solution.py:16
  25.4 1.9 %collective-permute-done.3 = bf16[2,256,256]{1,2,0:T(8,128)(2,1)S(1)} collective-permute-done((bf16[2,256,256]{1,2,0:T(8,128)(2,1)S(1)}, bf16[2,256,256]{1,2,0:T(8,128)(2,1)S(1)}, u32[]{:S(2)}, u32[]{:S(2)}) %collective-permute-start.3) | collective-permute-done | bytes 262176 | tf_op jit(solution)/shard_map/ppermute | solution.py:16
  27.4 0.1 fusion.21
  27.5 4.8 %fusion.6 = (f32[2,2,256]{2,1,0:T(2,128)S(1)}, f32[2,2,256,1280]{2,3,1,0:T(8,128)}) fusion(pred[256,1280]{0,1:T(8,128)(4,1)S(1)} %and_and_fusion, bf16[1280,2,128,1]{0,2,3,1:T(8,128)(2,1)S(1)} %bitcast.75, bf16[256,2,2,128]{0,3,2,1:T(8,128)(2,1)S(1)} %bitcast.84), kind=kOutput, calls=%fused_computation.10 | convolution fusion | flops 342099200 | bytes 6492160 | tf_op jit(solution)/shard_map/sub | solution.py:38
  32.3 35.5 %all-gather.2.cloned.1.call-done = bf16[256,5376]{1,0:T(8,128)(2,1)} async-done(((bf16[64,5376]{1,0:T(8,128)(2,1)}), bf16[256,5376]{1,0:T(8,128)(2,1)}) %all-gather.2.cloned.1.call-update) | async-done | bytes 2752528 | tf_op jit(solution)/shard_map/all_gather | solution.py:69
  67.8 5.0 %convolution_convert_fusion = bf16[256,512]{1,0:T(8,128)(2,1)S(1)} fusion(bf16[256,5376]{1,0:T(8,128)(2,1)} %all-gather.2.cloned.1.call-done, bf16[512,5376]{1,0:T(8,128)(2,1)} %param.9), kind=kOutput, calls=%fused_computation.21 | convolution fusion | flops 1409417216 | bytes 8519680 | tf_op jit(solution)/shard_map/dot_general | solution.py:68
  72.8 0.1 copy.46
  72.9 4.1 %fusion.9 = f32[2,128,1280,1]{2,1,3,0:T(8,128)} fusion(bf16[256,2,2,128]{0,3,2,1:T(8,128)(2,1)S(1)} %bitcast.88, f32[2,2,256]{2,1,0:T(2,128)S(1)} %get-tuple-element.17, pred[256,1280]{0,1:T(8,128)(4,1)S(1)} %and_and_fusion, bf16[1280,2,128,1]{0,2,3,1:T(8,128)(2,1)S(1)} %bitcast.76, bf16[256,2,2,128]{0,3,2,1:T(8,128)(2,1)S(1)} %bitcast.85), kind=kOutput, calls=%fused_computation.17 | convolution fusion | flops 678955264 | bytes 2822144 | tf_op jit(solution)/shard_map/grse,sgrd->egd/dot_general | solution.py:47
  77.1 0.0 slice-start
  77.1 0.0 copy-done
  77.1 0.0 slice-start.1
  77.1 4.3 %fusion.2 = (f32[2,2,256]{2,1,0:T(2,128)S(1)}, f32[2,1280,256,2]{2,1,3,0:T(8,128)S(1)}) fusion(f32[2,2,256]{2,1,0:T(2,128)S(1)} %get-tuple-element.17, f32[2,2,256,1280]{2,3,1,0:T(8,128)} %get-tuple-element.18, pred[256,1280]{0,1:T(8,128)(4,1)S(1)} %and_and_fusion, bf16[1280,2,128,1]{0,2,3,1:T(8,128)(2,1)S(1)} %bitcast.87, ...), kind=kOutput, calls=%fused_computation.4 | convolution fusion | flops 340786176 | bytes 11739136 | tf_op jit(solution)/shard_map/sgrd,egd->grse/dot_general | solution.py:40
  81.4 0.0 slice-done
  81.4 0.0 slice-done.1
  81.4 2.3 %fusion.4 = bf16[2,2,256,1280]{2,3,1,0:T(8,128)(2,1)S(1)} fusion(f32[2,1280,256,2]{2,1,3,0:T(8,128)S(1)} %get-tuple-element.20, f32[2,2,256]{2,1,0:T(2,128)S(1)} %get-tuple-element.19, f32[2,2,256]{2,1,0:T(2,128)S(1)} %get-tuple-element.17, f32[2,2,256,1280]{2,3,1,0:T(8,128)S(1)} %bitcast.73, pred[256,1280]{0,1:T(8,128)(4,1)} %copy-done), kind=kLoop, calls=%fused_computation.6 | loop fusion | flops 6553600 | bytes 13443072 | tf_op jit(solution)/shard_map/convert_element_type | solution.py:46
  83.7 2.1 %fusion.7 = f32[2,1280,128]{1,2,0:T(8,128)} fusion(bf16[2,2,256,1280]{2,3,1,0:T(8,128)(2,1)S(1)} %fusion.4, bf16[256,2,2,128]{0,3,2,1:T(8,128)(2,1)S(1)} %bitcast.86), kind=kOutput, calls=%fused_computation.15 | convolution fusion | flops 335872000 | bytes 4194304 | tf_op jit(solution)/shard_map/grse,sgrd->egd/dot_general | solution.py:53
  85.7 2.8 %copy.30 = f32[1,1280,256]{2,1,0:T(8,128)} copy(f32[1,1280,256]{1,2,0:T(8,128)} %bitcast.74) | data formatting | bytes 2621440 | tf_op jit(solution)/shard_map/stack;reshape | solution.py:87
  88.5 2.8 %copy.31 = f32[1,1280,256]{2,1,0:T(8,128)} copy(f32[1,1280,256]{1,2,0:T(8,128)} %bitcast.79) | data formatting | bytes 2621440 | tf_op jit(solution)/shard_map/stack;reshape | solution.py:87
  91.3 1.9 %fusion.8 = bf16[2,1280,256]{2,1,0:T(8,128)(2,1)S(1)} fusion(f32[1,1280,256]{2,1,0:T(8,128)} %copy.31, f32[1,1280,256]{2,1,0:T(8,128)} %copy.30), kind=kLoop, calls=%fused_computation.16 | loop fusion | flops 655360 | bytes 3932160 | tf_op jit(solution)/shard_map/convert
  93.2 1.0 fusion.20
  94.2 1.3 %collective-permute-start.4 = (bf16[2,256,256]{2,1,0:T(8,128)(2,1)}, bf16[2,256,256]{2,1,0:T(8,128)(2,1)S(1)}, u32[]{:S(2)}, u32[]{:S(2)}) collective-permute-start(bf16[2,256,256]{2,1,0:T(8,128)(2,1)} %get-tuple-element.9), channel_id=1, source_target_pairs={{16,0},{20,4},{24,8},{28,12},{17,1},{21,5},{25,9},{29,13},{18,2},{... | collective-permute-start | bytes 786440 | tf_op jit(solution)/shard_map/ppermute | solution.py:16
  95.5 2.8 %collective-permute-start.5 = (bf16[2,256,256]{2,1,0:T(8,128)(2,1)}, bf16[2,256,256]{2,1,0:T(8,128)(2,1)}, u32[]{:S(2)}, u32[]{:S(2)}) collective-permute-start(bf16[2,256,256]{2,1,0:T(8,128)(2,1)} %get-tuple-element.12), channel_id=1, source_target_pairs={{12,0},{16,4},{20,8},{24,12},{28,16},{13,1},{17,5},{21,9},{25,13},... | collective-permute-start | bytes 786440 | tf_op jit(solution)/shard_map/ppermute | solution.py:16
  98.3 1.9 %collective-permute-start.6 = (bf16[2,256,256]{2,1,0:T(8,128)(2,1)}, bf16[2,256,256]{2,1,0:T(8,128)(2,1)}, u32[]{:S(2)}, u32[]{:S(2)}) collective-permute-start(bf16[2,256,256]{2,1,0:T(8,128)(2,1)} %get-tuple-element.11), channel_id=1, source_target_pairs={{8,0},{12,4},{16,8},{20,12},{24,16},{28,20},{9,1},{13,5},{17,9},{2... | collective-permute-start | bytes 786440 | tf_op jit(solution)/shard_map/ppermute | solution.py:16
  100.2 1.9 %collective-permute-start.7 = (bf16[2,256,256]{2,1,0:T(8,128)(2,1)}, bf16[2,256,256]{2,1,0:T(8,128)(2,1)}, u32[]{:S(2)}, u32[]{:S(2)}) collective-permute-start(bf16[2,256,256]{2,1,0:T(8,128)(2,1)} %get-tuple-element.10), channel_id=1, source_target_pairs={{4,0},{8,4},{12,8},{16,12},{20,16},{24,20},{28,24},{5,1},{9,5},{13... | collective-permute-start | bytes 786440 | tf_op jit(solution)/shard_map/ppermute | solution.py:16
  102.2 1.3 %convolution_multiply_fusion = f32[2,128,2,256]{3,1,2,0:T(8,128)} fusion(bf16[1280,2,128,1]{0,2,3,1:T(8,128)(2,1)S(1)} %bitcast.77, bf16[2,2,256,1280]{2,3,1,0:T(8,128)(2,1)S(1)} %fusion.4), kind=kOutput, calls=%fused_computation.20 | convolution fusion | flops 335675392 | bytes 3801088 | tf_op jit(solution)/shard_map/grse,egd->sgrd/dot_general | solution.py:50
  103.5 2.0 %copy.32 = f32[256,512]{1,0:T(8,128)} copy(f32[256,512]{0,1:T(8,128)} %bitcast.78) | data formatting | bytes 1048576
  105.5 9.2 %collective-permute-done.4 = bf16[2,256,256]{2,1,0:T(8,128)(2,1)S(1)} collective-permute-done((bf16[2,256,256]{2,1,0:T(8,128)(2,1)}, bf16[2,256,256]{2,1,0:T(8,128)(2,1)S(1)}, u32[]{:S(2)}, u32[]{:S(2)}) %collective-permute-start.4) | collective-permute-done | bytes 262176 | tf_op jit(solution)/shard_map/ppermute | solution.py:16
  114.7 3.8 %collective-permute-done.5 = bf16[2,256,256]{2,1,0:T(8,128)(2,1)} collective-permute-done((bf16[2,256,256]{2,1,0:T(8,128)(2,1)}, bf16[2,256,256]{2,1,0:T(8,128)(2,1)}, u32[]{:S(2)}, u32[]{:S(2)}) %collective-permute-start.5) | collective-permute-done | bytes 262176 | tf_op jit(solution)/shard_map/ppermute | solution.py:16
  118.5 0.0 collective-permute-done.6
  118.5 0.0 collective-permute-done.7
  118.5 1.4 %fusion.15 = f32[2,256,256]{2,1,0:T(8,128)S(1)} fusion(f32[1,1280,256]{2,1,0:T(8,128)} %copy.30, f32[1,1280,256]{2,1,0:T(8,128)} %copy.31, bf16[2,256,256]{2,1,0:T(8,128)(2,1)} %collective-permute-done.7, bf16[2,256,256]{2,1,0:T(8,128)(2,1)} %collective-permute-done.6, bf16[2,256,256]{2,1,0:T(8,128)(2,1)} %collective-permute-done.5, ...), kind=kLoop, calls=%fused_computation.26 | loop fusion | flops 1179648 | bytes 4194304 | tf_op jit(solution)/shard_map/add | solution.py:94
  119.9 0.8 slice_bitcast_fusion
  (10 shorter events, 0.1 us)
Async XLA Ops:
  7.2 60.6 %all-gather.2.cloned.1.call-start = ((), (), s32[]{:S(2)}) async-start(), calls=%async_computation | async-start | bytes 3440640 | tf_op jit(solution)/shard_map/all_gather | solution.py:69
  10.0 12.0 %collective-permute-start = (bf16[2,256,256]{1,2,0:T(8,128)(2,1)S(1)}, bf16[2,256,256]{1,2,0:T(8,128)(2,1)S(1)}, u32[]{:S(2)}, u32[]{:S(2)}) collective-permute-start(bf16[2,256,256]{1,2,0:T(8,128)(2,1)S(1)} %pad_maximum_fusion.1), channel_id=1, source_target_pairs={{0,16},{4,20},{8,24},{12,28},{1,17},{5,21},{9,25},{13,29},{2,18},{... | collective-permute-start | bytes 786440 | tf_op jit(solution)/shard_map/ppermute | solution.py:16
  13.1 9.5 %collective-permute-start.1 = (bf16[2,256,256]{1,2,0:T(8,128)(2,1)S(1)}, bf16[2,256,256]{1,2,0:T(8,128)(2,1)S(1)}, u32[]{:S(2)}, u32[]{:S(2)}) collective-permute-start(bf16[2,256,256]{1,2,0:T(8,128)(2,1)S(1)} %pad_maximum_fusion.1), channel_id=1, source_target_pairs={{0,12},{4,16},{8,20},{12,24},{16,28},{1,13},{5,17},{9,21},{13,25},... | collective-permute-start | bytes 786440 | tf_op jit(solution)/shard_map/ppermute | solution.py:16
  15.0 10.4 %collective-permute-start.2 = (bf16[2,256,256]{1,2,0:T(8,128)(2,1)S(1)}, bf16[2,256,256]{1,2,0:T(8,128)(2,1)S(1)}, u32[]{:S(2)}, u32[]{:S(2)}) collective-permute-start(bf16[2,256,256]{1,2,0:T(8,128)(2,1)S(1)} %pad_maximum_fusion.1), channel_id=1, source_target_pairs={{0,8},{4,12},{8,16},{12,20},{16,24},{20,28},{1,9},{5,13},{9,17},{1... | collective-permute-start | bytes 786440 | tf_op jit(solution)/shard_map/ppermute | solution.py:16
  17.0 10.3 %collective-permute-start.3 = (bf16[2,256,256]{1,2,0:T(8,128)(2,1)S(1)}, bf16[2,256,256]{1,2,0:T(8,128)(2,1)S(1)}, u32[]{:S(2)}, u32[]{:S(2)}) collective-permute-start(bf16[2,256,256]{1,2,0:T(8,128)(2,1)S(1)} %pad_maximum_fusion.1), channel_id=1, source_target_pairs={{0,4},{4,8},{8,12},{12,16},{16,20},{20,24},{24,28},{1,5},{5,9},{9,... | collective-permute-start | bytes 786440 | tf_op jit(solution)/shard_map/ppermute | solution.py:16
  20.7 56.4 %copy-start = (pred[256,1280]{0,1:T(8,128)(4,1)}, pred[256,1280]{0,1:T(8,128)(4,1)S(1)}, u32[]{:S(2)}) copy-start(pred[256,1280]{0,1:T(8,128)(4,1)S(1)} %and_and_fusion) | copy-start | bytes 983044
  77.1 4.3 %slice-start = ((s8[5242880]{0:T(1024)(128)(4,1)}), s8[4194304]{0:T(1024)(128)(4,1)S(1)}, s32[]{:S(2)}) async-start(s8[5242880]{0:T(1024)(128)(4,1)} %bitcast.72), calls=%async_computation.1 | async-start | bytes 8388608
  77.1 4.3 %slice-start.1 = ((s8[5242880]{0:T(1024)(128)(4,1)}), s8[1048576]{0:T(1024)(128)(4,1)S(1)}, s32[]{:S(2)}) async-start(s8[5242880]{0:T(1024)(128)(4,1)} %bitcast.72), calls=%async_computation.2 | async-start | bytes 2097152
  94.2 20.5 %collective-permute-start.4 = (bf16[2,256,256]{2,1,0:T(8,128)(2,1)}, bf16[2,256,256]{2,1,0:T(8,128)(2,1)S(1)}, u32[]{:S(2)}, u32[]{:S(2)}) collective-permute-start(bf16[2,256,256]{2,1,0:T(8,128)(2,1)} %get-tuple-element.9), channel_id=1, source_target_pairs={{16,0},{20,4},{24,8},{28,12},{17,1},{21,5},{25,9},{29,13},{18,2},{... | collective-permute-start | bytes 786440 | tf_op jit(solution)/shard_map/ppermute | solution.py:16
  95.5 23.0 %collective-permute-start.5 = (bf16[2,256,256]{2,1,0:T(8,128)(2,1)}, bf16[2,256,256]{2,1,0:T(8,128)(2,1)}, u32[]{:S(2)}, u32[]{:S(2)}) collective-permute-start(bf16[2,256,256]{2,1,0:T(8,128)(2,1)} %get-tuple-element.12), channel_id=1, source_target_pairs={{12,0},{16,4},{20,8},{24,12},{28,16},{13,1},{17,5},{21,9},{25,13},... | collective-permute-start | bytes 786440 | tf_op jit(solution)/shard_map/ppermute | solution.py:16
  98.3 20.2 %collective-permute-start.6 = (bf16[2,256,256]{2,1,0:T(8,128)(2,1)}, bf16[2,256,256]{2,1,0:T(8,128)(2,1)}, u32[]{:S(2)}, u32[]{:S(2)}) collective-permute-start(bf16[2,256,256]{2,1,0:T(8,128)(2,1)} %get-tuple-element.11), channel_id=1, source_target_pairs={{8,0},{12,4},{16,8},{20,12},{24,16},{28,20},{9,1},{13,5},{17,9},{2... | collective-permute-start | bytes 786440 | tf_op jit(solution)/shard_map/ppermute | solution.py:16
  100.2 18.3 %collective-permute-start.7 = (bf16[2,256,256]{2,1,0:T(8,128)(2,1)}, bf16[2,256,256]{2,1,0:T(8,128)(2,1)}, u32[]{:S(2)}, u32[]{:S(2)}) collective-permute-start(bf16[2,256,256]{2,1,0:T(8,128)(2,1)} %get-tuple-element.10), channel_id=1, source_target_pairs={{4,0},{8,4},{12,8},{16,12},{20,16},{24,20},{28,24},{5,1},{9,5},{13... | collective-permute-start | bytes 786440 | tf_op jit(solution)/shard_map/ppermute | solution.py:16
Sparse Core Ops, SparseCore 0:
  9.6 58.1 all-gather.1
where the time goes:
time: 128 us
  waiting for transfers between devices  54.5 us (43%)
  matrix products  21.6 us (17%)
  starting transfers between devices  17.7 us (14%)
  between operations  14.3 us (11%)
  local copies, waits for them, and re-layouts  13 us (10%)
  other arithmetic  6.59 us (5%)
    all_gather x1, waiting for transfers between devices, on_device(): lax.all_gather(grad_out, 'tp', axis=0, tiled=True)  35.5 us
    ppermute x8, waiting for transfers between devices, passed_along(): return lax.ppermute(block, axis, route)  18.3 us
    ppermute x8, starting transfers between devices, passed_along(): return lax.ppermute(block, axis, route)  17.6 us
    another operation x2, local copies, waits for them, and re-layouts, on_device(): span_grads = jnp.stack([grad_key, grad_value])  5.6 us
    dot_general x1, matrix products, on_device(): lax.dot_general(lax.all_gather(grad_out, 'tp', axis=0, tiled=True), out_w...  5.01 us
    sub x1, matrix products, band_grads(): weights = jnp.where(allowed, jnp.exp(scores - row_max), 0.0)  4.82 us
    dot_general x1, matrix products, band_grads(): jnp.einsum('sgrd,egd->grse', dout_heads, value_heads, preferred_element_t...  4.3 us
    dot_general x1, matrix products, band_grads(): jnp.einsum('grse,sgrd->egd', probs_low, dout_heads, preferred_element_typ...  4.13 us
  transfers between devices with their start and end apart: 9, of which 6 were waited for; matrix products, arithmetic and copies ran while one was open for 10% of the time, Pallas kernels for 0%

commit v1 on v0

v1 whole, which is shorter than its diff:
```python
import functools

import jax
import jax.numpy as jnp
from jax import lax
from jax.experimental import pallas as pl
from jax.experimental.pallas import tpu as pltpu
from jax.sharding import PartitionSpec as P

HD = 128
WIN = 1024
SPAN_BLOCKS = 5
SCALE = 168.0 ** (-0.5)
NT = (((1,), (1,)), ((), ()))
NN = (((1,), (0,)), ((), ()))
F32 = jnp.float32
BF16 = jnp.bfloat16


def dot(a, b, dims):
    return lax.dot_general(a, b, dims, preferred_element_type=F32)


def pieces(x):
    hi = x.astype(BF16)
    rest = x - hi.astype(F32)
    mid = rest.astype(BF16)
    low = (rest - mid.astype(F32)).astype(BF16)
    return hi.astype(F32), mid.astype(F32), low.astype(F32)


def spread(x, first, width):
    lane = lax.broadcasted_iota(jnp.int32, (x.shape[0], width), 1)
    out = jnp.zeros((x.shape[0], width), F32)
    for n, piece in enumerate(pieces(x)):
        out = jnp.where(lane == first + n, piece, out)
    return out


def minus_ones(rows, first):
    lane = lax.broadcasted_iota(jnp.int32, (rows, HD), 1)
    return jnp.where((lane >= first) & (lane < first + 3), -1.0, 0.0).astype(BF16)


def params(limit=48 * 2**20):
    return pltpu.CompilerParams(vmem_limit_bytes=limit)


def probs_kernel(info, own, peer, recv, exch, probs, mixed, stats, span):
    head = pl.program_id(0)
    rows = own.shape[0]
    width = recv.shape[1]
    kv_width = width // 2
    core, shard = info[0], info[1]

    @pl.when(head == 0)
    def _():
        stats[...] = jnp.zeros_like(stats)
        span[4 * rows :, :] = own[:, :width]
        span[rows : 2 * rows, :] = exch[:rows, :]

        @pl.when(core == 0)
        def _():
            span[:rows, :] = exch[rows:, :]
            span[2 * rows : 4 * rows, :] = recv[...]

        @pl.when(core == 1)
        def _():
            span[:rows, :] = recv[:rows, :]
            span[2 * rows : 3 * rows, :] = exch[rows:, :]
            span[3 * rows : 4 * rows, :] = peer[:, :width]

    group = head // 2
    key = span[:, pl.ds(pl.multiple_of(group * HD, HD), HD)]
    value = span[:, pl.ds(pl.multiple_of(kv_width + group * HD, HD), HD)]
    query = own[:, pl.ds(pl.multiple_of(width + head * HD, HD), HD)]
    scores = dot(query, key, NT) * SCALE
    row = lax.broadcasted_iota(jnp.int32, (rows, 1), 0)
    col = lax.broadcasted_iota(jnp.int32, scores.shape, 1)
    first = jnp.maximum(row + 1, (SPAN_BLOCKS - 1 - shard) * rows)
    scores = jnp.where((col >= first) & (col <= row + WIN), scores, -1e30)
    top = jnp.max(scores, axis=1, keepdims=True)
    weights = jnp.exp(scores - top)
    total = jnp.sum(weights, axis=1, keepdims=True)
    probability = (weights * (1.0 / total)).astype(BF16)
    probs[0] = probability
    mixed[...] = dot(probability, value, NN)
    level = (top + jnp.log(total)) * (1.0 / SCALE)
    stats[...] += spread(level, 8 * head, HD).astype(BF16)


def attention_probs(info, own, peer, recv, exch):
    rows = own.shape[0]
    width = recv.shape[1]
    heads = (own.shape[1] - width) // HD
    span_rows = SPAN_BLOCKS * rows
    whole = lambda a: pl.BlockSpec(a.shape, lambda h, info: (0,) * a.ndim)
    return pl.pallas_call(
        probs_kernel,
        out_shape=(
            jax.ShapeDtypeStruct((heads, rows, span_rows), BF16),
            jax.ShapeDtypeStruct((rows, heads * HD), F32),
            jax.ShapeDtypeStruct((rows, HD), BF16),
            jax.ShapeDtypeStruct((span_rows, width), BF16),
        ),
        grid_spec=pltpu.PrefetchScalarGridSpec(
            num_scalar_prefetch=1,
            grid=(heads,),
            in_specs=[whole(own), whole(peer), whole(recv), whole(exch)],
            out_specs=(
                pl.BlockSpec((1, rows, span_rows), lambda h, info: (h, 0, 0)),
                pl.BlockSpec((rows, HD), lambda h, info: (0, h)),
                pl.BlockSpec((rows, HD), lambda h, info: (0, 0)),
                pl.BlockSpec((span_rows, width), lambda h, info: (0, 0)),
            ),
        ),
        compiler_params=params(),
        cost_estimate=pl.CostEstimate(
            flops=4 * heads * rows * span_rows * HD, bytes_accessed=8 * 2**20, transcendentals=heads * rows * span_rows
        ),
        name="attention_probs",
    )(info, own, peer, recv, exch)


def dout_kernel(slots, info, *refs):
    count = len(slots)
    sources = refs[: sum(slots.values())]
    weight, mixed, stats, pay, acc = refs[len(sources) :]
    step = pl.program_id(0)
    parts = []
    at = 0
    for n in slots.values():
        part = sources[at][...]
        for other in sources[at + 1 : at + n]:
            part = part + other[...]
        parts.append(part)
        at += n
    block = parts[0] if count == 1 else jnp.concatenate(parts, axis=0)

    @pl.when(step == 0)
    def _():
        acc[...] = jnp.zeros_like(acc)

    acc[...] += dot(block, weight[...], NT)

    @pl.when(step == pl.num_programs(0) - 1)
    def _():
        heads = weight.shape[0] // HD
        part_rows = acc.shape[0] // count
        for n, slot in enumerate(slots):
            start = pl.multiple_of(info[2 + slot], 16)
            dout = acc[n * part_rows : (n + 1) * part_rows, :].astype(BF16)
            row_stats = stats[pl.ds(start, part_rows), :].astype(F32)
            out_rows = mixed[pl.ds(start, part_rows), :]
            for head in range(heads):
                cols = slice(head * HD, (head + 1) * HD)
                delta = jnp.sum(dout[:, cols].astype(F32) * out_rows[:, cols], axis=1, keepdims=True)
                row_stats = row_stats + spread(delta, 8 * head + 3, HD)
            pay[n * part_rows : (n + 1) * part_rows, : heads * HD] = dout
            pay[n * part_rows : (n + 1) * part_rows, heads * HD :] = row_stats.astype(BF16)


def dout_rows(info, slots, sources, weight, mixed, stats, steps=3):
    rows = sources[0].shape[0]
    total = rows * len(slots)
    depth = weight.shape[1] // steps
    heads = weight.shape[0] // HD
    whole = lambda a: pl.BlockSpec(a.shape, lambda s, info: (0,) * a.ndim)
    return pl.pallas_call(
        functools.partial(dout_kernel, slots),
        out_shape=jax.ShapeDtypeStruct((total, (heads + 1) * HD), BF16),
        grid_spec=pltpu.PrefetchScalarGridSpec(
            num_scalar_prefetch=1,
            grid=(steps,),
            in_specs=[pl.BlockSpec((rows, depth), lambda s, info: (0, s)) for _ in sources]
            + [pl.BlockSpec((weight.shape[0], depth), lambda s, info: (0, s)), whole(mixed), whole(stats)],
            out_specs=pl.BlockSpec((total, (heads + 1) * HD), lambda s, info: (0, 0)),
            scratch_shapes=[pltpu.VMEM((total, heads * HD), F32)],
        ),
        compiler_params=params(),
        cost_estimate=pl.CostEstimate(
            flops=2 * total * weight.size, bytes_accessed=2 * weight.size + 4 * total * weight.shape[1], transcendentals=0
        ),
        name="dout_rows",
    )(info, *sources, weight, mixed, stats)


def query_kernel(slots, info, pay, probs, span, *refs):
    head = pl.program_id(0)
    before, out = refs if len(refs) == 2 else (None, refs[0])
    heads = pl.num_programs(0)
    kv_width = span.shape[1] // 2
    group = head // 2
    key = span[:, pl.ds(pl.multiple_of(group * HD, HD), HD)]
    value = span[:, pl.ds(pl.multiple_of(kv_width + group * HD, HD), HD)]
    dout = pay[:, pl.ds(pl.multiple_of(head * HD, HD), HD)]
    extra = pay[:, pay.shape[1] - HD :]
    value_more = jnp.concatenate([value, minus_ones(value.shape[0], 8 * head + 3)], axis=1)
    centred = dot(jnp.concatenate([dout, extra], axis=1), value_more, NT)
    part_rows = pay.shape[0] // len(slots)
    if before is not None:
        out[...] = before[...]
    else:
        out[...] = jnp.zeros_like(out)
    parts = []
    for n, slot in enumerate(slots):
        start = pl.multiple_of(info[2 + slot], 16)
        weights = probs[0, pl.ds(start, part_rows), :].astype(F32)
        parts.append((weights * centred[n * part_rows : (n + 1) * part_rows, :]).astype(BF16))
    dscores = parts[0] if len(parts) == 1 else jnp.concatenate(parts, axis=0)
    grads = dot(dscores, key, NN) * SCALE
    for n, slot in enumerate(slots):
        start = pl.multiple_of(info[2 + slot], 16)
        out[pl.ds(start, part_rows), :] = grads[n * part_rows : (n + 1) * part_rows, :]


def query_grads(info, slots, pay, probs, span, before=None):
    heads, rows, span_rows = probs.shape
    whole = lambda a: pl.BlockSpec(a.shape, lambda h, info: (0,) * a.ndim)
    column = pl.BlockSpec((rows, HD), lambda h, info: (0, h))
    return pl.pallas_call(
        functools.partial(query_kernel, slots),
        out_shape=jax.ShapeDtypeStruct((rows, heads * HD), F32),
        grid_spec=pltpu.PrefetchScalarGridSpec(
            num_scalar_prefetch=1,
            grid=(heads,),
            in_specs=[whole(pay), pl.BlockSpec((1, rows, span_rows), lambda h, info: (h, 0, 0)), whole(span)]
            + ([] if before is None else [column]),
            out_specs=column,
        ),
        compiler_params=params(),
        cost_estimate=pl.CostEstimate(
            flops=4 * heads * pay.shape[0] * span_rows * HD, bytes_accessed=5 * 2**20, transcendentals=0
        ),
        name="query_grads",
    )(info, pay, probs, span, *(() if before is None else (before,)))


def key_kernel(
    slots, with_before, info, own, peer, recv_q, exch_q, pay, pay_peer, pay_recv, pay_exch, *refs
):
    if with_before:
        before_k, before_v, grad_k, grad_v, q_cat, d_cat = refs
    else:
        grad_k, grad_v, q_cat, d_cat = refs
    core = info[0]
    rows = own.shape[0]
    kv_width = grad_k.shape[1]
    width = recv_q.shape[1]
    q_at = own.shape[1] - width
    total = pay.shape[0]
    part_rows = total // len(slots)

    def put(distance, q_ref, q_row, q_col, d_ref, d_row):
        for n, slot in enumerate(slots):
            start = pl.multiple_of(info[2 + slot] + q_row, 16)
            at = distance * total + n * part_rows
            q_cat[at : at + part_rows, :] = q_ref[pl.ds(start, part_rows), q_col : q_col + width]
        d_cat[distance * total : (distance + 1) * total, :] = d_ref[d_row : d_row + total, :]

    put(0, own, 0, q_at, pay, 0)
    put(3, recv_q, rows, 0, pay_recv, total)

    @pl.when(core == 0)
    def _():
        put(1, peer, 0, q_at, pay_peer, 0)
        put(2, recv_q, 0, 0, pay_recv, 0)
        put(4, exch_q, rows, 0, pay_exch, total)

    @pl.when(core == 1)
    def _():
        put(1, exch_q, 0, 0, pay_exch, 0)
        put(2, exch_q, rows, 0, pay_exch, total)
        put(4, recv_q, 0, 0, pay_recv, 0)

    lanes = SPAN_BLOCKS * total
    lane = lax.broadcasted_iota(jnp.int32, (1, lanes), 1)
    low = jnp.zeros((1, lanes), jnp.int32)
    high = jnp.full((1, lanes), rows, jnp.int32)
    for n, slot in enumerate(slots):
        at = n * part_rows
        inside = (lane >= at) & (lane < at + part_rows)
        high = jnp.where(inside, lane - at + info[2 + slot], high)
        at = (SPAN_BLOCKS - 1) * total + n * part_rows
        inside = (lane >= at) & (lane < at + part_rows)
        low = jnp.where(inside, lane - at + info[2 + slot] + 1, low)
    key_row = lax.broadcasted_iota(jnp.int32, (rows, lanes), 0)
    allowed = (key_row >= low) & (key_row <= high)
    extra = d_cat[:, width:]
    for group in range(kv_width // HD):
        cols = slice(group * HD, (group + 1) * HD)
        key = own[:, group * HD : (group + 1) * HD]
        value = own[:, kv_width + group * HD : kv_width + (group + 1) * HD]
        sum_k = None
        sum_v = None
        for head in (2 * group, 2 * group + 1):
            query = q_cat[:, head * HD : (head + 1) * HD]
            dout = d_cat[:, head * HD : (head + 1) * HD]
            scores = dot(
                jnp.concatenate([key, minus_ones(rows, 8 * head)], axis=1),
                jnp.concatenate([query, extra], axis=1),
                NT,
            )
            probability = jnp.where(allowed, jnp.exp(scores * SCALE), 0.0)
            centred = dot(
                jnp.concatenate([value, minus_ones(rows, 8 * head + 3)], axis=1),
                jnp.concatenate([dout, extra], axis=1),
                NT,
            )
            dscores = (probability * centred).astype(BF16)
            term_v = dot(probability.astype(BF16), dout, NN)
            term_k = dot(dscores, query, NN)
            sum_v = term_v if sum_v is None else sum_v + term_v
            sum_k = term_k if sum_k is None else sum_k + term_k
        sum_k = sum_k * SCALE
        if with_before:
            sum_k = sum_k + before_k[:, cols]
            sum_v = sum_v + before_v[:, cols]
        grad_k[:, cols] = sum_k
        grad_v[:, cols] = sum_v


def key_grads(info, slots, own, peer, recv_q, exch_q, pays, before=()):
    rows = own.shape[0]
    width = recv_q.shape[1]
    kv_width = (own.shape[1] - width) // 2
    total = pays[0].shape[0]
    vmem = pl.BlockSpec(memory_space=pltpu.VMEM)
    arrays = (own, peer, recv_q, exch_q, *pays, *before)
    return pl.pallas_call(
        functools.partial(key_kernel, slots, bool(before)),
        out_shape=(jax.ShapeDtypeStruct((rows, kv_width), F32),) * 2,
        in_specs=[pl.BlockSpec(memory_space=pltpu.SMEM)] + [vmem] * len(arrays),
        out_specs=(vmem, vmem),
        scratch_shapes=[
            pltpu.VMEM((SPAN_BLOCKS * total, width), BF16),
            pltpu.VMEM((SPAN_BLOCKS * total, width + HD), BF16),
        ],
        compiler_params=params(),
        cost_estimate=pl.CostEstimate(
            flops=8 * rows * width * SPAN_BLOCKS * total, bytes_accessed=6 * 2**20, transcendentals=4 * rows * total * 5
        ),
        name="key_grads",
    )(info, *arrays)


def on_device(ctx, queries, keys, values, grad_out, out_weight):
    rows = queries.shape[0]
    slot_rows = grad_out.shape[0]
    width = queries.shape[1]
    chips = ctx // 2
    swap = [(i, i ^ 1) for i in range(ctx)]
    ahead = [(2 * c + k, 2 * (c + 1 + k) + k) for c in range(chips) for k in (0, 1) if c + 1 + k < chips]
    back = [(d, s) for s, d in ahead]
    along = lambda x, pairs: lax.ppermute(x, "ctx", pairs)
    over = lambda x, pairs: lax.ppermute(x, "tp", pairs)

    shard = lax.axis_index("ctx")
    tp = lax.axis_index("tp")
    low_side = tp < 2
    slot_at = [tp, tp ^ 1, jnp.where(low_side, 2, 1), jnp.where(low_side, 3, 0)]
    info = jnp.stack([shard % 2, shard] + [s * slot_rows for s in slot_at]).astype(jnp.int32)

    middle = [(1, 2), (2, 1)]
    ends = [(0, 1), (1, 0), (2, 3), (3, 2)]
    outward = [(1, 0), (2, 3)]
    mid_first = over(grad_out, middle)
    end_first = over(grad_out, ends)

    own = jnp.concatenate([keys, values, queries], axis=1)
    peer = along(own, swap)
    kv_width = own.shape[1] - width
    kv_pair = jnp.concatenate([own[:, :kv_width], peer[:, :kv_width]], axis=0)
    q_pair = jnp.concatenate([own[:, kv_width:], peer[:, kv_width:]], axis=0)
    recv_kv = along(kv_pair, ahead)
    recv_q = along(q_pair, back)
    exch_kv = along(recv_kv, swap)
    exch_q = along(recv_q, swap)

    out_second = over(mid_first, outward)
    mid_second = over(end_first, middle)
    out_third = over(mid_second, outward)

    probs, mixed, stats, span = attention_probs(info, own, peer, recv_kv, exch_kv)

    def send(pay):
        pay_peer = along(pay, swap)
        pay_recv = along(jnp.concatenate([pay, pay_peer], axis=0), back)
        pay_exch = along(pay_recv, swap)
        return pay, pay_peer, pay_recv, pay_exch

    pay = dout_rows(
        info, {0: 1, 1: 1, 2: 2}, [grad_out, end_first, mid_first, out_second], out_weight, mixed, stats
    )
    pays = send(pay)
    early = (0, 1, 2)
    grad_q = query_grads(info, early, pay, probs, span)
    before = key_grads(info, early, own, peer, recv_q, exch_q, pays)

    pay = dout_rows(info, {3: 2}, [mid_second, out_third], out_weight, mixed, stats)
    pays = send(pay)
    grad_q = query_grads(info, (3,), pay, probs, span, grad_q)
    grad_k, grad_v = key_grads(info, (3,), own, peer, recv_q, exch_q, pays, before)
    return (grad_q, grad_k, grad_v)


def solution(mesh):
    in_specs = (
        P("ctx", "tp"),
        P("ctx", "tp"),
        P("ctx", "tp"),
        P(("ctx", "tp"), None),
        P("tp", None),
    )
    out_specs = (P("ctx", "tp"), P("ctx", "tp"), P("ctx", "tp"))
    return jax.shard_map(
        functools.partial(on_device, mesh.shape["ctx"]),
        mesh=mesh,
        in_specs=in_specs,
        out_specs=out_specs,
        check_vma=False,
    )
```

time: 128 us -> 106 us (0.83)
  Pallas kernels: 0 us -> 30.2 us
  matrix products: 21.6 us -> 0 us
  between operations: 14.3 us -> 0.82 us
  local copies, waits for them, and re-layouts: 13 us -> 3.01 us
  waiting for transfers between devices: 54.5 us -> 48.2 us
  other arithmetic: 6.59 us -> 1.1 us
  starting transfers between devices: 17.7 us -> 21.4 us
    all_gather x1 -> x0, waiting for transfers between devices: 35.5 us -> none  [on_device(): lax.all_gather(grad_out, 'tp', axis=0, tiled=True)]
    pallas_call x0 -> x7, Pallas kernels: none -> 30.2 us  [the longest x2 11.2 us: dout_rows(): pl.pallas_call(functools.partial(dout_kernel, slots), out_shape=jax.Shape...]
    ppermute x8 -> x16, waiting for transfers between devices: 18.3 us -> 48.2 us  [the longest x11 33.2 us: on_device(): along = lambda x, pairs: lax.ppermute(x, 'ctx', pairs)]
    dot_general x5 -> x0, matrix products: 16.8 us -> none  [the longest x1 5.01 us: on_device(): lax.dot_general(lax.all_gather(grad_out, 'tp', axis=0, tiled=True), out_w...]
    another operation x2 -> x1, local copies, waits for them, and re-layouts: 5.6 us -> 0.08 us  [on_device(): jnp.stack([shard % 2, shard] + [s * slot_rows for s in slot_at])]
    sub x1 -> x0, matrix products: 4.82 us -> none  [band_grads(): weights = jnp.where(allowed, jnp.exp(scores - row_max), 0.0)]
    ppermute x8 -> x16, starting transfers between devices: 17.6 us -> 21.4 us  [the longest x11 15.3 us: on_device(): along = lambda x, pairs: lax.ppermute(x, 'ctx', pairs)]
    unnamed x13 -> x8, local copies, waits for them, and re-layouts: 4.13 us -> 1.85 us
  transfers between devices with their start and end apart: 9 -> 16, of which waited for: 6 -> 7; matrix products, arithmetic and copies ran while one was open for 10% -> 1% of each run, Pallas kernels for 0% -> 26%
where the time goes in v1:
time: 106 us; the launch traced here: 105 us
  waiting for transfers between devices  48.2 us (45%)
  Pallas kernels  30.2 us (28%)
  starting transfers between devices  21.4 us (20%)
  local copies, waits for them, and re-layouts  3.01 us (3%)
  other arithmetic  1.1 us (1%)
    ppermute x11, waiting for transfers between devices, on_device(): along = lambda x, pairs: lax.ppermute(x, 'ctx', pairs)  33.2 us
    ppermute x11, starting transfers between devices, on_device(): along = lambda x, pairs: lax.ppermute(x, 'ctx', pairs)  15.3 us
    ppermute x5, waiting for transfers between devices, on_device(): over = lambda x, pairs: lax.ppermute(x, 'tp', pairs)  15 us
    pallas_call x2, Pallas kernels, dout_rows(): pl.pallas_call(functools.partial(dout_kernel, slots), out_shape=jax.Shape...  11.2 us
    pallas_call x1, Pallas kernels, attention_probs(): pl.pallas_call(probs_kernel, out_shape=(jax.ShapeDtypeStruct((heads, rows...  6.97 us
    pallas_call x2, Pallas kernels, query_grads(): pl.pallas_call(functools.partial(query_kernel, slots), out_shape=jax.Shap...  6.16 us
    ppermute x5, starting transfers between devices, on_device(): over = lambda x, pairs: lax.ppermute(x, 'tp', pairs)  6.08 us
    pallas_call x2, Pallas kernels, key_grads(): pl.pallas_call(functools.partial(key_kernel, slots, bool(before)), out_sh...  5.89 us
  transfers between devices with their start and end apart: 16, of which 7 were waited for; matrix products, arithmetic and copies ran while one was open for 1% of the time, Pallas kernels for 26%

profile of v1, /device:TPU:3, one launch (start us, length us, event | category | flops | bytes accessed | tf_op | source)
XLA Modules:
  0.0 104.7 jit_solution(14688140012673749258)
XLA Ops:
  0.6 0.9 constant_dynamic-update-slice_fusion.2
  1.5 0.9 constant_dynamic-update-slice_fusion.1
  2.5 0.0 copy-start.1
  2.5 1.0 constant_dynamic-update-slice_fusion.own
  3.5 0.7 collective-permute-start.3
  4.3 1.3 %collective-permute-start = (bf16[64,5376]{1,0:T(8,128)(2,1)}, bf16[64,5376]{1,0:T(8,128)(2,1)S(1)}, u32[]{:S(2)}, u32[]{:S(2)}) collective-permute-start(bf16[64,5376]{1,0:T(8,128)(2,1)} %refs_0_.1), channel_id=1, source_target_pairs={{0,1},{1,0},{2,3},{3,2},{4,5},{5,4},{6,7},{7,6},{8,9},{9,8},{10,11... | collective-permute-start | bytes 2064392 | tf_op jit(solution)/shard_map/ppermute | solution.py:356
  5.6 1.5 %collective-permute-start.6 = (bf16[64,5376]{1,0:T(8,128)(2,1)}, bf16[64,5376]{1,0:T(8,128)(2,1)}, u32[]{:S(2)}, u32[]{:S(2)}) collective-permute-start(bf16[64,5376]{1,0:T(8,128)(2,1)} %refs_0_.1), channel_id=1, source_target_pairs={{1,2},{2,1},{5,6},{6,5},{9,10},{10,9},{13,14},{14,13},{17,18},{18,... | collective-permute-start | bytes 2064392 | tf_op jit(solution)/shard_map/ppermute | solution.py:356
  7.1 0.0 collective-permute-done.3.peer
  7.1 1.0 pad_maximum_fusion
  8.1 4.0 %collective-permute-start.4 = (bf16[512,512]{1,0:T(8,128)(2,1)S(1)}, bf16[512,512]{1,0:T(8,128)(2,1)}, u32[]{:S(2)}, u32[]{:S(2)}) collective-permute-start(bf16[512,512]{1,0:T(8,128)(2,1)S(1)} %pad_maximum_fusion), channel_id=1, source_target_pairs={{0,8},{4,20},{8,16},{12,28},{16,24},{1,9},{5,21},{9,17},{13,29},{1... | collective-permute-start | bytes 1572872 | tf_op jit(solution)/shard_map/ppermute | solution.py:355
  12.1 0.0 collective-permute-done.6.refs_2_
  12.1 1.3 %collective-permute-start.7 = (bf16[64,5376]{1,0:T(8,128)(2,1)}, bf16[64,5376]{1,0:T(8,128)(2,1)}, u32[]{:S(2)}, u32[]{:S(2)}) collective-permute-start(bf16[64,5376]{1,0:T(8,128)(2,1)} %collective-permute-done.6.refs_2_), channel_id=1, source_target_pairs={{1,0},{2,3},{5,4},{6,7},{9,8},{10,11},{13,12},{14,15},{17,16},{18,... | collective-permute-start | bytes 2064392 | tf_op jit(solution)/shard_map/ppermute | solution.py:356
  13.4 4.0 %collective-permute-done.4.recv = bf16[512,512]{1,0:T(8,128)(2,1)} collective-permute-done((bf16[512,512]{1,0:T(8,128)(2,1)S(1)}, bf16[512,512]{1,0:T(8,128)(2,1)}, u32[]{:S(2)}, u32[]{:S(2)}) %collective-permute-start.4) | collective-permute-done | bytes 524320 | tf_op jit(solution)/shard_map/ppermute | solution.py:355
  17.4 2.3 %collective-permute-start.5 = (bf16[512,512]{1,0:T(8,128)(2,1)}, bf16[512,512]{1,0:T(8,128)(2,1)}, u32[]{:S(2)}, u32[]{:S(2)}) collective-permute-start(bf16[512,512]{1,0:T(8,128)(2,1)} %collective-permute-done.4.recv), channel_id=1, source_target_pairs={{0,4},{4,0},{8,12},{12,8},{16,20},{20,16},{24,28},{28,24},{1,5},{5... | collective-permute-start | bytes 1572872 | tf_op jit(solution)/shard_map/ppermute | solution.py:355
  19.7 1.8 %collective-permute-done.refs_1_ = bf16[64,5376]{1,0:T(8,128)(2,1)S(1)} collective-permute-done((bf16[64,5376]{1,0:T(8,128)(2,1)}, bf16[64,5376]{1,0:T(8,128)(2,1)S(1)}, u32[]{:S(2)}, u32[]{:S(2)}) %collective-permute-start) | collective-permute-done | bytes 688160 | tf_op jit(solution)/shard_map/ppermute | solution.py:356
  21.5 0.7 collective-permute-start.1
  22.2 0.1 stack.27.info
  22.3 0.0 collective-permute-done.5.exch
  22.3 7.0 %attention_probs.1 = (bf16[4,256,1280]{2,1,0:T(8,128)(2,1)}, f32[256,512]{1,0:T(8,128)S(1)}, bf16[256,128]{1,0:T(8,128)(2,1)S(1)}, bf16[1280,512]{1,0:T(8,128)(2,1)S(1)}) custom-call(s32[6]{0:T(128)S(1)} %stack.27.info, bf16[256,1024]{1,0:T(8,128)(2,1)S(1)} %constant_dynamic-update-slice_fusion.own, bf16[256,1024]{1,0:T(8,128)(2,1)S(1)} %collective-permute-done.3.peer, ...), custom_call_target="tpu_custom_call" | custom-call | flops 671088640 | bytes 8388608 | tf_op jit(solution)/shard_map/attention_probs/pallas_call | solution.py:98
  29.3 13.2 %collective-permute-done.7.refs_3_ = bf16[64,5376]{1,0:T(8,128)(2,1)} collective-permute-done((bf16[64,5376]{1,0:T(8,128)(2,1)}, bf16[64,5376]{1,0:T(8,128)(2,1)}, u32[]{:S(2)}, u32[]{:S(2)}) %collective-permute-start.7) | collective-permute-done | bytes 688160 | tf_op jit(solution)/shard_map/ppermute | solution.py:356
  42.5 0.0 copy-done.1
  42.5 0.0 copy-start.2
  42.5 6.0 %dout_rows.3.pay = bf16[192,640]{1,0:T(8,128)(2,1)S(1)} custom-call(s32[6]{0:T(128)S(1)} %stack.27.info, bf16[64,5376]{1,0:T(8,128)(2,1)S(1)} %copy-done.1, bf16[64,5376]{1,0:T(8,128)(2,1)S(1)} %collective-permute-done.refs_1_, bf16[64,5376]{1,0:T(8,128)(2,1)} %collective-permute-done.6.refs_2_, bf16[64,5376]{1,0:T(8,128)(2,1)} %collective-permute-done.7.refs_3_, ...), custom_call_target="tpu_custom_call" | custom-call | flops 1056964608 | bytes 9633792 | tf_op jit(solution)/shard_map/dout_rows/pallas_call | solution.py:169
  48.5 1.5 %collective-permute-start.13 = (bf16[192,640]{1,0:T(8,128)(2,1)S(1)}, bf16[192,640]{1,0:T(8,128)(2,1)S(1)}, u32[]{:S(2)}, u32[]{:S(2)}) collective-permute-start(bf16[192,640]{1,0:T(8,128)(2,1)S(1)} %dout_rows.3.pay), channel_id=1, source_target_pairs={{0,4},{4,0},{8,12},{12,8},{16,20},{20,16},{24,28},{28,24},{1,5},{5... | collective-permute-start | bytes 737288 | tf_op jit(solution)/shard_map/ppermute | solution.py:355
  50.0 0.0 collective-permute-done.1.refs_0_
  50.0 1.3 %collective-permute-start.2 = (bf16[64,5376]{1,0:T(8,128)(2,1)S(1)}, bf16[64,5376]{1,0:T(8,128)(2,1)S(1)}, u32[]{:S(2)}, u32[]{:S(2)}) collective-permute-start(bf16[64,5376]{1,0:T(8,128)(2,1)S(1)} %collective-permute-done.1.refs_0_), channel_id=1, source_target_pairs={{1,0},{2,3},{5,4},{6,7},{9,8},{10,11},{13,12},{14,15},{17,16},{18,... | collective-permute-start | bytes 2064392 | tf_op jit(solution)/shard_map/ppermute | solution.py:356
  51.3 0.0 copy-done.2
  51.3 1.3 %collective-permute-start.8 = (bf16[512,512]{1,0:T(8,128)(2,1)S(1)}, bf16[512,512]{1,0:T(8,128)(2,1)S(1)}, u32[]{:S(2)}, u32[]{:S(2)}) collective-permute-start(bf16[512,512]{1,0:T(8,128)(2,1)S(1)} %pad_maximum_fusion.1), channel_id=1, source_target_pairs={{8,0},{20,4},{16,8},{28,12},{24,16},{9,1},{21,5},{17,9},{29,13},{2... | collective-permute-start | bytes 1572872 | tf_op jit(solution)/shard_map/ppermute | solution.py:355
  52.6 0.0 collective-permute-done.13.pay_peer
  52.7 0.0 copy-start
  52.7 1.6 %collective-permute-start.14 = (bf16[384,640]{1,0:T(8,128)(2,1)S(1)}, bf16[384,640]{1,0:T(8,128)(2,1)S(1)}, u32[]{:S(2)}, u32[]{:S(2)}) collective-permute-start(bf16[384,640]{1,0:T(8,128)(2,1)S(1)} %pad_maximum_fusion.2), channel_id=1, source_target_pairs={{8,0},{20,4},{16,8},{28,12},{24,16},{9,1},{21,5},{17,9},{29,13},{2... | collective-permute-start | bytes 1474568 | tf_op jit(solution)/shard_map/ppermute | solution.py:355
  54.3 17.9 %collective-permute-done.8.recv_q = bf16[512,512]{1,0:T(8,128)(2,1)S(1)} collective-permute-done((bf16[512,512]{1,0:T(8,128)(2,1)S(1)}, bf16[512,512]{1,0:T(8,128)(2,1)S(1)}, u32[]{:S(2)}, u32[]{:S(2)}) %collective-permute-start.8) | collective-permute-done | bytes 524320 | tf_op jit(solution)/shard_map/ppermute | solution.py:355
  72.1 0.0 collective-permute-start.9
  72.1 5.3 %collective-permute-done.14.pay_recv = bf16[384,640]{1,0:T(8,128)(2,1)S(1)} collective-permute-done((bf16[384,640]{1,0:T(8,128)(2,1)S(1)}, bf16[384,640]{1,0:T(8,128)(2,1)S(1)}, u32[]{:S(2)}, u32[]{:S(2)}) %collective-permute-start.14) | collective-permute-done | bytes 491552 | tf_op jit(solution)/shard_map/ppermute | solution.py:355
  77.4 0.0 collective-permute-start.15
  77.4 0.0 collective-permute-done.2.refs_1_
  77.4 5.2 %dout_rows.2.pay = bf16[64,640]{1,0:T(8,128)(2,1)S(1)} custom-call(s32[6]{0:T(128)S(1)} %stack.27.info, bf16[64,5376]{1,0:T(8,128)(2,1)S(1)} %collective-permute-done.1.refs_0_, bf16[64,5376]{1,0:T(8,128)(2,1)S(1)} %collective-permute-done.2.refs_1_, bf16[512,5376]{1,0:T(8,128)(2,1)} %refs_4_.1, f32[256,512]{1,0:T(8,128)S(1)} %get-tuple-element.11.refs_3_.refs_5_, ...), custom_call_target="tpu_custom_call" | custom-call | flops 352321536 | bytes 6881280 | tf_op jit(solution)/shard_map/dout_rows/pallas_call | solution.py:169
  82.6 0.6 collective-permute-start.10
  83.2 0.9 collective-permute-done.10.pay_peer
  84.1 1.3 %collective-permute-start.11 = (bf16[128,640]{1,0:T(8,128)(2,1)S(1)}, bf16[128,640]{1,0:T(8,128)(2,1)S(1)}, u32[]{:S(2)}, u32[]{:S(2)}) collective-permute-start(bf16[128,640]{1,0:T(8,128)(2,1)S(1)} %pad_maximum_fusion.3), channel_id=1, source_target_pairs={{8,0},{20,4},{16,8},{28,12},{24,16},{9,1},{21,5},{17,9},{29,13},{2... | collective-permute-start | bytes 491528 | tf_op jit(solution)/shard_map/ppermute | solution.py:355
  85.4 5.1 %collective-permute-done.11.pay_recv = bf16[128,640]{1,0:T(8,128)(2,1)S(1)} collective-permute-done((bf16[128,640]{1,0:T(8,128)(2,1)S(1)}, bf16[128,640]{1,0:T(8,128)(2,1)S(1)}, u32[]{:S(2)}, u32[]{:S(2)}) %collective-permute-start.11) | collective-permute-done | bytes 163872 | tf_op jit(solution)/shard_map/ppermute | solution.py:355
  90.5 2.1 %collective-permute-start.12 = (bf16[128,640]{1,0:T(8,128)(2,1)S(1)}, bf16[128,640]{1,0:T(8,128)(2,1)S(1)}, u32[]{:S(2)}, u32[]{:S(2)}) collective-permute-start(bf16[128,640]{1,0:T(8,128)(2,1)S(1)} %collective-permute-done.11.pay_recv), channel_id=1, source_target_pairs={{0,4},{4,0},{8,12},{12,8},{16,20},{20,16},{24,28},{28,24},{1,5},{5... | collective-permute-start | bytes 491528 | tf_op jit(solution)/shard_map/ppermute | solution.py:355
  92.6 0.0 copy-done
  92.6 2.8 %query_grads.2.refs_0_ = f32[256,512]{1,0:T(8,128)S(1)} custom-call(s32[6]{0:T(128)S(1)} %stack.27.info, bf16[192,640]{1,0:T(8,128)(2,1)S(1)} %dout_rows.3.pay, bf16[4,256,1280]{2,1,0:T(8,128)(2,1)S(1)} %copy-done, bf16[1280,512]{1,0:T(8,128)(2,1)S(1)} %get-tuple-element.14.span), custom_call_target="tpu_custom_call" | custom-call | flops 503316480 | bytes 5242880 | tf_op jit(solution)/shard_map/query_grads/pallas_call | solution.py:221
  95.4 3.4 %query_grads.3 = f32[256,512]{1,0:T(8,128)} custom-call(s32[6]{0:T(128)S(1)} %stack.27.info, bf16[64,640]{1,0:T(8,128)(2,1)S(1)} %dout_rows.2.pay, bf16[4,256,1280]{2,1,0:T(8,128)(2,1)S(1)} %copy-done, bf16[1280,512]{1,0:T(8,128)(2,1)S(1)} %get-tuple-element.14.span, f32[256,512]{1,0:T(8,128)S(1)} %query_grads.2.refs_0_), custom_call_target="tpu_custom_call" | custom-call | flops 167772160 | bytes 5242880 | tf_op jit(solution)/shard_map/query_grads/pallas_call | solution.py:221
  98.8 0.0 collective-permute-done.9.exch_q
  98.8 0.0 collective-permute-done.15.pay_exch
  98.8 3.3 %key_grads.2 = (f32[256,256]{1,0:T(8,128)S(1)}, f32[256,256]{1,0:T(8,128)S(1)}) custom-call(s32[6]{0:T(128)S(1)} %stack.27.info, bf16[256,1024]{1,0:T(8,128)(2,1)S(1)} %constant_dynamic-update-slice_fusion.own, bf16[256,1024]{1,0:T(8,128)(2,1)S(1)} %collective-permute-done.3.peer, bf16[512,512]{1,0:T(8,128)(2,1)S(1)} %collective-permute-done.8.recv_q, ...), custom_call_target="tpu_custom_call" | custom-call | flops 1006632960 | bytes 6291456 | tf_op jit(solution)/shard_map/key_grads/pallas_call | solution.py:330
  102.1 0.0 collective-permute-done.12.pay_exch
  102.1 2.6 %key_grads.3 = (f32[256,256]{1,0:T(8,128)}, f32[256,256]{1,0:T(8,128)}) custom-call(s32[6]{0:T(128)S(1)} %stack.27.info, bf16[256,1024]{1,0:T(8,128)(2,1)S(1)} %constant_dynamic-update-slice_fusion.own, bf16[256,1024]{1,0:T(8,128)(2,1)S(1)} %collective-permute-done.3.peer, bf16[512,512]{1,0:T(8,128)(2,1)S(1)} %collective-permute-done.8.recv_q, ...), custom_call_target="tpu_custom_call" | custom-call | flops 335544320 | bytes 6291456 | tf_op jit(solution)/shard_map/key_grads/pallas_call | solution.py:330
  (4 shorter events, 0.1 us)
Async XLA Ops:
  2.5 40.0 %copy-start.1 = (bf16[64,5376]{1,0:T(8,128)(2,1)S(1)}, bf16[64,5376]{1,0:T(8,128)(2,1)}, u32[]{:S(2)}) copy-start(bf16[64,5376]{1,0:T(8,128)(2,1)} %refs_0_.1) | copy-start | bytes 2064388
  3.5 3.6 %collective-permute-start.3 = (bf16[256,1024]{1,0:T(8,128)(2,1)S(1)}, bf16[256,1024]{1,0:T(8,128)(2,1)S(1)}, u32[]{:S(2)}, u32[]{:S(2)}) collective-permute-start(bf16[256,1024]{1,0:T(8,128)(2,1)S(1)} %constant_dynamic-update-slice_fusion.own), channel_id=1, source_target_pairs={{0,4},{4,0},{8,12},{12,8},{16,20},{20,16},{24,28},{28,24},{1,5},{5... | collective-permute-start | bytes 1572872 | tf_op jit(solution)/shard_map/ppermute | solution.py:355
  4.3 17.2 %collective-permute-start = (bf16[64,5376]{1,0:T(8,128)(2,1)}, bf16[64,5376]{1,0:T(8,128)(2,1)S(1)}, u32[]{:S(2)}, u32[]{:S(2)}) collective-permute-start(bf16[64,5376]{1,0:T(8,128)(2,1)} %refs_0_.1), channel_id=1, source_target_pairs={{0,1},{1,0},{2,3},{3,2},{4,5},{5,4},{6,7},{7,6},{8,9},{9,8},{10,11... | collective-permute-start | bytes 2064392 | tf_op jit(solution)/shard_map/ppermute | solution.py:356
  5.6 6.5 %collective-permute-start.6 = (bf16[64,5376]{1,0:T(8,128)(2,1)}, bf16[64,5376]{1,0:T(8,128)(2,1)}, u32[]{:S(2)}, u32[]{:S(2)}) collective-permute-start(bf16[64,5376]{1,0:T(8,128)(2,1)} %refs_0_.1), channel_id=1, source_target_pairs={{1,2},{2,1},{5,6},{6,5},{9,10},{10,9},{13,14},{14,13},{17,18},{18,... | collective-permute-start | bytes 2064392 | tf_op jit(solution)/shard_map/ppermute | solution.py:356
  8.1 9.3 %collective-permute-start.4 = (bf16[512,512]{1,0:T(8,128)(2,1)S(1)}, bf16[512,512]{1,0:T(8,128)(2,1)}, u32[]{:S(2)}, u32[]{:S(2)}) collective-permute-start(bf16[512,512]{1,0:T(8,128)(2,1)S(1)} %pad_maximum_fusion), channel_id=1, source_target_pairs={{0,8},{4,20},{8,16},{12,28},{16,24},{1,9},{5,21},{9,17},{13,29},{1... | collective-permute-start | bytes 1572872 | tf_op jit(solution)/shard_map/ppermute | solution.py:355
  12.1 30.4 %collective-permute-start.7 = (bf16[64,5376]{1,0:T(8,128)(2,1)}, bf16[64,5376]{1,0:T(8,128)(2,1)}, u32[]{:S(2)}, u32[]{:S(2)}) collective-permute-start(bf16[64,5376]{1,0:T(8,128)(2,1)} %collective-permute-done.6.refs_2_), channel_id=1, source_target_pairs={{1,0},{2,3},{5,4},{6,7},{9,8},{10,11},{13,12},{14,15},{17,16},{18,... | collective-permute-start | bytes 2064392 | tf_op jit(solution)/shard_map/ppermute | solution.py:356
  17.4 4.9 %collective-permute-start.5 = (bf16[512,512]{1,0:T(8,128)(2,1)}, bf16[512,512]{1,0:T(8,128)(2,1)}, u32[]{:S(2)}, u32[]{:S(2)}) collective-permute-start(bf16[512,512]{1,0:T(8,128)(2,1)} %collective-permute-done.4.recv), channel_id=1, source_target_pairs={{0,4},{4,0},{8,12},{12,8},{16,20},{20,16},{24,28},{28,24},{1,5},{5... | collective-permute-start | bytes 1572872 | tf_op jit(solution)/shard_map/ppermute | solution.py:355
  21.5 28.5 %collective-permute-start.1 = (bf16[64,5376]{1,0:T(8,128)(2,1)S(1)}, bf16[64,5376]{1,0:T(8,128)(2,1)S(1)}, u32[]{:S(2)}, u32[]{:S(2)}) collective-permute-start(bf16[64,5376]{1,0:T(8,128)(2,1)S(1)} %collective-permute-done.refs_1_), channel_id=1, source_target_pairs={{1,2},{2,1},{5,6},{6,5},{9,10},{10,9},{13,14},{14,13},{17,18},{18,... | collective-permute-start | bytes 2064392 | tf_op jit(solution)/shard_map/ppermute | solution.py:356
  42.5 8.8 %copy-start.2 = (bf16[256,512]{1,0:T(8,128)(2,1)S(1)}, bf16[256,512]{1,0:T(8,128)(2,1)}, u32[]{:S(2)}) copy-start(bf16[256,512]{1,0:T(8,128)(2,1)} %param.5) | copy-start | bytes 786436
  48.5 4.1 %collective-permute-start.13 = (bf16[192,640]{1,0:T(8,128)(2,1)S(1)}, bf16[192,640]{1,0:T(8,128)(2,1)S(1)}, u32[]{:S(2)}, u32[]{:S(2)}) collective-permute-start(bf16[192,640]{1,0:T(8,128)(2,1)S(1)} %dout_rows.3.pay), channel_id=1, source_target_pairs={{0,4},{4,0},{8,12},{12,8},{16,20},{20,16},{24,28},{28,24},{1,5},{5... | collective-permute-start | bytes 737288 | tf_op jit(solution)/shard_map/ppermute | solution.py:355
  50.0 27.4 %collective-permute-start.2 = (bf16[64,5376]{1,0:T(8,128)(2,1)S(1)}, bf16[64,5376]{1,0:T(8,128)(2,1)S(1)}, u32[]{:S(2)}, u32[]{:S(2)}) collective-permute-start(bf16[64,5376]{1,0:T(8,128)(2,1)S(1)} %collective-permute-done.1.refs_0_), channel_id=1, source_target_pairs={{1,0},{2,3},{5,4},{6,7},{9,8},{10,11},{13,12},{14,15},{17,16},{18,... | collective-permute-start | bytes 2064392 | tf_op jit(solution)/shard_map/ppermute | solution.py:356
  51.3 20.8 %collective-permute-start.8 = (bf16[512,512]{1,0:T(8,128)(2,1)S(1)}, bf16[512,512]{1,0:T(8,128)(2,1)S(1)}, u32[]{:S(2)}, u32[]{:S(2)}) collective-permute-start(bf16[512,512]{1,0:T(8,128)(2,1)S(1)} %pad_maximum_fusion.1), channel_id=1, source_target_pairs={{8,0},{20,4},{16,8},{28,12},{24,16},{9,1},{21,5},{17,9},{29,13},{2... | collective-permute-start | bytes 1572872 | tf_op jit(solution)/shard_map/ppermute | solution.py:355
  52.7 39.9 %copy-start = (bf16[4,256,1280]{2,1,0:T(8,128)(2,1)S(1)}, bf16[4,256,1280]{2,1,0:T(8,128)(2,1)}, u32[]{:S(2)}) copy-start(bf16[4,256,1280]{2,1,0:T(8,128)(2,1)} %get-tuple-element.13.probs) | copy-start | bytes 7864324
  52.7 24.7 %collective-permute-start.14 = (bf16[384,640]{1,0:T(8,128)(2,1)S(1)}, bf16[384,640]{1,0:T(8,128)(2,1)S(1)}, u32[]{:S(2)}, u32[]{:S(2)}) collective-permute-start(bf16[384,640]{1,0:T(8,128)(2,1)S(1)} %pad_maximum_fusion.2), channel_id=1, source_target_pairs={{8,0},{20,4},{16,8},{28,12},{24,16},{9,1},{21,5},{17,9},{29,13},{2... | collective-permute-start | bytes 1474568 | tf_op jit(solution)/shard_map/ppermute | solution.py:355
  72.1 26.6 %collective-permute-start.9 = (bf16[512,512]{1,0:T(8,128)(2,1)S(1)}, bf16[512,512]{1,0:T(8,128)(2,1)S(1)}, u32[]{:S(2)}, u32[]{:S(2)}) collective-permute-start(bf16[512,512]{1,0:T(8,128)(2,1)S(1)} %collective-permute-done.8.recv_q), channel_id=1, source_target_pairs={{0,4},{4,0},{8,12},{12,8},{16,20},{20,16},{24,28},{28,24},{1,5},{5... | collective-permute-start | bytes 1572872 | tf_op jit(solution)/shard_map/ppermute | solution.py:355
  77.4 21.4 %collective-permute-start.15 = (bf16[384,640]{1,0:T(8,128)(2,1)S(1)}, bf16[384,640]{1,0:T(8,128)(2,1)S(1)}, u32[]{:S(2)}, u32[]{:S(2)}) collective-permute-start(bf16[384,640]{1,0:T(8,128)(2,1)S(1)} %collective-permute-done.14.pay_recv), channel_id=1, source_target_pairs={{0,4},{4,0},{8,12},{12,8},{16,20},{20,16},{24,28},{28,24},{1,5},{5... | collective-permute-start | bytes 1474568 | tf_op jit(solution)/shard_map/ppermute | solution.py:355
  82.6 1.5 %collective-permute-start.10 = (bf16[64,640]{1,0:T(8,128)(2,1)S(1)}, bf16[64,640]{1,0:T(8,128)(2,1)S(1)}, u32[]{:S(2)}, u32[]{:S(2)}) collective-permute-start(bf16[64,640]{1,0:T(8,128)(2,1)S(1)} %dout_rows.2.pay), channel_id=1, source_target_pairs={{0,4},{4,0},{8,12},{12,8},{16,20},{20,16},{24,28},{28,24},{1,5},{5... | collective-permute-start | bytes 245768 | tf_op jit(solution)/shard_map/ppermute | solution.py:355
  84.1 6.4 %collective-permute-start.11 = (bf16[128,640]{1,0:T(8,128)(2,1)S(1)}, bf16[128,640]{1,0:T(8,128)(2,1)S(1)}, u32[]{:S(2)}, u32[]{:S(2)}) collective-permute-start(bf16[128,640]{1,0:T(8,128)(2,1)S(1)} %pad_maximum_fusion.3), channel_id=1, source_target_pairs={{8,0},{20,4},{16,8},{28,12},{24,16},{9,1},{21,5},{17,9},{29,13},{2... | collective-permute-start | bytes 491528 | tf_op jit(solution)/shard_map/ppermute | solution.py:355
  90.5 11.6 %collective-permute-start.12 = (bf16[128,640]{1,0:T(8,128)(2,1)S(1)}, bf16[128,640]{1,0:T(8,128)(2,1)S(1)}, u32[]{:S(2)}, u32[]{:S(2)}) collective-permute-start(bf16[128,640]{1,0:T(8,128)(2,1)S(1)} %collective-permute-done.11.pay_recv), channel_id=1, source_target_pairs={{0,4},{4,0},{8,12},{12,8},{16,20},{20,16},{24,28},{28,24},{1,5},{5... | collective-permute-start | bytes 491528 | tf_op jit(solution)/shard_map/ppermute | solution.py:355

commit v2 on v0

v2 whole, which is shorter than its diff:
```python
import functools

import jax
import jax.numpy as jnp
from jax import lax
from jax.experimental import pallas as pl
from jax.experimental.pallas import tpu as pltpu
from jax.sharding import PartitionSpec as P

HD = 128
WIN = 1024
SPAN_BLOCKS = 5
SCALE = 168.0 ** (-0.5)
NT = (((1,), (1,)), ((), ()))
NN = (((1,), (0,)), ((), ()))
F32 = jnp.float32
BF16 = jnp.bfloat16
VMEM = pl.BlockSpec(memory_space=pltpu.VMEM)
SMEM = pl.BlockSpec(memory_space=pltpu.SMEM)
ANY = pl.BlockSpec(memory_space=pl.ANY)
COST = pl.CostEstimate(flops=1, bytes_accessed=1, transcendentals=0)


def dot(a, b, dims):
    return lax.dot_general(a, b, dims, preferred_element_type=F32)


def params(limit=20):
    return pltpu.CompilerParams(vmem_limit_bytes=limit * 2**20)


def call(kernel, name, shapes, info, arrays, scratch=(), outs=VMEM, in_place=()):
    return pl.pallas_call(
        kernel,
        out_shape=shapes,
        in_specs=[SMEM] + [VMEM] * len(arrays) + [ANY] * len(in_place),
        out_specs=outs if isinstance(outs, tuple) else jax.tree.map(lambda _: outs, shapes),
        scratch_shapes=list(scratch),
        input_output_aliases={1 + len(arrays) + n: n for n in range(len(in_place))},
        compiler_params=params(),
        cost_estimate=COST,
        name=name,
    )(info, *arrays, *in_place)


TOKEN = jax.ShapeDtypeStruct((8, HD), F32)


def pack_kernel(places, *refs):
    sources, outs, sems = refs[: len(places)], refs[len(places) : -1], refs[-1]
    copies = []
    for n, (source, (out, row, col)) in enumerate(zip(sources, places)):
        first, last, at = (0, source.shape[1], col) if isinstance(col, int) else (*col, 0)
        target = outs[out].at[row : row + source.shape[0], at : at + last - first]
        copies.append(pltpu.make_async_copy(source.at[:, first:last], target, sems.at[n]))
    for copy in copies:
        copy.start()
    for copy in copies:
        copy.wait()


def pack(arrays, places, shapes, limit=20, outs=ANY):
    return pl.pallas_call(
        functools.partial(pack_kernel, places),
        out_shape=tuple(jax.ShapeDtypeStruct(shape, BF16) for shape in shapes),
        in_specs=[ANY] * len(arrays),
        out_specs=(outs,) * len(shapes),
        scratch_shapes=[pltpu.SemaphoreType.DMA((len(arrays),))],
        compiler_params=params(limit),
        cost_estimate=COST,
        name="pack",
    )(*arrays)


def pair_kernel(nearer, count, info, *refs):
    own, near, far = (refs[n * count : (n + 1) * count] for n in range(3))
    pair = refs[-1]
    total = pair.shape[0] // 2

    def put(at, blocks):
        for block in blocks:
            pair[at : at + block.shape[0], :] = block[...]
            at += block.shape[0]

    @pl.when(info[0] == nearer)
    def _():
        put(0, own)
        put(total, near)

    @pl.when(info[0] != nearer)
    def _():
        put(0, near)
        put(total, far)


def pair_for_peer(info, nearer, own, near, far, after=()):
    total = sum(block.shape[0] for block in own)
    shape = jax.ShapeDtypeStruct((2 * total, own[0].shape[1]), BF16)
    kernel = functools.partial(pair_kernel, nearer, len(own))
    return call(kernel, "pair", shape, info, (*own, *near, *far, *after))


def pieces(x):
    hi = x.astype(BF16)
    rest = x - hi.astype(F32)
    mid = rest.astype(BF16)
    low = (rest - mid.astype(F32)).astype(BF16)
    return hi.astype(F32), mid.astype(F32), low.astype(F32)


def spread(x, first, into):
    lane = lax.broadcasted_iota(jnp.int32, into.shape, 1)
    for n, piece in enumerate(pieces(x)):
        into = jnp.where(lane == first + n, piece, into)
    return into


def minus_ones(rows, first):
    lane = lax.broadcasted_iota(jnp.int32, (rows, HD), 1)
    return jnp.where((lane >= first) & (lane < first + 3), -1.0, 0.0).astype(BF16)


def stacked(refs):
    blocks = [ref[...] for ref in refs]
    return blocks[0] if len(blocks) == 1 else jnp.concatenate(blocks, axis=0)


def head_cols(head):
    return slice(head * HD, (head + 1) * HD)


def probs_kernel(info, kv, query, near, far, odd, *refs):
    probs, mixed, stats, span = refs[-4:]
    rows, kv_width = kv.shape[0], kv.shape[1] // 2
    heads = query.shape[1] // HD
    shard = info[1]

    span[:rows, :] = far[...]
    span[rows : 2 * rows, :] = odd[rows:, :]
    span[2 * rows : 3 * rows, :] = near[...]
    span[3 * rows : 4 * rows, :] = odd[:rows, :]
    span[4 * rows :, :] = kv[...]

    span_rows = span.shape[0]
    row = lax.broadcasted_iota(jnp.int32, (rows, 1), 0)
    col = lax.broadcasted_iota(jnp.int32, (rows, span_rows), 1)
    first = jnp.maximum(row + 1, (SPAN_BLOCKS - 1 - shard) * rows)
    allowed = (col >= first) & (col <= row + WIN)
    row_stats = jnp.zeros((rows, HD), F32)
    for head in range(heads):
        group = head // 2
        scores = dot(query[:, head_cols(head)], span[:, head_cols(group)], NT) * SCALE
        scores = jnp.where(allowed, scores, -1e30)
        top = jnp.max(scores, axis=1, keepdims=True)
        weights = jnp.exp(scores - top)
        total = jnp.sum(weights, axis=1, keepdims=True)
        probability = (weights * (1.0 / total)).astype(BF16)
        probs[head] = probability
        value_span = span[:, kv_width + group * HD : kv_width + (group + 1) * HD]
        mixed[:, head_cols(head)] = dot(probability, value_span, NN)
        level = (top + jnp.log(total)) * (1.0 / SCALE)
        row_stats = spread(level, 8 * head, row_stats)
    stats[...] = row_stats.astype(BF16)


def attention_probs(info, kv, query, near, far, odd, after):
    rows, width = query.shape
    span_rows = SPAN_BLOCKS * rows
    shapes = (
        jax.ShapeDtypeStruct((width // HD, rows, span_rows), BF16),
        jax.ShapeDtypeStruct((rows, width), F32),
        jax.ShapeDtypeStruct((rows, HD), BF16),
        jax.ShapeDtypeStruct((span_rows, kv.shape[1]), BF16),
    )
    arrays = (kv, query, near, far, odd, *after)
    return call(probs_kernel, "attention_probs", shapes, info, arrays)


def finish_rows(info, slot, product, mixed, stats, pay, at):
    rows, width = product.shape
    start = pl.multiple_of(info[2 + slot], 16)
    dout = product.astype(BF16)
    row_stats = stats[pl.ds(start, rows), :].astype(F32)
    out_rows = mixed[pl.ds(start, rows), :]
    for head in range(width // HD):
        cols = head_cols(head)
        delta = jnp.sum(dout[:, cols].astype(F32) * out_rows[:, cols], axis=1, keepdims=True)
        row_stats = spread(delta, 8 * head + 3, row_stats)
    pay[at : at + rows, :width] = dout
    pay[at : at + rows, width:] = row_stats.astype(BF16)


def dout_kernel(slots, info, *refs):
    sources = refs[: sum(slots.values())]
    weight, mixed, stats = refs[len(sources) : len(sources) + 3]
    pay = refs[-1]
    rows = sources[0].shape[0]
    parts = []
    at = 0
    for n in slots.values():
        part = sources[at][...]
        for other in sources[at + 1 : at + n]:
            part = part + other[...]
        parts.append(part)
        at += n
    product = dot(jnp.concatenate(parts, axis=0), weight[...], NT)
    for n, slot in enumerate(slots):
        finish_rows(info, slot, product[n * rows : (n + 1) * rows], mixed, stats, pay, n * rows)


def dout_rows(info, slots, sources, weight, mixed, stats, after=()):
    total = sources[0].shape[0] * len(slots)
    shape = jax.ShapeDtypeStruct((total, weight.shape[0] + HD), BF16)
    arrays = (*sources, weight, mixed, stats, *after)
    return call(functools.partial(dout_kernel, slots), "dout_rows", shape, info, arrays)


def query_kernel(slots, count, info, probs, span, *refs):
    out, done, held, sems = refs[-4:]
    done[...] = jnp.zeros_like(done)
    pay = stacked(refs[:count])
    heads, rows, _ = probs.shape
    kv_width = span.shape[1] // 2
    total = pay.shape[0]
    part_rows = total // len(slots)
    starts = [pl.multiple_of(info[2 + slot], 16) for slot in slots]
    extra = pay[:, heads * HD :].astype(F32)
    lane = lax.broadcasted_iota(jnp.int32, extra.shape, 1)
    for group in range(heads // 2):
        key = span[:, head_cols(group)]
        value = span[:, kv_width + group * HD : kv_width + (group + 1) * HD]
        pair = (2 * group, 2 * group + 1)
        dprobs = dot(jnp.concatenate([pay[:, head_cols(head)] for head in pair], axis=0), value, NT)
        parts = []
        for m, head in enumerate(pair):
            first = 8 * head + 3
            delta = jnp.sum(
                jnp.where((lane >= first) & (lane < first + 3), extra, 0.0), axis=1, keepdims=True
            )
            for n, start in enumerate(starts):
                at = m * total + n * part_rows
                weights = probs[head, pl.ds(start, part_rows), :].astype(F32)
                centred = dprobs[at : at + part_rows, :] - delta[n * part_rows : (n + 1) * part_rows]
                parts.append((weights * centred).astype(BF16))
        grads = dot(jnp.concatenate(parts, axis=0), key, NN) * SCALE
        for m, head in enumerate(pair):
            held[:, head_cols(head)] = grads[m * total : (m + 1) * total, :]
    copies = [
        pltpu.make_async_copy(
            held.at[n * part_rows : (n + 1) * part_rows, :],
            out.at[pl.ds(start, part_rows), :],
            sems.at[n],
        )
        for n, start in enumerate(starts)
    ]
    for copy in copies:
        copy.start()
    for copy in copies:
        copy.wait()


def query_grads(info, slots, pays, probs, span, before=()):
    heads, rows, _ = probs.shape
    total = sum(pay.shape[0] for pay in pays)
    return call(
        functools.partial(query_kernel, slots, len(pays)),
        "query_grads",
        (
            jax.ShapeDtypeStruct((rows, heads * HD), F32),
            TOKEN,
        ),
        info,
        (probs, span, *pays),
        [pltpu.VMEM((total, heads * HD), F32), pltpu.SemaphoreType.DMA((len(slots),))],
        outs=(ANY, VMEM),
        in_place=before,
    )


def key_kernel(slots, blocks, q_count, d_count, info, kv, *refs):
    q_refs, d_refs = refs[:q_count], refs[q_count : q_count + d_count]
    before = refs[q_count + d_count : -7]
    grad_k, grad_v, q_cat, d_cat, held_k, held_v, sems = refs[-7:]
    rows, kv_width = kv.shape[0], kv.shape[1] // 2
    width = q_cat.shape[1]
    lanes = q_cat.shape[0]
    total = lanes // len(blocks)
    part_rows = total // len(slots)
    lane = lax.broadcasted_iota(jnp.int32, (1, lanes), 1)
    low = jnp.zeros((1, lanes), jnp.int32)
    high = jnp.full((1, lanes), rows, jnp.int32)
    for m, (distance, q_at, q_row, d_at, d_row) in enumerate(blocks):
        at = m * total
        for slot in slots:
            start = pl.multiple_of(info[2 + slot], 16)
            q_cat[at : at + part_rows, :] = q_refs[q_at][pl.ds(start + q_row, part_rows), :]
            inside = (lane >= at) & (lane < at + part_rows)
            if distance == 0:
                high = jnp.where(inside, lane - at + start, high)
            if distance == SPAN_BLOCKS - 1:
                low = jnp.where(inside, lane - at + start + 1, low)
            at += part_rows
        at = m * total
        for n in d_at:
            size = min(d_refs[n].shape[0], total)
            d_cat[at : at + size, :] = d_refs[n][d_row : d_row + size, :]
            at += size

    masked = any(block[0] in (0, SPAN_BLOCKS - 1) for block in blocks)
    key_row = lax.broadcasted_iota(jnp.int32, (rows, lanes), 0)
    allowed = (key_row >= low) & (key_row <= high)
    extra = d_cat[:, width:]
    copies = []
    for group in range(kv_width // HD):
        cols = head_cols(group)
        key = kv[:, cols]
        value = kv[:, kv_width + group * HD : kv_width + (group + 1) * HD]
        sum_k = None
        sum_v = None
        for head in (2 * group, 2 * group + 1):
            queries = q_cat[:, head_cols(head)]
            dout = d_cat[:, head_cols(head)]
            scores = dot(
                jnp.concatenate([key, minus_ones(rows, 8 * head)], axis=1),
                jnp.concatenate([queries, extra], axis=1),
                NT,
            )
            probability = jnp.exp(scores * SCALE)
            if masked:
                probability = jnp.where(allowed, probability, 0.0)
            centred = dot(
                jnp.concatenate([value, minus_ones(rows, 8 * head + 3)], axis=1),
                jnp.concatenate([dout, extra], axis=1),
                NT,
            )
            dscores = (probability * centred).astype(BF16)
            term_v = dot(probability.astype(BF16), dout, NN)
            term_k = dot(dscores, queries, NN)
            sum_v = term_v if sum_v is None else sum_v + term_v
            sum_k = term_k if sum_k is None else sum_k + term_k
        sum_k = sum_k * SCALE
        if before:
            sum_k = sum_k + before[0][:, cols]
            sum_v = sum_v + before[1][:, cols]
        held_k[:, cols] = sum_k
        held_v[:, cols] = sum_v
        for n, (held, out) in enumerate(((held_k, grad_k), (held_v, grad_v))):
            copy = pltpu.make_async_copy(held.at[:, cols], out.at[:, cols], sems.at[2 * group + n])
            copy.start()
            copies.append(copy)
    for copy in copies:
        copy.wait()


def key_grads(info, slots, blocks, kv, q_arrays, d_arrays, total, before=()):
    lanes = len(blocks) * total
    width = q_arrays[0].shape[1]
    kv_width = kv.shape[1] // 2
    shape = jax.ShapeDtypeStruct((kv.shape[0], kv_width), F32)
    held = pltpu.VMEM(shape.shape, F32)
    return call(
        functools.partial(key_kernel, slots, blocks, len(q_arrays), len(d_arrays)),
        "key_grads",
        (shape, shape),
        info,
        (kv, *q_arrays, *d_arrays, *before),
        [
            pltpu.VMEM((lanes, width), BF16),
            pltpu.VMEM((lanes, width + HD), BF16),
            held,
            held,
            pltpu.SemaphoreType.DMA((2 * (kv_width // HD),)),
        ],
        outs=ANY,
    )


def on_device(ctx, queries, keys, values, grad_out, out_weight):
    rows, width = queries.shape
    kv_width = 2 * keys.shape[1]
    slot_rows = grad_out.shape[0]
    swap = [(i, i ^ 1) for i in range(ctx)]

    def along(x, pairs, name):
        with jax.named_scope(name):
            return lax.ppermute(x, "ctx", pairs)

    def over(x, pairs, name):
        with jax.named_scope(name):
            return lax.ppermute(x, "tp", pairs)

    def moved(distance):
        return [(i, i + distance) for i in range(ctx) if 0 <= i + distance < ctx]

    shard = lax.axis_index("ctx")
    tp = lax.axis_index("tp")
    low_side = tp < 2
    slot_at = [tp, tp ^ 1, jnp.where(low_side, 2, 1), jnp.where(low_side, 3, 0)]
    info = jnp.stack([shard % 2, shard] + [s * slot_rows for s in slot_at]).astype(jnp.int32)

    middle = [(1, 2), (2, 1)]
    ends = [(0, 1), (1, 0), (2, 3), (3, 2)]
    outward = [(1, 0), (2, 3)]
    mid_first = over(grad_out, middle, "mid_first")
    end_first = over(grad_out, ends, "end_first")
    mid_second = over(end_first, middle, "mid_second")
    out_second = over(mid_first, outward, "out_second")

    kv, query = pack(
        [keys, values, queries],
        [(0, 0, 0), (0, 0, kv_width // 2), (1, 0, 0)],
        [(rows, kv_width), (rows, width)],
        limit=56,
        outs=VMEM,
    )
    near_kv = along(kv, moved(2), "kv_near")
    far_kv = along(kv, moved(4), "kv_far")
    near_q = along(query, moved(-2), "q_near")
    far_q = along(query, moved(-4), "q_far")
    odd_kv = along(pair_for_peer(info, 0, [kv], [near_kv], [far_kv]), swap, "kv_swap")
    odd_q = along(pair_for_peer(info, 1, [query], [near_q], [far_q]), swap, "q_swap")


    probs, mixed, stats, span = attention_probs(
        info, kv, query, near_kv, far_kv, odd_kv, (odd_q,)
    )

    def sent(pay, name):
        near = along(pay, moved(-2), name + "_near")
        far = along(pay, moved(-4), name + "_far")
        return near, far

    mid_second, out_second, stats = lax.optimization_barrier((mid_second, out_second, stats))
    out_third = over(mid_second, outward, "out_third")
    statistics = (out_weight, mixed, stats)
    early, late = {0: 1, 1: 1, 2: 2}, {3: 2}
    pay_a = dout_rows(info, early, (grad_out, end_first, mid_first, out_second), *statistics)
    near_a, far_a = sent(pay_a, "early")
    grad_q, queries_done = query_grads(info, early, (pay_a,), probs, span)

    pay_b = dout_rows(info, late, (mid_second, out_third), *statistics, (queries_done,))
    near_b, far_b = sent(pay_b, "late")
    grad_q, queries_done = query_grads(info, late, (pay_b,), probs, span, (grad_q,))
    pays = ((pay_a, pay_b), (near_a, near_b), (far_a, far_b))
    pair = pair_for_peer(info, 1, *pays, (queries_done,))
    odd = along(pair, swap, "pay_swap")
    slots = (0, 1, 2, 3)
    even_blocks = ((0, 0, 0, (0, 1), 0), (2, 1, 0, (2, 3), 0), (4, 2, 0, (4, 5), 0))
    even = key_grads(
        info, slots, even_blocks, kv, (query, near_q, far_q), sum(pays, ()), rows
    )
    odd_blocks = ((1, 0, 0, (0,), 0), (3, 0, rows, (0,), rows))
    grad_k, grad_v = key_grads(info, slots, odd_blocks, kv, (odd_q,), (odd,), rows, even)
    return (grad_q, grad_k, grad_v)


def solution(mesh):
    in_specs = (
        P("ctx", "tp"),
        P("ctx", "tp"),
        P("ctx", "tp"),
        P(("ctx", "tp"), None),
        P("tp", None),
    )
    out_specs = (P("ctx", "tp"), P("ctx", "tp"), P("ctx", "tp"))
    return jax.shard_map(
        functools.partial(on_device, mesh.shape["ctx"]),
        mesh=mesh,
        in_specs=in_specs,
        out_specs=out_specs,
        check_vma=False,
    )
```

time: 128 us -> 76.3 us (0.60)
  waiting for transfers between devices: 54.5 us -> 13.1 us
  Pallas kernels: 0 us -> 24.7 us
  matrix products: 21.6 us -> 0 us
  starting transfers between devices: 17.7 us -> 32.3 us
  between operations: 14.3 us -> 1.04 us
  local copies, waits for them, and re-layouts: 13 us -> 4.56 us
  other arithmetic: 6.59 us -> 0.01 us
    all_gather x1 -> x0, waiting for transfers between devices: 35.5 us -> none  [on_device(): lax.all_gather(grad_out, 'tp', axis=0, tiled=True)]
    pallas_call x0 -> x11, Pallas kernels: none -> 24.7 us  [the longest x10 22.7 us: call(): pl.pallas_call(kernel, out_shape=shapes, in_specs=[SMEM] + [VMEM] * len(a...]
    dot_general x5 -> x0, matrix products: 16.8 us -> none  [the longest x1 5.01 us: on_device(): lax.dot_general(lax.all_gather(grad_out, 'tp', axis=0, tiled=True), out_w...]
    ppermute x8 -> x16, starting transfers between devices: 17.6 us -> 32.3 us  [the longest x11 25.3 us: along(): return lax.ppermute(x, 'ctx', pairs)]
    another operation x2 -> x1, local copies, waits for them, and re-layouts: 5.6 us -> 0.08 us  [on_device(): jnp.stack([shard % 2, shard] + [s * slot_rows for s in slot_at])]
    ppermute x8 -> x16, waiting for transfers between devices: 18.3 us -> 13.1 us  [the longest x11 8.72 us: along(): return lax.ppermute(x, 'ctx', pairs)]
    sub x1 -> x0, matrix products: 4.82 us -> none  [band_grads(): weights = jnp.where(allowed, jnp.exp(scores - row_max), 0.0)]
    convert_element_type x1 -> x0, other arithmetic: 2.25 us -> none  [band_grads(): dscores_low = dscores.astype(jnp.bfloat16)]
  transfers between devices with their start and end apart: 9 -> 16, of which waited for: 6 -> 8; matrix products, arithmetic and copies ran while one was open for 10% -> 0% of each run, Pallas kernels for 0% -> 28%
where the time goes in v2:
time: 76.3 us; the launch traced here: 75.7 us
  starting transfers between devices  32.3 us (42%)
  Pallas kernels  24.7 us (32%)
  waiting for transfers between devices  13.1 us (17%)
  local copies, waits for them, and re-layouts  4.56 us (6%)
  between operations  1.04 us (1%)
    ppermute x11, starting transfers between devices, along(): return lax.ppermute(x, 'ctx', pairs)  25.3 us
    pallas_call x10, Pallas kernels, call(): pl.pallas_call(kernel, out_shape=shapes, in_specs=[SMEM] + [VMEM] * len(a...  22.7 us
    ppermute x11, waiting for transfers between devices, along(): return lax.ppermute(x, 'ctx', pairs)  8.72 us
    ppermute x5, starting transfers between devices, over(): return lax.ppermute(x, 'tp', pairs)  6.96 us
    unnamed x16, local copies, waits for them, and re-layouts  4.48 us
    ppermute x5, waiting for transfers between devices, over(): return lax.ppermute(x, 'tp', pairs)  4.42 us
    pallas_call x1, Pallas kernels, pack(): pl.pallas_call(functools.partial(pack_kernel, places), out_shape=tuple((j...  1.99 us
  transfers between devices with their start and end apart: 16, of which 8 were waited for; matrix products, arithmetic and copies ran while one was open for 0% of the time, Pallas kernels for 28%

profile of v2, /device:TPU:3, one launch (start us, length us, event | category | flops | bytes accessed | tf_op | source)
XLA Modules:
  0.0 75.7 jit_solution(14769943405124299211)
XLA Ops:
  0.6 1.4 %collective-permute-start.6 = (bf16[64,5376]{1,0:T(8,128)(2,1)}, bf16[64,5376]{1,0:T(8,128)(2,1)S(1)}, u32[]{:S(2)}, u32[]{:S(2)}) collective-permute-start(bf16[64,5376]{1,0:T(8,128)(2,1)} %refs_0_.3), channel_id=1, source_target_pairs={{0,1},{1,0},{2,3},{3,2},{4,5},{5,4},{6,7},{7,6},{8,9},{9,8},{10,11... | collective-permute-start | bytes 2064392 | tf_op jit(solution)/shard_map/end_first/ppermute | solution.py:390
  2.0 1.5 %collective-permute-start.8 = (bf16[64,5376]{1,0:T(8,128)(2,1)}, bf16[64,5376]{1,0:T(8,128)(2,1)}, u32[]{:S(2)}, u32[]{:S(2)}) collective-permute-start(bf16[64,5376]{1,0:T(8,128)(2,1)} %refs_0_.3), channel_id=1, source_target_pairs={{1,2},{2,1},{5,6},{6,5},{9,10},{10,9},{13,14},{14,13},{17,18},{18,... | collective-permute-start | bytes 2064392 | tf_op jit(solution)/shard_map/mid_first/ppermute | solution.py:390
  3.5 0.0 slice-start
  3.5 2.0 %pack.1 = (bf16[256,512]{1,0:T(8,128)(2,1)}, bf16[256,512]{1,0:T(8,128)(2,1)}) custom-call(bf16[256,256]{1,0:T(8,128)(2,1)} %refs_0_.2, bf16[256,256]{1,0:T(8,128)(2,1)} %refs_1_.1, bf16[256,512]{1,0:T(8,128)(2,1)} %refs_2_.2), custom_call_target="tpu_custom_call" | custom-call | flops 1 | bytes 1 | tf_op jit(solution)/shard_map/pack/pallas_call | solution.py:63
  5.5 2.2 %collective-permute-start.3 = (bf16[256,512]{1,0:T(8,128)(2,1)}, bf16[256,512]{1,0:T(8,128)(2,1)S(1)}, u32[]{:S(2)}, u32[]{:S(2)}) collective-permute-start(bf16[256,512]{1,0:T(8,128)(2,1)} %get-tuple-element.21.refs_0_.query), channel_id=1, source_target_pairs={{8,0},{12,4},{16,8},{20,12},{24,16},{28,20},{9,1},{13,5},{17,9},{2... | collective-permute-start | bytes 786440 | tf_op jit(solution)/shard_map/q_near/ppermute | solution.py:386
  7.7 1.3 %collective-permute-start.4 = (bf16[256,512]{1,0:T(8,128)(2,1)}, bf16[256,512]{1,0:T(8,128)(2,1)S(1)}, u32[]{:S(2)}, u32[]{:S(2)}) collective-permute-start(bf16[256,512]{1,0:T(8,128)(2,1)} %get-tuple-element.21.refs_0_.query), channel_id=1, source_target_pairs={{16,0},{20,4},{24,8},{28,12},{17,1},{21,5},{25,9},{29,13},{18,2},{... | collective-permute-start | bytes 786440 | tf_op jit(solution)/shard_map/q_far/ppermute | solution.py:386
  9.0 4.0 %collective-permute-start = (bf16[256,512]{1,0:T(8,128)(2,1)}, bf16[256,512]{1,0:T(8,128)(2,1)S(1)}, u32[]{:S(2)}, u32[]{:S(2)}) collective-permute-start(bf16[256,512]{1,0:T(8,128)(2,1)} %get-tuple-element.20.refs_0_.kv), channel_id=1, source_target_pairs={{0,8},{4,12},{8,16},{12,20},{16,24},{20,28},{1,9},{5,13},{9,17},{1... | collective-permute-start | bytes 786440 | tf_op jit(solution)/shard_map/kv_near/ppermute | solution.py:386
  13.0 2.4 %collective-permute-done.3.refs_1_ = bf16[256,512]{1,0:T(8,128)(2,1)S(1)} collective-permute-done((bf16[256,512]{1,0:T(8,128)(2,1)}, bf16[256,512]{1,0:T(8,128)(2,1)S(1)}, u32[]{:S(2)}, u32[]{:S(2)}) %collective-permute-start.3) | collective-permute-done | bytes 262176 | tf_op jit(solution)/shard_map/q_near/ppermute | solution.py:386
  15.4 1.3 %collective-permute-start.1 = (bf16[256,512]{1,0:T(8,128)(2,1)}, bf16[256,512]{1,0:T(8,128)(2,1)S(1)}, u32[]{:S(2)}, u32[]{:S(2)}) collective-permute-start(bf16[256,512]{1,0:T(8,128)(2,1)} %get-tuple-element.20.refs_0_.kv), channel_id=1, source_target_pairs={{0,16},{4,20},{8,24},{12,28},{1,17},{5,21},{9,25},{13,29},{2,18},{... | collective-permute-start | bytes 786440 | tf_op jit(solution)/shard_map/kv_far/ppermute | solution.py:386
  16.7 0.5 collective-permute-done.6.refs_1_
  17.2 1.5 %collective-permute-start.7 = (bf16[64,5376]{1,0:T(8,128)(2,1)S(1)}, bf16[64,5376]{1,0:T(8,128)(2,1)}, u32[]{:S(2)}, u32[]{:S(2)}) collective-permute-start(bf16[64,5376]{1,0:T(8,128)(2,1)S(1)} %collective-permute-done.6.refs_1_), channel_id=1, source_target_pairs={{1,2},{2,1},{5,6},{6,5},{9,10},{10,9},{13,14},{14,13},{17,18},{18,... | collective-permute-start | bytes 2064392 | tf_op jit(solution)/shard_map/mid_second/ppermute | solution.py:390
  18.7 0.0 collective-permute-done.8.refs_2_
  18.7 1.3 %collective-permute-start.9 = (bf16[64,5376]{1,0:T(8,128)(2,1)}, bf16[64,5376]{1,0:T(8,128)(2,1)}, u32[]{:S(2)}, u32[]{:S(2)}) collective-permute-start(bf16[64,5376]{1,0:T(8,128)(2,1)} %collective-permute-done.8.refs_2_), channel_id=1, source_target_pairs={{1,0},{2,3},{5,4},{6,7},{9,8},{10,11},{13,12},{14,15},{17,16},{18,... | collective-permute-start | bytes 2064392 | tf_op jit(solution)/shard_map/out_second/ppermute | solution.py:390
  20.0 0.1 stack.27.info
  20.1 2.3 %collective-permute-done.4.refs_2_ = bf16[256,512]{1,0:T(8,128)(2,1)S(1)} collective-permute-done((bf16[256,512]{1,0:T(8,128)(2,1)}, bf16[256,512]{1,0:T(8,128)(2,1)S(1)}, u32[]{:S(2)}, u32[]{:S(2)}) %collective-permute-start.4) | collective-permute-done | bytes 262176 | tf_op jit(solution)/shard_map/q_far/ppermute | solution.py:386
  22.4 0.0 copy-start.3
  22.4 0.9 %copy-done.3 = bf16[256,512]{1,0:T(8,128)(2,1)S(1)} copy-done((bf16[256,512]{1,0:T(8,128)(2,1)S(1)}, bf16[256,512]{1,0:T(8,128)(2,1)}, u32[]{:S(2)}) %copy-start.3) | copy-done | bytes 262168
  23.3 0.0 copy-start.4
  23.3 0.6 pair.4
  23.9 0.6 collective-permute-start.5
  24.5 0.0 collective-permute-done.refs_1_.near
  24.5 0.0 collective-permute-done.1.refs_2_.far
  24.5 0.0 copy-start.1
  24.5 0.9 %copy-done.1 = bf16[256,512]{1,0:T(8,128)(2,1)S(1)} copy-done((bf16[256,512]{1,0:T(8,128)(2,1)S(1)}, bf16[256,512]{1,0:T(8,128)(2,1)}, u32[]{:S(2)}) %copy-start.1) | copy-done | bytes 262168
  25.4 0.0 copy-start.5
  25.4 0.6 pair.3
  26.0 0.1 collective-permute-start.2
  26.1 0.0 collective-permute-done.5.refs_0_
  26.1 1.9 %collective-permute-done.2.odd = bf16[512,512]{1,0:T(8,128)(2,1)S(1)} collective-permute-done((bf16[512,512]{1,0:T(8,128)(2,1)S(1)}, bf16[512,512]{1,0:T(8,128)(2,1)S(1)}, u32[]{:S(2)}, u32[]{:S(2)}) %collective-permute-start.2) | collective-permute-done | bytes 524320 | tf_op jit(solution)/shard_map/kv_swap/ppermute | solution.py:386
  28.0 0.0 copy-done.4
  28.0 4.2 %attention_probs.1 = (bf16[4,256,1280]{2,1,0:T(8,128)(2,1)S(1)}, f32[256,512]{1,0:T(8,128)S(1)}, bf16[256,128]{1,0:T(8,128)(2,1)S(1)}, bf16[1280,512]{1,0:T(8,128)(2,1)S(1)}) custom-call(s32[6]{0:T(128)S(1)} %stack.27.info, bf16[256,512]{1,0:T(8,128)(2,1)S(1)} %copy-done.1, bf16[256,512]{1,0:T(8,128)(2,1)S(1)} %copy-done.4, ...), custom_call_target="tpu_custom_call" | custom-call | flops 1 | bytes 1 | tf_op jit(solution)/shard_map/attention_probs/pallas_call | solution.py:33
  32.3 0.0 collective-permute-done.7.refs_0_
  32.3 3.7 %collective-permute-done.9.refs_3_ = bf16[64,5376]{1,0:T(8,128)(2,1)} collective-permute-done((bf16[64,5376]{1,0:T(8,128)(2,1)}, bf16[64,5376]{1,0:T(8,128)(2,1)}, u32[]{:S(2)}, u32[]{:S(2)}) %collective-permute-start.9) | collective-permute-done | bytes 688160 | tf_op jit(solution)/shard_map/out_second/ppermute | solution.py:390
  36.0 1.3 %collective-permute-start.10 = (bf16[64,5376]{1,0:T(8,128)(2,1)}, bf16[64,5376]{1,0:T(8,128)(2,1)S(1)}, u32[]{:S(2)}, u32[]{:S(2)}) collective-permute-start(bf16[64,5376]{1,0:T(8,128)(2,1)} %collective-permute-done.7.refs_0_), channel_id=1, source_target_pairs={{1,0},{2,3},{5,4},{6,7},{9,8},{10,11},{13,12},{14,15},{17,16},{18,... | collective-permute-start | bytes 2064392 | tf_op jit(solution)/shard_map/out_third/ppermute | solution.py:390
  37.3 0.0 copy-done.5
  37.3 0.0 copy-start
  37.3 2.6 %copy-done = bf16[512,5376]{1,0:T(8,128)(2,1)S(1)} copy-done((bf16[512,5376]{1,0:T(8,128)(2,1)S(1)}, bf16[512,5376]{1,0:T(8,128)(2,1)}, u32[]{:S(2)}) %copy-start) | copy-done | bytes 5505048
  39.8 0.0 slice-start.1
  39.8 3.5 %dout_rows.2.refs_0_.refs_3_ = bf16[192,640]{1,0:T(8,128)(2,1)S(1)} custom-call(s32[6]{0:T(128)S(1)} %stack.27.info, bf16[64,5376]{1,0:T(8,128)(2,1)S(1)} %copy-done.5, bf16[64,5376]{1,0:T(8,128)(2,1)S(1)} %collective-permute-done.6.refs_1_, bf16[64,5376]{1,0:T(8,128)(2,1)} %collective-permute-done.8.refs_2_, ...), custom_call_target="tpu_custom_call" | custom-call | flops 1 | bytes 1 | tf_op jit(solution)/shard_map/dout_rows/pallas_call | solution.py:33
  43.4 3.6 %collective-permute-start.11 = (bf16[192,640]{1,0:T(8,128)(2,1)S(1)}, bf16[192,640]{1,0:T(8,128)(2,1)S(1)}, u32[]{:S(2)}, u32[]{:S(2)}) collective-permute-start(bf16[192,640]{1,0:T(8,128)(2,1)S(1)} %dout_rows.2.refs_0_.refs_3_), channel_id=1, source_target_pairs={{8,0},{12,4},{16,8},{20,12},{24,16},{28,20},{9,1},{13,5},{17,9},{2... | collective-permute-start | bytes 737288 | tf_op jit(solution)/shard_map/early_near/ppermute | solution.py:386
  47.0 1.3 %collective-permute-start.13 = (bf16[192,640]{1,0:T(8,128)(2,1)S(1)}, bf16[192,640]{1,0:T(8,128)(2,1)S(1)}, u32[]{:S(2)}, u32[]{:S(2)}) collective-permute-start(bf16[192,640]{1,0:T(8,128)(2,1)S(1)} %dout_rows.2.refs_0_.refs_3_), channel_id=1, source_target_pairs={{16,0},{20,4},{24,8},{28,12},{17,1},{21,5},{25,9},{29,13},{18,2},{... | collective-permute-start | bytes 737288 | tf_op jit(solution)/shard_map/early_far/ppermute | solution.py:386
  48.3 2.6 %query_grads.2 = (f32[256,512]{1,0:T(8,128)}, f32[8,128]{1,0:T(8,128)S(1)}) custom-call(s32[6]{0:T(128)S(1)} %stack.27.info, bf16[4,256,1280]{2,1,0:T(8,128)(2,1)S(1)} %get-tuple-element.22.probs, bf16[1280,512]{1,0:T(8,128)(2,1)S(1)} %get-tuple-element.23.span, bf16[192,640]{1,0:T(8,128)(2,1)S(1)} %dout_rows.2.refs_0_.refs_3_), custom_call_target="tpu_custom_call" | custom-call | flops 1 | bytes 1 | tf_op jit(solution)/shard_map/query_grads/pallas_call | solution.py:33
  50.9 0.3 collective-permute-done.10.refs_1_
  51.1 0.0 slice-done
  51.1 0.0 slice-done.1
  51.2 3.0 %dout_rows.3.refs_0_.refs_1_.refs_4_ = bf16[64,640]{1,0:T(8,128)(2,1)S(1)} custom-call(s32[6]{0:T(128)S(1)} %stack.27.info, bf16[64,5376]{1,0:T(8,128)(2,1)} %collective-permute-done.7.refs_0_, bf16[64,5376]{1,0:T(8,128)(2,1)S(1)} %collective-permute-done.10.refs_1_, bf16[512,5376]{1,0:T(8,128)(2,1)S(1)} %bitcast.7, ...), custom_call_target="tpu_custom_call" | custom-call | flops 1 | bytes 1 | tf_op jit(solution)/shard_map/dout_rows/pallas_call | solution.py:33
  54.1 4.2 %collective-permute-start.12 = (bf16[64,640]{1,0:T(8,128)(2,1)S(1)}, bf16[64,640]{1,0:T(8,128)(2,1)S(1)}, u32[]{:S(2)}, u32[]{:S(2)}) collective-permute-start(bf16[64,640]{1,0:T(8,128)(2,1)S(1)} %dout_rows.3.refs_0_.refs_1_.refs_4_), channel_id=1, source_target_pairs={{8,0},{12,4},{16,8},{20,12},{24,16},{28,20},{9,1},{13,5},{17,9},{2... | collective-permute-start | bytes 245768 | tf_op jit(solution)/shard_map/late_near/ppermute | solution.py:386
  58.3 1.3 %collective-permute-start.14 = (bf16[64,640]{1,0:T(8,128)(2,1)S(1)}, bf16[64,640]{1,0:T(8,128)(2,1)S(1)}, u32[]{:S(2)}, u32[]{:S(2)}) collective-permute-start(bf16[64,640]{1,0:T(8,128)(2,1)S(1)} %dout_rows.3.refs_0_.refs_1_.refs_4_), channel_id=1, source_target_pairs={{16,0},{20,4},{24,8},{28,12},{17,1},{21,5},{25,9},{29,13},{18,2},{... | collective-permute-start | bytes 245768 | tf_op jit(solution)/shard_map/late_far/ppermute | solution.py:386
  59.6 0.0 copy-start.2
  59.6 1.8 %query_grads.3 = (f32[256,512]{1,0:T(8,128)}, f32[8,128]{1,0:T(8,128)S(1)}) custom-call(s32[6]{0:T(128)S(1)} %stack.27.info, bf16[4,256,1280]{2,1,0:T(8,128)(2,1)S(1)} %get-tuple-element.22.probs, bf16[1280,512]{1,0:T(8,128)(2,1)S(1)} %get-tuple-element.23.span, ...), custom_call_target="tpu_custom_call", output_to_operand_aliasing={{0}: (4, {})} | custom-call | flops 1 | bytes 1 | tf_op jit(solution)/shard_map/query_grads/pallas_call | solution.py:33
  61.4 0.0 collective-permute-done.11.refs_2_.refs_5_
  61.4 0.0 collective-permute-done.13.refs_4_.refs_7_
  61.4 0.6 collective-permute-done.12.refs_3_.refs_6_
  62.0 1.6 %collective-permute-done.14.refs_5_.refs_8_ = bf16[64,640]{1,0:T(8,128)(2,1)S(1)} collective-permute-done((bf16[64,640]{1,0:T(8,128)(2,1)S(1)}, bf16[64,640]{1,0:T(8,128)(2,1)S(1)}, u32[]{:S(2)}, u32[]{:S(2)}) %collective-permute-start.14) | collective-permute-done | bytes 81952 | tf_op jit(solution)/shard_map/late_far/ppermute | solution.py:386
  63.6 0.8 %pair.5 = bf16[512,640]{1,0:T(8,128)(2,1)S(1)} custom-call(s32[6]{0:T(128)S(1)} %stack.27.info, bf16[192,640]{1,0:T(8,128)(2,1)S(1)} %dout_rows.2.refs_0_.refs_3_, bf16[64,640]{1,0:T(8,128)(2,1)S(1)} %dout_rows.3.refs_0_.refs_1_.refs_4_, bf16[192,640]{1,0:T(8,128)(2,1)S(1)} %collective-permute-done.11.refs_2_.refs_5_, ...), custom_call_target="tpu_custom_call" | custom-call | flops 1 | bytes 1 | tf_op jit(solution)/shard_map/pair/pallas_call | solution.py:33
  64.4 5.6 %collective-permute-start.15 = (bf16[512,640]{1,0:T(8,128)(2,1)S(1)}, bf16[512,640]{1,0:T(8,128)(2,1)S(1)}, u32[]{:S(2)}, u32[]{:S(2)}) collective-permute-start(bf16[512,640]{1,0:T(8,128)(2,1)S(1)} %pair.5), channel_id=1, source_target_pairs={{0,4},{4,0},{8,12},{12,8},{16,20},{20,16},{24,28},{28,24},{1,5},{5... | collective-permute-start | bytes 1966088 | tf_op jit(solution)/shard_map/pay_swap/ppermute | solution.py:386
  70.0 0.0 copy-done.2
  70.0 2.9 %key_grads.2 = (f32[256,256]{1,0:T(8,128)S(1)}, f32[256,256]{1,0:T(8,128)S(1)}) custom-call(s32[6]{0:T(128)S(1)} %stack.27.info, bf16[256,512]{1,0:T(8,128)(2,1)S(1)} %copy-done.2, bf16[256,512]{1,0:T(8,128)(2,1)S(1)} %copy-done.4, bf16[256,512]{1,0:T(8,128)(2,1)S(1)} %collective-permute-done.3.refs_1_, bf16[256,512]{1,0:T(8,128)(2,1)S(1)} %collective-permute-done.4.refs_2_, ...), custom_call_target="tpu_custom_call" | custom-call | flops 1 | bytes 1 | tf_op jit(solution)/shard_map/key_grads/pallas_call | solution.py:33
  72.9 0.0 collective-permute-done.15.refs_1_
  72.9 2.7 %key_grads.3 = (f32[256,256]{1,0:T(8,128)}, f32[256,256]{1,0:T(8,128)}) custom-call(s32[6]{0:T(128)S(1)} %stack.27.info, bf16[256,512]{1,0:T(8,128)(2,1)S(1)} %copy-done.2, bf16[512,512]{1,0:T(8,128)(2,1)S(1)} %collective-permute-done.5.refs_0_, bf16[512,640]{1,0:T(8,128)(2,1)S(1)} %collective-permute-done.15.refs_1_, ...), custom_call_target="tpu_custom_call" | custom-call | flops 1 | bytes 1 | tf_op jit(solution)/shard_map/key_grads/pallas_call | solution.py:33
  (1 shorter events, 0.0 us)
Async XLA Ops:
  0.6 16.6 %collective-permute-start.6 = (bf16[64,5376]{1,0:T(8,128)(2,1)}, bf16[64,5376]{1,0:T(8,128)(2,1)S(1)}, u32[]{:S(2)}, u32[]{:S(2)}) collective-permute-start(bf16[64,5376]{1,0:T(8,128)(2,1)} %refs_0_.3), channel_id=1, source_target_pairs={{0,1},{1,0},{2,3},{3,2},{4,5},{5,4},{6,7},{7,6},{8,9},{9,8},{10,11... | collective-permute-start | bytes 2064392 | tf_op jit(solution)/shard_map/end_first/ppermute | solution.py:390
  2.0 16.7 %collective-permute-start.8 = (bf16[64,5376]{1,0:T(8,128)(2,1)}, bf16[64,5376]{1,0:T(8,128)(2,1)}, u32[]{:S(2)}, u32[]{:S(2)}) collective-permute-start(bf16[64,5376]{1,0:T(8,128)(2,1)} %refs_0_.3), channel_id=1, source_target_pairs={{1,2},{2,1},{5,6},{6,5},{9,10},{10,9},{13,14},{14,13},{17,18},{18,... | collective-permute-start | bytes 2064392 | tf_op jit(solution)/shard_map/mid_first/ppermute | solution.py:390
  3.5 47.6 %slice-start = ((s8[5505024]{0:T(1024)(128)(4,1)}), s8[1310720]{0:T(1024)(128)(4,1)S(1)}, s32[]{:S(2)}) async-start(s8[5505024]{0:T(1024)(128)(4,1)} %bitcast.6), calls=%async_computation | async-start | bytes 2621440
  5.5 9.9 %collective-permute-start.3 = (bf16[256,512]{1,0:T(8,128)(2,1)}, bf16[256,512]{1,0:T(8,128)(2,1)S(1)}, u32[]{:S(2)}, u32[]{:S(2)}) collective-permute-start(bf16[256,512]{1,0:T(8,128)(2,1)} %get-tuple-element.21.refs_0_.query), channel_id=1, source_target_pairs={{8,0},{12,4},{16,8},{20,12},{24,16},{28,20},{9,1},{13,5},{17,9},{2... | collective-permute-start | bytes 786440 | tf_op jit(solution)/shard_map/q_near/ppermute | solution.py:386
  7.7 14.7 %collective-permute-start.4 = (bf16[256,512]{1,0:T(8,128)(2,1)}, bf16[256,512]{1,0:T(8,128)(2,1)S(1)}, u32[]{:S(2)}, u32[]{:S(2)}) collective-permute-start(bf16[256,512]{1,0:T(8,128)(2,1)} %get-tuple-element.21.refs_0_.query), channel_id=1, source_target_pairs={{16,0},{20,4},{24,8},{28,12},{17,1},{21,5},{25,9},{29,13},{18,2},{... | collective-permute-start | bytes 786440 | tf_op jit(solution)/shard_map/q_far/ppermute | solution.py:386
  9.0 15.5 %collective-permute-start = (bf16[256,512]{1,0:T(8,128)(2,1)}, bf16[256,512]{1,0:T(8,128)(2,1)S(1)}, u32[]{:S(2)}, u32[]{:S(2)}) collective-permute-start(bf16[256,512]{1,0:T(8,128)(2,1)} %get-tuple-element.20.refs_0_.kv), channel_id=1, source_target_pairs={{0,8},{4,12},{8,16},{12,20},{16,24},{20,28},{1,9},{5,13},{9,17},{1... | collective-permute-start | bytes 786440 | tf_op jit(solution)/shard_map/kv_near/ppermute | solution.py:386
  15.4 9.1 %collective-permute-start.1 = (bf16[256,512]{1,0:T(8,128)(2,1)}, bf16[256,512]{1,0:T(8,128)(2,1)S(1)}, u32[]{:S(2)}, u32[]{:S(2)}) collective-permute-start(bf16[256,512]{1,0:T(8,128)(2,1)} %get-tuple-element.20.refs_0_.kv), channel_id=1, source_target_pairs={{0,16},{4,20},{8,24},{12,28},{1,17},{5,21},{9,25},{13,29},{2,18},{... | collective-permute-start | bytes 786440 | tf_op jit(solution)/shard_map/kv_far/ppermute | solution.py:386
  17.2 15.1 %collective-permute-start.7 = (bf16[64,5376]{1,0:T(8,128)(2,1)S(1)}, bf16[64,5376]{1,0:T(8,128)(2,1)}, u32[]{:S(2)}, u32[]{:S(2)}) collective-permute-start(bf16[64,5376]{1,0:T(8,128)(2,1)S(1)} %collective-permute-done.6.refs_1_), channel_id=1, source_target_pairs={{1,2},{2,1},{5,6},{6,5},{9,10},{10,9},{13,14},{14,13},{17,18},{18,... | collective-permute-start | bytes 2064392 | tf_op jit(solution)/shard_map/mid_second/ppermute | solution.py:390
  18.7 17.2 %collective-permute-start.9 = (bf16[64,5376]{1,0:T(8,128)(2,1)}, bf16[64,5376]{1,0:T(8,128)(2,1)}, u32[]{:S(2)}, u32[]{:S(2)}) collective-permute-start(bf16[64,5376]{1,0:T(8,128)(2,1)} %collective-permute-done.8.refs_2_), channel_id=1, source_target_pairs={{1,0},{2,3},{5,4},{6,7},{9,8},{10,11},{13,12},{14,15},{17,16},{18,... | collective-permute-start | bytes 2064392 | tf_op jit(solution)/shard_map/out_second/ppermute | solution.py:390
  22.4 1.0 %copy-start.3 = (bf16[256,512]{1,0:T(8,128)(2,1)S(1)}, bf16[256,512]{1,0:T(8,128)(2,1)}, u32[]{:S(2)}) copy-start(bf16[256,512]{1,0:T(8,128)(2,1)} %get-tuple-element.21.refs_0_.query) | copy-start | bytes 786436
  23.3 4.7 %copy-start.4 = (bf16[256,512]{1,0:T(8,128)(2,1)S(1)}, bf16[256,512]{1,0:T(8,128)(2,1)}, u32[]{:S(2)}) copy-start(bf16[256,512]{1,0:T(8,128)(2,1)} %get-tuple-element.21.refs_0_.query) | copy-start | bytes 786436
  23.9 2.2 %collective-permute-start.5 = (bf16[512,512]{1,0:T(8,128)(2,1)S(1)}, bf16[512,512]{1,0:T(8,128)(2,1)S(1)}, u32[]{:S(2)}, u32[]{:S(2)}) collective-permute-start(bf16[512,512]{1,0:T(8,128)(2,1)S(1)} %pair.4), channel_id=1, source_target_pairs={{0,4},{4,0},{8,12},{12,8},{16,20},{20,16},{24,28},{28,24},{1,5},{5... | collective-permute-start | bytes 1572872 | tf_op jit(solution)/shard_map/q_swap/ppermute | solution.py:386
  24.5 1.0 %copy-start.1 = (bf16[256,512]{1,0:T(8,128)(2,1)S(1)}, bf16[256,512]{1,0:T(8,128)(2,1)}, u32[]{:S(2)}) copy-start(bf16[256,512]{1,0:T(8,128)(2,1)} %get-tuple-element.20.refs_0_.kv) | copy-start | bytes 786436
  25.4 11.8 %copy-start.5 = (bf16[64,5376]{1,0:T(8,128)(2,1)S(1)}, bf16[64,5376]{1,0:T(8,128)(2,1)}, u32[]{:S(2)}) copy-start(bf16[64,5376]{1,0:T(8,128)(2,1)} %refs_0_.3) | copy-start | bytes 2064388
  26.0 2.0 %collective-permute-start.2 = (bf16[512,512]{1,0:T(8,128)(2,1)S(1)}, bf16[512,512]{1,0:T(8,128)(2,1)S(1)}, u32[]{:S(2)}, u32[]{:S(2)}) collective-permute-start(bf16[512,512]{1,0:T(8,128)(2,1)S(1)} %pair.3), channel_id=1, source_target_pairs={{0,4},{4,0},{8,12},{12,8},{16,20},{20,16},{24,28},{28,24},{1,5},{5... | collective-permute-start | bytes 1572872 | tf_op jit(solution)/shard_map/kv_swap/ppermute | solution.py:386
  36.0 15.2 %collective-permute-start.10 = (bf16[64,5376]{1,0:T(8,128)(2,1)}, bf16[64,5376]{1,0:T(8,128)(2,1)S(1)}, u32[]{:S(2)}, u32[]{:S(2)}) collective-permute-start(bf16[64,5376]{1,0:T(8,128)(2,1)} %collective-permute-done.7.refs_0_), channel_id=1, source_target_pairs={{1,0},{2,3},{5,4},{6,7},{9,8},{10,11},{13,12},{14,15},{17,16},{18,... | collective-permute-start | bytes 2064392 | tf_op jit(solution)/shard_map/out_third/ppermute | solution.py:390
  37.3 2.6 %copy-start = (bf16[512,5376]{1,0:T(8,128)(2,1)S(1)}, bf16[512,5376]{1,0:T(8,128)(2,1)}, u32[]{:S(2)}) copy-start(bf16[512,5376]{1,0:T(8,128)(2,1)} %refs_2_.3) | copy-start | bytes 16515076
  39.8 11.3 %slice-start.1 = ((s8[5505024]{0:T(1024)(128)(4,1)}), s8[4194304]{0:T(1024)(128)(4,1)S(1)}, s32[]{:S(2)}) async-start(s8[5505024]{0:T(1024)(128)(4,1)} %bitcast.6), calls=%async_computation.1 | async-start | bytes 8388608
  43.4 18.0 %collective-permute-start.11 = (bf16[192,640]{1,0:T(8,128)(2,1)S(1)}, bf16[192,640]{1,0:T(8,128)(2,1)S(1)}, u32[]{:S(2)}, u32[]{:S(2)}) collective-permute-start(bf16[192,640]{1,0:T(8,128)(2,1)S(1)} %dout_rows.2.refs_0_.refs_3_), channel_id=1, source_target_pairs={{8,0},{12,4},{16,8},{20,12},{24,16},{28,20},{9,1},{13,5},{17,9},{2... | collective-permute-start | bytes 737288 | tf_op jit(solution)/shard_map/early_near/ppermute | solution.py:386
  47.0 14.5 %collective-permute-start.13 = (bf16[192,640]{1,0:T(8,128)(2,1)S(1)}, bf16[192,640]{1,0:T(8,128)(2,1)S(1)}, u32[]{:S(2)}, u32[]{:S(2)}) collective-permute-start(bf16[192,640]{1,0:T(8,128)(2,1)S(1)} %dout_rows.2.refs_0_.refs_3_), channel_id=1, source_target_pairs={{16,0},{20,4},{24,8},{28,12},{17,1},{21,5},{25,9},{29,13},{18,2},{... | collective-permute-start | bytes 737288 | tf_op jit(solution)/shard_map/early_far/ppermute | solution.py:386
  54.1 7.9 %collective-permute-start.12 = (bf16[64,640]{1,0:T(8,128)(2,1)S(1)}, bf16[64,640]{1,0:T(8,128)(2,1)S(1)}, u32[]{:S(2)}, u32[]{:S(2)}) collective-permute-start(bf16[64,640]{1,0:T(8,128)(2,1)S(1)} %dout_rows.3.refs_0_.refs_1_.refs_4_), channel_id=1, source_target_pairs={{8,0},{12,4},{16,8},{20,12},{24,16},{28,20},{9,1},{13,5},{17,9},{2... | collective-permute-start | bytes 245768 | tf_op jit(solution)/shard_map/late_near/ppermute | solution.py:386
  58.3 5.3 %collective-permute-start.14 = (bf16[64,640]{1,0:T(8,128)(2,1)S(1)}, bf16[64,640]{1,0:T(8,128)(2,1)S(1)}, u32[]{:S(2)}, u32[]{:S(2)}) collective-permute-start(bf16[64,640]{1,0:T(8,128)(2,1)S(1)} %dout_rows.3.refs_0_.refs_1_.refs_4_), channel_id=1, source_target_pairs={{16,0},{20,4},{24,8},{28,12},{17,1},{21,5},{25,9},{29,13},{18,2},{... | collective-permute-start | bytes 245768 | tf_op jit(solution)/shard_map/late_far/ppermute | solution.py:386
  59.6 10.4 %copy-start.2 = (bf16[256,512]{1,0:T(8,128)(2,1)S(1)}, bf16[256,512]{1,0:T(8,128)(2,1)}, u32[]{:S(2)}) copy-start(bf16[256,512]{1,0:T(8,128)(2,1)} %get-tuple-element.20.refs_0_.kv) | copy-start | bytes 786436
  64.4 8.5 %collective-permute-start.15 = (bf16[512,640]{1,0:T(8,128)(2,1)S(1)}, bf16[512,640]{1,0:T(8,128)(2,1)S(1)}, u32[]{:S(2)}, u32[]{:S(2)}) collective-permute-start(bf16[512,640]{1,0:T(8,128)(2,1)S(1)} %pair.5), channel_id=1, source_target_pairs={{0,4},{4,0},{8,12},{12,8},{16,20},{20,16},{24,28},{28,24},{1,5},{5... | collective-permute-start | bytes 1966088 | tf_op jit(solution)/shard_map/pay_swap/ppermute | solution.py:386

commit v3 on v2

--- a/solution.py
+++ b/solution.py
@@ -44,6 +44,22 @@
 
 
 TOKEN = jax.ShapeDtypeStruct((8, HD), F32)
+
+
+def token_kernel(*refs):
+    refs[-1][...] = jnp.zeros_like(refs[-1])
+
+
+def token_of(*arrays):
+    return pl.pallas_call(
+        token_kernel,
+        out_shape=TOKEN,
+        in_specs=[ANY] * len(arrays),
+        out_specs=VMEM,
+        compiler_params=params(),
+        cost_estimate=pl.CostEstimate(flops=2 * 10**9, bytes_accessed=1, transcendentals=0),
+        name="token",
+    )(*arrays)
 
 
 def pack_kernel(places, *refs):
@@ -277,20 +293,21 @@
     )
 
 
-def key_kernel(slots, blocks, q_count, d_count, info, kv, *refs):
+def key_kernel(blocks, q_count, d_count, info, kv, *refs):
     q_refs, d_refs = refs[:q_count], refs[q_count : q_count + d_count]
     before = refs[q_count + d_count : -7]
     grad_k, grad_v, q_cat, d_cat, held_k, held_v, sems = refs[-7:]
     rows, kv_width = kv.shape[0], kv.shape[1] // 2
     width = q_cat.shape[1]
     lanes = q_cat.shape[0]
-    total = lanes // len(blocks)
-    part_rows = total // len(slots)
+    part_rows = lanes // sum(len(block[1]) for block in blocks)
     lane = lax.broadcasted_iota(jnp.int32, (1, lanes), 1)
     low = jnp.zeros((1, lanes), jnp.int32)
     high = jnp.full((1, lanes), rows, jnp.int32)
-    for m, (distance, q_at, q_row, d_at, d_row) in enumerate(blocks):
-        at = m * total
+    at = 0
+    for distance, slots, q_at, q_row, d_at, d_row in blocks:
+        size = len(slots) * part_rows
+        d_cat[at : at + size, :] = d_refs[d_at][d_row : d_row + size, :]
         for slot in slots:
             start = pl.multiple_of(info[2 + slot], 16)
             q_cat[at : at + part_rows, :] = q_refs[q_at][pl.ds(start + q_row, part_rows), :]
@@ -300,11 +317,6 @@
             if distance == SPAN_BLOCKS - 1:
                 low = jnp.where(inside, lane - at + start + 1, low)
             at += part_rows
-        at = m * total
-        for n in d_at:
-            size = min(d_refs[n].shape[0], total)
-            d_cat[at : at + size, :] = d_refs[n][d_row : d_row + size, :]
-            at += size
 
     masked = any(block[0] in (0, SPAN_BLOCKS - 1) for block in blocks)
     key_row = lax.broadcasted_iota(jnp.int32, (rows, lanes), 0)
@@ -352,14 +364,14 @@
         copy.wait()
 
 
-def key_grads(info, slots, blocks, kv, q_arrays, d_arrays, total, before=()):
-    lanes = len(blocks) * total
+def key_grads(info, blocks, kv, q_arrays, d_arrays, slot_rows, before=()):
+    lanes = sum(len(block[1]) for block in blocks) * slot_rows
     width = q_arrays[0].shape[1]
     kv_width = kv.shape[1] // 2
     shape = jax.ShapeDtypeStruct((kv.shape[0], kv_width), F32)
     held = pltpu.VMEM(shape.shape, F32)
     return call(
-        functools.partial(key_kernel, slots, blocks, len(q_arrays), len(d_arrays)),
+        functools.partial(key_kernel, blocks, len(q_arrays), len(d_arrays)),
         "key_grads",
         (shape, shape),
         info,
@@ -430,27 +442,29 @@
         far = along(pay, moved(-4), name + "_far")
         return near, far
 
-    mid_second, out_second, stats = lax.optimization_barrier((mid_second, out_second, stats))
+    second_came = token_of(out_second, mid_second)
+    mid_second, second_came, stats = lax.optimization_barrier((mid_second, second_came, stats))
     out_third = over(mid_second, outward, "out_third")
     statistics = (out_weight, mixed, stats)
     early, late = {0: 1, 1: 1, 2: 2}, {3: 2}
-    pay_a = dout_rows(info, early, (grad_out, end_first, mid_first, out_second), *statistics)
+    pay_a = dout_rows(info, early, (grad_out, end_first, mid_first, out_second), *statistics, (second_came,))
     near_a, far_a = sent(pay_a, "early")
     grad_q, queries_done = query_grads(info, early, (pay_a,), probs, span)
 
     pay_b = dout_rows(info, late, (mid_second, out_third), *statistics, (queries_done,))
     near_b, far_b = sent(pay_b, "late")
     grad_q, queries_done = query_grads(info, late, (pay_b,), probs, span, (grad_q,))
+    a, b = (0, 1, 2), (3,)
+    evens = (query, near_q, far_q)
+    blocks = ((0, a, 0, 0, 0, 0), (2, a, 1, 0, 1, 0), (4, a, 2, 0, 2, 0), (0, b, 0, 0, 3, 0))
+    grads = key_grads(info, blocks, kv, evens, (pay_a, near_a, far_a, pay_b), slot_rows)
     pays = ((pay_a, pay_b), (near_a, near_b), (far_a, far_b))
-    pair = pair_for_peer(info, 1, *pays, (queries_done,))
+    pair = pair_for_peer(info, 1, *pays, (queries_done, grads[0]))
     odd = along(pair, swap, "pay_swap")
-    slots = (0, 1, 2, 3)
-    even_blocks = ((0, 0, 0, (0, 1), 0), (2, 1, 0, (2, 3), 0), (4, 2, 0, (4, 5), 0))
-    even = key_grads(
-        info, slots, even_blocks, kv, (query, near_q, far_q), sum(pays, ()), rows
-    )
-    odd_blocks = ((1, 0, 0, (0,), 0), (3, 0, rows, (0,), rows))
-    grad_k, grad_v = key_grads(info, slots, odd_blocks, kv, (odd_q,), (odd,), rows, even)
+    blocks = ((2, b, 0, 0, 0, 0), (4, b, 1, 0, 1, 0))
+    grads = key_grads(info, blocks, kv, evens[1:], (near_b, far_b), slot_rows, grads)
+    blocks = ((1, a + b, 0, 0, 0, 0), (3, a + b, 0, rows, 0, rows))
+    grad_k, grad_v = key_grads(info, blocks, kv, (odd_q,), (odd,), slot_rows, grads)
     return (grad_q, grad_k, grad_v)
 
 

time: 76.3 us -> 74.2 us (0.972)
  starting transfers between devices: 32.3 us -> 29.4 us
  waiting for transfers between devices: 13.1 us -> 15.7 us
  local copies, waits for them, and re-layouts: 4.56 us -> 2.01 us
    ppermute x5, waiting for transfers between devices: 4.42 us -> 9.13 us  [over(): return lax.ppermute(x, 'tp', pairs)]
    unnamed x16 -> x12, local copies, waits for them, and re-layouts: 4.48 us -> 1.92 us
    ppermute x11, waiting for transfers between devices: 8.72 us -> 6.54 us  [along(): return lax.ppermute(x, 'ctx', pairs)]
    ppermute x5, starting transfers between devices: 6.96 us -> 5.32 us  [over(): return lax.ppermute(x, 'tp', pairs)]
    ppermute x11, starting transfers between devices: 25.3 us -> 24.1 us  [along(): return lax.ppermute(x, 'ctx', pairs)]
    pallas_call x10 -> x11, Pallas kernels: 22.7 us -> 23.1 us  [call(): pl.pallas_call(kernel, out_shape=shapes, in_specs=[SMEM] + [VMEM] * len(a...]
  transfers between devices with their start and end apart: 16 -> 16, of which waited for: 8 -> 7; matrix products, arithmetic and copies ran while one was open for 0% -> 0% of each run, Pallas kernels for 28% -> 30%
where the time goes in v3:
time: 74.2 us; the launch traced here: 73 us
  starting transfers between devices  29.4 us (40%)
  Pallas kernels  25 us (34%)
  waiting for transfers between devices  15.7 us (21%)
  local copies, waits for them, and re-layouts  2.01 us (3%)
  between operations  0.94 us (1%)
    ppermute x11, starting transfers between devices, along(): return lax.ppermute(x, 'ctx', pairs)  24.1 us
    pallas_call x11, Pallas kernels, call(): pl.pallas_call(kernel, out_shape=shapes, in_specs=[SMEM] + [VMEM] * len(a...  23.1 us
    ppermute x5, waiting for transfers between devices, over(): return lax.ppermute(x, 'tp', pairs)  9.13 us
    ppermute x11, waiting for transfers between devices, along(): return lax.ppermute(x, 'ctx', pairs)  6.54 us
    ppermute x5, starting transfers between devices, over(): return lax.ppermute(x, 'tp', pairs)  5.32 us
    unnamed x12, local copies, waits for them, and re-layouts  1.92 us
    pallas_call x1, Pallas kernels, pack(): pl.pallas_call(functools.partial(pack_kernel, places), out_shape=tuple((j...  1.9 us
  transfers between devices with their start and end apart: 16, of which 7 were waited for; matrix products, arithmetic and copies ran while one was open for 0% of the time, Pallas kernels for 30%

profile of v3, /device:TPU:3, one launch (start us, length us, event | category | flops | bytes accessed | tf_op | source)
XLA Modules:
  0.0 73.0 jit_solution(7552730940113889296)
XLA Ops:
  0.6 1.4 %collective-permute-start.6 = (bf16[64,5376]{1,0:T(8,128)(2,1)}, bf16[64,5376]{1,0:T(8,128)(2,1)S(1)}, u32[]{:S(2)}, u32[]{:S(2)}) collective-permute-start(bf16[64,5376]{1,0:T(8,128)(2,1)} %refs_0_.3), channel_id=1, source_target_pairs={{0,1},{1,0},{2,3},{3,2},{4,5},{5,4},{6,7},{7,6},{8,9},{9,8},{10,11... | collective-permute-start | bytes 2064392 | tf_op jit(solution)/shard_map/end_first/ppermute | solution.py:402
  2.0 0.7 collective-permute-start.8
  2.7 1.9 %pack.1 = (bf16[256,512]{1,0:T(8,128)(2,1)}, bf16[256,512]{1,0:T(8,128)(2,1)}) custom-call(bf16[256,256]{1,0:T(8,128)(2,1)} %refs_0_.2, bf16[256,256]{1,0:T(8,128)(2,1)} %refs_1_.1, bf16[256,512]{1,0:T(8,128)(2,1)} %refs_2_.2), custom_call_target="tpu_custom_call" | custom-call | flops 1 | bytes 1 | tf_op jit(solution)/shard_map/pack/pallas_call | solution.py:79
  4.6 2.2 %collective-permute-start.3 = (bf16[256,512]{1,0:T(8,128)(2,1)}, bf16[256,512]{1,0:T(8,128)(2,1)S(1)}, u32[]{:S(2)}, u32[]{:S(2)}) collective-permute-start(bf16[256,512]{1,0:T(8,128)(2,1)} %get-tuple-element.23.refs_0_.query), channel_id=1, source_target_pairs={{8,0},{12,4},{16,8},{20,12},{24,16},{28,20},{9,1},{13,5},{17,9},{2... | collective-permute-start | bytes 786440 | tf_op jit(solution)/shard_map/q_near/ppermute | solution.py:398
  6.8 1.3 %collective-permute-start.4 = (bf16[256,512]{1,0:T(8,128)(2,1)}, bf16[256,512]{1,0:T(8,128)(2,1)S(1)}, u32[]{:S(2)}, u32[]{:S(2)}) collective-permute-start(bf16[256,512]{1,0:T(8,128)(2,1)} %get-tuple-element.23.refs_0_.query), channel_id=1, source_target_pairs={{16,0},{20,4},{24,8},{28,12},{17,1},{21,5},{25,9},{29,13},{18,2},{... | collective-permute-start | bytes 786440 | tf_op jit(solution)/shard_map/q_far/ppermute | solution.py:398
  8.1 4.0 %collective-permute-start = (bf16[256,512]{1,0:T(8,128)(2,1)}, bf16[256,512]{1,0:T(8,128)(2,1)S(1)}, u32[]{:S(2)}, u32[]{:S(2)}) collective-permute-start(bf16[256,512]{1,0:T(8,128)(2,1)} %get-tuple-element.22.refs_0_.kv), channel_id=1, source_target_pairs={{0,8},{4,12},{8,16},{12,20},{16,24},{20,28},{1,9},{5,13},{9,17},{1... | collective-permute-start | bytes 786440 | tf_op jit(solution)/shard_map/kv_near/ppermute | solution.py:398
  12.1 2.4 %collective-permute-done.3.refs_1_.refs_0_ = bf16[256,512]{1,0:T(8,128)(2,1)S(1)} collective-permute-done((bf16[256,512]{1,0:T(8,128)(2,1)}, bf16[256,512]{1,0:T(8,128)(2,1)S(1)}, u32[]{:S(2)}, u32[]{:S(2)}) %collective-permute-start.3) | collective-permute-done | bytes 262176 | tf_op jit(solution)/shard_map/q_near/ppermute | solution.py:398
  14.5 1.3 %collective-permute-start.1 = (bf16[256,512]{1,0:T(8,128)(2,1)}, bf16[256,512]{1,0:T(8,128)(2,1)S(1)}, u32[]{:S(2)}, u32[]{:S(2)}) collective-permute-start(bf16[256,512]{1,0:T(8,128)(2,1)} %get-tuple-element.22.refs_0_.kv), channel_id=1, source_target_pairs={{0,16},{4,20},{8,24},{12,28},{1,17},{5,21},{9,25},{13,29},{2,18},{... | collective-permute-start | bytes 786440 | tf_op jit(solution)/shard_map/kv_far/ppermute | solution.py:398
  15.8 1.4 %collective-permute-done.6.refs_1_ = bf16[64,5376]{1,0:T(8,128)(2,1)S(1)} collective-permute-done((bf16[64,5376]{1,0:T(8,128)(2,1)}, bf16[64,5376]{1,0:T(8,128)(2,1)S(1)}, u32[]{:S(2)}, u32[]{:S(2)}) %collective-permute-start.6) | collective-permute-done | bytes 688160 | tf_op jit(solution)/shard_map/end_first/ppermute | solution.py:402
  17.2 0.7 collective-permute-start.7
  17.9 0.0 collective-permute-done.8.refs_2_
  17.9 1.3 %collective-permute-start.9 = (bf16[64,5376]{1,0:T(8,128)(2,1)S(1)}, bf16[64,5376]{1,0:T(8,128)(2,1)}, u32[]{:S(2)}, u32[]{:S(2)}) collective-permute-start(bf16[64,5376]{1,0:T(8,128)(2,1)S(1)} %collective-permute-done.8.refs_2_), channel_id=1, source_target_pairs={{1,0},{2,3},{5,4},{6,7},{9,8},{10,11},{13,12},{14,15},{17,16},{18,... | collective-permute-start | bytes 2064392 | tf_op jit(solution)/shard_map/out_second/ppermute | solution.py:402
  19.2 0.1 stack.27.info
  19.3 2.1 %collective-permute-done.4.refs_2_.refs_1_ = bf16[256,512]{1,0:T(8,128)(2,1)S(1)} collective-permute-done((bf16[256,512]{1,0:T(8,128)(2,1)}, bf16[256,512]{1,0:T(8,128)(2,1)S(1)}, u32[]{:S(2)}, u32[]{:S(2)}) %collective-permute-start.4) | collective-permute-done | bytes 262176 | tf_op jit(solution)/shard_map/q_far/ppermute | solution.py:398
  21.4 0.0 copy-start.3
  21.4 0.9 %copy-done.3 = bf16[256,512]{1,0:T(8,128)(2,1)S(1)} copy-done((bf16[256,512]{1,0:T(8,128)(2,1)S(1)}, bf16[256,512]{1,0:T(8,128)(2,1)}, u32[]{:S(2)}) %copy-start.3) | copy-done | bytes 262168
  22.4 0.0 copy-start.4
  22.4 0.6 pair.4
  23.0 0.6 collective-permute-start.5
  23.6 0.0 collective-permute-done.refs_1_.near
  23.6 0.0 collective-permute-done.1.refs_2_.far
  23.6 0.0 copy-start.1
  23.6 0.9 %copy-done.1 = bf16[256,512]{1,0:T(8,128)(2,1)S(1)} copy-done((bf16[256,512]{1,0:T(8,128)(2,1)S(1)}, bf16[256,512]{1,0:T(8,128)(2,1)}, u32[]{:S(2)}) %copy-start.1) | copy-done | bytes 262168
  24.5 0.6 pair.3
  25.1 0.1 collective-permute-start.2
  25.2 0.0 collective-permute-done.5.refs_0_
  25.2 1.9 %collective-permute-done.2.odd = bf16[512,512]{1,0:T(8,128)(2,1)S(1)} collective-permute-done((bf16[512,512]{1,0:T(8,128)(2,1)S(1)}, bf16[512,512]{1,0:T(8,128)(2,1)S(1)}, u32[]{:S(2)}, u32[]{:S(2)}) %collective-permute-start.2) | collective-permute-done | bytes 524320 | tf_op jit(solution)/shard_map/kv_swap/ppermute | solution.py:398
  27.1 0.0 copy-done.4
  27.1 4.2 %attention_probs.1 = (bf16[4,256,1280]{2,1,0:T(8,128)(2,1)S(1)}, f32[256,512]{1,0:T(8,128)S(1)}, bf16[256,128]{1,0:T(8,128)(2,1)S(1)}, bf16[1280,512]{1,0:T(8,128)(2,1)S(1)}) custom-call(s32[6]{0:T(128)S(1)} %stack.27.info, bf16[256,512]{1,0:T(8,128)(2,1)S(1)} %copy-done.1, bf16[256,512]{1,0:T(8,128)(2,1)S(1)} %copy-done.4, ...), custom_call_target="tpu_custom_call" | custom-call | flops 1 | bytes 1 | tf_op jit(solution)/shard_map/attention_probs/pallas_call | solution.py:33
  31.3 0.0 copy-start
  31.3 0.0 copy-start.5
  31.4 0.0 collective-permute-done.7.refs_1_.refs_0_
  31.4 4.3 %collective-permute-done.9.refs_0_.refs_3_ = bf16[64,5376]{1,0:T(8,128)(2,1)} collective-permute-done((bf16[64,5376]{1,0:T(8,128)(2,1)S(1)}, bf16[64,5376]{1,0:T(8,128)(2,1)}, u32[]{:S(2)}, u32[]{:S(2)}) %collective-permute-start.9) | collective-permute-done | bytes 688160 | tf_op jit(solution)/shard_map/out_second/ppermute | solution.py:402
  35.7 1.3 %collective-permute-start.10 = (bf16[64,5376]{1,0:T(8,128)(2,1)S(1)}, bf16[64,5376]{1,0:T(8,128)(2,1)S(1)}, u32[]{:S(2)}, u32[]{:S(2)}) collective-permute-start(bf16[64,5376]{1,0:T(8,128)(2,1)S(1)} %collective-permute-done.7.refs_1_.refs_0_), channel_id=1, source_target_pairs={{1,0},{2,3},{5,4},{6,7},{9,8},{10,11},{13,12},{14,15},{17,16},{18,... | collective-permute-start | bytes 2064392 | tf_op jit(solution)/shard_map/out_third/ppermute | solution.py:402
  36.9 0.0 copy-done
  37.0 0.0 copy-done.5
  37.0 3.2 %dout_rows.2.refs_0_.refs_3_ = bf16[192,640]{1,0:T(8,128)(2,1)S(1)} custom-call(s32[6]{0:T(128)S(1)} %stack.27.info, bf16[64,5376]{1,0:T(8,128)(2,1)S(1)} %copy-done.5, bf16[64,5376]{1,0:T(8,128)(2,1)S(1)} %collective-permute-done.6.refs_1_, bf16[64,5376]{1,0:T(8,128)(2,1)S(1)} %collective-permute-done.8.refs_2_, ...), custom_call_target="tpu_custom_call" | custom-call | flops 1 | bytes 1 | tf_op jit(solution)/shard_map/dout_rows/pallas_call | solution.py:33
  40.2 3.4 %collective-permute-start.11 = (bf16[192,640]{1,0:T(8,128)(2,1)S(1)}, bf16[192,640]{1,0:T(8,128)(2,1)S(1)}, u32[]{:S(2)}, u32[]{:S(2)}) collective-permute-start(bf16[192,640]{1,0:T(8,128)(2,1)S(1)} %dout_rows.2.refs_0_.refs_3_), channel_id=1, source_target_pairs={{8,0},{12,4},{16,8},{20,12},{24,16},{28,20},{9,1},{13,5},{17,9},{2... | collective-permute-start | bytes 737288 | tf_op jit(solution)/shard_map/early_near/ppermute | solution.py:398
  43.5 1.3 %collective-permute-start.13 = (bf16[192,640]{1,0:T(8,128)(2,1)S(1)}, bf16[192,640]{1,0:T(8,128)(2,1)S(1)}, u32[]{:S(2)}, u32[]{:S(2)}) collective-permute-start(bf16[192,640]{1,0:T(8,128)(2,1)S(1)} %dout_rows.2.refs_0_.refs_3_), channel_id=1, source_target_pairs={{16,0},{20,4},{24,8},{28,12},{17,1},{21,5},{25,9},{29,13},{18,2},{... | collective-permute-start | bytes 737288 | tf_op jit(solution)/shard_map/early_far/ppermute | solution.py:398
  44.8 2.6 %query_grads.2 = (f32[256,512]{1,0:T(8,128)}, f32[8,128]{1,0:T(8,128)S(1)}) custom-call(s32[6]{0:T(128)S(1)} %stack.27.info, bf16[4,256,1280]{2,1,0:T(8,128)(2,1)S(1)} %get-tuple-element.24.probs, bf16[1280,512]{1,0:T(8,128)(2,1)S(1)} %get-tuple-element.25.span, bf16[192,640]{1,0:T(8,128)(2,1)S(1)} %dout_rows.2.refs_0_.refs_3_), custom_call_target="tpu_custom_call" | custom-call | flops 1 | bytes 1 | tf_op jit(solution)/shard_map/query_grads/pallas_call | solution.py:33
  47.5 3.4 %collective-permute-done.10.refs_1_ = bf16[64,5376]{1,0:T(8,128)(2,1)S(1)} collective-permute-done((bf16[64,5376]{1,0:T(8,128)(2,1)S(1)}, bf16[64,5376]{1,0:T(8,128)(2,1)S(1)}, u32[]{:S(2)}, u32[]{:S(2)}) %collective-permute-start.10) | collective-permute-done | bytes 688160 | tf_op jit(solution)/shard_map/out_third/ppermute | solution.py:402
  50.9 2.4 %dout_rows.3.refs_0_.refs_6_.refs_1_ = bf16[64,640]{1,0:T(8,128)(2,1)S(1)} custom-call(s32[6]{0:T(128)S(1)} %stack.27.info, bf16[64,5376]{1,0:T(8,128)(2,1)S(1)} %collective-permute-done.7.refs_1_.refs_0_, bf16[64,5376]{1,0:T(8,128)(2,1)S(1)} %collective-permute-done.10.refs_1_, bf16[512,5376]{1,0:T(8,128)(2,1)S(1)} %copy-done, ...), custom_call_target="tpu_custom_call" | custom-call | flops 1 | bytes 1 | tf_op jit(solution)/shard_map/dout_rows/pallas_call | solution.py:33
  53.3 0.0 copy-start.2
  53.3 3.7 %collective-permute-start.12 = (bf16[64,640]{1,0:T(8,128)(2,1)S(1)}, bf16[64,640]{1,0:T(8,128)(2,1)S(1)}, u32[]{:S(2)}, u32[]{:S(2)}) collective-permute-start(bf16[64,640]{1,0:T(8,128)(2,1)S(1)} %dout_rows.3.refs_0_.refs_6_.refs_1_), channel_id=1, source_target_pairs={{8,0},{12,4},{16,8},{20,12},{24,16},{28,20},{9,1},{13,5},{17,9},{2... | collective-permute-start | bytes 245768 | tf_op jit(solution)/shard_map/late_near/ppermute | solution.py:398
  57.0 1.3 %collective-permute-start.14 = (bf16[64,640]{1,0:T(8,128)(2,1)S(1)}, bf16[64,640]{1,0:T(8,128)(2,1)S(1)}, u32[]{:S(2)}, u32[]{:S(2)}) collective-permute-start(bf16[64,640]{1,0:T(8,128)(2,1)S(1)} %dout_rows.3.refs_0_.refs_6_.refs_1_), channel_id=1, source_target_pairs={{16,0},{20,4},{24,8},{28,12},{17,1},{21,5},{25,9},{29,13},{18,2},{... | collective-permute-start | bytes 245768 | tf_op jit(solution)/shard_map/late_far/ppermute | solution.py:398
  58.3 1.8 %query_grads.3 = (f32[256,512]{1,0:T(8,128)}, f32[8,128]{1,0:T(8,128)S(1)}) custom-call(s32[6]{0:T(128)S(1)} %stack.27.info, bf16[4,256,1280]{2,1,0:T(8,128)(2,1)S(1)} %get-tuple-element.24.probs, bf16[1280,512]{1,0:T(8,128)(2,1)S(1)} %get-tuple-element.25.span, ...), custom_call_target="tpu_custom_call", output_to_operand_aliasing={{0}: (4, {})} | custom-call | flops 1 | bytes 1 | tf_op jit(solution)/shard_map/query_grads/pallas_call | solution.py:33
  60.1 0.0 collective-permute-done.11.refs_4_.refs_2_
  60.1 0.0 collective-permute-done.13.refs_5_.refs_4_
  60.2 0.0 copy-done.2
  60.2 2.8 %key_grads.3 = (f32[256,256]{1,0:T(8,128)S(1)}, f32[256,256]{1,0:T(8,128)S(1)}) custom-call(s32[6]{0:T(128)S(1)} %stack.27.info, bf16[256,512]{1,0:T(8,128)(2,1)S(1)} %copy-done.2, bf16[256,512]{1,0:T(8,128)(2,1)S(1)} %copy-done.4, bf16[256,512]{1,0:T(8,128)(2,1)S(1)} %collective-permute-done.3.refs_1_.refs_0_, ...), custom_call_target="tpu_custom_call" | custom-call | flops 1 | bytes 1 | tf_op jit(solution)/shard_map/key_grads/pallas_call | solution.py:33
  63.0 0.0 collective-permute-done.12.refs_3_.refs_2_
  63.0 0.0 collective-permute-done.14.refs_5_.refs_3_
  63.0 0.6 pair.5
  63.6 5.0 %collective-permute-start.15 = (bf16[512,640]{1,0:T(8,128)(2,1)S(1)}, bf16[512,640]{1,0:T(8,128)(2,1)S(1)}, u32[]{:S(2)}, u32[]{:S(2)}) collective-permute-start(bf16[512,640]{1,0:T(8,128)(2,1)S(1)} %pair.5), channel_id=1, source_target_pairs={{0,4},{4,0},{8,12},{12,8},{16,20},{20,16},{24,28},{28,24},{1,5},{5... | collective-permute-start | bytes 1966088 | tf_op jit(solution)/shard_map/pay_swap/ppermute | solution.py:398
  68.6 1.6 %key_grads.4 = (f32[256,256]{1,0:T(8,128)S(1)}, f32[256,256]{1,0:T(8,128)S(1)}) custom-call(s32[6]{0:T(128)S(1)} %stack.27.info, bf16[256,512]{1,0:T(8,128)(2,1)S(1)} %copy-done.2, bf16[256,512]{1,0:T(8,128)(2,1)S(1)} %collective-permute-done.3.refs_1_.refs_0_, bf16[256,512]{1,0:T(8,128)(2,1)S(1)} %collective-permute-done.4.refs_2_.refs_1_, ...), custom_call_target="tpu_custom_call" | custom-call | flops 1 | bytes 1 | tf_op jit(solution)/shard_map/key_grads/pallas_call | solution.py:33
  70.2 0.1 collective-permute-done.15.refs_1_
  70.3 2.7 %key_grads.5 = (f32[256,256]{1,0:T(8,128)}, f32[256,256]{1,0:T(8,128)}) custom-call(s32[6]{0:T(128)S(1)} %stack.27.info, bf16[256,512]{1,0:T(8,128)(2,1)S(1)} %copy-done.2, bf16[512,512]{1,0:T(8,128)(2,1)S(1)} %collective-permute-done.5.refs_0_, bf16[512,640]{1,0:T(8,128)(2,1)S(1)} %collective-permute-done.15.refs_1_, ...), custom_call_target="tpu_custom_call" | custom-call | flops 1 | bytes 1 | tf_op jit(solution)/shard_map/key_grads/pallas_call | solution.py:33
  (1 shorter events, 0.0 us)
Async XLA Ops:
  0.6 16.6 %collective-permute-start.6 = (bf16[64,5376]{1,0:T(8,128)(2,1)}, bf16[64,5376]{1,0:T(8,128)(2,1)S(1)}, u32[]{:S(2)}, u32[]{:S(2)}) collective-permute-start(bf16[64,5376]{1,0:T(8,128)(2,1)} %refs_0_.3), channel_id=1, source_target_pairs={{0,1},{1,0},{2,3},{3,2},{4,5},{5,4},{6,7},{7,6},{8,9},{9,8},{10,11... | collective-permute-start | bytes 2064392 | tf_op jit(solution)/shard_map/end_first/ppermute | solution.py:402
  2.0 15.9 %collective-permute-start.8 = (bf16[64,5376]{1,0:T(8,128)(2,1)}, bf16[64,5376]{1,0:T(8,128)(2,1)S(1)}, u32[]{:S(2)}, u32[]{:S(2)}) collective-permute-start(bf16[64,5376]{1,0:T(8,128)(2,1)} %refs_0_.3), channel_id=1, source_target_pairs={{1,2},{2,1},{5,6},{6,5},{9,10},{10,9},{13,14},{14,13},{17,18},{18,... | collective-permute-start | bytes 2064392 | tf_op jit(solution)/shard_map/mid_first/ppermute | solution.py:402
  4.6 9.9 %collective-permute-start.3 = (bf16[256,512]{1,0:T(8,128)(2,1)}, bf16[256,512]{1,0:T(8,128)(2,1)S(1)}, u32[]{:S(2)}, u32[]{:S(2)}) collective-permute-start(bf16[256,512]{1,0:T(8,128)(2,1)} %get-tuple-element.23.refs_0_.query), channel_id=1, source_target_pairs={{8,0},{12,4},{16,8},{20,12},{24,16},{28,20},{9,1},{13,5},{17,9},{2... | collective-permute-start | bytes 786440 | tf_op jit(solution)/shard_map/q_near/ppermute | solution.py:398
  6.8 14.7 %collective-permute-start.4 = (bf16[256,512]{1,0:T(8,128)(2,1)}, bf16[256,512]{1,0:T(8,128)(2,1)S(1)}, u32[]{:S(2)}, u32[]{:S(2)}) collective-permute-start(bf16[256,512]{1,0:T(8,128)(2,1)} %get-tuple-element.23.refs_0_.query), channel_id=1, source_target_pairs={{16,0},{20,4},{24,8},{28,12},{17,1},{21,5},{25,9},{29,13},{18,2},{... | collective-permute-start | bytes 786440 | tf_op jit(solution)/shard_map/q_far/ppermute | solution.py:398
  8.1 15.5 %collective-permute-start = (bf16[256,512]{1,0:T(8,128)(2,1)}, bf16[256,512]{1,0:T(8,128)(2,1)S(1)}, u32[]{:S(2)}, u32[]{:S(2)}) collective-permute-start(bf16[256,512]{1,0:T(8,128)(2,1)} %get-tuple-element.22.refs_0_.kv), channel_id=1, source_target_pairs={{0,8},{4,12},{8,16},{12,20},{16,24},{20,28},{1,9},{5,13},{9,17},{1... | collective-permute-start | bytes 786440 | tf_op jit(solution)/shard_map/kv_near/ppermute | solution.py:398
  14.5 9.1 %collective-permute-start.1 = (bf16[256,512]{1,0:T(8,128)(2,1)}, bf16[256,512]{1,0:T(8,128)(2,1)S(1)}, u32[]{:S(2)}, u32[]{:S(2)}) collective-permute-start(bf16[256,512]{1,0:T(8,128)(2,1)} %get-tuple-element.22.refs_0_.kv), channel_id=1, source_target_pairs={{0,16},{4,20},{8,24},{12,28},{1,17},{5,21},{9,25},{13,29},{2,18},{... | collective-permute-start | bytes 786440 | tf_op jit(solution)/shard_map/kv_far/ppermute | solution.py:398
  17.2 14.2 %collective-permute-start.7 = (bf16[64,5376]{1,0:T(8,128)(2,1)S(1)}, bf16[64,5376]{1,0:T(8,128)(2,1)S(1)}, u32[]{:S(2)}, u32[]{:S(2)}) collective-permute-start(bf16[64,5376]{1,0:T(8,128)(2,1)S(1)} %collective-permute-done.6.refs_1_), channel_id=1, source_target_pairs={{1,2},{2,1},{5,6},{6,5},{9,10},{10,9},{13,14},{14,13},{17,18},{18,... | collective-permute-start | bytes 2064392 | tf_op jit(solution)/shard_map/mid_second/ppermute | solution.py:402
  17.9 17.7 %collective-permute-start.9 = (bf16[64,5376]{1,0:T(8,128)(2,1)S(1)}, bf16[64,5376]{1,0:T(8,128)(2,1)}, u32[]{:S(2)}, u32[]{:S(2)}) collective-permute-start(bf16[64,5376]{1,0:T(8,128)(2,1)S(1)} %collective-permute-done.8.refs_2_), channel_id=1, source_target_pairs={{1,0},{2,3},{5,4},{6,7},{9,8},{10,11},{13,12},{14,15},{17,16},{18,... | collective-permute-start | bytes 2064392 | tf_op jit(solution)/shard_map/out_second/ppermute | solution.py:402
  21.4 1.0 %copy-start.3 = (bf16[256,512]{1,0:T(8,128)(2,1)S(1)}, bf16[256,512]{1,0:T(8,128)(2,1)}, u32[]{:S(2)}) copy-start(bf16[256,512]{1,0:T(8,128)(2,1)} %get-tuple-element.23.refs_0_.query) | copy-start | bytes 786436
  22.4 4.7 %copy-start.4 = (bf16[256,512]{1,0:T(8,128)(2,1)S(1)}, bf16[256,512]{1,0:T(8,128)(2,1)}, u32[]{:S(2)}) copy-start(bf16[256,512]{1,0:T(8,128)(2,1)} %get-tuple-element.23.refs_0_.query) | copy-start | bytes 786436
  23.0 2.2 %collective-permute-start.5 = (bf16[512,512]{1,0:T(8,128)(2,1)S(1)}, bf16[512,512]{1,0:T(8,128)(2,1)S(1)}, u32[]{:S(2)}, u32[]{:S(2)}) collective-permute-start(bf16[512,512]{1,0:T(8,128)(2,1)S(1)} %pair.4), channel_id=1, source_target_pairs={{0,4},{4,0},{8,12},{12,8},{16,20},{20,16},{24,28},{28,24},{1,5},{5... | collective-permute-start | bytes 1572872 | tf_op jit(solution)/shard_map/q_swap/ppermute | solution.py:398
  23.6 1.0 %copy-start.1 = (bf16[256,512]{1,0:T(8,128)(2,1)S(1)}, bf16[256,512]{1,0:T(8,128)(2,1)}, u32[]{:S(2)}) copy-start(bf16[256,512]{1,0:T(8,128)(2,1)} %get-tuple-element.22.refs_0_.kv) | copy-start | bytes 786436
  25.1 2.0 %collective-permute-start.2 = (bf16[512,512]{1,0:T(8,128)(2,1)S(1)}, bf16[512,512]{1,0:T(8,128)(2,1)S(1)}, u32[]{:S(2)}, u32[]{:S(2)}) collective-permute-start(bf16[512,512]{1,0:T(8,128)(2,1)S(1)} %pair.3), channel_id=1, source_target_pairs={{0,4},{4,0},{8,12},{12,8},{16,20},{20,16},{24,28},{28,24},{1,5},{5... | collective-permute-start | bytes 1572872 | tf_op jit(solution)/shard_map/kv_swap/ppermute | solution.py:398
  31.3 5.6 %copy-start = (bf16[512,5376]{1,0:T(8,128)(2,1)S(1)}, bf16[512,5376]{1,0:T(8,128)(2,1)}, u32[]{:S(2)}) copy-start(bf16[512,5376]{1,0:T(8,128)(2,1)} %refs_2_.3) | copy-start | bytes 16515076
  31.3 5.6 %copy-start.5 = (bf16[64,5376]{1,0:T(8,128)(2,1)S(1)}, bf16[64,5376]{1,0:T(8,128)(2,1)}, u32[]{:S(2)}) copy-start(bf16[64,5376]{1,0:T(8,128)(2,1)} %refs_0_.3) | copy-start | bytes 2064388
  35.7 15.2 %collective-permute-start.10 = (bf16[64,5376]{1,0:T(8,128)(2,1)S(1)}, bf16[64,5376]{1,0:T(8,128)(2,1)S(1)}, u32[]{:S(2)}, u32[]{:S(2)}) collective-permute-start(bf16[64,5376]{1,0:T(8,128)(2,1)S(1)} %collective-permute-done.7.refs_1_.refs_0_), channel_id=1, source_target_pairs={{1,0},{2,3},{5,4},{6,7},{9,8},{10,11},{13,12},{14,15},{17,16},{18,... | collective-permute-start | bytes 2064392 | tf_op jit(solution)/shard_map/out_third/ppermute | solution.py:402
  40.2 20.0 %collective-permute-start.11 = (bf16[192,640]{1,0:T(8,128)(2,1)S(1)}, bf16[192,640]{1,0:T(8,128)(2,1)S(1)}, u32[]{:S(2)}, u32[]{:S(2)}) collective-permute-start(bf16[192,640]{1,0:T(8,128)(2,1)S(1)} %dout_rows.2.refs_0_.refs_3_), channel_id=1, source_target_pairs={{8,0},{12,4},{16,8},{20,12},{24,16},{28,20},{9,1},{13,5},{17,9},{2... | collective-permute-start | bytes 737288 | tf_op jit(solution)/shard_map/early_near/ppermute | solution.py:398
  43.5 16.6 %collective-permute-start.13 = (bf16[192,640]{1,0:T(8,128)(2,1)S(1)}, bf16[192,640]{1,0:T(8,128)(2,1)S(1)}, u32[]{:S(2)}, u32[]{:S(2)}) collective-permute-start(bf16[192,640]{1,0:T(8,128)(2,1)S(1)} %dout_rows.2.refs_0_.refs_3_), channel_id=1, source_target_pairs={{16,0},{20,4},{24,8},{28,12},{17,1},{21,5},{25,9},{29,13},{18,2},{... | collective-permute-start | bytes 737288 | tf_op jit(solution)/shard_map/early_far/ppermute | solution.py:398
  53.3 6.8 %copy-start.2 = (bf16[256,512]{1,0:T(8,128)(2,1)S(1)}, bf16[256,512]{1,0:T(8,128)(2,1)}, u32[]{:S(2)}) copy-start(bf16[256,512]{1,0:T(8,128)(2,1)} %get-tuple-element.22.refs_0_.kv) | copy-start | bytes 786436
  53.3 9.6 %collective-permute-start.12 = (bf16[64,640]{1,0:T(8,128)(2,1)S(1)}, bf16[64,640]{1,0:T(8,128)(2,1)S(1)}, u32[]{:S(2)}, u32[]{:S(2)}) collective-permute-start(bf16[64,640]{1,0:T(8,128)(2,1)S(1)} %dout_rows.3.refs_0_.refs_6_.refs_1_), channel_id=1, source_target_pairs={{8,0},{12,4},{16,8},{20,12},{24,16},{28,20},{9,1},{13,5},{17,9},{2... | collective-permute-start | bytes 245768 | tf_op jit(solution)/shard_map/late_near/ppermute | solution.py:398
  57.0 6.0 %collective-permute-start.14 = (bf16[64,640]{1,0:T(8,128)(2,1)S(1)}, bf16[64,640]{1,0:T(8,128)(2,1)S(1)}, u32[]{:S(2)}, u32[]{:S(2)}) collective-permute-start(bf16[64,640]{1,0:T(8,128)(2,1)S(1)} %dout_rows.3.refs_0_.refs_6_.refs_1_), channel_id=1, source_target_pairs={{16,0},{20,4},{24,8},{28,12},{17,1},{21,5},{25,9},{29,13},{18,2},{... | collective-permute-start | bytes 245768 | tf_op jit(solution)/shard_map/late_far/ppermute | solution.py:398
  63.6 6.7 %collective-permute-start.15 = (bf16[512,640]{1,0:T(8,128)(2,1)S(1)}, bf16[512,640]{1,0:T(8,128)(2,1)S(1)}, u32[]{:S(2)}, u32[]{:S(2)}) collective-permute-start(bf16[512,640]{1,0:T(8,128)(2,1)S(1)} %pair.5), channel_id=1, source_target_pairs={{0,4},{4,0},{8,12},{12,8},{16,20},{20,16},{24,28},{28,24},{1,5},{5... | collective-permute-start | bytes 1966088 | tf_op jit(solution)/shard_map/pay_swap/ppermute | solution.py:398

commit v4 on v3

--- a/solution.py
+++ b/solution.py
@@ -16,7 +16,6 @@
 F32 = jnp.float32
 BF16 = jnp.bfloat16
 VMEM = pl.BlockSpec(memory_space=pltpu.VMEM)
-SMEM = pl.BlockSpec(memory_space=pltpu.SMEM)
 ANY = pl.BlockSpec(memory_space=pl.ANY)
 COST = pl.CostEstimate(flops=1, bytes_accessed=1, transcendentals=0)
 
@@ -29,18 +28,26 @@
     return pltpu.CompilerParams(vmem_limit_bytes=limit * 2**20)
 
 
+def device_info(slot_rows):
+    shard = lax.axis_index("ctx")
+    tp = lax.axis_index("tp")
+    near_side = jnp.where(tp < 2, 1, 0)
+    slot_at = [tp, tp + 1 - 2 * lax.rem(tp, 2), 1 + near_side, 3 * near_side]
+    return [lax.rem(shard, 2), shard] + [slot * slot_rows for slot in slot_at]
+
+
 def call(kernel, name, shapes, info, arrays, scratch=(), outs=VMEM, in_place=()):
     return pl.pallas_call(
-        kernel,
+        lambda *refs: kernel(device_info(info), *refs),
         out_shape=shapes,
-        in_specs=[SMEM] + [VMEM] * len(arrays) + [ANY] * len(in_place),
+        in_specs=[VMEM] * len(arrays) + [ANY] * len(in_place),
         out_specs=outs if isinstance(outs, tuple) else jax.tree.map(lambda _: outs, shapes),
         scratch_shapes=list(scratch),
-        input_output_aliases={1 + len(arrays) + n: n for n in range(len(in_place))},
+        input_output_aliases={len(arrays) + n: n for n in range(len(in_place))},
         compiler_params=params(),
         cost_estimate=COST,
         name=name,
-    )(info, *arrays, *in_place)
+    )(*arrays, *in_place)
 
 
 TOKEN = jax.ShapeDtypeStruct((8, HD), F32)
@@ -404,11 +411,7 @@
     def moved(distance):
         return [(i, i + distance) for i in range(ctx) if 0 <= i + distance < ctx]
 
-    shard = lax.axis_index("ctx")
-    tp = lax.axis_index("tp")
-    low_side = tp < 2
-    slot_at = [tp, tp ^ 1, jnp.where(low_side, 2, 1), jnp.where(low_side, 3, 0)]
-    info = jnp.stack([shard % 2, shard] + [s * slot_rows for s in slot_at]).astype(jnp.int32)
+    info = slot_rows
 
     middle = [(1, 2), (2, 1)]
     ends = [(0, 1), (1, 0), (2, 3), (3, 2)]

time: 74.2 us -> 72.8 us (0.981)
  Pallas kernels: 25 us -> 18.4 us
  waiting for transfers between devices: 15.7 us -> 21.1 us
    pallas_call x11, Pallas kernels: 23.1 us -> 16.5 us  [call(): pl.pallas_call(lambda *refs: kernel(device_info(info), *refs), out_shape=...]
    ppermute x5, waiting for transfers between devices: 9.13 us -> 12.8 us  [over(): return lax.ppermute(x, 'tp', pairs)]
    ppermute x11, waiting for transfers between devices: 6.54 us -> 8.28 us  [along(): return lax.ppermute(x, 'ctx', pairs)]
  transfers between devices with their start and end apart: 16 -> 16, of which waited for: 7 -> 8; matrix products, arithmetic and copies ran while one was open for 0% -> 0% of each run, Pallas kernels for 30% -> 23%
where the time goes in v4:
time: 72.8 us; the launch traced here: 71.4 us
  starting transfers between devices  29.1 us (40%)
  waiting for transfers between devices  21.1 us (29%)
  Pallas kernels  18.4 us (25%)
  local copies, waits for them, and re-layouts  1.92 us (3%)
  between operations  0.92 us (1%)
    ppermute x11, starting transfers between devices, along(): return lax.ppermute(x, 'ctx', pairs)  23.8 us
    pallas_call x11, Pallas kernels, call(): pl.pallas_call(lambda *refs: kernel(device_info(info), *refs), out_shape=...  16.5 us
    ppermute x5, waiting for transfers between devices, over(): return lax.ppermute(x, 'tp', pairs)  12.8 us
    ppermute x11, waiting for transfers between devices, along(): return lax.ppermute(x, 'ctx', pairs)  8.28 us
    ppermute x5, starting transfers between devices, over(): return lax.ppermute(x, 'tp', pairs)  5.32 us
    unnamed x12, local copies, waits for them, and re-layouts  1.92 us
    pallas_call x1, Pallas kernels, pack(): pl.pallas_call(functools.partial(pack_kernel, places), out_shape=tuple((j...  1.9 us
  transfers between devices with their start and end apart: 16, of which 8 were waited for; matrix products, arithmetic and copies ran while one was open for 0% of the time, Pallas kernels for 23%

profile of v4, /device:TPU:3, one launch (start us, length us, event | category | flops | bytes accessed | tf_op | source)
XLA Modules:
  0.0 71.4 jit_solution(6000470816371007339)
XLA Ops:
  0.6 1.4 %collective-permute-start.6 = (bf16[64,5376]{1,0:T(8,128)(2,1)}, bf16[64,5376]{1,0:T(8,128)(2,1)S(1)}, u32[]{:S(2)}, u32[]{:S(2)}) collective-permute-start(bf16[64,5376]{1,0:T(8,128)(2,1)} %refs_0_.3), channel_id=1, source_target_pairs={{0,1},{1,0},{2,3},{3,2},{4,5},{5,4},{6,7},{7,6},{8,9},{9,8},{10,11... | collective-permute-start | bytes 2064392 | tf_op jit(solution)/shard_map/end_first/ppermute | solution.py:409
  2.0 0.7 collective-permute-start.8
  2.7 1.9 %pack.1 = (bf16[256,512]{1,0:T(8,128)(2,1)}, bf16[256,512]{1,0:T(8,128)(2,1)}) custom-call(bf16[256,256]{1,0:T(8,128)(2,1)} %refs_0_.2, bf16[256,256]{1,0:T(8,128)(2,1)} %refs_1_.1, bf16[256,512]{1,0:T(8,128)(2,1)} %refs_2_.2), custom_call_target="tpu_custom_call" | custom-call | flops 1 | bytes 1 | tf_op jit(solution)/shard_map/pack/pallas_call | solution.py:86
  4.6 3.1 %collective-permute-start = (bf16[256,512]{1,0:T(8,128)(2,1)}, bf16[256,512]{1,0:T(8,128)(2,1)S(1)}, u32[]{:S(2)}, u32[]{:S(2)}) collective-permute-start(bf16[256,512]{1,0:T(8,128)(2,1)} %get-tuple-element.22.refs_0_), channel_id=1, source_target_pairs={{0,8},{4,12},{8,16},{12,20},{16,24},{20,28},{1,9},{5,13},{9,17},{1... | collective-permute-start | bytes 786440 | tf_op jit(solution)/shard_map/kv_near/ppermute | solution.py:405
  7.7 1.3 %collective-permute-start.1 = (bf16[256,512]{1,0:T(8,128)(2,1)}, bf16[256,512]{1,0:T(8,128)(2,1)S(1)}, u32[]{:S(2)}, u32[]{:S(2)}) collective-permute-start(bf16[256,512]{1,0:T(8,128)(2,1)} %get-tuple-element.22.refs_0_), channel_id=1, source_target_pairs={{0,16},{4,20},{8,24},{12,28},{1,17},{5,21},{9,25},{13,29},{2,18},{... | collective-permute-start | bytes 786440 | tf_op jit(solution)/shard_map/kv_far/ppermute | solution.py:405
  9.1 4.0 %collective-permute-start.3 = (bf16[256,512]{1,0:T(8,128)(2,1)}, bf16[256,512]{1,0:T(8,128)(2,1)S(1)}, u32[]{:S(2)}, u32[]{:S(2)}) collective-permute-start(bf16[256,512]{1,0:T(8,128)(2,1)} %get-tuple-element.23.refs_0_.refs_1_), channel_id=1, source_target_pairs={{8,0},{12,4},{16,8},{20,12},{24,16},{28,20},{9,1},{13,5},{17,9},{2... | collective-permute-start | bytes 786440 | tf_op jit(solution)/shard_map/q_near/ppermute | solution.py:405
  13.1 0.5 collective-permute-done.refs_1_.refs_2_
  13.6 1.3 %collective-permute-start.4 = (bf16[256,512]{1,0:T(8,128)(2,1)}, bf16[256,512]{1,0:T(8,128)(2,1)S(1)}, u32[]{:S(2)}, u32[]{:S(2)}) collective-permute-start(bf16[256,512]{1,0:T(8,128)(2,1)} %get-tuple-element.23.refs_0_.refs_1_), channel_id=1, source_target_pairs={{16,0},{20,4},{24,8},{28,12},{17,1},{21,5},{25,9},{29,13},{18,2},{... | collective-permute-start | bytes 786440 | tf_op jit(solution)/shard_map/q_far/ppermute | solution.py:405
  14.8 2.4 %collective-permute-done.6.refs_1_ = bf16[64,5376]{1,0:T(8,128)(2,1)S(1)} collective-permute-done((bf16[64,5376]{1,0:T(8,128)(2,1)}, bf16[64,5376]{1,0:T(8,128)(2,1)S(1)}, u32[]{:S(2)}, u32[]{:S(2)}) %collective-permute-start.6) | collective-permute-done | bytes 688160 | tf_op jit(solution)/shard_map/end_first/ppermute | solution.py:409
  17.2 0.7 collective-permute-start.7
  17.9 0.0 collective-permute-done.8.refs_2_
  17.9 1.3 %collective-permute-start.9 = (bf16[64,5376]{1,0:T(8,128)(2,1)S(1)}, bf16[64,5376]{1,0:T(8,128)(2,1)S(1)}, u32[]{:S(2)}, u32[]{:S(2)}) collective-permute-start(bf16[64,5376]{1,0:T(8,128)(2,1)S(1)} %collective-permute-done.8.refs_2_), channel_id=1, source_target_pairs={{1,0},{2,3},{5,4},{6,7},{9,8},{10,11},{13,12},{14,15},{17,16},{18,... | collective-permute-start | bytes 2064392 | tf_op jit(solution)/shard_map/out_second/ppermute | solution.py:409
  19.2 0.0 collective-permute-done.1.refs_2_.refs_3_
  19.2 0.0 copy-start.1
  19.2 0.9 %copy-done.1 = bf16[256,512]{1,0:T(8,128)(2,1)S(1)} copy-done((bf16[256,512]{1,0:T(8,128)(2,1)S(1)}, bf16[256,512]{1,0:T(8,128)(2,1)}, u32[]{:S(2)}) %copy-start.1) | copy-done | bytes 262168
  20.2 0.0 copy-start.2
  20.2 1.6 %collective-permute-start.2 = (bf16[512,512]{1,0:T(8,128)(2,1)S(1)}, bf16[512,512]{1,0:T(8,128)(2,1)S(1)}, u32[]{:S(2)}, u32[]{:S(2)}) collective-permute-start(bf16[512,512]{1,0:T(8,128)(2,1)S(1)} %pair.3), channel_id=1, source_target_pairs={{0,4},{4,0},{8,12},{12,8},{16,20},{20,16},{24,28},{28,24},{1,5},{5... | collective-permute-start | bytes 1572872 | tf_op jit(solution)/shard_map/kv_swap/ppermute | solution.py:405
  21.8 0.0 collective-permute-done.3.refs_1_.refs_2_
  21.8 5.3 %collective-permute-done.4.refs_2_.refs_3_ = bf16[256,512]{1,0:T(8,128)(2,1)S(1)} collective-permute-done((bf16[256,512]{1,0:T(8,128)(2,1)}, bf16[256,512]{1,0:T(8,128)(2,1)S(1)}, u32[]{:S(2)}, u32[]{:S(2)}) %collective-permute-start.4) | collective-permute-done | bytes 262176 | tf_op jit(solution)/shard_map/q_far/ppermute | solution.py:405
  27.1 0.0 copy-start.3
  27.1 0.9 %copy-done.3 = bf16[256,512]{1,0:T(8,128)(2,1)S(1)} copy-done((bf16[256,512]{1,0:T(8,128)(2,1)S(1)}, bf16[256,512]{1,0:T(8,128)(2,1)}, u32[]{:S(2)}) %copy-start.3) | copy-done | bytes 262168
  28.1 0.6 collective-permute-start.5
  28.7 0.0 collective-permute-done.2.refs_4_
  28.7 1.5 %collective-permute-done.5.refs_5_.refs_1_ = bf16[512,512]{1,0:T(8,128)(2,1)S(1)} collective-permute-done((bf16[512,512]{1,0:T(8,128)(2,1)S(1)}, bf16[512,512]{1,0:T(8,128)(2,1)S(1)}, u32[]{:S(2)}, u32[]{:S(2)}) %collective-permute-start.5) | collective-permute-done | bytes 524320 | tf_op jit(solution)/shard_map/q_swap/ppermute | solution.py:405
  30.2 0.0 copy-done.2
  30.2 3.6 %attention_probs.1 = (bf16[4,256,1280]{2,1,0:T(8,128)(2,1)S(1)}, f32[256,512]{1,0:T(8,128)S(1)}, bf16[256,128]{1,0:T(8,128)(2,1)S(1)}, bf16[1280,512]{1,0:T(8,128)(2,1)S(1)}) custom-call(bf16[256,512]{1,0:T(8,128)(2,1)S(1)} %copy-done.2, bf16[256,512]{1,0:T(8,128)(2,1)S(1)} %copy-done.3, bf16[256,512]{1,0:T(8,128)(2,1)S(1)} %collective-permute-done.refs_1_.refs_2_, ...), custom_call_target="tpu_custom_call" | custom-call | flops 1 | bytes 1 | tf_op jit(solution)/shard_map/attention_probs/pallas_call | solution.py:40
  33.8 0.0 copy-start
  33.9 0.0 copy-start.5
  33.9 0.0 collective-permute-done.7.refs_1_.refs_0_
  33.9 3.0 %collective-permute-done.9.refs_0_.refs_3_ = bf16[64,5376]{1,0:T(8,128)(2,1)S(1)} collective-permute-done((bf16[64,5376]{1,0:T(8,128)(2,1)S(1)}, bf16[64,5376]{1,0:T(8,128)(2,1)S(1)}, u32[]{:S(2)}, u32[]{:S(2)}) %collective-permute-start.9) | collective-permute-done | bytes 688160 | tf_op jit(solution)/shard_map/out_second/ppermute | solution.py:409
  36.9 1.3 %collective-permute-start.10 = (bf16[64,5376]{1,0:T(8,128)(2,1)S(1)}, bf16[64,5376]{1,0:T(8,128)(2,1)S(1)}, u32[]{:S(2)}, u32[]{:S(2)}) collective-permute-start(bf16[64,5376]{1,0:T(8,128)(2,1)S(1)} %collective-permute-done.7.refs_1_.refs_0_), channel_id=1, source_target_pairs={{1,0},{2,3},{5,4},{6,7},{9,8},{10,11},{13,12},{14,15},{17,16},{18,... | collective-permute-start | bytes 2064392 | tf_op jit(solution)/shard_map/out_third/ppermute | solution.py:409
  38.2 0.0 copy-done
  38.2 0.0 copy-done.5
  38.2 2.1 %dout_rows.2.refs_2_.refs_4_.refs_0_ = bf16[192,640]{1,0:T(8,128)(2,1)S(1)} custom-call(bf16[64,5376]{1,0:T(8,128)(2,1)S(1)} %copy-done.5, bf16[64,5376]{1,0:T(8,128)(2,1)S(1)} %collective-permute-done.6.refs_1_, bf16[64,5376]{1,0:T(8,128)(2,1)S(1)} %collective-permute-done.8.refs_2_, bf16[64,5376]{1,0:T(8,128)(2,1)S(1)} %collective-permute-done.9.refs_0_.refs_3_, ...), custom_call_target="tpu_custom_call" | custom-call | flops 1 | bytes 1 | tf_op jit(solution)/shard_map/dout_rows/pallas_call | solution.py:40
  40.3 2.2 %collective-permute-start.11 = (bf16[192,640]{1,0:T(8,128)(2,1)S(1)}, bf16[192,640]{1,0:T(8,128)(2,1)S(1)}, u32[]{:S(2)}, u32[]{:S(2)}) collective-permute-start(bf16[192,640]{1,0:T(8,128)(2,1)S(1)} %dout_rows.2.refs_2_.refs_4_.refs_0_), channel_id=1, source_target_pairs={{8,0},{12,4},{16,8},{20,12},{24,16},{28,20},{9,1},{13,5},{17,9},{2... | collective-permute-start | bytes 737288 | tf_op jit(solution)/shard_map/early_near/ppermute | solution.py:405
  42.5 1.3 %collective-permute-start.13 = (bf16[192,640]{1,0:T(8,128)(2,1)S(1)}, bf16[192,640]{1,0:T(8,128)(2,1)S(1)}, u32[]{:S(2)}, u32[]{:S(2)}) collective-permute-start(bf16[192,640]{1,0:T(8,128)(2,1)S(1)} %dout_rows.2.refs_2_.refs_4_.refs_0_), channel_id=1, source_target_pairs={{16,0},{20,4},{24,8},{28,12},{17,1},{21,5},{25,9},{29,13},{18,2},{... | collective-permute-start | bytes 737288 | tf_op jit(solution)/shard_map/early_far/ppermute | solution.py:405
  43.8 2.1 %query_grads.2 = (f32[256,512]{1,0:T(8,128)}, f32[8,128]{1,0:T(8,128)S(1)}) custom-call(bf16[4,256,1280]{2,1,0:T(8,128)(2,1)S(1)} %get-tuple-element.24.refs_0_, bf16[1280,512]{1,0:T(8,128)(2,1)S(1)} %get-tuple-element.25.refs_1_, bf16[192,640]{1,0:T(8,128)(2,1)S(1)} %dout_rows.2.refs_2_.refs_4_.refs_0_), custom_call_target="tpu_custom_call" | custom-call | flops 1 | bytes 1 | tf_op jit(solution)/shard_map/query_grads/pallas_call | solution.py:40
  45.9 7.4 %collective-permute-done.10.refs_1_ = bf16[64,5376]{1,0:T(8,128)(2,1)S(1)} collective-permute-done((bf16[64,5376]{1,0:T(8,128)(2,1)S(1)}, bf16[64,5376]{1,0:T(8,128)(2,1)S(1)}, u32[]{:S(2)}, u32[]{:S(2)}) %collective-permute-start.10) | collective-permute-done | bytes 688160 | tf_op jit(solution)/shard_map/out_third/ppermute | solution.py:409
  53.3 1.9 %dout_rows.3.refs_2_.refs_7_.refs_1_ = bf16[64,640]{1,0:T(8,128)(2,1)S(1)} custom-call(bf16[64,5376]{1,0:T(8,128)(2,1)S(1)} %collective-permute-done.7.refs_1_.refs_0_, bf16[64,5376]{1,0:T(8,128)(2,1)S(1)} %collective-permute-done.10.refs_1_, bf16[512,5376]{1,0:T(8,128)(2,1)S(1)} %copy-done, f32[256,512]{1,0:T(8,128)S(1)} %get-tuple-element.28.refs_5_.refs_3_, ...), custom_call_target="tpu_custom_call" | custom-call | flops 1 | bytes 1 | tf_op jit(solution)/shard_map/dout_rows/pallas_call | solution.py:40
  55.1 0.0 copy-start.4
  55.2 2.3 %collective-permute-start.12 = (bf16[64,640]{1,0:T(8,128)(2,1)S(1)}, bf16[64,640]{1,0:T(8,128)(2,1)S(1)}, u32[]{:S(2)}, u32[]{:S(2)}) collective-permute-start(bf16[64,640]{1,0:T(8,128)(2,1)S(1)} %dout_rows.3.refs_2_.refs_7_.refs_1_), channel_id=1, source_target_pairs={{8,0},{12,4},{16,8},{20,12},{24,16},{28,20},{9,1},{13,5},{17,9},{2... | collective-permute-start | bytes 245768 | tf_op jit(solution)/shard_map/late_near/ppermute | solution.py:405
  57.5 1.3 %collective-permute-start.14 = (bf16[64,640]{1,0:T(8,128)(2,1)S(1)}, bf16[64,640]{1,0:T(8,128)(2,1)S(1)}, u32[]{:S(2)}, u32[]{:S(2)}) collective-permute-start(bf16[64,640]{1,0:T(8,128)(2,1)S(1)} %dout_rows.3.refs_2_.refs_7_.refs_1_), channel_id=1, source_target_pairs={{16,0},{20,4},{24,8},{28,12},{17,1},{21,5},{25,9},{29,13},{18,2},{... | collective-permute-start | bytes 245768 | tf_op jit(solution)/shard_map/late_far/ppermute | solution.py:405
  58.8 1.3 %query_grads.3 = (f32[256,512]{1,0:T(8,128)}, f32[8,128]{1,0:T(8,128)S(1)}) custom-call(bf16[4,256,1280]{2,1,0:T(8,128)(2,1)S(1)} %get-tuple-element.24.refs_0_, bf16[1280,512]{1,0:T(8,128)(2,1)S(1)} %get-tuple-element.25.refs_1_, bf16[64,640]{1,0:T(8,128)(2,1)S(1)} %dout_rows.3.refs_2_.refs_7_.refs_1_, ...), custom_call_target="tpu_custom_call", output_to_operand_aliasing={{0}: (3, {})} | custom-call | flops 1 | bytes 1 | tf_op jit(solution)/shard_map/query_grads/pallas_call | solution.py:40
  60.0 0.0 collective-permute-done.11.refs_5_.refs_2_
  60.0 0.0 collective-permute-done.13.refs_6_.refs_4_
  60.1 0.0 copy-done.4
  60.1 2.3 %key_grads.3 = (f32[256,256]{1,0:T(8,128)S(1)}, f32[256,256]{1,0:T(8,128)S(1)}) custom-call(bf16[256,512]{1,0:T(8,128)(2,1)S(1)} %copy-done.2, bf16[256,512]{1,0:T(8,128)(2,1)S(1)} %copy-done.4, bf16[256,512]{1,0:T(8,128)(2,1)S(1)} %collective-permute-done.3.refs_1_.refs_2_, bf16[256,512]{1,0:T(8,128)(2,1)S(1)} %collective-permute-done.4.refs_2_.refs_3_, ...), custom_call_target="tpu_custom_call" | custom-call | flops 1 | bytes 1 | tf_op jit(solution)/shard_map/key_grads/pallas_call | solution.py:40
  62.3 0.0 collective-permute-done.12.refs_3_
  62.3 0.3 collective-permute-done.14.refs_5_.refs_4_
  62.6 0.1 pair.5
  62.7 4.9 %collective-permute-start.15 = (bf16[512,640]{1,0:T(8,128)(2,1)S(1)}, bf16[512,640]{1,0:T(8,128)(2,1)S(1)}, u32[]{:S(2)}, u32[]{:S(2)}) collective-permute-start(bf16[512,640]{1,0:T(8,128)(2,1)S(1)} %pair.5), channel_id=1, source_target_pairs={{0,4},{4,0},{8,12},{12,8},{16,20},{20,16},{24,28},{28,24},{1,5},{5... | collective-permute-start | bytes 1966088 | tf_op jit(solution)/shard_map/pay_swap/ppermute | solution.py:405
  67.6 1.1 %key_grads.4 = (f32[256,256]{1,0:T(8,128)S(1)}, f32[256,256]{1,0:T(8,128)S(1)}) custom-call(bf16[256,512]{1,0:T(8,128)(2,1)S(1)} %copy-done.2, bf16[256,512]{1,0:T(8,128)(2,1)S(1)} %collective-permute-done.3.refs_1_.refs_2_, bf16[256,512]{1,0:T(8,128)(2,1)S(1)} %collective-permute-done.4.refs_2_.refs_3_, ...), custom_call_target="tpu_custom_call" | custom-call | flops 1 | bytes 1 | tf_op jit(solution)/shard_map/key_grads/pallas_call | solution.py:40
  68.6 0.7 collective-permute-done.15.refs_2_
  69.3 2.1 %key_grads.5 = (f32[256,256]{1,0:T(8,128)}, f32[256,256]{1,0:T(8,128)}) custom-call(bf16[256,512]{1,0:T(8,128)(2,1)S(1)} %copy-done.2, bf16[512,512]{1,0:T(8,128)(2,1)S(1)} %collective-permute-done.5.refs_5_.refs_1_, bf16[512,640]{1,0:T(8,128)(2,1)S(1)} %collective-permute-done.15.refs_2_, f32[256,256]{1,0:T(8,128)S(1)} %get-tuple-element.37.refs_3_, ...), custom_call_target="tpu_custom_call" | custom-call | flops 1 | bytes 1 | tf_op jit(solution)/shard_map/key_grads/pallas_call | solution.py:40
  (3 shorter events, 0.1 us)
Async XLA Ops:
  0.6 16.6 %collective-permute-start.6 = (bf16[64,5376]{1,0:T(8,128)(2,1)}, bf16[64,5376]{1,0:T(8,128)(2,1)S(1)}, u32[]{:S(2)}, u32[]{:S(2)}) collective-permute-start(bf16[64,5376]{1,0:T(8,128)(2,1)} %refs_0_.3), channel_id=1, source_target_pairs={{0,1},{1,0},{2,3},{3,2},{4,5},{5,4},{6,7},{7,6},{8,9},{9,8},{10,11... | collective-permute-start | bytes 2064392 | tf_op jit(solution)/shard_map/end_first/ppermute | solution.py:409
  2.0 15.9 %collective-permute-start.8 = (bf16[64,5376]{1,0:T(8,128)(2,1)}, bf16[64,5376]{1,0:T(8,128)(2,1)S(1)}, u32[]{:S(2)}, u32[]{:S(2)}) collective-permute-start(bf16[64,5376]{1,0:T(8,128)(2,1)} %refs_0_.3), channel_id=1, source_target_pairs={{1,2},{2,1},{5,6},{6,5},{9,10},{10,9},{13,14},{14,13},{17,18},{18,... | collective-permute-start | bytes 2064392 | tf_op jit(solution)/shard_map/mid_first/ppermute | solution.py:409
  4.6 9.0 %collective-permute-start = (bf16[256,512]{1,0:T(8,128)(2,1)}, bf16[256,512]{1,0:T(8,128)(2,1)S(1)}, u32[]{:S(2)}, u32[]{:S(2)}) collective-permute-start(bf16[256,512]{1,0:T(8,128)(2,1)} %get-tuple-element.22.refs_0_), channel_id=1, source_target_pairs={{0,8},{4,12},{8,16},{12,20},{16,24},{20,28},{1,9},{5,13},{9,17},{1... | collective-permute-start | bytes 786440 | tf_op jit(solution)/shard_map/kv_near/ppermute | solution.py:405
  7.7 11.5 %collective-permute-start.1 = (bf16[256,512]{1,0:T(8,128)(2,1)}, bf16[256,512]{1,0:T(8,128)(2,1)S(1)}, u32[]{:S(2)}, u32[]{:S(2)}) collective-permute-start(bf16[256,512]{1,0:T(8,128)(2,1)} %get-tuple-element.22.refs_0_), channel_id=1, source_target_pairs={{0,16},{4,20},{8,24},{12,28},{1,17},{5,21},{9,25},{13,29},{2,18},{... | collective-permute-start | bytes 786440 | tf_op jit(solution)/shard_map/kv_far/ppermute | solution.py:405
  9.1 12.8 %collective-permute-start.3 = (bf16[256,512]{1,0:T(8,128)(2,1)}, bf16[256,512]{1,0:T(8,128)(2,1)S(1)}, u32[]{:S(2)}, u32[]{:S(2)}) collective-permute-start(bf16[256,512]{1,0:T(8,128)(2,1)} %get-tuple-element.23.refs_0_.refs_1_), channel_id=1, source_target_pairs={{8,0},{12,4},{16,8},{20,12},{24,16},{28,20},{9,1},{13,5},{17,9},{2... | collective-permute-start | bytes 786440 | tf_op jit(solution)/shard_map/q_near/ppermute | solution.py:405
  13.6 13.6 %collective-permute-start.4 = (bf16[256,512]{1,0:T(8,128)(2,1)}, bf16[256,512]{1,0:T(8,128)(2,1)S(1)}, u32[]{:S(2)}, u32[]{:S(2)}) collective-permute-start(bf16[256,512]{1,0:T(8,128)(2,1)} %get-tuple-element.23.refs_0_.refs_1_), channel_id=1, source_target_pairs={{16,0},{20,4},{24,8},{28,12},{17,1},{21,5},{25,9},{29,13},{18,2},{... | collective-permute-start | bytes 786440 | tf_op jit(solution)/shard_map/q_far/ppermute | solution.py:405
  17.2 16.7 %collective-permute-start.7 = (bf16[64,5376]{1,0:T(8,128)(2,1)S(1)}, bf16[64,5376]{1,0:T(8,128)(2,1)S(1)}, u32[]{:S(2)}, u32[]{:S(2)}) collective-permute-start(bf16[64,5376]{1,0:T(8,128)(2,1)S(1)} %collective-permute-done.6.refs_1_), channel_id=1, source_target_pairs={{1,2},{2,1},{5,6},{6,5},{9,10},{10,9},{13,14},{14,13},{17,18},{18,... | collective-permute-start | bytes 2064392 | tf_op jit(solution)/shard_map/mid_second/ppermute | solution.py:409
  17.9 19.0 %collective-permute-start.9 = (bf16[64,5376]{1,0:T(8,128)(2,1)S(1)}, bf16[64,5376]{1,0:T(8,128)(2,1)S(1)}, u32[]{:S(2)}, u32[]{:S(2)}) collective-permute-start(bf16[64,5376]{1,0:T(8,128)(2,1)S(1)} %collective-permute-done.8.refs_2_), channel_id=1, source_target_pairs={{1,0},{2,3},{5,4},{6,7},{9,8},{10,11},{13,12},{14,15},{17,16},{18,... | collective-permute-start | bytes 2064392 | tf_op jit(solution)/shard_map/out_second/ppermute | solution.py:409
  19.2 1.0 %copy-start.1 = (bf16[256,512]{1,0:T(8,128)(2,1)S(1)}, bf16[256,512]{1,0:T(8,128)(2,1)}, u32[]{:S(2)}) copy-start(bf16[256,512]{1,0:T(8,128)(2,1)} %get-tuple-element.22.refs_0_) | copy-start | bytes 786436
  20.2 10.0 %copy-start.2 = (bf16[256,512]{1,0:T(8,128)(2,1)S(1)}, bf16[256,512]{1,0:T(8,128)(2,1)}, u32[]{:S(2)}) copy-start(bf16[256,512]{1,0:T(8,128)(2,1)} %get-tuple-element.22.refs_0_) | copy-start | bytes 786436
  20.2 8.4 %collective-permute-start.2 = (bf16[512,512]{1,0:T(8,128)(2,1)S(1)}, bf16[512,512]{1,0:T(8,128)(2,1)S(1)}, u32[]{:S(2)}, u32[]{:S(2)}) collective-permute-start(bf16[512,512]{1,0:T(8,128)(2,1)S(1)} %pair.3), channel_id=1, source_target_pairs={{0,4},{4,0},{8,12},{12,8},{16,20},{20,16},{24,28},{28,24},{1,5},{5... | collective-permute-start | bytes 1572872 | tf_op jit(solution)/shard_map/kv_swap/ppermute | solution.py:405
  27.1 1.0 %copy-start.3 = (bf16[256,512]{1,0:T(8,128)(2,1)S(1)}, bf16[256,512]{1,0:T(8,128)(2,1)}, u32[]{:S(2)}) copy-start(bf16[256,512]{1,0:T(8,128)(2,1)} %get-tuple-element.23.refs_0_.refs_1_) | copy-start | bytes 786436
  28.1 2.1 %collective-permute-start.5 = (bf16[512,512]{1,0:T(8,128)(2,1)S(1)}, bf16[512,512]{1,0:T(8,128)(2,1)S(1)}, u32[]{:S(2)}, u32[]{:S(2)}) collective-permute-start(bf16[512,512]{1,0:T(8,128)(2,1)S(1)} %pair.4), channel_id=1, source_target_pairs={{0,4},{4,0},{8,12},{12,8},{16,20},{20,16},{24,28},{28,24},{1,5},{5... | collective-permute-start | bytes 1572872 | tf_op jit(solution)/shard_map/q_swap/ppermute | solution.py:405
  33.8 4.4 %copy-start = (bf16[512,5376]{1,0:T(8,128)(2,1)S(1)}, bf16[512,5376]{1,0:T(8,128)(2,1)}, u32[]{:S(2)}) copy-start(bf16[512,5376]{1,0:T(8,128)(2,1)} %refs_2_.3) | copy-start | bytes 16515076
  33.9 4.4 %copy-start.5 = (bf16[64,5376]{1,0:T(8,128)(2,1)S(1)}, bf16[64,5376]{1,0:T(8,128)(2,1)}, u32[]{:S(2)}) copy-start(bf16[64,5376]{1,0:T(8,128)(2,1)} %refs_0_.3) | copy-start | bytes 2064388
  36.9 16.3 %collective-permute-start.10 = (bf16[64,5376]{1,0:T(8,128)(2,1)S(1)}, bf16[64,5376]{1,0:T(8,128)(2,1)S(1)}, u32[]{:S(2)}, u32[]{:S(2)}) collective-permute-start(bf16[64,5376]{1,0:T(8,128)(2,1)S(1)} %collective-permute-done.7.refs_1_.refs_0_), channel_id=1, source_target_pairs={{1,0},{2,3},{5,4},{6,7},{9,8},{10,11},{13,12},{14,15},{17,16},{18,... | collective-permute-start | bytes 2064392 | tf_op jit(solution)/shard_map/out_third/ppermute | solution.py:409
  40.3 19.7 %collective-permute-start.11 = (bf16[192,640]{1,0:T(8,128)(2,1)S(1)}, bf16[192,640]{1,0:T(8,128)(2,1)S(1)}, u32[]{:S(2)}, u32[]{:S(2)}) collective-permute-start(bf16[192,640]{1,0:T(8,128)(2,1)S(1)} %dout_rows.2.refs_2_.refs_4_.refs_0_), channel_id=1, source_target_pairs={{8,0},{12,4},{16,8},{20,12},{24,16},{28,20},{9,1},{13,5},{17,9},{2... | collective-permute-start | bytes 737288 | tf_op jit(solution)/shard_map/early_near/ppermute | solution.py:405
  42.5 17.6 %collective-permute-start.13 = (bf16[192,640]{1,0:T(8,128)(2,1)S(1)}, bf16[192,640]{1,0:T(8,128)(2,1)S(1)}, u32[]{:S(2)}, u32[]{:S(2)}) collective-permute-start(bf16[192,640]{1,0:T(8,128)(2,1)S(1)} %dout_rows.2.refs_2_.refs_4_.refs_0_), channel_id=1, source_target_pairs={{16,0},{20,4},{24,8},{28,12},{17,1},{21,5},{25,9},{29,13},{18,2},{... | collective-permute-start | bytes 737288 | tf_op jit(solution)/shard_map/early_far/ppermute | solution.py:405
  55.1 4.9 %copy-start.4 = (bf16[256,512]{1,0:T(8,128)(2,1)S(1)}, bf16[256,512]{1,0:T(8,128)(2,1)}, u32[]{:S(2)}) copy-start(bf16[256,512]{1,0:T(8,128)(2,1)} %get-tuple-element.23.refs_0_.refs_1_) | copy-start | bytes 786436
  55.2 7.2 %collective-permute-start.12 = (bf16[64,640]{1,0:T(8,128)(2,1)S(1)}, bf16[64,640]{1,0:T(8,128)(2,1)S(1)}, u32[]{:S(2)}, u32[]{:S(2)}) collective-permute-start(bf16[64,640]{1,0:T(8,128)(2,1)S(1)} %dout_rows.3.refs_2_.refs_7_.refs_1_), channel_id=1, source_target_pairs={{8,0},{12,4},{16,8},{20,12},{24,16},{28,20},{9,1},{13,5},{17,9},{2... | collective-permute-start | bytes 245768 | tf_op jit(solution)/shard_map/late_near/ppermute | solution.py:405
  57.5 5.2 %collective-permute-start.14 = (bf16[64,640]{1,0:T(8,128)(2,1)S(1)}, bf16[64,640]{1,0:T(8,128)(2,1)S(1)}, u32[]{:S(2)}, u32[]{:S(2)}) collective-permute-start(bf16[64,640]{1,0:T(8,128)(2,1)S(1)} %dout_rows.3.refs_2_.refs_7_.refs_1_), channel_id=1, source_target_pairs={{16,0},{20,4},{24,8},{28,12},{17,1},{21,5},{25,9},{29,13},{18,2},{... | collective-permute-start | bytes 245768 | tf_op jit(solution)/shard_map/late_far/ppermute | solution.py:405
  62.7 6.6 %collective-permute-start.15 = (bf16[512,640]{1,0:T(8,128)(2,1)S(1)}, bf16[512,640]{1,0:T(8,128)(2,1)S(1)}, u32[]{:S(2)}, u32[]{:S(2)}) collective-permute-start(bf16[512,640]{1,0:T(8,128)(2,1)S(1)} %pair.5), channel_id=1, source_target_pairs={{0,4},{4,0},{8,12},{12,8},{16,20},{20,16},{24,28},{28,24},{1,5},{5... | collective-permute-start | bytes 1966088 | tf_op jit(solution)/shard_map/pay_swap/ppermute | solution.py:405

commit v5 on v4

--- a/solution.py
+++ b/solution.py
@@ -96,7 +96,7 @@
 
 
 def pair_kernel(nearer, count, info, *refs):
-    own, near, far = (refs[n * count : (n + 1) * count] for n in range(3))
+    own, far, near = (refs[n * count : (n + 1) * count] for n in range(3))
     pair = refs[-1]
     total = pair.shape[0] // 2
 
@@ -120,7 +120,7 @@
     total = sum(block.shape[0] for block in own)
     shape = jax.ShapeDtypeStruct((2 * total, own[0].shape[1]), BF16)
     kernel = functools.partial(pair_kernel, nearer, len(own))
-    return call(kernel, "pair", shape, info, (*own, *near, *far, *after))
+    return call(kernel, "pair", shape, info, (*own, *far, *near, *after))
 
 
 def pieces(x):
@@ -441,8 +441,8 @@
     )
 
     def sent(pay, name):
+        far = along(pay, moved(-4), name + "_far")
         near = along(pay, moved(-2), name + "_near")
-        far = along(pay, moved(-4), name + "_far")
         return near, far
 
     second_came = token_of(out_second, mid_second)
@@ -464,8 +464,8 @@
     pays = ((pay_a, pay_b), (near_a, near_b), (far_a, far_b))
     pair = pair_for_peer(info, 1, *pays, (queries_done, grads[0]))
     odd = along(pair, swap, "pay_swap")
-    blocks = ((2, b, 0, 0, 0, 0), (4, b, 1, 0, 1, 0))
-    grads = key_grads(info, blocks, kv, evens[1:], (near_b, far_b), slot_rows, grads)
+    blocks = ((2, b, 0, 0, 1, 0), (4, b, 1, 0, 0, 0))
+    grads = key_grads(info, blocks, kv, evens[1:], (far_b, near_b), slot_rows, grads)
     blocks = ((1, a + b, 0, 0, 0, 0), (3, a + b, 0, rows, 0, rows))
     grad_k, grad_v = key_grads(info, blocks, kv, (odd_q,), (odd,), slot_rows, grads)
     return (grad_q, grad_k, grad_v)

time: 72.8 us -> 71.9 us (0.988)
    ppermute x11, waiting for transfers between devices: 8.28 us -> 6.46 us  [along(): return lax.ppermute(x, 'ctx', pairs)]
    ppermute x5, waiting for transfers between devices: 12.8 us -> 14.3 us  [over(): return lax.ppermute(x, 'tp', pairs)]
where the time goes in v5:
time: 71.9 us; the launch traced here: 71.2 us
  starting transfers between devices  29.2 us (41%)
  waiting for transfers between devices  20.7 us (29%)
  Pallas kernels  18.4 us (26%)
  local copies, waits for them, and re-layouts  1.92 us (3%)
  between operations  0.92 us (1%)
    ppermute x11, starting transfers between devices, along(): return lax.ppermute(x, 'ctx', pairs)  23.9 us
    pallas_call x11, Pallas kernels, call(): pl.pallas_call(lambda *refs: kernel(device_info(info), *refs), out_shape=...  16.5 us
    ppermute x5, waiting for transfers between devices, over(): return lax.ppermute(x, 'tp', pairs)  14.3 us
    ppermute x11, waiting for transfers between devices, along(): return lax.ppermute(x, 'ctx', pairs)  6.46 us
    ppermute x5, starting transfers between devices, over(): return lax.ppermute(x, 'tp', pairs)  5.32 us
    unnamed x12, local copies, waits for them, and re-layouts  1.92 us
    pallas_call x1, Pallas kernels, pack(): pl.pallas_call(functools.partial(pack_kernel, places), out_shape=tuple((j...  1.9 us
  transfers between devices with their start and end apart: 16, of which 8 were waited for; matrix products, arithmetic and copies ran while one was open for 0% of the time, Pallas kernels for 23%

profile of v5, /device:TPU:3, one launch (start us, length us, event | category | flops | bytes accessed | tf_op | source)
XLA Modules:
  0.0 71.2 jit_solution(10282779262359323539)
XLA Ops:
  0.6 1.4 %collective-permute-start.6 = (bf16[64,5376]{1,0:T(8,128)(2,1)}, bf16[64,5376]{1,0:T(8,128)(2,1)S(1)}, u32[]{:S(2)}, u32[]{:S(2)}) collective-permute-start(bf16[64,5376]{1,0:T(8,128)(2,1)} %refs_0_.3), channel_id=1, source_target_pairs={{0,1},{1,0},{2,3},{3,2},{4,5},{5,4},{6,7},{7,6},{8,9},{9,8},{10,11... | collective-permute-start | bytes 2064392 | tf_op jit(solution)/shard_map/end_first/ppermute | solution.py:409
  2.0 0.7 collective-permute-start.8
  2.7 1.9 %pack.1 = (bf16[256,512]{1,0:T(8,128)(2,1)}, bf16[256,512]{1,0:T(8,128)(2,1)}) custom-call(bf16[256,256]{1,0:T(8,128)(2,1)} %refs_0_.2, bf16[256,256]{1,0:T(8,128)(2,1)} %refs_1_.1, bf16[256,512]{1,0:T(8,128)(2,1)} %refs_2_.2), custom_call_target="tpu_custom_call" | custom-call | flops 1 | bytes 1 | tf_op jit(solution)/shard_map/pack/pallas_call | solution.py:86
  4.6 3.1 %collective-permute-start = (bf16[256,512]{1,0:T(8,128)(2,1)}, bf16[256,512]{1,0:T(8,128)(2,1)S(1)}, u32[]{:S(2)}, u32[]{:S(2)}) collective-permute-start(bf16[256,512]{1,0:T(8,128)(2,1)} %get-tuple-element.22.refs_0_), channel_id=1, source_target_pairs={{0,8},{4,12},{8,16},{12,20},{16,24},{20,28},{1,9},{5,13},{9,17},{1... | collective-permute-start | bytes 786440 | tf_op jit(solution)/shard_map/kv_near/ppermute | solution.py:405
  7.7 1.3 %collective-permute-start.1 = (bf16[256,512]{1,0:T(8,128)(2,1)}, bf16[256,512]{1,0:T(8,128)(2,1)S(1)}, u32[]{:S(2)}, u32[]{:S(2)}) collective-permute-start(bf16[256,512]{1,0:T(8,128)(2,1)} %get-tuple-element.22.refs_0_), channel_id=1, source_target_pairs={{0,16},{4,20},{8,24},{12,28},{1,17},{5,21},{9,25},{13,29},{2,18},{... | collective-permute-start | bytes 786440 | tf_op jit(solution)/shard_map/kv_far/ppermute | solution.py:405
  9.1 1.3 %collective-permute-start.3 = (bf16[256,512]{1,0:T(8,128)(2,1)}, bf16[256,512]{1,0:T(8,128)(2,1)S(1)}, u32[]{:S(2)}, u32[]{:S(2)}) collective-permute-start(bf16[256,512]{1,0:T(8,128)(2,1)} %get-tuple-element.23.refs_0_.refs_1_), channel_id=1, source_target_pairs={{16,0},{20,4},{24,8},{28,12},{17,1},{21,5},{25,9},{29,13},{18,2},{... | collective-permute-start | bytes 786440 | tf_op jit(solution)/shard_map/q_far/ppermute | solution.py:405
  10.4 3.2 %collective-permute-done.refs_2_ = bf16[256,512]{1,0:T(8,128)(2,1)S(1)} collective-permute-done((bf16[256,512]{1,0:T(8,128)(2,1)}, bf16[256,512]{1,0:T(8,128)(2,1)S(1)}, u32[]{:S(2)}, u32[]{:S(2)}) %collective-permute-start) | collective-permute-done | bytes 262176 | tf_op jit(solution)/shard_map/kv_near/ppermute | solution.py:405
  13.6 1.9 %collective-permute-start.4 = (bf16[256,512]{1,0:T(8,128)(2,1)}, bf16[256,512]{1,0:T(8,128)(2,1)S(1)}, u32[]{:S(2)}, u32[]{:S(2)}) collective-permute-start(bf16[256,512]{1,0:T(8,128)(2,1)} %get-tuple-element.23.refs_0_.refs_1_), channel_id=1, source_target_pairs={{8,0},{12,4},{16,8},{20,12},{24,16},{28,20},{9,1},{13,5},{17,9},{2... | collective-permute-start | bytes 786440 | tf_op jit(solution)/shard_map/q_near/ppermute | solution.py:405
  15.5 1.7 %collective-permute-done.6.refs_1_ = bf16[64,5376]{1,0:T(8,128)(2,1)S(1)} collective-permute-done((bf16[64,5376]{1,0:T(8,128)(2,1)}, bf16[64,5376]{1,0:T(8,128)(2,1)S(1)}, u32[]{:S(2)}, u32[]{:S(2)}) %collective-permute-start.6) | collective-permute-done | bytes 688160 | tf_op jit(solution)/shard_map/end_first/ppermute | solution.py:409
  17.2 0.7 collective-permute-start.7
  17.9 0.0 collective-permute-done.8.refs_2_
  17.9 1.3 %collective-permute-start.9 = (bf16[64,5376]{1,0:T(8,128)(2,1)S(1)}, bf16[64,5376]{1,0:T(8,128)(2,1)S(1)}, u32[]{:S(2)}, u32[]{:S(2)}) collective-permute-start(bf16[64,5376]{1,0:T(8,128)(2,1)S(1)} %collective-permute-done.8.refs_2_), channel_id=1, source_target_pairs={{1,0},{2,3},{5,4},{6,7},{9,8},{10,11},{13,12},{14,15},{17,16},{18,... | collective-permute-start | bytes 2064392 | tf_op jit(solution)/shard_map/out_second/ppermute | solution.py:409
  19.2 0.0 collective-permute-done.1.refs_1_.refs_3_
  19.2 0.0 copy-start.1
  19.2 0.9 %copy-done.1 = bf16[256,512]{1,0:T(8,128)(2,1)S(1)} copy-done((bf16[256,512]{1,0:T(8,128)(2,1)S(1)}, bf16[256,512]{1,0:T(8,128)(2,1)}, u32[]{:S(2)}) %copy-start.1) | copy-done | bytes 262168
  20.2 0.0 copy-start.2
  20.2 1.6 %collective-permute-start.2 = (bf16[512,512]{1,0:T(8,128)(2,1)S(1)}, bf16[512,512]{1,0:T(8,128)(2,1)S(1)}, u32[]{:S(2)}, u32[]{:S(2)}) collective-permute-start(bf16[512,512]{1,0:T(8,128)(2,1)S(1)} %pair.3), channel_id=1, source_target_pairs={{0,4},{4,0},{8,12},{12,8},{16,20},{20,16},{24,28},{28,24},{1,5},{5... | collective-permute-start | bytes 1572872 | tf_op jit(solution)/shard_map/kv_swap/ppermute | solution.py:405
  21.8 0.0 collective-permute-done.3.refs_1_.refs_3_.refs_2_
  21.8 0.7 %collective-permute-done.4.refs_2_.refs_1_ = bf16[256,512]{1,0:T(8,128)(2,1)S(1)} collective-permute-done((bf16[256,512]{1,0:T(8,128)(2,1)}, bf16[256,512]{1,0:T(8,128)(2,1)S(1)}, u32[]{:S(2)}, u32[]{:S(2)}) %collective-permute-start.4) | collective-permute-done | bytes 262176 | tf_op jit(solution)/shard_map/q_near/ppermute | solution.py:405
  22.6 0.0 copy-start.3
  22.6 0.9 %copy-done.3 = bf16[256,512]{1,0:T(8,128)(2,1)S(1)} copy-done((bf16[256,512]{1,0:T(8,128)(2,1)S(1)}, bf16[256,512]{1,0:T(8,128)(2,1)}, u32[]{:S(2)}) %copy-start.3) | copy-done | bytes 262168
  23.6 3.0 %collective-permute-start.5 = (bf16[512,512]{1,0:T(8,128)(2,1)S(1)}, bf16[512,512]{1,0:T(8,128)(2,1)S(1)}, u32[]{:S(2)}, u32[]{:S(2)}) collective-permute-start(bf16[512,512]{1,0:T(8,128)(2,1)S(1)} %pair.4), channel_id=1, source_target_pairs={{0,4},{4,0},{8,12},{12,8},{16,20},{20,16},{24,28},{28,24},{1,5},{5... | collective-permute-start | bytes 1572872 | tf_op jit(solution)/shard_map/q_swap/ppermute | solution.py:405
  26.6 0.0 collective-permute-done.2.refs_4_
  26.6 1.5 %collective-permute-done.5.refs_5_.refs_1_ = bf16[512,512]{1,0:T(8,128)(2,1)S(1)} collective-permute-done((bf16[512,512]{1,0:T(8,128)(2,1)S(1)}, bf16[512,512]{1,0:T(8,128)(2,1)S(1)}, u32[]{:S(2)}, u32[]{:S(2)}) %collective-permute-start.5) | collective-permute-done | bytes 524320 | tf_op jit(solution)/shard_map/q_swap/ppermute | solution.py:405
  28.1 0.0 copy-done.2
  28.1 3.6 %attention_probs.1 = (bf16[4,256,1280]{2,1,0:T(8,128)(2,1)S(1)}, f32[256,512]{1,0:T(8,128)S(1)}, bf16[256,128]{1,0:T(8,128)(2,1)S(1)}, bf16[1280,512]{1,0:T(8,128)(2,1)S(1)}) custom-call(bf16[256,512]{1,0:T(8,128)(2,1)S(1)} %copy-done.2, bf16[256,512]{1,0:T(8,128)(2,1)S(1)} %copy-done.3, bf16[256,512]{1,0:T(8,128)(2,1)S(1)} %collective-permute-done.refs_2_, ...), custom_call_target="tpu_custom_call" | custom-call | flops 1 | bytes 1 | tf_op jit(solution)/shard_map/attention_probs/pallas_call | solution.py:40
  31.7 0.0 copy-start
  31.7 0.0 copy-start.5
  31.8 0.0 collective-permute-done.7.refs_1_.refs_0_
  31.8 5.1 %collective-permute-done.9.refs_0_.refs_3_ = bf16[64,5376]{1,0:T(8,128)(2,1)S(1)} collective-permute-done((bf16[64,5376]{1,0:T(8,128)(2,1)S(1)}, bf16[64,5376]{1,0:T(8,128)(2,1)S(1)}, u32[]{:S(2)}, u32[]{:S(2)}) %collective-permute-start.9) | collective-permute-done | bytes 688160 | tf_op jit(solution)/shard_map/out_second/ppermute | solution.py:409
  36.9 1.3 %collective-permute-start.10 = (bf16[64,5376]{1,0:T(8,128)(2,1)S(1)}, bf16[64,5376]{1,0:T(8,128)(2,1)S(1)}, u32[]{:S(2)}, u32[]{:S(2)}) collective-permute-start(bf16[64,5376]{1,0:T(8,128)(2,1)S(1)} %collective-permute-done.7.refs_1_.refs_0_), channel_id=1, source_target_pairs={{1,0},{2,3},{5,4},{6,7},{9,8},{10,11},{13,12},{14,15},{17,16},{18,... | collective-permute-start | bytes 2064392 | tf_op jit(solution)/shard_map/out_third/ppermute | solution.py:409
  38.2 0.0 copy-done
  38.2 0.0 copy-done.5
  38.2 2.1 %dout_rows.2.refs_2_.refs_4_.refs_0_ = bf16[192,640]{1,0:T(8,128)(2,1)S(1)} custom-call(bf16[64,5376]{1,0:T(8,128)(2,1)S(1)} %copy-done.5, bf16[64,5376]{1,0:T(8,128)(2,1)S(1)} %collective-permute-done.6.refs_1_, bf16[64,5376]{1,0:T(8,128)(2,1)S(1)} %collective-permute-done.8.refs_2_, bf16[64,5376]{1,0:T(8,128)(2,1)S(1)} %collective-permute-done.9.refs_0_.refs_3_, ...), custom_call_target="tpu_custom_call" | custom-call | flops 1 | bytes 1 | tf_op jit(solution)/shard_map/dout_rows/pallas_call | solution.py:40
  40.3 1.3 %collective-permute-start.11 = (bf16[192,640]{1,0:T(8,128)(2,1)S(1)}, bf16[192,640]{1,0:T(8,128)(2,1)S(1)}, u32[]{:S(2)}, u32[]{:S(2)}) collective-permute-start(bf16[192,640]{1,0:T(8,128)(2,1)S(1)} %dout_rows.2.refs_2_.refs_4_.refs_0_), channel_id=1, source_target_pairs={{16,0},{20,4},{24,8},{28,12},{17,1},{21,5},{25,9},{29,13},{18,2},{... | collective-permute-start | bytes 737288 | tf_op jit(solution)/shard_map/early_far/ppermute | solution.py:405
  41.6 2.2 %collective-permute-start.13 = (bf16[192,640]{1,0:T(8,128)(2,1)S(1)}, bf16[192,640]{1,0:T(8,128)(2,1)S(1)}, u32[]{:S(2)}, u32[]{:S(2)}) collective-permute-start(bf16[192,640]{1,0:T(8,128)(2,1)S(1)} %dout_rows.2.refs_2_.refs_4_.refs_0_), channel_id=1, source_target_pairs={{8,0},{12,4},{16,8},{20,12},{24,16},{28,20},{9,1},{13,5},{17,9},{2... | collective-permute-start | bytes 737288 | tf_op jit(solution)/shard_map/early_near/ppermute | solution.py:405
  43.8 2.1 %query_grads.2 = (f32[256,512]{1,0:T(8,128)}, f32[8,128]{1,0:T(8,128)S(1)}) custom-call(bf16[4,256,1280]{2,1,0:T(8,128)(2,1)S(1)} %get-tuple-element.24.refs_0_, bf16[1280,512]{1,0:T(8,128)(2,1)S(1)} %get-tuple-element.25.refs_1_, bf16[192,640]{1,0:T(8,128)(2,1)S(1)} %dout_rows.2.refs_2_.refs_4_.refs_0_), custom_call_target="tpu_custom_call" | custom-call | flops 1 | bytes 1 | tf_op jit(solution)/shard_map/query_grads/pallas_call | solution.py:40
  45.9 7.4 %collective-permute-done.10.refs_1_ = bf16[64,5376]{1,0:T(8,128)(2,1)S(1)} collective-permute-done((bf16[64,5376]{1,0:T(8,128)(2,1)S(1)}, bf16[64,5376]{1,0:T(8,128)(2,1)S(1)}, u32[]{:S(2)}, u32[]{:S(2)}) %collective-permute-start.10) | collective-permute-done | bytes 688160 | tf_op jit(solution)/shard_map/out_third/ppermute | solution.py:409
  53.3 1.9 %dout_rows.3.refs_2_.refs_7_.refs_1_ = bf16[64,640]{1,0:T(8,128)(2,1)S(1)} custom-call(bf16[64,5376]{1,0:T(8,128)(2,1)S(1)} %collective-permute-done.7.refs_1_.refs_0_, bf16[64,5376]{1,0:T(8,128)(2,1)S(1)} %collective-permute-done.10.refs_1_, bf16[512,5376]{1,0:T(8,128)(2,1)S(1)} %copy-done, f32[256,512]{1,0:T(8,128)S(1)} %get-tuple-element.28.refs_5_.refs_3_, ...), custom_call_target="tpu_custom_call" | custom-call | flops 1 | bytes 1 | tf_op jit(solution)/shard_map/dout_rows/pallas_call | solution.py:40
  55.1 0.0 copy-start.4
  55.2 1.4 %collective-permute-start.12 = (bf16[64,640]{1,0:T(8,128)(2,1)S(1)}, bf16[64,640]{1,0:T(8,128)(2,1)S(1)}, u32[]{:S(2)}, u32[]{:S(2)}) collective-permute-start(bf16[64,640]{1,0:T(8,128)(2,1)S(1)} %dout_rows.3.refs_2_.refs_7_.refs_1_), channel_id=1, source_target_pairs={{16,0},{20,4},{24,8},{28,12},{17,1},{21,5},{25,9},{29,13},{18,2},{... | collective-permute-start | bytes 245768 | tf_op jit(solution)/shard_map/late_far/ppermute | solution.py:405
  56.6 2.2 %collective-permute-start.14 = (bf16[64,640]{1,0:T(8,128)(2,1)S(1)}, bf16[64,640]{1,0:T(8,128)(2,1)S(1)}, u32[]{:S(2)}, u32[]{:S(2)}) collective-permute-start(bf16[64,640]{1,0:T(8,128)(2,1)S(1)} %dout_rows.3.refs_2_.refs_7_.refs_1_), channel_id=1, source_target_pairs={{8,0},{12,4},{16,8},{20,12},{24,16},{28,20},{9,1},{13,5},{17,9},{2... | collective-permute-start | bytes 245768 | tf_op jit(solution)/shard_map/late_near/ppermute | solution.py:405
  58.8 1.3 %query_grads.3 = (f32[256,512]{1,0:T(8,128)}, f32[8,128]{1,0:T(8,128)S(1)}) custom-call(bf16[4,256,1280]{2,1,0:T(8,128)(2,1)S(1)} %get-tuple-element.24.refs_0_, bf16[1280,512]{1,0:T(8,128)(2,1)S(1)} %get-tuple-element.25.refs_1_, bf16[64,640]{1,0:T(8,128)(2,1)S(1)} %dout_rows.3.refs_2_.refs_7_.refs_1_, ...), custom_call_target="tpu_custom_call", output_to_operand_aliasing={{0}: (3, {})} | custom-call | flops 1 | bytes 1 | tf_op jit(solution)/shard_map/query_grads/pallas_call | solution.py:40
  60.0 0.0 collective-permute-done.11.refs_6_.refs_2_
  60.0 0.0 collective-permute-done.13.refs_5_.refs_4_
  60.1 0.0 copy-done.4
  60.1 2.3 %key_grads.3 = (f32[256,256]{1,0:T(8,128)S(1)}, f32[256,256]{1,0:T(8,128)S(1)}) custom-call(bf16[256,512]{1,0:T(8,128)(2,1)S(1)} %copy-done.2, bf16[256,512]{1,0:T(8,128)(2,1)S(1)} %copy-done.4, bf16[256,512]{1,0:T(8,128)(2,1)S(1)} %collective-permute-done.4.refs_2_.refs_1_, bf16[256,512]{1,0:T(8,128)(2,1)S(1)} %collective-permute-done.3.refs_1_.refs_3_.refs_2_, ...), custom_call_target="tpu_custom_call" | custom-call | flops 1 | bytes 1 | tf_op jit(solution)/shard_map/key_grads/pallas_call | solution.py:40
  62.3 0.0 collective-permute-done.12.refs_3_
  62.3 0.3 collective-permute-done.14.refs_5_.refs_4_
  62.7 0.1 pair.5
  62.7 4.6 %collective-permute-start.15 = (bf16[512,640]{1,0:T(8,128)(2,1)S(1)}, bf16[512,640]{1,0:T(8,128)(2,1)S(1)}, u32[]{:S(2)}, u32[]{:S(2)}) collective-permute-start(bf16[512,640]{1,0:T(8,128)(2,1)S(1)} %pair.5), channel_id=1, source_target_pairs={{0,4},{4,0},{8,12},{12,8},{16,20},{20,16},{24,28},{28,24},{1,5},{5... | collective-permute-start | bytes 1966088 | tf_op jit(solution)/shard_map/pay_swap/ppermute | solution.py:405
  67.3 1.0 %key_grads.4 = (f32[256,256]{1,0:T(8,128)S(1)}, f32[256,256]{1,0:T(8,128)S(1)}) custom-call(bf16[256,512]{1,0:T(8,128)(2,1)S(1)} %copy-done.2, bf16[256,512]{1,0:T(8,128)(2,1)S(1)} %collective-permute-done.4.refs_2_.refs_1_, bf16[256,512]{1,0:T(8,128)(2,1)S(1)} %collective-permute-done.3.refs_1_.refs_3_.refs_2_, ...), custom_call_target="tpu_custom_call" | custom-call | flops 1 | bytes 1 | tf_op jit(solution)/shard_map/key_grads/pallas_call | solution.py:40
  68.4 0.7 collective-permute-done.15.refs_2_
  69.1 2.1 %key_grads.5 = (f32[256,256]{1,0:T(8,128)}, f32[256,256]{1,0:T(8,128)}) custom-call(bf16[256,512]{1,0:T(8,128)(2,1)S(1)} %copy-done.2, bf16[512,512]{1,0:T(8,128)(2,1)S(1)} %collective-permute-done.5.refs_5_.refs_1_, bf16[512,640]{1,0:T(8,128)(2,1)S(1)} %collective-permute-done.15.refs_2_, f32[256,256]{1,0:T(8,128)S(1)} %get-tuple-element.37.refs_3_, ...), custom_call_target="tpu_custom_call" | custom-call | flops 1 | bytes 1 | tf_op jit(solution)/shard_map/key_grads/pallas_call | solution.py:40
  (3 shorter events, 0.1 us)
Async XLA Ops:
  0.6 16.6 %collective-permute-start.6 = (bf16[64,5376]{1,0:T(8,128)(2,1)}, bf16[64,5376]{1,0:T(8,128)(2,1)S(1)}, u32[]{:S(2)}, u32[]{:S(2)}) collective-permute-start(bf16[64,5376]{1,0:T(8,128)(2,1)} %refs_0_.3), channel_id=1, source_target_pairs={{0,1},{1,0},{2,3},{3,2},{4,5},{5,4},{6,7},{7,6},{8,9},{9,8},{10,11... | collective-permute-start | bytes 2064392 | tf_op jit(solution)/shard_map/end_first/ppermute | solution.py:409
  2.0 15.9 %collective-permute-start.8 = (bf16[64,5376]{1,0:T(8,128)(2,1)}, bf16[64,5376]{1,0:T(8,128)(2,1)S(1)}, u32[]{:S(2)}, u32[]{:S(2)}) collective-permute-start(bf16[64,5376]{1,0:T(8,128)(2,1)} %refs_0_.3), channel_id=1, source_target_pairs={{1,2},{2,1},{5,6},{6,5},{9,10},{10,9},{13,14},{14,13},{17,18},{18,... | collective-permute-start | bytes 2064392 | tf_op jit(solution)/shard_map/mid_first/ppermute | solution.py:409
  4.6 9.0 %collective-permute-start = (bf16[256,512]{1,0:T(8,128)(2,1)}, bf16[256,512]{1,0:T(8,128)(2,1)S(1)}, u32[]{:S(2)}, u32[]{:S(2)}) collective-permute-start(bf16[256,512]{1,0:T(8,128)(2,1)} %get-tuple-element.22.refs_0_), channel_id=1, source_target_pairs={{0,8},{4,12},{8,16},{12,20},{16,24},{20,28},{1,9},{5,13},{9,17},{1... | collective-permute-start | bytes 786440 | tf_op jit(solution)/shard_map/kv_near/ppermute | solution.py:405
  7.7 11.5 %collective-permute-start.1 = (bf16[256,512]{1,0:T(8,128)(2,1)}, bf16[256,512]{1,0:T(8,128)(2,1)S(1)}, u32[]{:S(2)}, u32[]{:S(2)}) collective-permute-start(bf16[256,512]{1,0:T(8,128)(2,1)} %get-tuple-element.22.refs_0_), channel_id=1, source_target_pairs={{0,16},{4,20},{8,24},{12,28},{1,17},{5,21},{9,25},{13,29},{2,18},{... | collective-permute-start | bytes 786440 | tf_op jit(solution)/shard_map/kv_far/ppermute | solution.py:405
  9.1 12.8 %collective-permute-start.3 = (bf16[256,512]{1,0:T(8,128)(2,1)}, bf16[256,512]{1,0:T(8,128)(2,1)S(1)}, u32[]{:S(2)}, u32[]{:S(2)}) collective-permute-start(bf16[256,512]{1,0:T(8,128)(2,1)} %get-tuple-element.23.refs_0_.refs_1_), channel_id=1, source_target_pairs={{16,0},{20,4},{24,8},{28,12},{17,1},{21,5},{25,9},{29,13},{18,2},{... | collective-permute-start | bytes 786440 | tf_op jit(solution)/shard_map/q_far/ppermute | solution.py:405
  13.6 9.0 %collective-permute-start.4 = (bf16[256,512]{1,0:T(8,128)(2,1)}, bf16[256,512]{1,0:T(8,128)(2,1)S(1)}, u32[]{:S(2)}, u32[]{:S(2)}) collective-permute-start(bf16[256,512]{1,0:T(8,128)(2,1)} %get-tuple-element.23.refs_0_.refs_1_), channel_id=1, source_target_pairs={{8,0},{12,4},{16,8},{20,12},{24,16},{28,20},{9,1},{13,5},{17,9},{2... | collective-permute-start | bytes 786440 | tf_op jit(solution)/shard_map/q_near/ppermute | solution.py:405
  17.2 14.6 %collective-permute-start.7 = (bf16[64,5376]{1,0:T(8,128)(2,1)S(1)}, bf16[64,5376]{1,0:T(8,128)(2,1)S(1)}, u32[]{:S(2)}, u32[]{:S(2)}) collective-permute-start(bf16[64,5376]{1,0:T(8,128)(2,1)S(1)} %collective-permute-done.6.refs_1_), channel_id=1, source_target_pairs={{1,2},{2,1},{5,6},{6,5},{9,10},{10,9},{13,14},{14,13},{17,18},{18,... | collective-permute-start | bytes 2064392 | tf_op jit(solution)/shard_map/mid_second/ppermute | solution.py:409
  17.9 19.0 %collective-permute-start.9 = (bf16[64,5376]{1,0:T(8,128)(2,1)S(1)}, bf16[64,5376]{1,0:T(8,128)(2,1)S(1)}, u32[]{:S(2)}, u32[]{:S(2)}) collective-permute-start(bf16[64,5376]{1,0:T(8,128)(2,1)S(1)} %collective-permute-done.8.refs_2_), channel_id=1, source_target_pairs={{1,0},{2,3},{5,4},{6,7},{9,8},{10,11},{13,12},{14,15},{17,16},{18,... | collective-permute-start | bytes 2064392 | tf_op jit(solution)/shard_map/out_second/ppermute | solution.py:409
  19.2 1.0 %copy-start.1 = (bf16[256,512]{1,0:T(8,128)(2,1)S(1)}, bf16[256,512]{1,0:T(8,128)(2,1)}, u32[]{:S(2)}) copy-start(bf16[256,512]{1,0:T(8,128)(2,1)} %get-tuple-element.22.refs_0_) | copy-start | bytes 786436
  20.2 7.9 %copy-start.2 = (bf16[256,512]{1,0:T(8,128)(2,1)S(1)}, bf16[256,512]{1,0:T(8,128)(2,1)}, u32[]{:S(2)}) copy-start(bf16[256,512]{1,0:T(8,128)(2,1)} %get-tuple-element.22.refs_0_) | copy-start | bytes 786436
  20.2 6.3 %collective-permute-start.2 = (bf16[512,512]{1,0:T(8,128)(2,1)S(1)}, bf16[512,512]{1,0:T(8,128)(2,1)S(1)}, u32[]{:S(2)}, u32[]{:S(2)}) collective-permute-start(bf16[512,512]{1,0:T(8,128)(2,1)S(1)} %pair.3), channel_id=1, source_target_pairs={{0,4},{4,0},{8,12},{12,8},{16,20},{20,16},{24,28},{28,24},{1,5},{5... | collective-permute-start | bytes 1572872 | tf_op jit(solution)/shard_map/kv_swap/ppermute | solution.py:405
  22.6 1.0 %copy-start.3 = (bf16[256,512]{1,0:T(8,128)(2,1)S(1)}, bf16[256,512]{1,0:T(8,128)(2,1)}, u32[]{:S(2)}) copy-start(bf16[256,512]{1,0:T(8,128)(2,1)} %get-tuple-element.23.refs_0_.refs_1_) | copy-start | bytes 786436
  23.6 4.5 %collective-permute-start.5 = (bf16[512,512]{1,0:T(8,128)(2,1)S(1)}, bf16[512,512]{1,0:T(8,128)(2,1)S(1)}, u32[]{:S(2)}, u32[]{:S(2)}) collective-permute-start(bf16[512,512]{1,0:T(8,128)(2,1)S(1)} %pair.4), channel_id=1, source_target_pairs={{0,4},{4,0},{8,12},{12,8},{16,20},{20,16},{24,28},{28,24},{1,5},{5... | collective-permute-start | bytes 1572872 | tf_op jit(solution)/shard_map/q_swap/ppermute | solution.py:405
  31.7 6.5 %copy-start = (bf16[512,5376]{1,0:T(8,128)(2,1)S(1)}, bf16[512,5376]{1,0:T(8,128)(2,1)}, u32[]{:S(2)}) copy-start(bf16[512,5376]{1,0:T(8,128)(2,1)} %refs_2_.3) | copy-start | bytes 16515076
  31.7 6.5 %copy-start.5 = (bf16[64,5376]{1,0:T(8,128)(2,1)S(1)}, bf16[64,5376]{1,0:T(8,128)(2,1)}, u32[]{:S(2)}) copy-start(bf16[64,5376]{1,0:T(8,128)(2,1)} %refs_0_.3) | copy-start | bytes 2064388
  36.9 16.3 %collective-permute-start.10 = (bf16[64,5376]{1,0:T(8,128)(2,1)S(1)}, bf16[64,5376]{1,0:T(8,128)(2,1)S(1)}, u32[]{:S(2)}, u32[]{:S(2)}) collective-permute-start(bf16[64,5376]{1,0:T(8,128)(2,1)S(1)} %collective-permute-done.7.refs_1_.refs_0_), channel_id=1, source_target_pairs={{1,0},{2,3},{5,4},{6,7},{9,8},{10,11},{13,12},{14,15},{17,16},{18,... | collective-permute-start | bytes 2064392 | tf_op jit(solution)/shard_map/out_third/ppermute | solution.py:409
  40.3 19.7 %collective-permute-start.11 = (bf16[192,640]{1,0:T(8,128)(2,1)S(1)}, bf16[192,640]{1,0:T(8,128)(2,1)S(1)}, u32[]{:S(2)}, u32[]{:S(2)}) collective-permute-start(bf16[192,640]{1,0:T(8,128)(2,1)S(1)} %dout_rows.2.refs_2_.refs_4_.refs_0_), channel_id=1, source_target_pairs={{16,0},{20,4},{24,8},{28,12},{17,1},{21,5},{25,9},{29,13},{18,2},{... | collective-permute-start | bytes 737288 | tf_op jit(solution)/shard_map/early_far/ppermute | solution.py:405
  41.6 18.4 %collective-permute-start.13 = (bf16[192,640]{1,0:T(8,128)(2,1)S(1)}, bf16[192,640]{1,0:T(8,128)(2,1)S(1)}, u32[]{:S(2)}, u32[]{:S(2)}) collective-permute-start(bf16[192,640]{1,0:T(8,128)(2,1)S(1)} %dout_rows.2.refs_2_.refs_4_.refs_0_), channel_id=1, source_target_pairs={{8,0},{12,4},{16,8},{20,12},{24,16},{28,20},{9,1},{13,5},{17,9},{2... | collective-permute-start | bytes 737288 | tf_op jit(solution)/shard_map/early_near/ppermute | solution.py:405
  55.1 4.9 %copy-start.4 = (bf16[256,512]{1,0:T(8,128)(2,1)S(1)}, bf16[256,512]{1,0:T(8,128)(2,1)}, u32[]{:S(2)}) copy-start(bf16[256,512]{1,0:T(8,128)(2,1)} %get-tuple-element.23.refs_0_.refs_1_) | copy-start | bytes 786436
  55.2 7.2 %collective-permute-start.12 = (bf16[64,640]{1,0:T(8,128)(2,1)S(1)}, bf16[64,640]{1,0:T(8,128)(2,1)S(1)}, u32[]{:S(2)}, u32[]{:S(2)}) collective-permute-start(bf16[64,640]{1,0:T(8,128)(2,1)S(1)} %dout_rows.3.refs_2_.refs_7_.refs_1_), channel_id=1, source_target_pairs={{16,0},{20,4},{24,8},{28,12},{17,1},{21,5},{25,9},{29,13},{18,2},{... | collective-permute-start | bytes 245768 | tf_op jit(solution)/shard_map/late_far/ppermute | solution.py:405
  56.6 6.1 %collective-permute-start.14 = (bf16[64,640]{1,0:T(8,128)(2,1)S(1)}, bf16[64,640]{1,0:T(8,128)(2,1)S(1)}, u32[]{:S(2)}, u32[]{:S(2)}) collective-permute-start(bf16[64,640]{1,0:T(8,128)(2,1)S(1)} %dout_rows.3.refs_2_.refs_7_.refs_1_), channel_id=1, source_target_pairs={{8,0},{12,4},{16,8},{20,12},{24,16},{28,20},{9,1},{13,5},{17,9},{2... | collective-permute-start | bytes 245768 | tf_op jit(solution)/shard_map/late_near/ppermute | solution.py:405
  62.7 6.3 %collective-permute-start.15 = (bf16[512,640]{1,0:T(8,128)(2,1)S(1)}, bf16[512,640]{1,0:T(8,128)(2,1)S(1)}, u32[]{:S(2)}, u32[]{:S(2)}) collective-permute-start(bf16[512,640]{1,0:T(8,128)(2,1)S(1)} %pair.5), channel_id=1, source_target_pairs={{0,4},{4,0},{8,12},{12,8},{16,20},{20,16},{24,28},{28,24},{1,5},{5... | collective-permute-start | bytes 1966088 | tf_op jit(solution)/shard_map/pay_swap/ppermute | solution.py:405

commit v6 on v5

--- a/solution.py
+++ b/solution.py
@@ -15,6 +15,7 @@
 NN = (((1,), (0,)), ((), ()))
 F32 = jnp.float32
 BF16 = jnp.bfloat16
+FETCH = pl.CostEstimate(flops=2 * 10**9, bytes_accessed=1, transcendentals=0)
 VMEM = pl.BlockSpec(memory_space=pltpu.VMEM)
 ANY = pl.BlockSpec(memory_space=pl.ANY)
 COST = pl.CostEstimate(flops=1, bytes_accessed=1, transcendentals=0)
@@ -57,14 +58,14 @@
     refs[-1][...] = jnp.zeros_like(refs[-1])
 
 
-def token_of(*arrays):
+def token_of(*arrays, cost=COST):
     return pl.pallas_call(
         token_kernel,
         out_shape=TOKEN,
         in_specs=[ANY] * len(arrays),
         out_specs=VMEM,
         compiler_params=params(),
-        cost_estimate=pl.CostEstimate(flops=2 * 10**9, bytes_accessed=1, transcendentals=0),
+        cost_estimate=cost,
         name="token",
     )(*arrays)
 
@@ -300,10 +301,13 @@
     )
 
 
-def key_kernel(blocks, q_count, d_count, info, kv, *refs):
+def key_kernel(blocks, q_count, d_count, before_count, last, info, kv, *refs):
     q_refs, d_refs = refs[:q_count], refs[q_count : q_count + d_count]
-    before = refs[q_count + d_count : -7]
-    grad_k, grad_v, q_cat, d_cat, held_k, held_v, sems = refs[-7:]
+    before = refs[q_count + d_count : q_count + d_count + before_count]
+    if last:
+        grad_k, grad_v, q_cat, d_cat, held_k, held_v, sems = refs[-7:]
+    else:
+        held_k, held_v, q_cat, d_cat = refs[-4:]
     rows, kv_width = kv.shape[0], kv.shape[1] // 2
     width = q_cat.shape[1]
     lanes = q_cat.shape[0]
@@ -363,7 +367,7 @@
             sum_v = sum_v + before[1][:, cols]
         held_k[:, cols] = sum_k
         held_v[:, cols] = sum_v
-        for n, (held, out) in enumerate(((held_k, grad_k), (held_v, grad_v))):
+        for n, (held, out) in enumerate(((held_k, grad_k), (held_v, grad_v)) if last else ()):
             copy = pltpu.make_async_copy(held.at[:, cols], out.at[:, cols], sems.at[2 * group + n])
             copy.start()
             copies.append(copy)
@@ -371,26 +375,24 @@
         copy.wait()
 
 
-def key_grads(info, blocks, kv, q_arrays, d_arrays, slot_rows, before=()):
+def key_grads(info, blocks, kv, q_arrays, d_arrays, slot_rows, before=(), after=(), last=False):
     lanes = sum(len(block[1]) for block in blocks) * slot_rows
     width = q_arrays[0].shape[1]
     kv_width = kv.shape[1] // 2
     shape = jax.ShapeDtypeStruct((kv.shape[0], kv_width), F32)
     held = pltpu.VMEM(shape.shape, F32)
     return call(
-        functools.partial(key_kernel, blocks, len(q_arrays), len(d_arrays)),
+        functools.partial(key_kernel, blocks, len(q_arrays), len(d_arrays), len(before), last),
         "key_grads",
         (shape, shape),
         info,
-        (kv, *q_arrays, *d_arrays, *before),
+        (kv, *q_arrays, *d_arrays, *before, *after),
         [
             pltpu.VMEM((lanes, width), BF16),
             pltpu.VMEM((lanes, width + HD), BF16),
-            held,
-            held,
-            pltpu.SemaphoreType.DMA((2 * (kv_width // HD),)),
-        ],
-        outs=ANY,
+        ]
+        + ([held, held, pltpu.SemaphoreType.DMA((2 * (kv_width // HD),))] if last else []),
+        outs=ANY if last else VMEM,
     )
 
 
@@ -445,7 +447,7 @@
         near = along(pay, moved(-2), name + "_near")
         return near, far
 
-    second_came = token_of(out_second, mid_second)
+    second_came = token_of(token_of(out_second), mid_second, cost=FETCH)
     mid_second, second_came, stats = lax.optimization_barrier((mid_second, second_came, stats))
     out_third = over(mid_second, outward, "out_third")
     statistics = (out_weight, mixed, stats)
@@ -454,20 +456,31 @@
     near_a, far_a = sent(pay_a, "early")
     grad_q, queries_done = query_grads(info, early, (pay_a,), probs, span)
 
+    a, b = (0, 1, 2), (3,)
+    pair = pair_for_peer(info, 1, (pay_a,), (near_a,), (far_a,), (queries_done,))
+    odd_a = along(pair, swap, "early_swap")
+
     pay_b = dout_rows(info, late, (mid_second, out_third), *statistics, (queries_done,))
     near_b, far_b = sent(pay_b, "late")
     grad_q, queries_done = query_grads(info, late, (pay_b,), probs, span, (grad_q,))
-    a, b = (0, 1, 2), (3,)
-    evens = (query, near_q, far_q)
-    blocks = ((0, a, 0, 0, 0, 0), (2, a, 1, 0, 1, 0), (4, a, 2, 0, 2, 0), (0, b, 0, 0, 3, 0))
-    grads = key_grads(info, blocks, kv, evens, (pay_a, near_a, far_a, pay_b), slot_rows)
-    pays = ((pay_a, pay_b), (near_a, near_b), (far_a, far_b))
-    pair = pair_for_peer(info, 1, *pays, (queries_done, grads[0]))
-    odd = along(pair, swap, "pay_swap")
+    blocks = (
+        (0, a, 0, 0, 0, 0),
+        (2, a, 1, 0, 2, 0),
+        (4, a, 2, 0, 1, 0),
+        (1, a, 3, 0, 3, 0),
+        (3, a, 3, rows, 3, len(a) * slot_rows),
+        (0, b, 0, 0, 4, 0),
+    )
+    q_arrays = (query, near_q, far_q, odd_q)
+    d_arrays = (pay_a, far_a, near_a, odd_a, pay_b)
+    grads = key_grads(info, blocks, kv, q_arrays, d_arrays, slot_rows)
+    after = (queries_done, grads[0])
+    pair = pair_for_peer(info, 1, (pay_b,), (near_b,), (far_b,), after)
+    odd_b = along(pair, swap, "late_swap")
     blocks = ((2, b, 0, 0, 1, 0), (4, b, 1, 0, 0, 0))
-    grads = key_grads(info, blocks, kv, evens[1:], (far_b, near_b), slot_rows, grads)
-    blocks = ((1, a + b, 0, 0, 0, 0), (3, a + b, 0, rows, 0, rows))
-    grad_k, grad_v = key_grads(info, blocks, kv, (odd_q,), (odd,), slot_rows, grads)
+    grads = key_grads(info, blocks, kv, (near_q, far_q), (far_b, near_b), slot_rows, grads)
+    blocks = ((1, b, 0, 0, 0, 0), (3, b, 0, rows, 0, slot_rows))
+    grad_k, grad_v = key_grads(info, blocks, kv, (odd_q,), (odd_b,), slot_rows, grads, last=True)
     return (grad_q, grad_k, grad_v)
 
 

time: 71.9 us -> 70.8 us (0.985)
  waiting for transfers between devices: 20.7 us -> 15.3 us
  starting transfers between devices: 29.2 us -> 32.3 us
  local copies, waits for them, and re-layouts: 1.92 us -> 3.04 us
    ppermute x5, waiting for transfers between devices: 14.3 us -> 2.48 us  [over(): return lax.ppermute(x, 'tp', pairs)]
    ppermute x11 -> x12, waiting for transfers between devices: 6.46 us -> 12.8 us  [along(): return lax.ppermute(x, 'ctx', pairs)]
    ppermute x5, starting transfers between devices: 5.32 us -> 8.11 us  [over(): return lax.ppermute(x, 'tp', pairs)]
    unnamed x12, local copies, waits for them, and re-layouts: 1.92 us -> 3.04 us
    pallas_call x11 -> x12, Pallas kernels: 16.5 us -> 16.1 us  [call(): pl.pallas_call(lambda *refs: kernel(device_info(info), *refs), out_shape=...]
    ppermute x11 -> x12, starting transfers between devices: 23.9 us -> 24.2 us  [along(): return lax.ppermute(x, 'ctx', pairs)]
  transfers between devices with their start and end apart: 16 -> 17, of which waited for: 8 -> 8; matrix products, arithmetic and copies ran while one was open for 0% -> 0% of each run, Pallas kernels for 23% -> 24%
where the time goes in v6:
time: 70.8 us; the launch traced here: 69.5 us
  starting transfers between devices  32.3 us (46%)
  Pallas kernels  18 us (25%)
  waiting for transfers between devices  15.3 us (22%)
  local copies, waits for them, and re-layouts  3.04 us (4%)
  between operations  0.89 us (1%)
    ppermute x12, starting transfers between devices, along(): return lax.ppermute(x, 'ctx', pairs)  24.2 us
    pallas_call x12, Pallas kernels, call(): pl.pallas_call(lambda *refs: kernel(device_info(info), *refs), out_shape=...  16.1 us
    ppermute x12, waiting for transfers between devices, along(): return lax.ppermute(x, 'ctx', pairs)  12.8 us
    ppermute x5, starting transfers between devices, over(): return lax.ppermute(x, 'tp', pairs)  8.11 us
    unnamed x12, local copies, waits for them, and re-layouts  3.04 us
    ppermute x5, waiting for transfers between devices, over(): return lax.ppermute(x, 'tp', pairs)  2.48 us
    pallas_call x1, Pallas kernels, pack(): pl.pallas_call(functools.partial(pack_kernel, places), out_shape=tuple((j...  1.9 us
  transfers between devices with their start and end apart: 17, of which 8 were waited for; matrix products, arithmetic and copies ran while one was open for 0% of the time, Pallas kernels for 24%

profile of v6, /device:TPU:3, one launch (start us, length us, event | category | flops | bytes accessed | tf_op | source)
XLA Modules:
  0.0 69.5 jit_solution(18110338868781780688)
XLA Ops:
  0.6 0.7 %collective-permute-start.8 = (bf16[64,5376]{1,0:T(8,128)(2,1)}, bf16[64,5376]{1,0:T(8,128)(2,1)S(1)}, u32[]{:S(2)}, u32[]{:S(2)}) collective-permute-start(bf16[64,5376]{1,0:T(8,128)(2,1)} %refs_0_.3), channel_id=1, source_target_pairs={{1,2},{2,1},{5,6},{6,5},{9,10},{10,9},{13,14},{14,13},{17,18},{18,... | collective-permute-start | bytes 2064392 | tf_op jit(solution)/shard_map/mid_first/ppermute | solution.py:411
  1.3 3.9 %collective-permute-start.6 = (bf16[64,5376]{1,0:T(8,128)(2,1)}, bf16[64,5376]{1,0:T(8,128)(2,1)S(1)}, u32[]{:S(2)}, u32[]{:S(2)}) collective-permute-start(bf16[64,5376]{1,0:T(8,128)(2,1)} %refs_0_.3), channel_id=1, source_target_pairs={{0,1},{1,0},{2,3},{3,2},{4,5},{5,4},{6,7},{7,6},{8,9},{9,8},{10,11... | collective-permute-start | bytes 2064392 | tf_op jit(solution)/shard_map/end_first/ppermute | solution.py:411
  5.2 1.9 %pack.1 = (bf16[256,512]{1,0:T(8,128)(2,1)}, bf16[256,512]{1,0:T(8,128)(2,1)}) custom-call(bf16[256,256]{1,0:T(8,128)(2,1)} %refs_0_.2, bf16[256,256]{1,0:T(8,128)(2,1)} %refs_1_.1, bf16[256,512]{1,0:T(8,128)(2,1)} %refs_2_.2), custom_call_target="tpu_custom_call" | custom-call | flops 1 | bytes 1 | tf_op jit(solution)/shard_map/pack/pallas_call | solution.py:87
  7.1 3.1 %collective-permute-start = (bf16[256,512]{1,0:T(8,128)(2,1)}, bf16[256,512]{1,0:T(8,128)(2,1)S(1)}, u32[]{:S(2)}, u32[]{:S(2)}) collective-permute-start(bf16[256,512]{1,0:T(8,128)(2,1)} %get-tuple-element.22.refs_0_), channel_id=1, source_target_pairs={{0,8},{4,12},{8,16},{12,20},{16,24},{20,28},{1,9},{5,13},{9,17},{1... | collective-permute-start | bytes 786440 | tf_op jit(solution)/shard_map/kv_near/ppermute | solution.py:407
  10.2 1.3 %collective-permute-start.1 = (bf16[256,512]{1,0:T(8,128)(2,1)}, bf16[256,512]{1,0:T(8,128)(2,1)S(1)}, u32[]{:S(2)}, u32[]{:S(2)}) collective-permute-start(bf16[256,512]{1,0:T(8,128)(2,1)} %get-tuple-element.22.refs_0_), channel_id=1, source_target_pairs={{0,16},{4,20},{8,24},{12,28},{1,17},{5,21},{9,25},{13,29},{2,18},{... | collective-permute-start | bytes 786440 | tf_op jit(solution)/shard_map/kv_far/ppermute | solution.py:407
  11.6 1.3 %collective-permute-start.3 = (bf16[256,512]{1,0:T(8,128)(2,1)}, bf16[256,512]{1,0:T(8,128)(2,1)S(1)}, u32[]{:S(2)}, u32[]{:S(2)}) collective-permute-start(bf16[256,512]{1,0:T(8,128)(2,1)} %get-tuple-element.23.refs_0_.refs_1_), channel_id=1, source_target_pairs={{16,0},{20,4},{24,8},{28,12},{17,1},{21,5},{25,9},{29,13},{18,2},{... | collective-permute-start | bytes 786440 | tf_op jit(solution)/shard_map/q_far/ppermute | solution.py:407
  12.9 2.9 %collective-permute-done.refs_2_ = bf16[256,512]{1,0:T(8,128)(2,1)S(1)} collective-permute-done((bf16[256,512]{1,0:T(8,128)(2,1)}, bf16[256,512]{1,0:T(8,128)(2,1)S(1)}, u32[]{:S(2)}, u32[]{:S(2)}) %collective-permute-start) | collective-permute-done | bytes 262176 | tf_op jit(solution)/shard_map/kv_near/ppermute | solution.py:407
  15.8 1.9 %collective-permute-start.4 = (bf16[256,512]{1,0:T(8,128)(2,1)}, bf16[256,512]{1,0:T(8,128)(2,1)S(1)}, u32[]{:S(2)}, u32[]{:S(2)}) collective-permute-start(bf16[256,512]{1,0:T(8,128)(2,1)} %get-tuple-element.23.refs_0_.refs_1_), channel_id=1, source_target_pairs={{8,0},{12,4},{16,8},{20,12},{24,16},{28,20},{9,1},{13,5},{17,9},{2... | collective-permute-start | bytes 786440 | tf_op jit(solution)/shard_map/q_near/ppermute | solution.py:407
  17.7 0.0 collective-permute-done.8.refs_2_
  17.7 1.3 %collective-permute-start.9 = (bf16[64,5376]{1,0:T(8,128)(2,1)S(1)}, bf16[64,5376]{1,0:T(8,128)(2,1)S(1)}, u32[]{:S(2)}, u32[]{:S(2)}) collective-permute-start(bf16[64,5376]{1,0:T(8,128)(2,1)S(1)} %collective-permute-done.8.refs_2_), channel_id=1, source_target_pairs={{1,0},{2,3},{5,4},{6,7},{9,8},{10,11},{13,12},{14,15},{17,16},{18,... | collective-permute-start | bytes 2064392 | tf_op jit(solution)/shard_map/out_second/ppermute | solution.py:411
  19.0 1.3 %collective-permute-done.6.refs_1_ = bf16[64,5376]{1,0:T(8,128)(2,1)S(1)} collective-permute-done((bf16[64,5376]{1,0:T(8,128)(2,1)}, bf16[64,5376]{1,0:T(8,128)(2,1)S(1)}, u32[]{:S(2)}, u32[]{:S(2)}) %collective-permute-start.6) | collective-permute-done | bytes 688160 | tf_op jit(solution)/shard_map/end_first/ppermute | solution.py:411
  20.3 0.7 collective-permute-start.7
  21.0 0.0 collective-permute-done.1.refs_1_.refs_3_
  21.0 0.0 copy-start.1
  21.0 0.9 %copy-done.1 = bf16[256,512]{1,0:T(8,128)(2,1)S(1)} copy-done((bf16[256,512]{1,0:T(8,128)(2,1)S(1)}, bf16[256,512]{1,0:T(8,128)(2,1)}, u32[]{:S(2)}) %copy-start.1) | copy-done | bytes 262168
  21.9 0.0 copy-start.2
  22.0 1.6 %collective-permute-start.2 = (bf16[512,512]{1,0:T(8,128)(2,1)S(1)}, bf16[512,512]{1,0:T(8,128)(2,1)S(1)}, u32[]{:S(2)}, u32[]{:S(2)}) collective-permute-start(bf16[512,512]{1,0:T(8,128)(2,1)S(1)} %pair.4), channel_id=1, source_target_pairs={{0,4},{4,0},{8,12},{12,8},{16,20},{20,16},{24,28},{28,24},{1,5},{5... | collective-permute-start | bytes 1572872 | tf_op jit(solution)/shard_map/kv_swap/ppermute | solution.py:407
  23.6 0.0 collective-permute-done.3.refs_1_.refs_3_.refs_2_
  23.6 0.9 %collective-permute-done.4.refs_2_.refs_1_ = bf16[256,512]{1,0:T(8,128)(2,1)S(1)} collective-permute-done((bf16[256,512]{1,0:T(8,128)(2,1)}, bf16[256,512]{1,0:T(8,128)(2,1)S(1)}, u32[]{:S(2)}, u32[]{:S(2)}) %collective-permute-start.4) | collective-permute-done | bytes 262176 | tf_op jit(solution)/shard_map/q_near/ppermute | solution.py:407
  24.5 0.0 copy-start.3
  24.5 0.9 %copy-done.3 = bf16[256,512]{1,0:T(8,128)(2,1)S(1)} copy-done((bf16[256,512]{1,0:T(8,128)(2,1)S(1)}, bf16[256,512]{1,0:T(8,128)(2,1)}, u32[]{:S(2)}) %copy-start.3) | copy-done | bytes 262168
  25.5 3.6 %collective-permute-start.5 = (bf16[512,512]{1,0:T(8,128)(2,1)S(1)}, bf16[512,512]{1,0:T(8,128)(2,1)S(1)}, u32[]{:S(2)}, u32[]{:S(2)}) collective-permute-start(bf16[512,512]{1,0:T(8,128)(2,1)S(1)} %pair.5), channel_id=1, source_target_pairs={{0,4},{4,0},{8,12},{12,8},{16,20},{20,16},{24,28},{28,24},{1,5},{5... | collective-permute-start | bytes 1572872 | tf_op jit(solution)/shard_map/q_swap/ppermute | solution.py:407
  29.1 0.0 collective-permute-done.2.refs_4_
  29.1 1.5 %collective-permute-done.5.refs_5_.refs_4_.refs_1_ = bf16[512,512]{1,0:T(8,128)(2,1)S(1)} collective-permute-done((bf16[512,512]{1,0:T(8,128)(2,1)S(1)}, bf16[512,512]{1,0:T(8,128)(2,1)S(1)}, u32[]{:S(2)}, u32[]{:S(2)}) %collective-permute-start.5) | collective-permute-done | bytes 524320 | tf_op jit(solution)/shard_map/q_swap/ppermute | solution.py:407
  30.6 0.0 copy-done.2
  30.6 3.6 %attention_probs.1 = (bf16[4,256,1280]{2,1,0:T(8,128)(2,1)S(1)}, f32[256,512]{1,0:T(8,128)S(1)}, bf16[256,128]{1,0:T(8,128)(2,1)S(1)}, bf16[1280,512]{1,0:T(8,128)(2,1)S(1)}) custom-call(bf16[256,512]{1,0:T(8,128)(2,1)S(1)} %copy-done.2, bf16[256,512]{1,0:T(8,128)(2,1)S(1)} %copy-done.3, bf16[256,512]{1,0:T(8,128)(2,1)S(1)} %collective-permute-done.refs_2_, ...), custom_call_target="tpu_custom_call" | custom-call | flops 1 | bytes 1 | tf_op jit(solution)/shard_map/attention_probs/pallas_call | solution.py:41
  34.2 1.2 %collective-permute-done.9.refs_0_.refs_3_ = bf16[64,5376]{1,0:T(8,128)(2,1)S(1)} collective-permute-done((bf16[64,5376]{1,0:T(8,128)(2,1)S(1)}, bf16[64,5376]{1,0:T(8,128)(2,1)S(1)}, u32[]{:S(2)}, u32[]{:S(2)}) %collective-permute-start.9) | collective-permute-done | bytes 688160 | tf_op jit(solution)/shard_map/out_second/ppermute | solution.py:411
  35.5 0.0 copy-start
  35.5 0.0 copy-start.5
  35.5 0.0 collective-permute-done.7.refs_1_.refs_0_
  35.5 1.6 %collective-permute-start.10 = (bf16[64,5376]{1,0:T(8,128)(2,1)S(1)}, bf16[64,5376]{1,0:T(8,128)(2,1)S(1)}, u32[]{:S(2)}, u32[]{:S(2)}) collective-permute-start(bf16[64,5376]{1,0:T(8,128)(2,1)S(1)} %collective-permute-done.7.refs_1_.refs_0_), channel_id=1, source_target_pairs={{1,0},{2,3},{5,4},{6,7},{9,8},{10,11},{13,12},{14,15},{17,16},{18,... | collective-permute-start | bytes 2064392 | tf_op jit(solution)/shard_map/out_third/ppermute | solution.py:411
  37.0 1.0 %copy-done = bf16[512,5376]{1,0:T(8,128)(2,1)S(1)} copy-done((bf16[512,5376]{1,0:T(8,128)(2,1)S(1)}, bf16[512,5376]{1,0:T(8,128)(2,1)}, u32[]{:S(2)}) %copy-start) | copy-done | bytes 5505048
  38.0 0.2 copy-done.5
  38.2 2.1 %dout_rows.2.refs_2_.refs_0_.refs_5_ = bf16[192,640]{1,0:T(8,128)(2,1)S(1)} custom-call(bf16[64,5376]{1,0:T(8,128)(2,1)S(1)} %copy-done.5, bf16[64,5376]{1,0:T(8,128)(2,1)S(1)} %collective-permute-done.6.refs_1_, bf16[64,5376]{1,0:T(8,128)(2,1)S(1)} %collective-permute-done.8.refs_2_, bf16[64,5376]{1,0:T(8,128)(2,1)S(1)} %collective-permute-done.9.refs_0_.refs_3_, ...), custom_call_target="tpu_custom_call" | custom-call | flops 1 | bytes 1 | tf_op jit(solution)/shard_map/dout_rows/pallas_call | solution.py:41
  40.3 1.3 %collective-permute-start.13 = (bf16[192,640]{1,0:T(8,128)(2,1)S(1)}, bf16[192,640]{1,0:T(8,128)(2,1)S(1)}, u32[]{:S(2)}, u32[]{:S(2)}) collective-permute-start(bf16[192,640]{1,0:T(8,128)(2,1)S(1)} %dout_rows.2.refs_2_.refs_0_.refs_5_), channel_id=1, source_target_pairs={{16,0},{20,4},{24,8},{28,12},{17,1},{21,5},{25,9},{29,13},{18,2},{... | collective-permute-start | bytes 737288 | tf_op jit(solution)/shard_map/early_far/ppermute | solution.py:407
  41.6 2.5 %collective-permute-start.14 = (bf16[192,640]{1,0:T(8,128)(2,1)S(1)}, bf16[192,640]{1,0:T(8,128)(2,1)S(1)}, u32[]{:S(2)}, u32[]{:S(2)}) collective-permute-start(bf16[192,640]{1,0:T(8,128)(2,1)S(1)} %dout_rows.2.refs_2_.refs_0_.refs_5_), channel_id=1, source_target_pairs={{8,0},{12,4},{16,8},{20,12},{24,16},{28,20},{9,1},{13,5},{17,9},{2... | collective-permute-start | bytes 737288 | tf_op jit(solution)/shard_map/early_near/ppermute | solution.py:407
  44.1 2.1 %query_grads.2 = (f32[256,512]{1,0:T(8,128)}, f32[8,128]{1,0:T(8,128)S(1)}) custom-call(bf16[4,256,1280]{2,1,0:T(8,128)(2,1)S(1)} %get-tuple-element.24.refs_0_, bf16[1280,512]{1,0:T(8,128)(2,1)S(1)} %get-tuple-element.25.refs_1_, bf16[192,640]{1,0:T(8,128)(2,1)S(1)} %dout_rows.2.refs_2_.refs_0_.refs_5_), custom_call_target="tpu_custom_call" | custom-call | flops 1 | bytes 1 | tf_op jit(solution)/shard_map/query_grads/pallas_call | solution.py:41
  46.2 6.8 %collective-permute-done.13.refs_1_.refs_6_ = bf16[192,640]{1,0:T(8,128)(2,1)S(1)} collective-permute-done((bf16[192,640]{1,0:T(8,128)(2,1)S(1)}, bf16[192,640]{1,0:T(8,128)(2,1)S(1)}, u32[]{:S(2)}, u32[]{:S(2)}) %collective-permute-start.13) | collective-permute-done | bytes 245792 | tf_op jit(solution)/shard_map/early_far/ppermute | solution.py:407
  53.0 0.0 collective-permute-done.14.refs_2_.refs_7_
  53.0 2.9 %collective-permute-start.15 = (bf16[384,640]{1,0:T(8,128)(2,1)S(1)}, bf16[384,640]{1,0:T(8,128)(2,1)S(1)}, u32[]{:S(2)}, u32[]{:S(2)}) collective-permute-start(bf16[384,640]{1,0:T(8,128)(2,1)S(1)} %pair.6), channel_id=1, source_target_pairs={{0,4},{4,0},{8,12},{12,8},{16,20},{20,16},{24,28},{28,24},{1,5},{5... | collective-permute-start | bytes 1474568 | tf_op jit(solution)/shard_map/early_swap/ppermute | solution.py:407
  55.9 0.0 collective-permute-done.10.refs_1_
  55.9 1.9 %dout_rows.3.refs_2_.refs_9_.refs_0_ = bf16[64,640]{1,0:T(8,128)(2,1)S(1)} custom-call(bf16[64,5376]{1,0:T(8,128)(2,1)S(1)} %collective-permute-done.7.refs_1_.refs_0_, bf16[64,5376]{1,0:T(8,128)(2,1)S(1)} %collective-permute-done.10.refs_1_, bf16[512,5376]{1,0:T(8,128)(2,1)S(1)} %copy-done, f32[256,512]{1,0:T(8,128)S(1)} %get-tuple-element.28.refs_5_.refs_3_, ...), custom_call_target="tpu_custom_call" | custom-call | flops 1 | bytes 1 | tf_op jit(solution)/shard_map/dout_rows/pallas_call | solution.py:41
  57.8 0.0 copy-start.4
  57.8 1.4 %collective-permute-start.11 = (bf16[64,640]{1,0:T(8,128)(2,1)S(1)}, bf16[64,640]{1,0:T(8,128)(2,1)S(1)}, u32[]{:S(2)}, u32[]{:S(2)}) collective-permute-start(bf16[64,640]{1,0:T(8,128)(2,1)S(1)} %dout_rows.3.refs_2_.refs_9_.refs_0_), channel_id=1, source_target_pairs={{16,0},{20,4},{24,8},{28,12},{17,1},{21,5},{25,9},{29,13},{18,2},{... | collective-permute-start | bytes 245768 | tf_op jit(solution)/shard_map/late_far/ppermute | solution.py:407
  59.2 1.9 %collective-permute-start.12 = (bf16[64,640]{1,0:T(8,128)(2,1)S(1)}, bf16[64,640]{1,0:T(8,128)(2,1)S(1)}, u32[]{:S(2)}, u32[]{:S(2)}) collective-permute-start(bf16[64,640]{1,0:T(8,128)(2,1)S(1)} %dout_rows.3.refs_2_.refs_9_.refs_0_), channel_id=1, source_target_pairs={{8,0},{12,4},{16,8},{20,12},{24,16},{28,20},{9,1},{13,5},{17,9},{2... | collective-permute-start | bytes 245768 | tf_op jit(solution)/shard_map/late_near/ppermute | solution.py:407
  61.2 1.3 %query_grads.3 = (f32[256,512]{1,0:T(8,128)}, f32[8,128]{1,0:T(8,128)S(1)}) custom-call(bf16[4,256,1280]{2,1,0:T(8,128)(2,1)S(1)} %get-tuple-element.24.refs_0_, bf16[1280,512]{1,0:T(8,128)(2,1)S(1)} %get-tuple-element.25.refs_1_, bf16[64,640]{1,0:T(8,128)(2,1)S(1)} %dout_rows.3.refs_2_.refs_9_.refs_0_, ...), custom_call_target="tpu_custom_call", output_to_operand_aliasing={{0}: (3, {})} | custom-call | flops 1 | bytes 1 | tf_op jit(solution)/shard_map/query_grads/pallas_call | solution.py:41
  62.4 0.0 collective-permute-done.15.refs_8_
  62.4 0.0 copy-done.4
  62.5 2.8 %key_grads.3 = (f32[256,256]{1,0:T(8,128)S(1)}, f32[256,256]{1,0:T(8,128)S(1)}) custom-call(bf16[256,512]{1,0:T(8,128)(2,1)S(1)} %copy-done.2, bf16[256,512]{1,0:T(8,128)(2,1)S(1)} %copy-done.4, bf16[256,512]{1,0:T(8,128)(2,1)S(1)} %collective-permute-done.4.refs_2_.refs_1_, bf16[256,512]{1,0:T(8,128)(2,1)S(1)} %collective-permute-done.3.refs_1_.refs_3_.refs_2_, ...), custom_call_target="tpu_custom_call" | custom-call | flops 1 | bytes 1 | tf_op jit(solution)/shard_map/key_grads/pallas_call | solution.py:41
  65.2 0.0 collective-permute-done.11.refs_1_.refs_3_
  65.3 0.4 collective-permute-done.12.refs_2_.refs_4_
  65.7 1.3 %collective-permute-start.16 = (bf16[128,640]{1,0:T(8,128)(2,1)S(1)}, bf16[128,640]{1,0:T(8,128)(2,1)S(1)}, u32[]{:S(2)}, u32[]{:S(2)}) collective-permute-start(bf16[128,640]{1,0:T(8,128)(2,1)S(1)} %pair.7), channel_id=1, source_target_pairs={{0,4},{4,0},{8,12},{12,8},{16,20},{20,16},{24,28},{28,24},{1,5},{5... | collective-permute-start | bytes 491528 | tf_op jit(solution)/shard_map/late_swap/ppermute | solution.py:407
  67.0 0.8 %key_grads.4 = (f32[256,256]{1,0:T(8,128)S(1)}, f32[256,256]{1,0:T(8,128)S(1)}) custom-call(bf16[256,512]{1,0:T(8,128)(2,1)S(1)} %copy-done.2, bf16[256,512]{1,0:T(8,128)(2,1)S(1)} %collective-permute-done.4.refs_2_.refs_1_, bf16[256,512]{1,0:T(8,128)(2,1)S(1)} %collective-permute-done.3.refs_1_.refs_3_.refs_2_, ...), custom_call_target="tpu_custom_call" | custom-call | flops 1 | bytes 1 | tf_op jit(solution)/shard_map/key_grads/pallas_call | solution.py:41
  67.8 0.2 collective-permute-done.16.refs_2_
  68.0 1.5 %key_grads.5 = (f32[256,256]{1,0:T(8,128)}, f32[256,256]{1,0:T(8,128)}) custom-call(bf16[256,512]{1,0:T(8,128)(2,1)S(1)} %copy-done.2, bf16[512,512]{1,0:T(8,128)(2,1)S(1)} %collective-permute-done.5.refs_5_.refs_4_.refs_1_, bf16[128,640]{1,0:T(8,128)(2,1)S(1)} %collective-permute-done.16.refs_2_, f32[256,256]{1,0:T(8,128)S(1)} %get-tuple-element.37.refs_3_, ...), custom_call_target="tpu_custom_call" | custom-call | flops 1 | bytes 1 | tf_op jit(solution)/shard_map/key_grads/pallas_call | solution.py:41
  (6 shorter events, 0.1 us)
Async XLA Ops:
  0.6 17.1 %collective-permute-start.8 = (bf16[64,5376]{1,0:T(8,128)(2,1)}, bf16[64,5376]{1,0:T(8,128)(2,1)S(1)}, u32[]{:S(2)}, u32[]{:S(2)}) collective-permute-start(bf16[64,5376]{1,0:T(8,128)(2,1)} %refs_0_.3), channel_id=1, source_target_pairs={{1,2},{2,1},{5,6},{6,5},{9,10},{10,9},{13,14},{14,13},{17,18},{18,... | collective-permute-start | bytes 2064392 | tf_op jit(solution)/shard_map/mid_first/ppermute | solution.py:411
  1.3 18.9 %collective-permute-start.6 = (bf16[64,5376]{1,0:T(8,128)(2,1)}, bf16[64,5376]{1,0:T(8,128)(2,1)S(1)}, u32[]{:S(2)}, u32[]{:S(2)}) collective-permute-start(bf16[64,5376]{1,0:T(8,128)(2,1)} %refs_0_.3), channel_id=1, source_target_pairs={{0,1},{1,0},{2,3},{3,2},{4,5},{5,4},{6,7},{7,6},{8,9},{9,8},{10,11... | collective-permute-start | bytes 2064392 | tf_op jit(solution)/shard_map/end_first/ppermute | solution.py:411
  7.1 8.7 %collective-permute-start = (bf16[256,512]{1,0:T(8,128)(2,1)}, bf16[256,512]{1,0:T(8,128)(2,1)S(1)}, u32[]{:S(2)}, u32[]{:S(2)}) collective-permute-start(bf16[256,512]{1,0:T(8,128)(2,1)} %get-tuple-element.22.refs_0_), channel_id=1, source_target_pairs={{0,8},{4,12},{8,16},{12,20},{16,24},{20,28},{1,9},{5,13},{9,17},{1... | collective-permute-start | bytes 786440 | tf_op jit(solution)/shard_map/kv_near/ppermute | solution.py:407
  10.2 10.7 %collective-permute-start.1 = (bf16[256,512]{1,0:T(8,128)(2,1)}, bf16[256,512]{1,0:T(8,128)(2,1)S(1)}, u32[]{:S(2)}, u32[]{:S(2)}) collective-permute-start(bf16[256,512]{1,0:T(8,128)(2,1)} %get-tuple-element.22.refs_0_), channel_id=1, source_target_pairs={{0,16},{4,20},{8,24},{12,28},{1,17},{5,21},{9,25},{13,29},{2,18},{... | collective-permute-start | bytes 786440 | tf_op jit(solution)/shard_map/kv_far/ppermute | solution.py:407
  11.6 12.0 %collective-permute-start.3 = (bf16[256,512]{1,0:T(8,128)(2,1)}, bf16[256,512]{1,0:T(8,128)(2,1)S(1)}, u32[]{:S(2)}, u32[]{:S(2)}) collective-permute-start(bf16[256,512]{1,0:T(8,128)(2,1)} %get-tuple-element.23.refs_0_.refs_1_), channel_id=1, source_target_pairs={{16,0},{20,4},{24,8},{28,12},{17,1},{21,5},{25,9},{29,13},{18,2},{... | collective-permute-start | bytes 786440 | tf_op jit(solution)/shard_map/q_far/ppermute | solution.py:407
  15.8 8.7 %collective-permute-start.4 = (bf16[256,512]{1,0:T(8,128)(2,1)}, bf16[256,512]{1,0:T(8,128)(2,1)S(1)}, u32[]{:S(2)}, u32[]{:S(2)}) collective-permute-start(bf16[256,512]{1,0:T(8,128)(2,1)} %get-tuple-element.23.refs_0_.refs_1_), channel_id=1, source_target_pairs={{8,0},{12,4},{16,8},{20,12},{24,16},{28,20},{9,1},{13,5},{17,9},{2... | collective-permute-start | bytes 786440 | tf_op jit(solution)/shard_map/q_near/ppermute | solution.py:407
  17.7 17.7 %collective-permute-start.9 = (bf16[64,5376]{1,0:T(8,128)(2,1)S(1)}, bf16[64,5376]{1,0:T(8,128)(2,1)S(1)}, u32[]{:S(2)}, u32[]{:S(2)}) collective-permute-start(bf16[64,5376]{1,0:T(8,128)(2,1)S(1)} %collective-permute-done.8.refs_2_), channel_id=1, source_target_pairs={{1,0},{2,3},{5,4},{6,7},{9,8},{10,11},{13,12},{14,15},{17,16},{18,... | collective-permute-start | bytes 2064392 | tf_op jit(solution)/shard_map/out_second/ppermute | solution.py:411
  20.3 15.2 %collective-permute-start.7 = (bf16[64,5376]{1,0:T(8,128)(2,1)S(1)}, bf16[64,5376]{1,0:T(8,128)(2,1)S(1)}, u32[]{:S(2)}, u32[]{:S(2)}) collective-permute-start(bf16[64,5376]{1,0:T(8,128)(2,1)S(1)} %collective-permute-done.6.refs_1_), channel_id=1, source_target_pairs={{1,2},{2,1},{5,6},{6,5},{9,10},{10,9},{13,14},{14,13},{17,18},{18,... | collective-permute-start | bytes 2064392 | tf_op jit(solution)/shard_map/mid_second/ppermute | solution.py:411
  21.0 1.0 %copy-start.1 = (bf16[256,512]{1,0:T(8,128)(2,1)S(1)}, bf16[256,512]{1,0:T(8,128)(2,1)}, u32[]{:S(2)}) copy-start(bf16[256,512]{1,0:T(8,128)(2,1)} %get-tuple-element.22.refs_0_) | copy-start | bytes 786436
  21.9 8.7 %copy-start.2 = (bf16[256,512]{1,0:T(8,128)(2,1)S(1)}, bf16[256,512]{1,0:T(8,128)(2,1)}, u32[]{:S(2)}) copy-start(bf16[256,512]{1,0:T(8,128)(2,1)} %get-tuple-element.22.refs_0_) | copy-start | bytes 786436
  22.0 7.1 %collective-permute-start.2 = (bf16[512,512]{1,0:T(8,128)(2,1)S(1)}, bf16[512,512]{1,0:T(8,128)(2,1)S(1)}, u32[]{:S(2)}, u32[]{:S(2)}) collective-permute-start(bf16[512,512]{1,0:T(8,128)(2,1)S(1)} %pair.4), channel_id=1, source_target_pairs={{0,4},{4,0},{8,12},{12,8},{16,20},{20,16},{24,28},{28,24},{1,5},{5... | collective-permute-start | bytes 1572872 | tf_op jit(solution)/shard_map/kv_swap/ppermute | solution.py:407
  24.5 1.0 %copy-start.3 = (bf16[256,512]{1,0:T(8,128)(2,1)S(1)}, bf16[256,512]{1,0:T(8,128)(2,1)}, u32[]{:S(2)}) copy-start(bf16[256,512]{1,0:T(8,128)(2,1)} %get-tuple-element.23.refs_0_.refs_1_) | copy-start | bytes 786436
  25.5 5.1 %collective-permute-start.5 = (bf16[512,512]{1,0:T(8,128)(2,1)S(1)}, bf16[512,512]{1,0:T(8,128)(2,1)S(1)}, u32[]{:S(2)}, u32[]{:S(2)}) collective-permute-start(bf16[512,512]{1,0:T(8,128)(2,1)S(1)} %pair.5), channel_id=1, source_target_pairs={{0,4},{4,0},{8,12},{12,8},{16,20},{20,16},{24,28},{28,24},{1,5},{5... | collective-permute-start | bytes 1572872 | tf_op jit(solution)/shard_map/q_swap/ppermute | solution.py:407
  35.5 2.6 %copy-start = (bf16[512,5376]{1,0:T(8,128)(2,1)S(1)}, bf16[512,5376]{1,0:T(8,128)(2,1)}, u32[]{:S(2)}) copy-start(bf16[512,5376]{1,0:T(8,128)(2,1)} %refs_2_.3) | copy-start | bytes 16515076
  35.5 2.7 %copy-start.5 = (bf16[64,5376]{1,0:T(8,128)(2,1)S(1)}, bf16[64,5376]{1,0:T(8,128)(2,1)}, u32[]{:S(2)}) copy-start(bf16[64,5376]{1,0:T(8,128)(2,1)} %refs_0_.3) | copy-start | bytes 2064388
  35.5 20.4 %collective-permute-start.10 = (bf16[64,5376]{1,0:T(8,128)(2,1)S(1)}, bf16[64,5376]{1,0:T(8,128)(2,1)S(1)}, u32[]{:S(2)}, u32[]{:S(2)}) collective-permute-start(bf16[64,5376]{1,0:T(8,128)(2,1)S(1)} %collective-permute-done.7.refs_1_.refs_0_), channel_id=1, source_target_pairs={{1,0},{2,3},{5,4},{6,7},{9,8},{10,11},{13,12},{14,15},{17,16},{18,... | collective-permute-start | bytes 2064392 | tf_op jit(solution)/shard_map/out_third/ppermute | solution.py:411
  40.3 12.7 %collective-permute-start.13 = (bf16[192,640]{1,0:T(8,128)(2,1)S(1)}, bf16[192,640]{1,0:T(8,128)(2,1)S(1)}, u32[]{:S(2)}, u32[]{:S(2)}) collective-permute-start(bf16[192,640]{1,0:T(8,128)(2,1)S(1)} %dout_rows.2.refs_2_.refs_0_.refs_5_), channel_id=1, source_target_pairs={{16,0},{20,4},{24,8},{28,12},{17,1},{21,5},{25,9},{29,13},{18,2},{... | collective-permute-start | bytes 737288 | tf_op jit(solution)/shard_map/early_far/ppermute | solution.py:407
  41.6 11.4 %collective-permute-start.14 = (bf16[192,640]{1,0:T(8,128)(2,1)S(1)}, bf16[192,640]{1,0:T(8,128)(2,1)S(1)}, u32[]{:S(2)}, u32[]{:S(2)}) collective-permute-start(bf16[192,640]{1,0:T(8,128)(2,1)S(1)} %dout_rows.2.refs_2_.refs_0_.refs_5_), channel_id=1, source_target_pairs={{8,0},{12,4},{16,8},{20,12},{24,16},{28,20},{9,1},{13,5},{17,9},{2... | collective-permute-start | bytes 737288 | tf_op jit(solution)/shard_map/early_near/ppermute | solution.py:407
  53.0 9.4 %collective-permute-start.15 = (bf16[384,640]{1,0:T(8,128)(2,1)S(1)}, bf16[384,640]{1,0:T(8,128)(2,1)S(1)}, u32[]{:S(2)}, u32[]{:S(2)}) collective-permute-start(bf16[384,640]{1,0:T(8,128)(2,1)S(1)} %pair.6), channel_id=1, source_target_pairs={{0,4},{4,0},{8,12},{12,8},{16,20},{20,16},{24,28},{28,24},{1,5},{5... | collective-permute-start | bytes 1474568 | tf_op jit(solution)/shard_map/early_swap/ppermute | solution.py:407
  57.8 4.7 %copy-start.4 = (bf16[256,512]{1,0:T(8,128)(2,1)S(1)}, bf16[256,512]{1,0:T(8,128)(2,1)}, u32[]{:S(2)}) copy-start(bf16[256,512]{1,0:T(8,128)(2,1)} %get-tuple-element.23.refs_0_.refs_1_) | copy-start | bytes 786436
  57.8 7.4 %collective-permute-start.11 = (bf16[64,640]{1,0:T(8,128)(2,1)S(1)}, bf16[64,640]{1,0:T(8,128)(2,1)S(1)}, u32[]{:S(2)}, u32[]{:S(2)}) collective-permute-start(bf16[64,640]{1,0:T(8,128)(2,1)S(1)} %dout_rows.3.refs_2_.refs_9_.refs_0_), channel_id=1, source_target_pairs={{16,0},{20,4},{24,8},{28,12},{17,1},{21,5},{25,9},{29,13},{18,2},{... | collective-permute-start | bytes 245768 | tf_op jit(solution)/shard_map/late_far/ppermute | solution.py:407
  59.2 6.5 %collective-permute-start.12 = (bf16[64,640]{1,0:T(8,128)(2,1)S(1)}, bf16[64,640]{1,0:T(8,128)(2,1)S(1)}, u32[]{:S(2)}, u32[]{:S(2)}) collective-permute-start(bf16[64,640]{1,0:T(8,128)(2,1)S(1)} %dout_rows.3.refs_2_.refs_9_.refs_0_), channel_id=1, source_target_pairs={{8,0},{12,4},{16,8},{20,12},{24,16},{28,20},{9,1},{13,5},{17,9},{2... | collective-permute-start | bytes 245768 | tf_op jit(solution)/shard_map/late_near/ppermute | solution.py:407
  65.7 2.3 %collective-permute-start.16 = (bf16[128,640]{1,0:T(8,128)(2,1)S(1)}, bf16[128,640]{1,0:T(8,128)(2,1)S(1)}, u32[]{:S(2)}, u32[]{:S(2)}) collective-permute-start(bf16[128,640]{1,0:T(8,128)(2,1)S(1)} %pair.7), channel_id=1, source_target_pairs={{0,4},{4,0},{8,12},{12,8},{16,20},{20,16},{24,28},{28,24},{1,5},{5... | collective-permute-start | bytes 491528 | tf_op jit(solution)/shard_map/late_swap/ppermute | solution.py:407

commit v7 on v6

--- a/solution.py
+++ b/solution.py
@@ -15,7 +15,7 @@
 NN = (((1,), (0,)), ((), ()))
 F32 = jnp.float32
 BF16 = jnp.bfloat16
-FETCH = pl.CostEstimate(flops=2 * 10**9, bytes_accessed=1, transcendentals=0)
+FETCH = pl.CostEstimate(flops=10**9, bytes_accessed=1, transcendentals=0)
 VMEM = pl.BlockSpec(memory_space=pltpu.VMEM)
 ANY = pl.BlockSpec(memory_space=pl.ANY)
 COST = pl.CostEstimate(flops=1, bytes_accessed=1, transcendentals=0)
@@ -457,14 +457,14 @@
     grad_q, queries_done = query_grads(info, early, (pay_a,), probs, span)
 
     a, b = (0, 1, 2), (3,)
-    pair = pair_for_peer(info, 1, (pay_a,), (near_a,), (far_a,), (queries_done,))
+    grads = key_grads(info, ((0, a, 0, 0, 0, 0),), kv, (query,), (pay_a,), slot_rows)
+    pair = pair_for_peer(info, 1, (pay_a,), (near_a,), (far_a,), (queries_done, grads[0]))
     odd_a = along(pair, swap, "early_swap")
 
     pay_b = dout_rows(info, late, (mid_second, out_third), *statistics, (queries_done,))
     near_b, far_b = sent(pay_b, "late")
     grad_q, queries_done = query_grads(info, late, (pay_b,), probs, span, (grad_q,))
     blocks = (
-        (0, a, 0, 0, 0, 0),
         (2, a, 1, 0, 2, 0),
         (4, a, 2, 0, 1, 0),
         (1, a, 3, 0, 3, 0),
@@ -473,7 +473,7 @@
     )
     q_arrays = (query, near_q, far_q, odd_q)
     d_arrays = (pay_a, far_a, near_a, odd_a, pay_b)
-    grads = key_grads(info, blocks, kv, q_arrays, d_arrays, slot_rows)
+    grads = key_grads(info, blocks, kv, q_arrays, d_arrays, slot_rows, grads)
     after = (queries_done, grads[0])
     pair = pair_for_peer(info, 1, (pay_b,), (near_b,), (far_b,), after)
     odd_b = along(pair, swap, "late_swap")

time: 70.8 us -> 70.8 us (level)
  starting transfers between devices: 32.3 us -> 33.6 us
  local copies, waits for them, and re-layouts: 3.04 us -> 1.92 us
  waiting for transfers between devices: 15.3 us -> 14.2 us
    ppermute x12, starting transfers between devices: 24.2 us -> 25.8 us  [along(): return lax.ppermute(x, 'ctx', pairs)]
    unnamed x12, local copies, waits for them, and re-layouts: 3.04 us -> 1.92 us
    ppermute x12, waiting for transfers between devices: 12.8 us -> 11.7 us  [along(): return lax.ppermute(x, 'ctx', pairs)]
    pallas_call x12 -> x13, Pallas kernels: 16.1 us -> 16.8 us  [call(): pl.pallas_call(lambda *refs: kernel(device_info(info), *refs), out_shape=...]
  transfers between devices with their start and end apart: 17 -> 17, of which waited for: 8 -> 8; matrix products, arithmetic and copies ran while one was open for 0% -> 0% of each run, Pallas kernels for 24% -> 25%
where the time goes in v7:
time: 70.8 us; the launch traced here: 69.5 us
  starting transfers between devices  33.6 us (47%)
  Pallas kernels  18.7 us (26%)
  waiting for transfers between devices  14.2 us (20%)
  local copies, waits for them, and re-layouts  1.92 us (3%)
  between operations  1.07 us (2%)
    ppermute x12, starting transfers between devices, along(): return lax.ppermute(x, 'ctx', pairs)  25.8 us
    pallas_call x13, Pallas kernels, call(): pl.pallas_call(lambda *refs: kernel(device_info(info), *refs), out_shape=...  16.8 us
    ppermute x12, waiting for transfers between devices, along(): return lax.ppermute(x, 'ctx', pairs)  11.7 us
    ppermute x5, starting transfers between devices, over(): return lax.ppermute(x, 'tp', pairs)  7.84 us
    ppermute x5, waiting for transfers between devices, over(): return lax.ppermute(x, 'tp', pairs)  2.47 us
    unnamed x12, local copies, waits for them, and re-layouts  1.92 us
    pallas_call x1, Pallas kernels, pack(): pl.pallas_call(functools.partial(pack_kernel, places), out_shape=tuple((j...  1.9 us
  transfers between devices with their start and end apart: 17, of which 8 were waited for; matrix products, arithmetic and copies ran while one was open for 0% of the time, Pallas kernels for 25%

profile of v7, /device:TPU:3, one launch (start us, length us, event | category | flops | bytes accessed | tf_op | source)
XLA Modules:
  0.0 69.5 jit_solution(13968840935132466025)
XLA Ops:
  0.6 0.7 %collective-permute-start.8 = (bf16[64,5376]{1,0:T(8,128)(2,1)}, bf16[64,5376]{1,0:T(8,128)(2,1)S(1)}, u32[]{:S(2)}, u32[]{:S(2)}) collective-permute-start(bf16[64,5376]{1,0:T(8,128)(2,1)} %refs_0_.3), channel_id=1, source_target_pairs={{1,2},{2,1},{5,6},{6,5},{9,10},{10,9},{13,14},{14,13},{17,18},{18,... | collective-permute-start | bytes 2064392 | tf_op jit(solution)/shard_map/mid_first/ppermute | solution.py:411
  1.3 3.9 %collective-permute-start.6 = (bf16[64,5376]{1,0:T(8,128)(2,1)}, bf16[64,5376]{1,0:T(8,128)(2,1)S(1)}, u32[]{:S(2)}, u32[]{:S(2)}) collective-permute-start(bf16[64,5376]{1,0:T(8,128)(2,1)} %refs_0_.3), channel_id=1, source_target_pairs={{0,1},{1,0},{2,3},{3,2},{4,5},{5,4},{6,7},{7,6},{8,9},{9,8},{10,11... | collective-permute-start | bytes 2064392 | tf_op jit(solution)/shard_map/end_first/ppermute | solution.py:411
  5.2 1.9 %pack.1 = (bf16[256,512]{1,0:T(8,128)(2,1)}, bf16[256,512]{1,0:T(8,128)(2,1)}) custom-call(bf16[256,256]{1,0:T(8,128)(2,1)} %refs_0_.2, bf16[256,256]{1,0:T(8,128)(2,1)} %refs_1_.1, bf16[256,512]{1,0:T(8,128)(2,1)} %refs_2_.2), custom_call_target="tpu_custom_call" | custom-call | flops 1 | bytes 1 | tf_op jit(solution)/shard_map/pack/pallas_call | solution.py:87
  7.1 3.1 %collective-permute-start = (bf16[256,512]{1,0:T(8,128)(2,1)}, bf16[256,512]{1,0:T(8,128)(2,1)S(1)}, u32[]{:S(2)}, u32[]{:S(2)}) collective-permute-start(bf16[256,512]{1,0:T(8,128)(2,1)} %get-tuple-element.24.refs_0_), channel_id=1, source_target_pairs={{0,8},{4,12},{8,16},{12,20},{16,24},{20,28},{1,9},{5,13},{9,17},{1... | collective-permute-start | bytes 786440 | tf_op jit(solution)/shard_map/kv_near/ppermute | solution.py:407
  10.2 1.3 %collective-permute-start.1 = (bf16[256,512]{1,0:T(8,128)(2,1)}, bf16[256,512]{1,0:T(8,128)(2,1)S(1)}, u32[]{:S(2)}, u32[]{:S(2)}) collective-permute-start(bf16[256,512]{1,0:T(8,128)(2,1)} %get-tuple-element.24.refs_0_), channel_id=1, source_target_pairs={{0,16},{4,20},{8,24},{12,28},{1,17},{5,21},{9,25},{13,29},{2,18},{... | collective-permute-start | bytes 786440 | tf_op jit(solution)/shard_map/kv_far/ppermute | solution.py:407
  11.6 1.3 %collective-permute-start.3 = (bf16[256,512]{1,0:T(8,128)(2,1)}, bf16[256,512]{1,0:T(8,128)(2,1)S(1)}, u32[]{:S(2)}, u32[]{:S(2)}) collective-permute-start(bf16[256,512]{1,0:T(8,128)(2,1)} %get-tuple-element.25.refs_0_.refs_1_), channel_id=1, source_target_pairs={{16,0},{20,4},{24,8},{28,12},{17,1},{21,5},{25,9},{29,13},{18,2},{... | collective-permute-start | bytes 786440 | tf_op jit(solution)/shard_map/q_far/ppermute | solution.py:407
  12.9 2.9 %collective-permute-done.refs_2_ = bf16[256,512]{1,0:T(8,128)(2,1)S(1)} collective-permute-done((bf16[256,512]{1,0:T(8,128)(2,1)}, bf16[256,512]{1,0:T(8,128)(2,1)S(1)}, u32[]{:S(2)}, u32[]{:S(2)}) %collective-permute-start) | collective-permute-done | bytes 262176 | tf_op jit(solution)/shard_map/kv_near/ppermute | solution.py:407
  15.8 1.9 %collective-permute-start.4 = (bf16[256,512]{1,0:T(8,128)(2,1)}, bf16[256,512]{1,0:T(8,128)(2,1)S(1)}, u32[]{:S(2)}, u32[]{:S(2)}) collective-permute-start(bf16[256,512]{1,0:T(8,128)(2,1)} %get-tuple-element.25.refs_0_.refs_1_), channel_id=1, source_target_pairs={{8,0},{12,4},{16,8},{20,12},{24,16},{28,20},{9,1},{13,5},{17,9},{2... | collective-permute-start | bytes 786440 | tf_op jit(solution)/shard_map/q_near/ppermute | solution.py:407
  17.7 0.0 collective-permute-done.8.refs_2_
  17.7 1.3 %collective-permute-start.9 = (bf16[64,5376]{1,0:T(8,128)(2,1)S(1)}, bf16[64,5376]{1,0:T(8,128)(2,1)S(1)}, u32[]{:S(2)}, u32[]{:S(2)}) collective-permute-start(bf16[64,5376]{1,0:T(8,128)(2,1)S(1)} %collective-permute-done.8.refs_2_), channel_id=1, source_target_pairs={{1,0},{2,3},{5,4},{6,7},{9,8},{10,11},{13,12},{14,15},{17,16},{18,... | collective-permute-start | bytes 2064392 | tf_op jit(solution)/shard_map/out_second/ppermute | solution.py:411
  19.0 1.3 %collective-permute-done.6.refs_1_ = bf16[64,5376]{1,0:T(8,128)(2,1)S(1)} collective-permute-done((bf16[64,5376]{1,0:T(8,128)(2,1)}, bf16[64,5376]{1,0:T(8,128)(2,1)S(1)}, u32[]{:S(2)}, u32[]{:S(2)}) %collective-permute-start.6) | collective-permute-done | bytes 688160 | tf_op jit(solution)/shard_map/end_first/ppermute | solution.py:411
  20.3 0.7 collective-permute-start.7
  21.0 0.0 collective-permute-done.1.refs_1_.refs_3_
  21.0 0.0 copy-start.1
  21.0 0.9 %copy-done.1 = bf16[256,512]{1,0:T(8,128)(2,1)S(1)} copy-done((bf16[256,512]{1,0:T(8,128)(2,1)S(1)}, bf16[256,512]{1,0:T(8,128)(2,1)}, u32[]{:S(2)}) %copy-start.1) | copy-done | bytes 262168
  21.9 0.0 copy-start.2
  22.0 1.6 %collective-permute-start.2 = (bf16[512,512]{1,0:T(8,128)(2,1)S(1)}, bf16[512,512]{1,0:T(8,128)(2,1)S(1)}, u32[]{:S(2)}, u32[]{:S(2)}) collective-permute-start(bf16[512,512]{1,0:T(8,128)(2,1)S(1)} %pair.4), channel_id=1, source_target_pairs={{0,4},{4,0},{8,12},{12,8},{16,20},{20,16},{24,28},{28,24},{1,5},{5... | collective-permute-start | bytes 1572872 | tf_op jit(solution)/shard_map/kv_swap/ppermute | solution.py:407
  23.6 0.0 collective-permute-done.3.refs_1_.refs_3_.refs_2_
  23.6 0.9 %collective-permute-done.4.refs_2_.refs_1_ = bf16[256,512]{1,0:T(8,128)(2,1)S(1)} collective-permute-done((bf16[256,512]{1,0:T(8,128)(2,1)}, bf16[256,512]{1,0:T(8,128)(2,1)S(1)}, u32[]{:S(2)}, u32[]{:S(2)}) %collective-permute-start.4) | collective-permute-done | bytes 262176 | tf_op jit(solution)/shard_map/q_near/ppermute | solution.py:407
  24.5 0.0 copy-start.3
  24.5 0.9 %copy-done.3 = bf16[256,512]{1,0:T(8,128)(2,1)S(1)} copy-done((bf16[256,512]{1,0:T(8,128)(2,1)S(1)}, bf16[256,512]{1,0:T(8,128)(2,1)}, u32[]{:S(2)}) %copy-start.3) | copy-done | bytes 262168
  25.5 3.6 %collective-permute-start.5 = (bf16[512,512]{1,0:T(8,128)(2,1)S(1)}, bf16[512,512]{1,0:T(8,128)(2,1)S(1)}, u32[]{:S(2)}, u32[]{:S(2)}) collective-permute-start(bf16[512,512]{1,0:T(8,128)(2,1)S(1)} %pair.5), channel_id=1, source_target_pairs={{0,4},{4,0},{8,12},{12,8},{16,20},{20,16},{24,28},{28,24},{1,5},{5... | collective-permute-start | bytes 1572872 | tf_op jit(solution)/shard_map/q_swap/ppermute | solution.py:407
  29.1 0.0 collective-permute-done.2.refs_4_
  29.1 1.5 %collective-permute-done.5.refs_5_.refs_4_.refs_1_ = bf16[512,512]{1,0:T(8,128)(2,1)S(1)} collective-permute-done((bf16[512,512]{1,0:T(8,128)(2,1)S(1)}, bf16[512,512]{1,0:T(8,128)(2,1)S(1)}, u32[]{:S(2)}, u32[]{:S(2)}) %collective-permute-start.5) | collective-permute-done | bytes 524320 | tf_op jit(solution)/shard_map/q_swap/ppermute | solution.py:407
  30.6 0.0 copy-done.2
  30.6 0.0 copy-start
  30.6 3.6 %attention_probs.1 = (bf16[4,256,1280]{2,1,0:T(8,128)(2,1)S(1)}, f32[256,512]{1,0:T(8,128)S(1)}, bf16[256,128]{1,0:T(8,128)(2,1)S(1)}, bf16[1280,512]{1,0:T(8,128)(2,1)S(1)}) custom-call(bf16[256,512]{1,0:T(8,128)(2,1)S(1)} %copy-done.2, bf16[256,512]{1,0:T(8,128)(2,1)S(1)} %copy-done.3, bf16[256,512]{1,0:T(8,128)(2,1)S(1)} %collective-permute-done.refs_2_, ...), custom_call_target="tpu_custom_call" | custom-call | flops 1 | bytes 1 | tf_op jit(solution)/shard_map/attention_probs/pallas_call | solution.py:41
  34.2 0.0 copy-start.5
  34.2 1.2 %collective-permute-done.9.refs_0_.refs_3_ = bf16[64,5376]{1,0:T(8,128)(2,1)S(1)} collective-permute-done((bf16[64,5376]{1,0:T(8,128)(2,1)S(1)}, bf16[64,5376]{1,0:T(8,128)(2,1)S(1)}, u32[]{:S(2)}, u32[]{:S(2)}) %collective-permute-start.9) | collective-permute-done | bytes 688160 | tf_op jit(solution)/shard_map/out_second/ppermute | solution.py:411
  35.5 0.0 collective-permute-done.7.refs_1_.refs_0_
  35.5 1.3 %collective-permute-start.10 = (bf16[64,5376]{1,0:T(8,128)(2,1)S(1)}, bf16[64,5376]{1,0:T(8,128)(2,1)S(1)}, u32[]{:S(2)}, u32[]{:S(2)}) collective-permute-start(bf16[64,5376]{1,0:T(8,128)(2,1)S(1)} %collective-permute-done.7.refs_1_.refs_0_), channel_id=1, source_target_pairs={{1,0},{2,3},{5,4},{6,7},{9,8},{10,11},{13,12},{14,15},{17,16},{18,... | collective-permute-start | bytes 2064392 | tf_op jit(solution)/shard_map/out_third/ppermute | solution.py:411
  36.8 0.0 copy-done
  36.8 0.0 copy-done.5
  36.8 0.0 copy-start.4
  36.8 2.1 %dout_rows.2.refs_2_.refs_0_.refs_5_ = bf16[192,640]{1,0:T(8,128)(2,1)S(1)} custom-call(bf16[64,5376]{1,0:T(8,128)(2,1)S(1)} %copy-done.5, bf16[64,5376]{1,0:T(8,128)(2,1)S(1)} %collective-permute-done.6.refs_1_, bf16[64,5376]{1,0:T(8,128)(2,1)S(1)} %collective-permute-done.8.refs_2_, bf16[64,5376]{1,0:T(8,128)(2,1)S(1)} %collective-permute-done.9.refs_0_.refs_3_, ...), custom_call_target="tpu_custom_call" | custom-call | flops 1 | bytes 1 | tf_op jit(solution)/shard_map/dout_rows/pallas_call | solution.py:41
  38.9 1.3 %collective-permute-start.13 = (bf16[192,640]{1,0:T(8,128)(2,1)S(1)}, bf16[192,640]{1,0:T(8,128)(2,1)S(1)}, u32[]{:S(2)}, u32[]{:S(2)}) collective-permute-start(bf16[192,640]{1,0:T(8,128)(2,1)S(1)} %dout_rows.2.refs_2_.refs_0_.refs_5_), channel_id=1, source_target_pairs={{16,0},{20,4},{24,8},{28,12},{17,1},{21,5},{25,9},{29,13},{18,2},{... | collective-permute-start | bytes 737288 | tf_op jit(solution)/shard_map/early_far/ppermute | solution.py:407
  40.2 2.5 %collective-permute-start.14 = (bf16[192,640]{1,0:T(8,128)(2,1)S(1)}, bf16[192,640]{1,0:T(8,128)(2,1)S(1)}, u32[]{:S(2)}, u32[]{:S(2)}) collective-permute-start(bf16[192,640]{1,0:T(8,128)(2,1)S(1)} %dout_rows.2.refs_2_.refs_0_.refs_5_), channel_id=1, source_target_pairs={{8,0},{12,4},{16,8},{20,12},{24,16},{28,20},{9,1},{13,5},{17,9},{2... | collective-permute-start | bytes 737288 | tf_op jit(solution)/shard_map/early_near/ppermute | solution.py:407
  42.7 0.0 copy-done.4
  42.7 0.9 %key_grads.4 = (f32[256,256]{1,0:T(8,128)S(1)}, f32[256,256]{1,0:T(8,128)S(1)}) custom-call(bf16[256,512]{1,0:T(8,128)(2,1)S(1)} %copy-done.2, bf16[256,512]{1,0:T(8,128)(2,1)S(1)} %copy-done.4, bf16[192,640]{1,0:T(8,128)(2,1)S(1)} %dout_rows.2.refs_2_.refs_0_.refs_5_), custom_call_target="tpu_custom_call" | custom-call | flops 1 | bytes 1 | tf_op jit(solution)/shard_map/key_grads/pallas_call | solution.py:41
  43.6 2.1 %query_grads.2 = (f32[256,512]{1,0:T(8,128)}, f32[8,128]{1,0:T(8,128)S(1)}) custom-call(bf16[4,256,1280]{2,1,0:T(8,128)(2,1)S(1)} %get-tuple-element.26.refs_0_, bf16[1280,512]{1,0:T(8,128)(2,1)S(1)} %get-tuple-element.27.refs_1_, bf16[192,640]{1,0:T(8,128)(2,1)S(1)} %dout_rows.2.refs_2_.refs_0_.refs_5_), custom_call_target="tpu_custom_call" | custom-call | flops 1 | bytes 1 | tf_op jit(solution)/shard_map/query_grads/pallas_call | solution.py:41
  45.7 5.9 %collective-permute-done.13.refs_1_.refs_6_ = bf16[192,640]{1,0:T(8,128)(2,1)S(1)} collective-permute-done((bf16[192,640]{1,0:T(8,128)(2,1)S(1)}, bf16[192,640]{1,0:T(8,128)(2,1)S(1)}, u32[]{:S(2)}, u32[]{:S(2)}) %collective-permute-start.13) | collective-permute-done | bytes 245792 | tf_op jit(solution)/shard_map/early_far/ppermute | solution.py:407
  51.6 0.0 collective-permute-done.14.refs_2_.refs_7_
  51.6 2.9 %collective-permute-start.15 = (bf16[384,640]{1,0:T(8,128)(2,1)S(1)}, bf16[384,640]{1,0:T(8,128)(2,1)S(1)}, u32[]{:S(2)}, u32[]{:S(2)}) collective-permute-start(bf16[384,640]{1,0:T(8,128)(2,1)S(1)} %pair.6), channel_id=1, source_target_pairs={{0,4},{4,0},{8,12},{12,8},{16,20},{20,16},{24,28},{28,24},{1,5},{5... | collective-permute-start | bytes 1474568 | tf_op jit(solution)/shard_map/early_swap/ppermute | solution.py:407
  54.5 0.0 collective-permute-done.10.refs_1_
  54.5 1.9 %dout_rows.3.refs_2_.refs_9_.refs_0_ = bf16[64,640]{1,0:T(8,128)(2,1)S(1)} custom-call(bf16[64,5376]{1,0:T(8,128)(2,1)S(1)} %collective-permute-done.7.refs_1_.refs_0_, bf16[64,5376]{1,0:T(8,128)(2,1)S(1)} %collective-permute-done.10.refs_1_, bf16[512,5376]{1,0:T(8,128)(2,1)S(1)} %copy-done, f32[256,512]{1,0:T(8,128)S(1)} %get-tuple-element.30.refs_5_.refs_3_, ...), custom_call_target="tpu_custom_call" | custom-call | flops 1 | bytes 1 | tf_op jit(solution)/shard_map/dout_rows/pallas_call | solution.py:41
  56.4 1.3 %collective-permute-start.11 = (bf16[64,640]{1,0:T(8,128)(2,1)S(1)}, bf16[64,640]{1,0:T(8,128)(2,1)S(1)}, u32[]{:S(2)}, u32[]{:S(2)}) collective-permute-start(bf16[64,640]{1,0:T(8,128)(2,1)S(1)} %dout_rows.3.refs_2_.refs_9_.refs_0_), channel_id=1, source_target_pairs={{16,0},{20,4},{24,8},{28,12},{17,1},{21,5},{25,9},{29,13},{18,2},{... | collective-permute-start | bytes 245768 | tf_op jit(solution)/shard_map/late_far/ppermute | solution.py:407
  57.7 2.1 %collective-permute-start.12 = (bf16[64,640]{1,0:T(8,128)(2,1)S(1)}, bf16[64,640]{1,0:T(8,128)(2,1)S(1)}, u32[]{:S(2)}, u32[]{:S(2)}) collective-permute-start(bf16[64,640]{1,0:T(8,128)(2,1)S(1)} %dout_rows.3.refs_2_.refs_9_.refs_0_), channel_id=1, source_target_pairs={{8,0},{12,4},{16,8},{20,12},{24,16},{28,20},{9,1},{13,5},{17,9},{2... | collective-permute-start | bytes 245768 | tf_op jit(solution)/shard_map/late_near/ppermute | solution.py:407
  59.8 1.3 %query_grads.3 = (f32[256,512]{1,0:T(8,128)}, f32[8,128]{1,0:T(8,128)S(1)}) custom-call(bf16[4,256,1280]{2,1,0:T(8,128)(2,1)S(1)} %get-tuple-element.26.refs_0_, bf16[1280,512]{1,0:T(8,128)(2,1)S(1)} %get-tuple-element.27.refs_1_, bf16[64,640]{1,0:T(8,128)(2,1)S(1)} %dout_rows.3.refs_2_.refs_9_.refs_0_, ...), custom_call_target="tpu_custom_call", output_to_operand_aliasing={{0}: (3, {})} | custom-call | flops 1 | bytes 1 | tf_op jit(solution)/shard_map/query_grads/pallas_call | solution.py:41
  61.1 0.0 collective-permute-done.15.refs_8_
  61.1 2.5 %key_grads.5 = (f32[256,256]{1,0:T(8,128)S(1)}, f32[256,256]{1,0:T(8,128)S(1)}) custom-call(bf16[256,512]{1,0:T(8,128)(2,1)S(1)} %copy-done.2, bf16[256,512]{1,0:T(8,128)(2,1)S(1)} %copy-done.4, bf16[256,512]{1,0:T(8,128)(2,1)S(1)} %collective-permute-done.4.refs_2_.refs_1_, bf16[256,512]{1,0:T(8,128)(2,1)S(1)} %collective-permute-done.3.refs_1_.refs_3_.refs_2_, ...), custom_call_target="tpu_custom_call" | custom-call | flops 1 | bytes 1 | tf_op jit(solution)/shard_map/key_grads/pallas_call | solution.py:41
  63.6 0.0 collective-permute-done.11.refs_1_.refs_3_
  63.6 0.3 collective-permute-done.12.refs_2_.refs_4_
  63.9 2.9 %collective-permute-start.16 = (bf16[128,640]{1,0:T(8,128)(2,1)S(1)}, bf16[128,640]{1,0:T(8,128)(2,1)S(1)}, u32[]{:S(2)}, u32[]{:S(2)}) collective-permute-start(bf16[128,640]{1,0:T(8,128)(2,1)S(1)} %pair.7), channel_id=1, source_target_pairs={{0,4},{4,0},{8,12},{12,8},{16,20},{20,16},{24,28},{28,24},{1,5},{5... | collective-permute-start | bytes 491528 | tf_op jit(solution)/shard_map/late_swap/ppermute | solution.py:407
  66.8 0.8 %key_grads.6 = (f32[256,256]{1,0:T(8,128)S(1)}, f32[256,256]{1,0:T(8,128)S(1)}) custom-call(bf16[256,512]{1,0:T(8,128)(2,1)S(1)} %copy-done.2, bf16[256,512]{1,0:T(8,128)(2,1)S(1)} %collective-permute-done.4.refs_2_.refs_1_, bf16[256,512]{1,0:T(8,128)(2,1)S(1)} %collective-permute-done.3.refs_1_.refs_3_.refs_2_, ...), custom_call_target="tpu_custom_call" | custom-call | flops 1 | bytes 1 | tf_op jit(solution)/shard_map/key_grads/pallas_call | solution.py:41
  67.6 0.2 collective-permute-done.16.refs_2_
  67.8 1.5 %key_grads.7 = (f32[256,256]{1,0:T(8,128)}, f32[256,256]{1,0:T(8,128)}) custom-call(bf16[256,512]{1,0:T(8,128)(2,1)S(1)} %copy-done.2, bf16[512,512]{1,0:T(8,128)(2,1)S(1)} %collective-permute-done.5.refs_5_.refs_4_.refs_1_, bf16[128,640]{1,0:T(8,128)(2,1)S(1)} %collective-permute-done.16.refs_2_, f32[256,256]{1,0:T(8,128)S(1)} %get-tuple-element.41.refs_3_, ...), custom_call_target="tpu_custom_call" | custom-call | flops 1 | bytes 1 | tf_op jit(solution)/shard_map/key_grads/pallas_call | solution.py:41
  (6 shorter events, 0.1 us)
Async XLA Ops:
  0.6 17.1 %collective-permute-start.8 = (bf16[64,5376]{1,0:T(8,128)(2,1)}, bf16[64,5376]{1,0:T(8,128)(2,1)S(1)}, u32[]{:S(2)}, u32[]{:S(2)}) collective-permute-start(bf16[64,5376]{1,0:T(8,128)(2,1)} %refs_0_.3), channel_id=1, source_target_pairs={{1,2},{2,1},{5,6},{6,5},{9,10},{10,9},{13,14},{14,13},{17,18},{18,... | collective-permute-start | bytes 2064392 | tf_op jit(solution)/shard_map/mid_first/ppermute | solution.py:411
  1.3 18.9 %collective-permute-start.6 = (bf16[64,5376]{1,0:T(8,128)(2,1)}, bf16[64,5376]{1,0:T(8,128)(2,1)S(1)}, u32[]{:S(2)}, u32[]{:S(2)}) collective-permute-start(bf16[64,5376]{1,0:T(8,128)(2,1)} %refs_0_.3), channel_id=1, source_target_pairs={{0,1},{1,0},{2,3},{3,2},{4,5},{5,4},{6,7},{7,6},{8,9},{9,8},{10,11... | collective-permute-start | bytes 2064392 | tf_op jit(solution)/shard_map/end_first/ppermute | solution.py:411
  7.1 8.7 %collective-permute-start = (bf16[256,512]{1,0:T(8,128)(2,1)}, bf16[256,512]{1,0:T(8,128)(2,1)S(1)}, u32[]{:S(2)}, u32[]{:S(2)}) collective-permute-start(bf16[256,512]{1,0:T(8,128)(2,1)} %get-tuple-element.24.refs_0_), channel_id=1, source_target_pairs={{0,8},{4,12},{8,16},{12,20},{16,24},{20,28},{1,9},{5,13},{9,17},{1... | collective-permute-start | bytes 786440 | tf_op jit(solution)/shard_map/kv_near/ppermute | solution.py:407
  10.2 10.7 %collective-permute-start.1 = (bf16[256,512]{1,0:T(8,128)(2,1)}, bf16[256,512]{1,0:T(8,128)(2,1)S(1)}, u32[]{:S(2)}, u32[]{:S(2)}) collective-permute-start(bf16[256,512]{1,0:T(8,128)(2,1)} %get-tuple-element.24.refs_0_), channel_id=1, source_target_pairs={{0,16},{4,20},{8,24},{12,28},{1,17},{5,21},{9,25},{13,29},{2,18},{... | collective-permute-start | bytes 786440 | tf_op jit(solution)/shard_map/kv_far/ppermute | solution.py:407
  11.6 12.0 %collective-permute-start.3 = (bf16[256,512]{1,0:T(8,128)(2,1)}, bf16[256,512]{1,0:T(8,128)(2,1)S(1)}, u32[]{:S(2)}, u32[]{:S(2)}) collective-permute-start(bf16[256,512]{1,0:T(8,128)(2,1)} %get-tuple-element.25.refs_0_.refs_1_), channel_id=1, source_target_pairs={{16,0},{20,4},{24,8},{28,12},{17,1},{21,5},{25,9},{29,13},{18,2},{... | collective-permute-start | bytes 786440 | tf_op jit(solution)/shard_map/q_far/ppermute | solution.py:407
  15.8 8.7 %collective-permute-start.4 = (bf16[256,512]{1,0:T(8,128)(2,1)}, bf16[256,512]{1,0:T(8,128)(2,1)S(1)}, u32[]{:S(2)}, u32[]{:S(2)}) collective-permute-start(bf16[256,512]{1,0:T(8,128)(2,1)} %get-tuple-element.25.refs_0_.refs_1_), channel_id=1, source_target_pairs={{8,0},{12,4},{16,8},{20,12},{24,16},{28,20},{9,1},{13,5},{17,9},{2... | collective-permute-start | bytes 786440 | tf_op jit(solution)/shard_map/q_near/ppermute | solution.py:407
  17.7 17.7 %collective-permute-start.9 = (bf16[64,5376]{1,0:T(8,128)(2,1)S(1)}, bf16[64,5376]{1,0:T(8,128)(2,1)S(1)}, u32[]{:S(2)}, u32[]{:S(2)}) collective-permute-start(bf16[64,5376]{1,0:T(8,128)(2,1)S(1)} %collective-permute-done.8.refs_2_), channel_id=1, source_target_pairs={{1,0},{2,3},{5,4},{6,7},{9,8},{10,11},{13,12},{14,15},{17,16},{18,... | collective-permute-start | bytes 2064392 | tf_op jit(solution)/shard_map/out_second/ppermute | solution.py:411
  20.3 15.2 %collective-permute-start.7 = (bf16[64,5376]{1,0:T(8,128)(2,1)S(1)}, bf16[64,5376]{1,0:T(8,128)(2,1)S(1)}, u32[]{:S(2)}, u32[]{:S(2)}) collective-permute-start(bf16[64,5376]{1,0:T(8,128)(2,1)S(1)} %collective-permute-done.6.refs_1_), channel_id=1, source_target_pairs={{1,2},{2,1},{5,6},{6,5},{9,10},{10,9},{13,14},{14,13},{17,18},{18,... | collective-permute-start | bytes 2064392 | tf_op jit(solution)/shard_map/mid_second/ppermute | solution.py:411
  21.0 1.0 %copy-start.1 = (bf16[256,512]{1,0:T(8,128)(2,1)S(1)}, bf16[256,512]{1,0:T(8,128)(2,1)}, u32[]{:S(2)}) copy-start(bf16[256,512]{1,0:T(8,128)(2,1)} %get-tuple-element.24.refs_0_) | copy-start | bytes 786436
  21.9 8.7 %copy-start.2 = (bf16[256,512]{1,0:T(8,128)(2,1)S(1)}, bf16[256,512]{1,0:T(8,128)(2,1)}, u32[]{:S(2)}) copy-start(bf16[256,512]{1,0:T(8,128)(2,1)} %get-tuple-element.24.refs_0_) | copy-start | bytes 786436
  22.0 7.1 %collective-permute-start.2 = (bf16[512,512]{1,0:T(8,128)(2,1)S(1)}, bf16[512,512]{1,0:T(8,128)(2,1)S(1)}, u32[]{:S(2)}, u32[]{:S(2)}) collective-permute-start(bf16[512,512]{1,0:T(8,128)(2,1)S(1)} %pair.4), channel_id=1, source_target_pairs={{0,4},{4,0},{8,12},{12,8},{16,20},{20,16},{24,28},{28,24},{1,5},{5... | collective-permute-start | bytes 1572872 | tf_op jit(solution)/shard_map/kv_swap/ppermute | solution.py:407
  24.5 1.0 %copy-start.3 = (bf16[256,512]{1,0:T(8,128)(2,1)S(1)}, bf16[256,512]{1,0:T(8,128)(2,1)}, u32[]{:S(2)}) copy-start(bf16[256,512]{1,0:T(8,128)(2,1)} %get-tuple-element.25.refs_0_.refs_1_) | copy-start | bytes 786436
  25.5 5.1 %collective-permute-start.5 = (bf16[512,512]{1,0:T(8,128)(2,1)S(1)}, bf16[512,512]{1,0:T(8,128)(2,1)S(1)}, u32[]{:S(2)}, u32[]{:S(2)}) collective-permute-start(bf16[512,512]{1,0:T(8,128)(2,1)S(1)} %pair.5), channel_id=1, source_target_pairs={{0,4},{4,0},{8,12},{12,8},{16,20},{20,16},{24,28},{28,24},{1,5},{5... | collective-permute-start | bytes 1572872 | tf_op jit(solution)/shard_map/q_swap/ppermute | solution.py:407
  30.6 6.1 %copy-start = (bf16[512,5376]{1,0:T(8,128)(2,1)S(1)}, bf16[512,5376]{1,0:T(8,128)(2,1)}, u32[]{:S(2)}) copy-start(bf16[512,5376]{1,0:T(8,128)(2,1)} %refs_2_.3) | copy-start | bytes 16515076
  34.2 2.5 %copy-start.5 = (bf16[64,5376]{1,0:T(8,128)(2,1)S(1)}, bf16[64,5376]{1,0:T(8,128)(2,1)}, u32[]{:S(2)}) copy-start(bf16[64,5376]{1,0:T(8,128)(2,1)} %refs_0_.3) | copy-start | bytes 2064388
  35.5 19.1 %collective-permute-start.10 = (bf16[64,5376]{1,0:T(8,128)(2,1)S(1)}, bf16[64,5376]{1,0:T(8,128)(2,1)S(1)}, u32[]{:S(2)}, u32[]{:S(2)}) collective-permute-start(bf16[64,5376]{1,0:T(8,128)(2,1)S(1)} %collective-permute-done.7.refs_1_.refs_0_), channel_id=1, source_target_pairs={{1,0},{2,3},{5,4},{6,7},{9,8},{10,11},{13,12},{14,15},{17,16},{18,... | collective-permute-start | bytes 2064392 | tf_op jit(solution)/shard_map/out_third/ppermute | solution.py:411
  36.8 5.9 %copy-start.4 = (bf16[256,512]{1,0:T(8,128)(2,1)S(1)}, bf16[256,512]{1,0:T(8,128)(2,1)}, u32[]{:S(2)}) copy-start(bf16[256,512]{1,0:T(8,128)(2,1)} %get-tuple-element.25.refs_0_.refs_1_) | copy-start | bytes 786436
  38.9 12.7 %collective-permute-start.13 = (bf16[192,640]{1,0:T(8,128)(2,1)S(1)}, bf16[192,640]{1,0:T(8,128)(2,1)S(1)}, u32[]{:S(2)}, u32[]{:S(2)}) collective-permute-start(bf16[192,640]{1,0:T(8,128)(2,1)S(1)} %dout_rows.2.refs_2_.refs_0_.refs_5_), channel_id=1, source_target_pairs={{16,0},{20,4},{24,8},{28,12},{17,1},{21,5},{25,9},{29,13},{18,2},{... | collective-permute-start | bytes 737288 | tf_op jit(solution)/shard_map/early_far/ppermute | solution.py:407
  40.2 11.4 %collective-permute-start.14 = (bf16[192,640]{1,0:T(8,128)(2,1)S(1)}, bf16[192,640]{1,0:T(8,128)(2,1)S(1)}, u32[]{:S(2)}, u32[]{:S(2)}) collective-permute-start(bf16[192,640]{1,0:T(8,128)(2,1)S(1)} %dout_rows.2.refs_2_.refs_0_.refs_5_), channel_id=1, source_target_pairs={{8,0},{12,4},{16,8},{20,12},{24,16},{28,20},{9,1},{13,5},{17,9},{2... | collective-permute-start | bytes 737288 | tf_op jit(solution)/shard_map/early_near/ppermute | solution.py:407
  51.6 9.5 %collective-permute-start.15 = (bf16[384,640]{1,0:T(8,128)(2,1)S(1)}, bf16[384,640]{1,0:T(8,128)(2,1)S(1)}, u32[]{:S(2)}, u32[]{:S(2)}) collective-permute-start(bf16[384,640]{1,0:T(8,128)(2,1)S(1)} %pair.6), channel_id=1, source_target_pairs={{0,4},{4,0},{8,12},{12,8},{16,20},{20,16},{24,28},{28,24},{1,5},{5... | collective-permute-start | bytes 1474568 | tf_op jit(solution)/shard_map/early_swap/ppermute | solution.py:407
  56.4 7.2 %collective-permute-start.11 = (bf16[64,640]{1,0:T(8,128)(2,1)S(1)}, bf16[64,640]{1,0:T(8,128)(2,1)S(1)}, u32[]{:S(2)}, u32[]{:S(2)}) collective-permute-start(bf16[64,640]{1,0:T(8,128)(2,1)S(1)} %dout_rows.3.refs_2_.refs_9_.refs_0_), channel_id=1, source_target_pairs={{16,0},{20,4},{24,8},{28,12},{17,1},{21,5},{25,9},{29,13},{18,2},{... | collective-permute-start | bytes 245768 | tf_op jit(solution)/shard_map/late_far/ppermute | solution.py:407
  57.7 6.2 %collective-permute-start.12 = (bf16[64,640]{1,0:T(8,128)(2,1)S(1)}, bf16[64,640]{1,0:T(8,128)(2,1)S(1)}, u32[]{:S(2)}, u32[]{:S(2)}) collective-permute-start(bf16[64,640]{1,0:T(8,128)(2,1)S(1)} %dout_rows.3.refs_2_.refs_9_.refs_0_), channel_id=1, source_target_pairs={{8,0},{12,4},{16,8},{20,12},{24,16},{28,20},{9,1},{13,5},{17,9},{2... | collective-permute-start | bytes 245768 | tf_op jit(solution)/shard_map/late_near/ppermute | solution.py:407
  63.9 3.9 %collective-permute-start.16 = (bf16[128,640]{1,0:T(8,128)(2,1)S(1)}, bf16[128,640]{1,0:T(8,128)(2,1)S(1)}, u32[]{:S(2)}, u32[]{:S(2)}) collective-permute-start(bf16[128,640]{1,0:T(8,128)(2,1)S(1)} %pair.7), channel_id=1, source_target_pairs={{0,4},{4,0},{8,12},{12,8},{16,20},{20,16},{24,28},{28,24},{1,5},{5... | collective-permute-start | bytes 491528 | tf_op jit(solution)/shard_map/late_swap/ppermute | solution.py:407

commit v8 on v7

--- a/solution.py
+++ b/solution.py
@@ -227,7 +227,10 @@
             part = part + other[...]
         parts.append(part)
         at += n
-    product = dot(jnp.concatenate(parts, axis=0), weight[...], NT)
+    if len(parts) == 1:
+        product = dot(weight[...], parts[0], NT).T
+    else:
+        product = dot(jnp.concatenate(parts, axis=0), weight[...], NT)
     for n, slot in enumerate(slots):
         finish_rows(info, slot, product[n * rows : (n + 1) * rows], mixed, stats, pay, n * rows)
 

time: 70.8 us -> 70.7 us (level)
  no operation moved by 1% of the time
where the time goes in v8:
time: 70.7 us; the launch traced here: 69.4 us
  starting transfers between devices  33.6 us (48%)
  Pallas kernels  18.6 us (26%)
  waiting for transfers between devices  14.2 us (20%)
  local copies, waits for them, and re-layouts  1.92 us (3%)
  between operations  1.07 us (2%)
    ppermute x12, starting transfers between devices, along(): return lax.ppermute(x, 'ctx', pairs)  25.8 us
    pallas_call x13, Pallas kernels, call(): pl.pallas_call(lambda *refs: kernel(device_info(info), *refs), out_shape=...  16.7 us
    ppermute x12, waiting for transfers between devices, along(): return lax.ppermute(x, 'ctx', pairs)  11.7 us
    ppermute x5, starting transfers between devices, over(): return lax.ppermute(x, 'tp', pairs)  7.84 us
    ppermute x5, waiting for transfers between devices, over(): return lax.ppermute(x, 'tp', pairs)  2.47 us
    unnamed x12, local copies, waits for them, and re-layouts  1.92 us
    pallas_call x1, Pallas kernels, pack(): pl.pallas_call(functools.partial(pack_kernel, places), out_shape=tuple((j...  1.9 us
  transfers between devices with their start and end apart: 17, of which 8 were waited for; matrix products, arithmetic and copies ran while one was open for 0% of the time, Pallas kernels for 25%

profile of v8, /device:TPU:3, one launch (start us, length us, event | category | flops | bytes accessed | tf_op | source)
XLA Modules:
  0.0 69.4 jit_solution(13351643291410198094)
XLA Ops:
  0.6 0.7 %collective-permute-start.8 = (bf16[64,5376]{1,0:T(8,128)(2,1)}, bf16[64,5376]{1,0:T(8,128)(2,1)S(1)}, u32[]{:S(2)}, u32[]{:S(2)}) collective-permute-start(bf16[64,5376]{1,0:T(8,128)(2,1)} %refs_0_.3), channel_id=1, source_target_pairs={{1,2},{2,1},{5,6},{6,5},{9,10},{10,9},{13,14},{14,13},{17,18},{18,... | collective-permute-start | bytes 2064392 | tf_op jit(solution)/shard_map/mid_first/ppermute | solution.py:414
  1.3 3.9 %collective-permute-start.6 = (bf16[64,5376]{1,0:T(8,128)(2,1)}, bf16[64,5376]{1,0:T(8,128)(2,1)S(1)}, u32[]{:S(2)}, u32[]{:S(2)}) collective-permute-start(bf16[64,5376]{1,0:T(8,128)(2,1)} %refs_0_.3), channel_id=1, source_target_pairs={{0,1},{1,0},{2,3},{3,2},{4,5},{5,4},{6,7},{7,6},{8,9},{9,8},{10,11... | collective-permute-start | bytes 2064392 | tf_op jit(solution)/shard_map/end_first/ppermute | solution.py:414
  5.2 1.9 %pack.1 = (bf16[256,512]{1,0:T(8,128)(2,1)}, bf16[256,512]{1,0:T(8,128)(2,1)}) custom-call(bf16[256,256]{1,0:T(8,128)(2,1)} %refs_0_.2, bf16[256,256]{1,0:T(8,128)(2,1)} %refs_1_.1, bf16[256,512]{1,0:T(8,128)(2,1)} %refs_2_.2), custom_call_target="tpu_custom_call" | custom-call | flops 1 | bytes 1 | tf_op jit(solution)/shard_map/pack/pallas_call | solution.py:87
  7.1 3.1 %collective-permute-start = (bf16[256,512]{1,0:T(8,128)(2,1)}, bf16[256,512]{1,0:T(8,128)(2,1)S(1)}, u32[]{:S(2)}, u32[]{:S(2)}) collective-permute-start(bf16[256,512]{1,0:T(8,128)(2,1)} %get-tuple-element.24.refs_0_), channel_id=1, source_target_pairs={{0,8},{4,12},{8,16},{12,20},{16,24},{20,28},{1,9},{5,13},{9,17},{1... | collective-permute-start | bytes 786440 | tf_op jit(solution)/shard_map/kv_near/ppermute | solution.py:410
  10.2 1.3 %collective-permute-start.1 = (bf16[256,512]{1,0:T(8,128)(2,1)}, bf16[256,512]{1,0:T(8,128)(2,1)S(1)}, u32[]{:S(2)}, u32[]{:S(2)}) collective-permute-start(bf16[256,512]{1,0:T(8,128)(2,1)} %get-tuple-element.24.refs_0_), channel_id=1, source_target_pairs={{0,16},{4,20},{8,24},{12,28},{1,17},{5,21},{9,25},{13,29},{2,18},{... | collective-permute-start | bytes 786440 | tf_op jit(solution)/shard_map/kv_far/ppermute | solution.py:410
  11.6 1.3 %collective-permute-start.3 = (bf16[256,512]{1,0:T(8,128)(2,1)}, bf16[256,512]{1,0:T(8,128)(2,1)S(1)}, u32[]{:S(2)}, u32[]{:S(2)}) collective-permute-start(bf16[256,512]{1,0:T(8,128)(2,1)} %get-tuple-element.25.refs_0_.refs_1_), channel_id=1, source_target_pairs={{16,0},{20,4},{24,8},{28,12},{17,1},{21,5},{25,9},{29,13},{18,2},{... | collective-permute-start | bytes 786440 | tf_op jit(solution)/shard_map/q_far/ppermute | solution.py:410
  12.9 2.9 %collective-permute-done.refs_2_ = bf16[256,512]{1,0:T(8,128)(2,1)S(1)} collective-permute-done((bf16[256,512]{1,0:T(8,128)(2,1)}, bf16[256,512]{1,0:T(8,128)(2,1)S(1)}, u32[]{:S(2)}, u32[]{:S(2)}) %collective-permute-start) | collective-permute-done | bytes 262176 | tf_op jit(solution)/shard_map/kv_near/ppermute | solution.py:410
  15.8 1.9 %collective-permute-start.4 = (bf16[256,512]{1,0:T(8,128)(2,1)}, bf16[256,512]{1,0:T(8,128)(2,1)S(1)}, u32[]{:S(2)}, u32[]{:S(2)}) collective-permute-start(bf16[256,512]{1,0:T(8,128)(2,1)} %get-tuple-element.25.refs_0_.refs_1_), channel_id=1, source_target_pairs={{8,0},{12,4},{16,8},{20,12},{24,16},{28,20},{9,1},{13,5},{17,9},{2... | collective-permute-start | bytes 786440 | tf_op jit(solution)/shard_map/q_near/ppermute | solution.py:410
  17.7 0.0 collective-permute-done.8.refs_2_
  17.7 1.3 %collective-permute-start.9 = (bf16[64,5376]{1,0:T(8,128)(2,1)S(1)}, bf16[64,5376]{1,0:T(8,128)(2,1)S(1)}, u32[]{:S(2)}, u32[]{:S(2)}) collective-permute-start(bf16[64,5376]{1,0:T(8,128)(2,1)S(1)} %collective-permute-done.8.refs_2_), channel_id=1, source_target_pairs={{1,0},{2,3},{5,4},{6,7},{9,8},{10,11},{13,12},{14,15},{17,16},{18,... | collective-permute-start | bytes 2064392 | tf_op jit(solution)/shard_map/out_second/ppermute | solution.py:414
  19.0 1.3 %collective-permute-done.6.refs_1_ = bf16[64,5376]{1,0:T(8,128)(2,1)S(1)} collective-permute-done((bf16[64,5376]{1,0:T(8,128)(2,1)}, bf16[64,5376]{1,0:T(8,128)(2,1)S(1)}, u32[]{:S(2)}, u32[]{:S(2)}) %collective-permute-start.6) | collective-permute-done | bytes 688160 | tf_op jit(solution)/shard_map/end_first/ppermute | solution.py:414
  20.3 0.7 collective-permute-start.7
  21.0 0.0 collective-permute-done.1.refs_1_.refs_3_
  21.0 0.0 copy-start.1
  21.0 0.9 %copy-done.1 = bf16[256,512]{1,0:T(8,128)(2,1)S(1)} copy-done((bf16[256,512]{1,0:T(8,128)(2,1)S(1)}, bf16[256,512]{1,0:T(8,128)(2,1)}, u32[]{:S(2)}) %copy-start.1) | copy-done | bytes 262168
  21.9 0.0 copy-start.2
  22.0 1.6 %collective-permute-start.2 = (bf16[512,512]{1,0:T(8,128)(2,1)S(1)}, bf16[512,512]{1,0:T(8,128)(2,1)S(1)}, u32[]{:S(2)}, u32[]{:S(2)}) collective-permute-start(bf16[512,512]{1,0:T(8,128)(2,1)S(1)} %pair.4), channel_id=1, source_target_pairs={{0,4},{4,0},{8,12},{12,8},{16,20},{20,16},{24,28},{28,24},{1,5},{5... | collective-permute-start | bytes 1572872 | tf_op jit(solution)/shard_map/kv_swap/ppermute | solution.py:410
  23.6 0.0 collective-permute-done.3.refs_1_.refs_3_.refs_2_
  23.6 0.9 %collective-permute-done.4.refs_2_.refs_1_ = bf16[256,512]{1,0:T(8,128)(2,1)S(1)} collective-permute-done((bf16[256,512]{1,0:T(8,128)(2,1)}, bf16[256,512]{1,0:T(8,128)(2,1)S(1)}, u32[]{:S(2)}, u32[]{:S(2)}) %collective-permute-start.4) | collective-permute-done | bytes 262176 | tf_op jit(solution)/shard_map/q_near/ppermute | solution.py:410
  24.5 0.0 copy-start.3
  24.5 0.9 %copy-done.3 = bf16[256,512]{1,0:T(8,128)(2,1)S(1)} copy-done((bf16[256,512]{1,0:T(8,128)(2,1)S(1)}, bf16[256,512]{1,0:T(8,128)(2,1)}, u32[]{:S(2)}) %copy-start.3) | copy-done | bytes 262168
  25.5 3.6 %collective-permute-start.5 = (bf16[512,512]{1,0:T(8,128)(2,1)S(1)}, bf16[512,512]{1,0:T(8,128)(2,1)S(1)}, u32[]{:S(2)}, u32[]{:S(2)}) collective-permute-start(bf16[512,512]{1,0:T(8,128)(2,1)S(1)} %pair.5), channel_id=1, source_target_pairs={{0,4},{4,0},{8,12},{12,8},{16,20},{20,16},{24,28},{28,24},{1,5},{5... | collective-permute-start | bytes 1572872 | tf_op jit(solution)/shard_map/q_swap/ppermute | solution.py:410
  29.1 0.0 collective-permute-done.2.refs_4_
  29.1 1.5 %collective-permute-done.5.refs_5_.refs_4_.refs_1_ = bf16[512,512]{1,0:T(8,128)(2,1)S(1)} collective-permute-done((bf16[512,512]{1,0:T(8,128)(2,1)S(1)}, bf16[512,512]{1,0:T(8,128)(2,1)S(1)}, u32[]{:S(2)}, u32[]{:S(2)}) %collective-permute-start.5) | collective-permute-done | bytes 524320 | tf_op jit(solution)/shard_map/q_swap/ppermute | solution.py:410
  30.6 0.0 copy-done.2
  30.6 0.0 copy-start
  30.6 3.6 %attention_probs.1 = (bf16[4,256,1280]{2,1,0:T(8,128)(2,1)S(1)}, f32[256,512]{1,0:T(8,128)S(1)}, bf16[256,128]{1,0:T(8,128)(2,1)S(1)}, bf16[1280,512]{1,0:T(8,128)(2,1)S(1)}) custom-call(bf16[256,512]{1,0:T(8,128)(2,1)S(1)} %copy-done.2, bf16[256,512]{1,0:T(8,128)(2,1)S(1)} %copy-done.3, bf16[256,512]{1,0:T(8,128)(2,1)S(1)} %collective-permute-done.refs_2_, ...), custom_call_target="tpu_custom_call" | custom-call | flops 1 | bytes 1 | tf_op jit(solution)/shard_map/attention_probs/pallas_call | solution.py:41
  34.2 0.0 copy-start.5
  34.2 1.2 %collective-permute-done.9.refs_0_.refs_3_ = bf16[64,5376]{1,0:T(8,128)(2,1)S(1)} collective-permute-done((bf16[64,5376]{1,0:T(8,128)(2,1)S(1)}, bf16[64,5376]{1,0:T(8,128)(2,1)S(1)}, u32[]{:S(2)}, u32[]{:S(2)}) %collective-permute-start.9) | collective-permute-done | bytes 688160 | tf_op jit(solution)/shard_map/out_second/ppermute | solution.py:414
  35.5 0.0 collective-permute-done.7.refs_1_.refs_0_
  35.5 1.3 %collective-permute-start.10 = (bf16[64,5376]{1,0:T(8,128)(2,1)S(1)}, bf16[64,5376]{1,0:T(8,128)(2,1)S(1)}, u32[]{:S(2)}, u32[]{:S(2)}) collective-permute-start(bf16[64,5376]{1,0:T(8,128)(2,1)S(1)} %collective-permute-done.7.refs_1_.refs_0_), channel_id=1, source_target_pairs={{1,0},{2,3},{5,4},{6,7},{9,8},{10,11},{13,12},{14,15},{17,16},{18,... | collective-permute-start | bytes 2064392 | tf_op jit(solution)/shard_map/out_third/ppermute | solution.py:414
  36.8 0.0 copy-done
  36.8 0.0 copy-done.5
  36.8 0.0 copy-start.4
  36.8 2.1 %dout_rows.2.refs_2_.refs_0_.refs_5_ = bf16[192,640]{1,0:T(8,128)(2,1)S(1)} custom-call(bf16[64,5376]{1,0:T(8,128)(2,1)S(1)} %copy-done.5, bf16[64,5376]{1,0:T(8,128)(2,1)S(1)} %collective-permute-done.6.refs_1_, bf16[64,5376]{1,0:T(8,128)(2,1)S(1)} %collective-permute-done.8.refs_2_, bf16[64,5376]{1,0:T(8,128)(2,1)S(1)} %collective-permute-done.9.refs_0_.refs_3_, ...), custom_call_target="tpu_custom_call" | custom-call | flops 1 | bytes 1 | tf_op jit(solution)/shard_map/dout_rows/pallas_call | solution.py:41
  38.9 1.3 %collective-permute-start.13 = (bf16[192,640]{1,0:T(8,128)(2,1)S(1)}, bf16[192,640]{1,0:T(8,128)(2,1)S(1)}, u32[]{:S(2)}, u32[]{:S(2)}) collective-permute-start(bf16[192,640]{1,0:T(8,128)(2,1)S(1)} %dout_rows.2.refs_2_.refs_0_.refs_5_), channel_id=1, source_target_pairs={{16,0},{20,4},{24,8},{28,12},{17,1},{21,5},{25,9},{29,13},{18,2},{... | collective-permute-start | bytes 737288 | tf_op jit(solution)/shard_map/early_far/ppermute | solution.py:410
  40.2 2.5 %collective-permute-start.14 = (bf16[192,640]{1,0:T(8,128)(2,1)S(1)}, bf16[192,640]{1,0:T(8,128)(2,1)S(1)}, u32[]{:S(2)}, u32[]{:S(2)}) collective-permute-start(bf16[192,640]{1,0:T(8,128)(2,1)S(1)} %dout_rows.2.refs_2_.refs_0_.refs_5_), channel_id=1, source_target_pairs={{8,0},{12,4},{16,8},{20,12},{24,16},{28,20},{9,1},{13,5},{17,9},{2... | collective-permute-start | bytes 737288 | tf_op jit(solution)/shard_map/early_near/ppermute | solution.py:410
  42.7 0.0 copy-done.4
  42.7 0.9 %key_grads.4 = (f32[256,256]{1,0:T(8,128)S(1)}, f32[256,256]{1,0:T(8,128)S(1)}) custom-call(bf16[256,512]{1,0:T(8,128)(2,1)S(1)} %copy-done.2, bf16[256,512]{1,0:T(8,128)(2,1)S(1)} %copy-done.4, bf16[192,640]{1,0:T(8,128)(2,1)S(1)} %dout_rows.2.refs_2_.refs_0_.refs_5_), custom_call_target="tpu_custom_call" | custom-call | flops 1 | bytes 1 | tf_op jit(solution)/shard_map/key_grads/pallas_call | solution.py:41
  43.6 2.1 %query_grads.2 = (f32[256,512]{1,0:T(8,128)}, f32[8,128]{1,0:T(8,128)S(1)}) custom-call(bf16[4,256,1280]{2,1,0:T(8,128)(2,1)S(1)} %get-tuple-element.26.refs_0_, bf16[1280,512]{1,0:T(8,128)(2,1)S(1)} %get-tuple-element.27.refs_1_, bf16[192,640]{1,0:T(8,128)(2,1)S(1)} %dout_rows.2.refs_2_.refs_0_.refs_5_), custom_call_target="tpu_custom_call" | custom-call | flops 1 | bytes 1 | tf_op jit(solution)/shard_map/query_grads/pallas_call | solution.py:41
  45.7 5.9 %collective-permute-done.13.refs_1_.refs_6_ = bf16[192,640]{1,0:T(8,128)(2,1)S(1)} collective-permute-done((bf16[192,640]{1,0:T(8,128)(2,1)S(1)}, bf16[192,640]{1,0:T(8,128)(2,1)S(1)}, u32[]{:S(2)}, u32[]{:S(2)}) %collective-permute-start.13) | collective-permute-done | bytes 245792 | tf_op jit(solution)/shard_map/early_far/ppermute | solution.py:410
  51.6 0.0 collective-permute-done.14.refs_2_.refs_7_
  51.6 2.9 %collective-permute-start.15 = (bf16[384,640]{1,0:T(8,128)(2,1)S(1)}, bf16[384,640]{1,0:T(8,128)(2,1)S(1)}, u32[]{:S(2)}, u32[]{:S(2)}) collective-permute-start(bf16[384,640]{1,0:T(8,128)(2,1)S(1)} %pair.6), channel_id=1, source_target_pairs={{0,4},{4,0},{8,12},{12,8},{16,20},{20,16},{24,28},{28,24},{1,5},{5... | collective-permute-start | bytes 1474568 | tf_op jit(solution)/shard_map/early_swap/ppermute | solution.py:410
  54.5 0.0 collective-permute-done.10.refs_1_
  54.5 1.8 %dout_rows.3.refs_2_.refs_9_.refs_0_ = bf16[64,640]{1,0:T(8,128)(2,1)S(1)} custom-call(bf16[64,5376]{1,0:T(8,128)(2,1)S(1)} %collective-permute-done.7.refs_1_.refs_0_, bf16[64,5376]{1,0:T(8,128)(2,1)S(1)} %collective-permute-done.10.refs_1_, bf16[512,5376]{1,0:T(8,128)(2,1)S(1)} %copy-done, f32[256,512]{1,0:T(8,128)S(1)} %get-tuple-element.30.refs_5_.refs_3_, ...), custom_call_target="tpu_custom_call" | custom-call | flops 1 | bytes 1 | tf_op jit(solution)/shard_map/dout_rows/pallas_call | solution.py:41
  56.3 1.3 %collective-permute-start.11 = (bf16[64,640]{1,0:T(8,128)(2,1)S(1)}, bf16[64,640]{1,0:T(8,128)(2,1)S(1)}, u32[]{:S(2)}, u32[]{:S(2)}) collective-permute-start(bf16[64,640]{1,0:T(8,128)(2,1)S(1)} %dout_rows.3.refs_2_.refs_9_.refs_0_), channel_id=1, source_target_pairs={{16,0},{20,4},{24,8},{28,12},{17,1},{21,5},{25,9},{29,13},{18,2},{... | collective-permute-start | bytes 245768 | tf_op jit(solution)/shard_map/late_far/ppermute | solution.py:410
  57.6 2.1 %collective-permute-start.12 = (bf16[64,640]{1,0:T(8,128)(2,1)S(1)}, bf16[64,640]{1,0:T(8,128)(2,1)S(1)}, u32[]{:S(2)}, u32[]{:S(2)}) collective-permute-start(bf16[64,640]{1,0:T(8,128)(2,1)S(1)} %dout_rows.3.refs_2_.refs_9_.refs_0_), channel_id=1, source_target_pairs={{8,0},{12,4},{16,8},{20,12},{24,16},{28,20},{9,1},{13,5},{17,9},{2... | collective-permute-start | bytes 245768 | tf_op jit(solution)/shard_map/late_near/ppermute | solution.py:410
  59.7 1.3 %query_grads.3 = (f32[256,512]{1,0:T(8,128)}, f32[8,128]{1,0:T(8,128)S(1)}) custom-call(bf16[4,256,1280]{2,1,0:T(8,128)(2,1)S(1)} %get-tuple-element.26.refs_0_, bf16[1280,512]{1,0:T(8,128)(2,1)S(1)} %get-tuple-element.27.refs_1_, bf16[64,640]{1,0:T(8,128)(2,1)S(1)} %dout_rows.3.refs_2_.refs_9_.refs_0_, ...), custom_call_target="tpu_custom_call", output_to_operand_aliasing={{0}: (3, {})} | custom-call | flops 1 | bytes 1 | tf_op jit(solution)/shard_map/query_grads/pallas_call | solution.py:41
  61.0 0.0 collective-permute-done.15.refs_8_
  61.0 2.5 %key_grads.5 = (f32[256,256]{1,0:T(8,128)S(1)}, f32[256,256]{1,0:T(8,128)S(1)}) custom-call(bf16[256,512]{1,0:T(8,128)(2,1)S(1)} %copy-done.2, bf16[256,512]{1,0:T(8,128)(2,1)S(1)} %copy-done.4, bf16[256,512]{1,0:T(8,128)(2,1)S(1)} %collective-permute-done.4.refs_2_.refs_1_, bf16[256,512]{1,0:T(8,128)(2,1)S(1)} %collective-permute-done.3.refs_1_.refs_3_.refs_2_, ...), custom_call_target="tpu_custom_call" | custom-call | flops 1 | bytes 1 | tf_op jit(solution)/shard_map/key_grads/pallas_call | solution.py:41
  63.5 0.0 collective-permute-done.11.refs_1_.refs_3_
  63.5 0.3 collective-permute-done.12.refs_2_.refs_4_
  63.8 2.9 %collective-permute-start.16 = (bf16[128,640]{1,0:T(8,128)(2,1)S(1)}, bf16[128,640]{1,0:T(8,128)(2,1)S(1)}, u32[]{:S(2)}, u32[]{:S(2)}) collective-permute-start(bf16[128,640]{1,0:T(8,128)(2,1)S(1)} %pair.7), channel_id=1, source_target_pairs={{0,4},{4,0},{8,12},{12,8},{16,20},{20,16},{24,28},{28,24},{1,5},{5... | collective-permute-start | bytes 491528 | tf_op jit(solution)/shard_map/late_swap/ppermute | solution.py:410
  66.7 0.8 %key_grads.6 = (f32[256,256]{1,0:T(8,128)S(1)}, f32[256,256]{1,0:T(8,128)S(1)}) custom-call(bf16[256,512]{1,0:T(8,128)(2,1)S(1)} %copy-done.2, bf16[256,512]{1,0:T(8,128)(2,1)S(1)} %collective-permute-done.4.refs_2_.refs_1_, bf16[256,512]{1,0:T(8,128)(2,1)S(1)} %collective-permute-done.3.refs_1_.refs_3_.refs_2_, ...), custom_call_target="tpu_custom_call" | custom-call | flops 1 | bytes 1 | tf_op jit(solution)/shard_map/key_grads/pallas_call | solution.py:41
  67.5 0.2 collective-permute-done.16.refs_2_
  67.7 1.5 %key_grads.7 = (f32[256,256]{1,0:T(8,128)}, f32[256,256]{1,0:T(8,128)}) custom-call(bf16[256,512]{1,0:T(8,128)(2,1)S(1)} %copy-done.2, bf16[512,512]{1,0:T(8,128)(2,1)S(1)} %collective-permute-done.5.refs_5_.refs_4_.refs_1_, bf16[128,640]{1,0:T(8,128)(2,1)S(1)} %collective-permute-done.16.refs_2_, f32[256,256]{1,0:T(8,128)S(1)} %get-tuple-element.41.refs_3_, ...), custom_call_target="tpu_custom_call" | custom-call | flops 1 | bytes 1 | tf_op jit(solution)/shard_map/key_grads/pallas_call | solution.py:41
  (6 shorter events, 0.1 us)
Async XLA Ops:
  0.6 17.1 %collective-permute-start.8 = (bf16[64,5376]{1,0:T(8,128)(2,1)}, bf16[64,5376]{1,0:T(8,128)(2,1)S(1)}, u32[]{:S(2)}, u32[]{:S(2)}) collective-permute-start(bf16[64,5376]{1,0:T(8,128)(2,1)} %refs_0_.3), channel_id=1, source_target_pairs={{1,2},{2,1},{5,6},{6,5},{9,10},{10,9},{13,14},{14,13},{17,18},{18,... | collective-permute-start | bytes 2064392 | tf_op jit(solution)/shard_map/mid_first/ppermute | solution.py:414
  1.3 18.9 %collective-permute-start.6 = (bf16[64,5376]{1,0:T(8,128)(2,1)}, bf16[64,5376]{1,0:T(8,128)(2,1)S(1)}, u32[]{:S(2)}, u32[]{:S(2)}) collective-permute-start(bf16[64,5376]{1,0:T(8,128)(2,1)} %refs_0_.3), channel_id=1, source_target_pairs={{0,1},{1,0},{2,3},{3,2},{4,5},{5,4},{6,7},{7,6},{8,9},{9,8},{10,11... | collective-permute-start | bytes 2064392 | tf_op jit(solution)/shard_map/end_first/ppermute | solution.py:414
  7.1 8.7 %collective-permute-start = (bf16[256,512]{1,0:T(8,128)(2,1)}, bf16[256,512]{1,0:T(8,128)(2,1)S(1)}, u32[]{:S(2)}, u32[]{:S(2)}) collective-permute-start(bf16[256,512]{1,0:T(8,128)(2,1)} %get-tuple-element.24.refs_0_), channel_id=1, source_target_pairs={{0,8},{4,12},{8,16},{12,20},{16,24},{20,28},{1,9},{5,13},{9,17},{1... | collective-permute-start | bytes 786440 | tf_op jit(solution)/shard_map/kv_near/ppermute | solution.py:410
  10.2 10.7 %collective-permute-start.1 = (bf16[256,512]{1,0:T(8,128)(2,1)}, bf16[256,512]{1,0:T(8,128)(2,1)S(1)}, u32[]{:S(2)}, u32[]{:S(2)}) collective-permute-start(bf16[256,512]{1,0:T(8,128)(2,1)} %get-tuple-element.24.refs_0_), channel_id=1, source_target_pairs={{0,16},{4,20},{8,24},{12,28},{1,17},{5,21},{9,25},{13,29},{2,18},{... | collective-permute-start | bytes 786440 | tf_op jit(solution)/shard_map/kv_far/ppermute | solution.py:410
  11.6 12.0 %collective-permute-start.3 = (bf16[256,512]{1,0:T(8,128)(2,1)}, bf16[256,512]{1,0:T(8,128)(2,1)S(1)}, u32[]{:S(2)}, u32[]{:S(2)}) collective-permute-start(bf16[256,512]{1,0:T(8,128)(2,1)} %get-tuple-element.25.refs_0_.refs_1_), channel_id=1, source_target_pairs={{16,0},{20,4},{24,8},{28,12},{17,1},{21,5},{25,9},{29,13},{18,2},{... | collective-permute-start | bytes 786440 | tf_op jit(solution)/shard_map/q_far/ppermute | solution.py:410
  15.8 8.7 %collective-permute-start.4 = (bf16[256,512]{1,0:T(8,128)(2,1)}, bf16[256,512]{1,0:T(8,128)(2,1)S(1)}, u32[]{:S(2)}, u32[]{:S(2)}) collective-permute-start(bf16[256,512]{1,0:T(8,128)(2,1)} %get-tuple-element.25.refs_0_.refs_1_), channel_id=1, source_target_pairs={{8,0},{12,4},{16,8},{20,12},{24,16},{28,20},{9,1},{13,5},{17,9},{2... | collective-permute-start | bytes 786440 | tf_op jit(solution)/shard_map/q_near/ppermute | solution.py:410
  17.7 17.7 %collective-permute-start.9 = (bf16[64,5376]{1,0:T(8,128)(2,1)S(1)}, bf16[64,5376]{1,0:T(8,128)(2,1)S(1)}, u32[]{:S(2)}, u32[]{:S(2)}) collective-permute-start(bf16[64,5376]{1,0:T(8,128)(2,1)S(1)} %collective-permute-done.8.refs_2_), channel_id=1, source_target_pairs={{1,0},{2,3},{5,4},{6,7},{9,8},{10,11},{13,12},{14,15},{17,16},{18,... | collective-permute-start | bytes 2064392 | tf_op jit(solution)/shard_map/out_second/ppermute | solution.py:414
  20.3 15.2 %collective-permute-start.7 = (bf16[64,5376]{1,0:T(8,128)(2,1)S(1)}, bf16[64,5376]{1,0:T(8,128)(2,1)S(1)}, u32[]{:S(2)}, u32[]{:S(2)}) collective-permute-start(bf16[64,5376]{1,0:T(8,128)(2,1)S(1)} %collective-permute-done.6.refs_1_), channel_id=1, source_target_pairs={{1,2},{2,1},{5,6},{6,5},{9,10},{10,9},{13,14},{14,13},{17,18},{18,... | collective-permute-start | bytes 2064392 | tf_op jit(solution)/shard_map/mid_second/ppermute | solution.py:414
  21.0 1.0 %copy-start.1 = (bf16[256,512]{1,0:T(8,128)(2,1)S(1)}, bf16[256,512]{1,0:T(8,128)(2,1)}, u32[]{:S(2)}) copy-start(bf16[256,512]{1,0:T(8,128)(2,1)} %get-tuple-element.24.refs_0_) | copy-start | bytes 786436
  21.9 8.7 %copy-start.2 = (bf16[256,512]{1,0:T(8,128)(2,1)S(1)}, bf16[256,512]{1,0:T(8,128)(2,1)}, u32[]{:S(2)}) copy-start(bf16[256,512]{1,0:T(8,128)(2,1)} %get-tuple-element.24.refs_0_) | copy-start | bytes 786436
  22.0 7.1 %collective-permute-start.2 = (bf16[512,512]{1,0:T(8,128)(2,1)S(1)}, bf16[512,512]{1,0:T(8,128)(2,1)S(1)}, u32[]{:S(2)}, u32[]{:S(2)}) collective-permute-start(bf16[512,512]{1,0:T(8,128)(2,1)S(1)} %pair.4), channel_id=1, source_target_pairs={{0,4},{4,0},{8,12},{12,8},{16,20},{20,16},{24,28},{28,24},{1,5},{5... | collective-permute-start | bytes 1572872 | tf_op jit(solution)/shard_map/kv_swap/ppermute | solution.py:410
  24.5 1.0 %copy-start.3 = (bf16[256,512]{1,0:T(8,128)(2,1)S(1)}, bf16[256,512]{1,0:T(8,128)(2,1)}, u32[]{:S(2)}) copy-start(bf16[256,512]{1,0:T(8,128)(2,1)} %get-tuple-element.25.refs_0_.refs_1_) | copy-start | bytes 786436
  25.5 5.1 %collective-permute-start.5 = (bf16[512,512]{1,0:T(8,128)(2,1)S(1)}, bf16[512,512]{1,0:T(8,128)(2,1)S(1)}, u32[]{:S(2)}, u32[]{:S(2)}) collective-permute-start(bf16[512,512]{1,0:T(8,128)(2,1)S(1)} %pair.5), channel_id=1, source_target_pairs={{0,4},{4,0},{8,12},{12,8},{16,20},{20,16},{24,28},{28,24},{1,5},{5... | collective-permute-start | bytes 1572872 | tf_op jit(solution)/shard_map/q_swap/ppermute | solution.py:410
  30.6 6.1 %copy-start = (bf16[512,5376]{1,0:T(8,128)(2,1)S(1)}, bf16[512,5376]{1,0:T(8,128)(2,1)}, u32[]{:S(2)}) copy-start(bf16[512,5376]{1,0:T(8,128)(2,1)} %refs_2_.3) | copy-start | bytes 16515076
  34.2 2.5 %copy-start.5 = (bf16[64,5376]{1,0:T(8,128)(2,1)S(1)}, bf16[64,5376]{1,0:T(8,128)(2,1)}, u32[]{:S(2)}) copy-start(bf16[64,5376]{1,0:T(8,128)(2,1)} %refs_0_.3) | copy-start | bytes 2064388
  35.5 19.1 %collective-permute-start.10 = (bf16[64,5376]{1,0:T(8,128)(2,1)S(1)}, bf16[64,5376]{1,0:T(8,128)(2,1)S(1)}, u32[]{:S(2)}, u32[]{:S(2)}) collective-permute-start(bf16[64,5376]{1,0:T(8,128)(2,1)S(1)} %collective-permute-done.7.refs_1_.refs_0_), channel_id=1, source_target_pairs={{1,0},{2,3},{5,4},{6,7},{9,8},{10,11},{13,12},{14,15},{17,16},{18,... | collective-permute-start | bytes 2064392 | tf_op jit(solution)/shard_map/out_third/ppermute | solution.py:414
  36.8 5.9 %copy-start.4 = (bf16[256,512]{1,0:T(8,128)(2,1)S(1)}, bf16[256,512]{1,0:T(8,128)(2,1)}, u32[]{:S(2)}) copy-start(bf16[256,512]{1,0:T(8,128)(2,1)} %get-tuple-element.25.refs_0_.refs_1_) | copy-start | bytes 786436
  38.9 12.7 %collective-permute-start.13 = (bf16[192,640]{1,0:T(8,128)(2,1)S(1)}, bf16[192,640]{1,0:T(8,128)(2,1)S(1)}, u32[]{:S(2)}, u32[]{:S(2)}) collective-permute-start(bf16[192,640]{1,0:T(8,128)(2,1)S(1)} %dout_rows.2.refs_2_.refs_0_.refs_5_), channel_id=1, source_target_pairs={{16,0},{20,4},{24,8},{28,12},{17,1},{21,5},{25,9},{29,13},{18,2},{... | collective-permute-start | bytes 737288 | tf_op jit(solution)/shard_map/early_far/ppermute | solution.py:410
  40.2 11.4 %collective-permute-start.14 = (bf16[192,640]{1,0:T(8,128)(2,1)S(1)}, bf16[192,640]{1,0:T(8,128)(2,1)S(1)}, u32[]{:S(2)}, u32[]{:S(2)}) collective-permute-start(bf16[192,640]{1,0:T(8,128)(2,1)S(1)} %dout_rows.2.refs_2_.refs_0_.refs_5_), channel_id=1, source_target_pairs={{8,0},{12,4},{16,8},{20,12},{24,16},{28,20},{9,1},{13,5},{17,9},{2... | collective-permute-start | bytes 737288 | tf_op jit(solution)/shard_map/early_near/ppermute | solution.py:410
  51.6 9.3 %collective-permute-start.15 = (bf16[384,640]{1,0:T(8,128)(2,1)S(1)}, bf16[384,640]{1,0:T(8,128)(2,1)S(1)}, u32[]{:S(2)}, u32[]{:S(2)}) collective-permute-start(bf16[384,640]{1,0:T(8,128)(2,1)S(1)} %pair.6), channel_id=1, source_target_pairs={{0,4},{4,0},{8,12},{12,8},{16,20},{20,16},{24,28},{28,24},{1,5},{5... | collective-permute-start | bytes 1474568 | tf_op jit(solution)/shard_map/early_swap/ppermute | solution.py:410
  56.3 7.2 %collective-permute-start.11 = (bf16[64,640]{1,0:T(8,128)(2,1)S(1)}, bf16[64,640]{1,0:T(8,128)(2,1)S(1)}, u32[]{:S(2)}, u32[]{:S(2)}) collective-permute-start(bf16[64,640]{1,0:T(8,128)(2,1)S(1)} %dout_rows.3.refs_2_.refs_9_.refs_0_), channel_id=1, source_target_pairs={{16,0},{20,4},{24,8},{28,12},{17,1},{21,5},{25,9},{29,13},{18,2},{... | collective-permute-start | bytes 245768 | tf_op jit(solution)/shard_map/late_far/ppermute | solution.py:410
  57.6 6.2 %collective-permute-start.12 = (bf16[64,640]{1,0:T(8,128)(2,1)S(1)}, bf16[64,640]{1,0:T(8,128)(2,1)S(1)}, u32[]{:S(2)}, u32[]{:S(2)}) collective-permute-start(bf16[64,640]{1,0:T(8,128)(2,1)S(1)} %dout_rows.3.refs_2_.refs_9_.refs_0_), channel_id=1, source_target_pairs={{8,0},{12,4},{16,8},{20,12},{24,16},{28,20},{9,1},{13,5},{17,9},{2... | collective-permute-start | bytes 245768 | tf_op jit(solution)/shard_map/late_near/ppermute | solution.py:410
  63.8 3.9 %collective-permute-start.16 = (bf16[128,640]{1,0:T(8,128)(2,1)S(1)}, bf16[128,640]{1,0:T(8,128)(2,1)S(1)}, u32[]{:S(2)}, u32[]{:S(2)}) collective-permute-start(bf16[128,640]{1,0:T(8,128)(2,1)S(1)} %pair.7), channel_id=1, source_target_pairs={{0,4},{4,0},{8,12},{12,8},{16,20},{20,16},{24,28},{28,24},{1,5},{5... | collective-permute-start | bytes 491528 | tf_op jit(solution)/shard_map/late_swap/ppermute | solution.py:410

commit v9 on v8

--- a/solution.py
+++ b/solution.py
@@ -450,7 +450,7 @@
         near = along(pay, moved(-2), name + "_near")
         return near, far
 
-    second_came = token_of(token_of(out_second), mid_second, cost=FETCH)
+    second_came = token_of(out_second, mid_second, cost=FETCH)
     mid_second, second_came, stats = lax.optimization_barrier((mid_second, second_came, stats))
     out_third = over(mid_second, outward, "out_third")
     statistics = (out_weight, mixed, stats)

time: 70.7 us -> 70.8 us (level)
  waiting for transfers between devices: 14.2 us -> 19.1 us
  starting transfers between devices: 33.6 us -> 29.1 us
    ppermute x5, waiting for transfers between devices: 2.47 us -> 6.91 us  [over(): return lax.ppermute(x, 'tp', pairs)]
    ppermute x5, starting transfers between devices: 7.84 us -> 5.32 us  [over(): return lax.ppermute(x, 'tp', pairs)]
    ppermute x12, starting transfers between devices: 25.8 us -> 23.8 us  [along(): return lax.ppermute(x, 'ctx', pairs)]
  transfers between devices with their start and end apart: 17 -> 17, of which waited for: 8 -> 8; matrix products, arithmetic and copies ran while one was open for 0% -> 0% of each run, Pallas kernels for 25% -> 24%
where the time goes in v9:
time: 70.8 us; the launch traced here: 69.8 us
  starting transfers between devices  29.1 us (41%)
  waiting for transfers between devices  19.1 us (27%)
  Pallas kernels  18.6 us (26%)
  local copies, waits for them, and re-layouts  1.92 us (3%)
  between operations  1.08 us (2%)
    ppermute x12, starting transfers between devices, along(): return lax.ppermute(x, 'ctx', pairs)  23.8 us
    pallas_call x13, Pallas kernels, call(): pl.pallas_call(lambda *refs: kernel(device_info(info), *refs), out_shape=...  16.7 us
    ppermute x12, waiting for transfers between devices, along(): return lax.ppermute(x, 'ctx', pairs)  12.2 us
    ppermute x5, waiting for transfers between devices, over(): return lax.ppermute(x, 'tp', pairs)  6.91 us
    ppermute x5, starting transfers between devices, over(): return lax.ppermute(x, 'tp', pairs)  5.32 us
    unnamed x12, local copies, waits for them, and re-layouts  1.92 us
    pallas_call x1, Pallas kernels, pack(): pl.pallas_call(functools.partial(pack_kernel, places), out_shape=tuple((j...  1.9 us
  transfers between devices with their start and end apart: 17, of which 8 were waited for; matrix products, arithmetic and copies ran while one was open for 0% of the time, Pallas kernels for 24%

profile of v9, /device:TPU:3, one launch (start us, length us, event | category | flops | bytes accessed | tf_op | source)
XLA Modules:
  0.0 69.8 jit_solution(3288195728613035377)
XLA Ops:
  0.6 1.4 %collective-permute-start.6 = (bf16[64,5376]{1,0:T(8,128)(2,1)}, bf16[64,5376]{1,0:T(8,128)(2,1)S(1)}, u32[]{:S(2)}, u32[]{:S(2)}) collective-permute-start(bf16[64,5376]{1,0:T(8,128)(2,1)} %refs_0_.3), channel_id=1, source_target_pairs={{0,1},{1,0},{2,3},{3,2},{4,5},{5,4},{6,7},{7,6},{8,9},{9,8},{10,11... | collective-permute-start | bytes 2064392 | tf_op jit(solution)/shard_map/end_first/ppermute | solution.py:414
  2.0 0.7 collective-permute-start.8
  2.7 1.9 %pack.1 = (bf16[256,512]{1,0:T(8,128)(2,1)}, bf16[256,512]{1,0:T(8,128)(2,1)}) custom-call(bf16[256,256]{1,0:T(8,128)(2,1)} %refs_0_.2, bf16[256,256]{1,0:T(8,128)(2,1)} %refs_1_.1, bf16[256,512]{1,0:T(8,128)(2,1)} %refs_2_.2), custom_call_target="tpu_custom_call" | custom-call | flops 1 | bytes 1 | tf_op jit(solution)/shard_map/pack/pallas_call | solution.py:87
  4.6 3.1 %collective-permute-start = (bf16[256,512]{1,0:T(8,128)(2,1)}, bf16[256,512]{1,0:T(8,128)(2,1)S(1)}, u32[]{:S(2)}, u32[]{:S(2)}) collective-permute-start(bf16[256,512]{1,0:T(8,128)(2,1)} %get-tuple-element.24.refs_0_), channel_id=1, source_target_pairs={{0,8},{4,12},{8,16},{12,20},{16,24},{20,28},{1,9},{5,13},{9,17},{1... | collective-permute-start | bytes 786440 | tf_op jit(solution)/shard_map/kv_near/ppermute | solution.py:410
  7.7 1.3 %collective-permute-start.1 = (bf16[256,512]{1,0:T(8,128)(2,1)}, bf16[256,512]{1,0:T(8,128)(2,1)S(1)}, u32[]{:S(2)}, u32[]{:S(2)}) collective-permute-start(bf16[256,512]{1,0:T(8,128)(2,1)} %get-tuple-element.24.refs_0_), channel_id=1, source_target_pairs={{0,16},{4,20},{8,24},{12,28},{1,17},{5,21},{9,25},{13,29},{2,18},{... | collective-permute-start | bytes 786440 | tf_op jit(solution)/shard_map/kv_far/ppermute | solution.py:410
  9.1 1.3 %collective-permute-start.3 = (bf16[256,512]{1,0:T(8,128)(2,1)}, bf16[256,512]{1,0:T(8,128)(2,1)S(1)}, u32[]{:S(2)}, u32[]{:S(2)}) collective-permute-start(bf16[256,512]{1,0:T(8,128)(2,1)} %get-tuple-element.25.refs_0_.refs_1_), channel_id=1, source_target_pairs={{16,0},{20,4},{24,8},{28,12},{17,1},{21,5},{25,9},{29,13},{18,2},{... | collective-permute-start | bytes 786440 | tf_op jit(solution)/shard_map/q_far/ppermute | solution.py:410
  10.4 3.2 %collective-permute-done.refs_2_ = bf16[256,512]{1,0:T(8,128)(2,1)S(1)} collective-permute-done((bf16[256,512]{1,0:T(8,128)(2,1)}, bf16[256,512]{1,0:T(8,128)(2,1)S(1)}, u32[]{:S(2)}, u32[]{:S(2)}) %collective-permute-start) | collective-permute-done | bytes 262176 | tf_op jit(solution)/shard_map/kv_near/ppermute | solution.py:410
  13.6 1.9 %collective-permute-start.4 = (bf16[256,512]{1,0:T(8,128)(2,1)}, bf16[256,512]{1,0:T(8,128)(2,1)S(1)}, u32[]{:S(2)}, u32[]{:S(2)}) collective-permute-start(bf16[256,512]{1,0:T(8,128)(2,1)} %get-tuple-element.25.refs_0_.refs_1_), channel_id=1, source_target_pairs={{8,0},{12,4},{16,8},{20,12},{24,16},{28,20},{9,1},{13,5},{17,9},{2... | collective-permute-start | bytes 786440 | tf_op jit(solution)/shard_map/q_near/ppermute | solution.py:410
  15.5 1.7 %collective-permute-done.6.refs_1_ = bf16[64,5376]{1,0:T(8,128)(2,1)S(1)} collective-permute-done((bf16[64,5376]{1,0:T(8,128)(2,1)}, bf16[64,5376]{1,0:T(8,128)(2,1)S(1)}, u32[]{:S(2)}, u32[]{:S(2)}) %collective-permute-start.6) | collective-permute-done | bytes 688160 | tf_op jit(solution)/shard_map/end_first/ppermute | solution.py:414
  17.2 0.7 collective-permute-start.7
  17.9 0.0 collective-permute-done.8.refs_2_
  17.9 1.3 %collective-permute-start.9 = (bf16[64,5376]{1,0:T(8,128)(2,1)S(1)}, bf16[64,5376]{1,0:T(8,128)(2,1)S(1)}, u32[]{:S(2)}, u32[]{:S(2)}) collective-permute-start(bf16[64,5376]{1,0:T(8,128)(2,1)S(1)} %collective-permute-done.8.refs_2_), channel_id=1, source_target_pairs={{1,0},{2,3},{5,4},{6,7},{9,8},{10,11},{13,12},{14,15},{17,16},{18,... | collective-permute-start | bytes 2064392 | tf_op jit(solution)/shard_map/out_second/ppermute | solution.py:414
  19.2 0.0 collective-permute-done.1.refs_1_.refs_3_
  19.2 0.0 copy-start.1
  19.2 0.9 %copy-done.1 = bf16[256,512]{1,0:T(8,128)(2,1)S(1)} copy-done((bf16[256,512]{1,0:T(8,128)(2,1)S(1)}, bf16[256,512]{1,0:T(8,128)(2,1)}, u32[]{:S(2)}) %copy-start.1) | copy-done | bytes 262168
  20.2 0.0 copy-start.2
  20.2 1.6 %collective-permute-start.2 = (bf16[512,512]{1,0:T(8,128)(2,1)S(1)}, bf16[512,512]{1,0:T(8,128)(2,1)S(1)}, u32[]{:S(2)}, u32[]{:S(2)}) collective-permute-start(bf16[512,512]{1,0:T(8,128)(2,1)S(1)} %pair.4), channel_id=1, source_target_pairs={{0,4},{4,0},{8,12},{12,8},{16,20},{20,16},{24,28},{28,24},{1,5},{5... | collective-permute-start | bytes 1572872 | tf_op jit(solution)/shard_map/kv_swap/ppermute | solution.py:410
  21.8 0.0 collective-permute-done.3.refs_1_.refs_3_.refs_2_
  21.8 0.7 %collective-permute-done.4.refs_2_.refs_1_ = bf16[256,512]{1,0:T(8,128)(2,1)S(1)} collective-permute-done((bf16[256,512]{1,0:T(8,128)(2,1)}, bf16[256,512]{1,0:T(8,128)(2,1)S(1)}, u32[]{:S(2)}, u32[]{:S(2)}) %collective-permute-start.4) | collective-permute-done | bytes 262176 | tf_op jit(solution)/shard_map/q_near/ppermute | solution.py:410
  22.6 0.0 copy-start.3
  22.6 0.9 %copy-done.3 = bf16[256,512]{1,0:T(8,128)(2,1)S(1)} copy-done((bf16[256,512]{1,0:T(8,128)(2,1)S(1)}, bf16[256,512]{1,0:T(8,128)(2,1)}, u32[]{:S(2)}) %copy-start.3) | copy-done | bytes 262168
  23.5 0.0 copy-start.5
  23.6 0.0 copy-start
  23.6 3.0 %collective-permute-start.5 = (bf16[512,512]{1,0:T(8,128)(2,1)S(1)}, bf16[512,512]{1,0:T(8,128)(2,1)S(1)}, u32[]{:S(2)}, u32[]{:S(2)}) collective-permute-start(bf16[512,512]{1,0:T(8,128)(2,1)S(1)} %pair.5), channel_id=1, source_target_pairs={{0,4},{4,0},{8,12},{12,8},{16,20},{20,16},{24,28},{28,24},{1,5},{5... | collective-permute-start | bytes 1572872 | tf_op jit(solution)/shard_map/q_swap/ppermute | solution.py:410
  26.6 0.0 collective-permute-done.2.refs_4_
  26.6 1.5 %collective-permute-done.5.refs_5_.refs_4_.refs_1_ = bf16[512,512]{1,0:T(8,128)(2,1)S(1)} collective-permute-done((bf16[512,512]{1,0:T(8,128)(2,1)S(1)}, bf16[512,512]{1,0:T(8,128)(2,1)S(1)}, u32[]{:S(2)}, u32[]{:S(2)}) %collective-permute-start.5) | collective-permute-done | bytes 524320 | tf_op jit(solution)/shard_map/q_swap/ppermute | solution.py:410
  28.1 0.0 copy-done.2
  28.1 3.6 %attention_probs.1 = (bf16[4,256,1280]{2,1,0:T(8,128)(2,1)S(1)}, f32[256,512]{1,0:T(8,128)S(1)}, bf16[256,128]{1,0:T(8,128)(2,1)S(1)}, bf16[1280,512]{1,0:T(8,128)(2,1)S(1)}) custom-call(bf16[256,512]{1,0:T(8,128)(2,1)S(1)} %copy-done.2, bf16[256,512]{1,0:T(8,128)(2,1)S(1)} %copy-done.3, bf16[256,512]{1,0:T(8,128)(2,1)S(1)} %collective-permute-done.refs_2_, ...), custom_call_target="tpu_custom_call" | custom-call | flops 1 | bytes 1 | tf_op jit(solution)/shard_map/attention_probs/pallas_call | solution.py:41
  31.7 0.0 collective-permute-done.7.refs_1_.refs_0_
  31.7 5.2 %collective-permute-done.9.refs_0_.refs_3_ = bf16[64,5376]{1,0:T(8,128)(2,1)S(1)} collective-permute-done((bf16[64,5376]{1,0:T(8,128)(2,1)S(1)}, bf16[64,5376]{1,0:T(8,128)(2,1)S(1)}, u32[]{:S(2)}, u32[]{:S(2)}) %collective-permute-start.9) | collective-permute-done | bytes 688160 | tf_op jit(solution)/shard_map/out_second/ppermute | solution.py:414
  36.9 1.3 %collective-permute-start.10 = (bf16[64,5376]{1,0:T(8,128)(2,1)S(1)}, bf16[64,5376]{1,0:T(8,128)(2,1)S(1)}, u32[]{:S(2)}, u32[]{:S(2)}) collective-permute-start(bf16[64,5376]{1,0:T(8,128)(2,1)S(1)} %collective-permute-done.7.refs_1_.refs_0_), channel_id=1, source_target_pairs={{1,0},{2,3},{5,4},{6,7},{9,8},{10,11},{13,12},{14,15},{17,16},{18,... | collective-permute-start | bytes 2064392 | tf_op jit(solution)/shard_map/out_third/ppermute | solution.py:414
  38.2 0.0 copy-done.5
  38.2 0.0 copy-done
  38.2 0.0 copy-start.4
  38.2 2.1 %dout_rows.2.refs_2_.refs_0_.refs_5_ = bf16[192,640]{1,0:T(8,128)(2,1)S(1)} custom-call(bf16[64,5376]{1,0:T(8,128)(2,1)S(1)} %copy-done.5, bf16[64,5376]{1,0:T(8,128)(2,1)S(1)} %collective-permute-done.6.refs_1_, bf16[64,5376]{1,0:T(8,128)(2,1)S(1)} %collective-permute-done.8.refs_2_, bf16[64,5376]{1,0:T(8,128)(2,1)S(1)} %collective-permute-done.9.refs_0_.refs_3_, ...), custom_call_target="tpu_custom_call" | custom-call | flops 1 | bytes 1 | tf_op jit(solution)/shard_map/dout_rows/pallas_call | solution.py:41
  40.3 1.3 %collective-permute-start.13 = (bf16[192,640]{1,0:T(8,128)(2,1)S(1)}, bf16[192,640]{1,0:T(8,128)(2,1)S(1)}, u32[]{:S(2)}, u32[]{:S(2)}) collective-permute-start(bf16[192,640]{1,0:T(8,128)(2,1)S(1)} %dout_rows.2.refs_2_.refs_0_.refs_5_), channel_id=1, source_target_pairs={{16,0},{20,4},{24,8},{28,12},{17,1},{21,5},{25,9},{29,13},{18,2},{... | collective-permute-start | bytes 737288 | tf_op jit(solution)/shard_map/early_far/ppermute | solution.py:410
  41.6 2.2 %collective-permute-start.14 = (bf16[192,640]{1,0:T(8,128)(2,1)S(1)}, bf16[192,640]{1,0:T(8,128)(2,1)S(1)}, u32[]{:S(2)}, u32[]{:S(2)}) collective-permute-start(bf16[192,640]{1,0:T(8,128)(2,1)S(1)} %dout_rows.2.refs_2_.refs_0_.refs_5_), channel_id=1, source_target_pairs={{8,0},{12,4},{16,8},{20,12},{24,16},{28,20},{9,1},{13,5},{17,9},{2... | collective-permute-start | bytes 737288 | tf_op jit(solution)/shard_map/early_near/ppermute | solution.py:410
  43.8 0.0 copy-done.4
  43.8 0.9 %key_grads.4 = (f32[256,256]{1,0:T(8,128)S(1)}, f32[256,256]{1,0:T(8,128)S(1)}) custom-call(bf16[256,512]{1,0:T(8,128)(2,1)S(1)} %copy-done.2, bf16[256,512]{1,0:T(8,128)(2,1)S(1)} %copy-done.4, bf16[192,640]{1,0:T(8,128)(2,1)S(1)} %dout_rows.2.refs_2_.refs_0_.refs_5_), custom_call_target="tpu_custom_call" | custom-call | flops 1 | bytes 1 | tf_op jit(solution)/shard_map/key_grads/pallas_call | solution.py:41
  44.7 2.1 %query_grads.2 = (f32[256,512]{1,0:T(8,128)}, f32[8,128]{1,0:T(8,128)S(1)}) custom-call(bf16[4,256,1280]{2,1,0:T(8,128)(2,1)S(1)} %get-tuple-element.26.refs_0_, bf16[1280,512]{1,0:T(8,128)(2,1)S(1)} %get-tuple-element.27.refs_1_, bf16[192,640]{1,0:T(8,128)(2,1)S(1)} %dout_rows.2.refs_2_.refs_0_.refs_5_), custom_call_target="tpu_custom_call" | custom-call | flops 1 | bytes 1 | tf_op jit(solution)/shard_map/query_grads/pallas_call | solution.py:41
  46.8 6.3 %collective-permute-done.13.refs_1_.refs_6_ = bf16[192,640]{1,0:T(8,128)(2,1)S(1)} collective-permute-done((bf16[192,640]{1,0:T(8,128)(2,1)S(1)}, bf16[192,640]{1,0:T(8,128)(2,1)S(1)}, u32[]{:S(2)}, u32[]{:S(2)}) %collective-permute-start.13) | collective-permute-done | bytes 245792 | tf_op jit(solution)/shard_map/early_far/ppermute | solution.py:410
  53.1 0.0 collective-permute-done.14.refs_2_.refs_7_
  53.1 2.8 %collective-permute-start.15 = (bf16[384,640]{1,0:T(8,128)(2,1)S(1)}, bf16[384,640]{1,0:T(8,128)(2,1)S(1)}, u32[]{:S(2)}, u32[]{:S(2)}) collective-permute-start(bf16[384,640]{1,0:T(8,128)(2,1)S(1)} %pair.6), channel_id=1, source_target_pairs={{0,4},{4,0},{8,12},{12,8},{16,20},{20,16},{24,28},{28,24},{1,5},{5... | collective-permute-start | bytes 1474568 | tf_op jit(solution)/shard_map/early_swap/ppermute | solution.py:410
  56.0 0.0 collective-permute-done.10.refs_1_
  56.0 1.8 %dout_rows.3.refs_2_.refs_9_.refs_0_ = bf16[64,640]{1,0:T(8,128)(2,1)S(1)} custom-call(bf16[64,5376]{1,0:T(8,128)(2,1)S(1)} %collective-permute-done.7.refs_1_.refs_0_, bf16[64,5376]{1,0:T(8,128)(2,1)S(1)} %collective-permute-done.10.refs_1_, bf16[512,5376]{1,0:T(8,128)(2,1)S(1)} %copy-done, f32[256,512]{1,0:T(8,128)S(1)} %get-tuple-element.30.refs_5_.refs_3_, ...), custom_call_target="tpu_custom_call" | custom-call | flops 1 | bytes 1 | tf_op jit(solution)/shard_map/dout_rows/pallas_call | solution.py:41
  57.8 1.3 %collective-permute-start.11 = (bf16[64,640]{1,0:T(8,128)(2,1)S(1)}, bf16[64,640]{1,0:T(8,128)(2,1)S(1)}, u32[]{:S(2)}, u32[]{:S(2)}) collective-permute-start(bf16[64,640]{1,0:T(8,128)(2,1)S(1)} %dout_rows.3.refs_2_.refs_9_.refs_0_), channel_id=1, source_target_pairs={{16,0},{20,4},{24,8},{28,12},{17,1},{21,5},{25,9},{29,13},{18,2},{... | collective-permute-start | bytes 245768 | tf_op jit(solution)/shard_map/late_far/ppermute | solution.py:410
  59.1 2.1 %collective-permute-start.12 = (bf16[64,640]{1,0:T(8,128)(2,1)S(1)}, bf16[64,640]{1,0:T(8,128)(2,1)S(1)}, u32[]{:S(2)}, u32[]{:S(2)}) collective-permute-start(bf16[64,640]{1,0:T(8,128)(2,1)S(1)} %dout_rows.3.refs_2_.refs_9_.refs_0_), channel_id=1, source_target_pairs={{8,0},{12,4},{16,8},{20,12},{24,16},{28,20},{9,1},{13,5},{17,9},{2... | collective-permute-start | bytes 245768 | tf_op jit(solution)/shard_map/late_near/ppermute | solution.py:410
  61.2 1.3 %query_grads.3 = (f32[256,512]{1,0:T(8,128)}, f32[8,128]{1,0:T(8,128)S(1)}) custom-call(bf16[4,256,1280]{2,1,0:T(8,128)(2,1)S(1)} %get-tuple-element.26.refs_0_, bf16[1280,512]{1,0:T(8,128)(2,1)S(1)} %get-tuple-element.27.refs_1_, bf16[64,640]{1,0:T(8,128)(2,1)S(1)} %dout_rows.3.refs_2_.refs_9_.refs_0_, ...), custom_call_target="tpu_custom_call", output_to_operand_aliasing={{0}: (3, {})} | custom-call | flops 1 | bytes 1 | tf_op jit(solution)/shard_map/query_grads/pallas_call | solution.py:41
  62.4 0.0 collective-permute-done.15.refs_8_
  62.4 2.5 %key_grads.5 = (f32[256,256]{1,0:T(8,128)S(1)}, f32[256,256]{1,0:T(8,128)S(1)}) custom-call(bf16[256,512]{1,0:T(8,128)(2,1)S(1)} %copy-done.2, bf16[256,512]{1,0:T(8,128)(2,1)S(1)} %copy-done.4, bf16[256,512]{1,0:T(8,128)(2,1)S(1)} %collective-permute-done.4.refs_2_.refs_1_, bf16[256,512]{1,0:T(8,128)(2,1)S(1)} %collective-permute-done.3.refs_1_.refs_3_.refs_2_, ...), custom_call_target="tpu_custom_call" | custom-call | flops 1 | bytes 1 | tf_op jit(solution)/shard_map/key_grads/pallas_call | solution.py:41
  64.9 0.0 collective-permute-done.11.refs_1_.refs_3_
  64.9 0.2 collective-permute-done.12.refs_2_.refs_4_
  65.2 1.9 %collective-permute-start.16 = (bf16[128,640]{1,0:T(8,128)(2,1)S(1)}, bf16[128,640]{1,0:T(8,128)(2,1)S(1)}, u32[]{:S(2)}, u32[]{:S(2)}) collective-permute-start(bf16[128,640]{1,0:T(8,128)(2,1)S(1)} %pair.7), channel_id=1, source_target_pairs={{0,4},{4,0},{8,12},{12,8},{16,20},{20,16},{24,28},{28,24},{1,5},{5... | collective-permute-start | bytes 491528 | tf_op jit(solution)/shard_map/late_swap/ppermute | solution.py:410
  67.0 0.8 %key_grads.6 = (f32[256,256]{1,0:T(8,128)S(1)}, f32[256,256]{1,0:T(8,128)S(1)}) custom-call(bf16[256,512]{1,0:T(8,128)(2,1)S(1)} %copy-done.2, bf16[256,512]{1,0:T(8,128)(2,1)S(1)} %collective-permute-done.4.refs_2_.refs_1_, bf16[256,512]{1,0:T(8,128)(2,1)S(1)} %collective-permute-done.3.refs_1_.refs_3_.refs_2_, ...), custom_call_target="tpu_custom_call" | custom-call | flops 1 | bytes 1 | tf_op jit(solution)/shard_map/key_grads/pallas_call | solution.py:41
  67.8 0.2 collective-permute-done.16.refs_2_
  68.1 1.5 %key_grads.7 = (f32[256,256]{1,0:T(8,128)}, f32[256,256]{1,0:T(8,128)}) custom-call(bf16[256,512]{1,0:T(8,128)(2,1)S(1)} %copy-done.2, bf16[512,512]{1,0:T(8,128)(2,1)S(1)} %collective-permute-done.5.refs_5_.refs_4_.refs_1_, bf16[128,640]{1,0:T(8,128)(2,1)S(1)} %collective-permute-done.16.refs_2_, f32[256,256]{1,0:T(8,128)S(1)} %get-tuple-element.41.refs_3_, ...), custom_call_target="tpu_custom_call" | custom-call | flops 1 | bytes 1 | tf_op jit(solution)/shard_map/key_grads/pallas_call | solution.py:41
  (5 shorter events, 0.1 us)
Async XLA Ops:
  0.6 16.6 %collective-permute-start.6 = (bf16[64,5376]{1,0:T(8,128)(2,1)}, bf16[64,5376]{1,0:T(8,128)(2,1)S(1)}, u32[]{:S(2)}, u32[]{:S(2)}) collective-permute-start(bf16[64,5376]{1,0:T(8,128)(2,1)} %refs_0_.3), channel_id=1, source_target_pairs={{0,1},{1,0},{2,3},{3,2},{4,5},{5,4},{6,7},{7,6},{8,9},{9,8},{10,11... | collective-permute-start | bytes 2064392 | tf_op jit(solution)/shard_map/end_first/ppermute | solution.py:414
  2.0 15.9 %collective-permute-start.8 = (bf16[64,5376]{1,0:T(8,128)(2,1)}, bf16[64,5376]{1,0:T(8,128)(2,1)S(1)}, u32[]{:S(2)}, u32[]{:S(2)}) collective-permute-start(bf16[64,5376]{1,0:T(8,128)(2,1)} %refs_0_.3), channel_id=1, source_target_pairs={{1,2},{2,1},{5,6},{6,5},{9,10},{10,9},{13,14},{14,13},{17,18},{18,... | collective-permute-start | bytes 2064392 | tf_op jit(solution)/shard_map/mid_first/ppermute | solution.py:414
  4.6 9.0 %collective-permute-start = (bf16[256,512]{1,0:T(8,128)(2,1)}, bf16[256,512]{1,0:T(8,128)(2,1)S(1)}, u32[]{:S(2)}, u32[]{:S(2)}) collective-permute-start(bf16[256,512]{1,0:T(8,128)(2,1)} %get-tuple-element.24.refs_0_), channel_id=1, source_target_pairs={{0,8},{4,12},{8,16},{12,20},{16,24},{20,28},{1,9},{5,13},{9,17},{1... | collective-permute-start | bytes 786440 | tf_op jit(solution)/shard_map/kv_near/ppermute | solution.py:410
  7.7 11.5 %collective-permute-start.1 = (bf16[256,512]{1,0:T(8,128)(2,1)}, bf16[256,512]{1,0:T(8,128)(2,1)S(1)}, u32[]{:S(2)}, u32[]{:S(2)}) collective-permute-start(bf16[256,512]{1,0:T(8,128)(2,1)} %get-tuple-element.24.refs_0_), channel_id=1, source_target_pairs={{0,16},{4,20},{8,24},{12,28},{1,17},{5,21},{9,25},{13,29},{2,18},{... | collective-permute-start | bytes 786440 | tf_op jit(solution)/shard_map/kv_far/ppermute | solution.py:410
  9.1 12.8 %collective-permute-start.3 = (bf16[256,512]{1,0:T(8,128)(2,1)}, bf16[256,512]{1,0:T(8,128)(2,1)S(1)}, u32[]{:S(2)}, u32[]{:S(2)}) collective-permute-start(bf16[256,512]{1,0:T(8,128)(2,1)} %get-tuple-element.25.refs_0_.refs_1_), channel_id=1, source_target_pairs={{16,0},{20,4},{24,8},{28,12},{17,1},{21,5},{25,9},{29,13},{18,2},{... | collective-permute-start | bytes 786440 | tf_op jit(solution)/shard_map/q_far/ppermute | solution.py:410
  13.6 9.0 %collective-permute-start.4 = (bf16[256,512]{1,0:T(8,128)(2,1)}, bf16[256,512]{1,0:T(8,128)(2,1)S(1)}, u32[]{:S(2)}, u32[]{:S(2)}) collective-permute-start(bf16[256,512]{1,0:T(8,128)(2,1)} %get-tuple-element.25.refs_0_.refs_1_), channel_id=1, source_target_pairs={{8,0},{12,4},{16,8},{20,12},{24,16},{28,20},{9,1},{13,5},{17,9},{2... | collective-permute-start | bytes 786440 | tf_op jit(solution)/shard_map/q_near/ppermute | solution.py:410
  17.2 14.5 %collective-permute-start.7 = (bf16[64,5376]{1,0:T(8,128)(2,1)S(1)}, bf16[64,5376]{1,0:T(8,128)(2,1)S(1)}, u32[]{:S(2)}, u32[]{:S(2)}) collective-permute-start(bf16[64,5376]{1,0:T(8,128)(2,1)S(1)} %collective-permute-done.6.refs_1_), channel_id=1, source_target_pairs={{1,2},{2,1},{5,6},{6,5},{9,10},{10,9},{13,14},{14,13},{17,18},{18,... | collective-permute-start | bytes 2064392 | tf_op jit(solution)/shard_map/mid_second/ppermute | solution.py:414
  17.9 19.0 %collective-permute-start.9 = (bf16[64,5376]{1,0:T(8,128)(2,1)S(1)}, bf16[64,5376]{1,0:T(8,128)(2,1)S(1)}, u32[]{:S(2)}, u32[]{:S(2)}) collective-permute-start(bf16[64,5376]{1,0:T(8,128)(2,1)S(1)} %collective-permute-done.8.refs_2_), channel_id=1, source_target_pairs={{1,0},{2,3},{5,4},{6,7},{9,8},{10,11},{13,12},{14,15},{17,16},{18,... | collective-permute-start | bytes 2064392 | tf_op jit(solution)/shard_map/out_second/ppermute | solution.py:414
  19.2 1.0 %copy-start.1 = (bf16[256,512]{1,0:T(8,128)(2,1)S(1)}, bf16[256,512]{1,0:T(8,128)(2,1)}, u32[]{:S(2)}) copy-start(bf16[256,512]{1,0:T(8,128)(2,1)} %get-tuple-element.24.refs_0_) | copy-start | bytes 786436
  20.2 7.9 %copy-start.2 = (bf16[256,512]{1,0:T(8,128)(2,1)S(1)}, bf16[256,512]{1,0:T(8,128)(2,1)}, u32[]{:S(2)}) copy-start(bf16[256,512]{1,0:T(8,128)(2,1)} %get-tuple-element.24.refs_0_) | copy-start | bytes 786436
  20.2 6.4 %collective-permute-start.2 = (bf16[512,512]{1,0:T(8,128)(2,1)S(1)}, bf16[512,512]{1,0:T(8,128)(2,1)S(1)}, u32[]{:S(2)}, u32[]{:S(2)}) collective-permute-start(bf16[512,512]{1,0:T(8,128)(2,1)S(1)} %pair.4), channel_id=1, source_target_pairs={{0,4},{4,0},{8,12},{12,8},{16,20},{20,16},{24,28},{28,24},{1,5},{5... | collective-permute-start | bytes 1572872 | tf_op jit(solution)/shard_map/kv_swap/ppermute | solution.py:410
  22.6 1.0 %copy-start.3 = (bf16[256,512]{1,0:T(8,128)(2,1)S(1)}, bf16[256,512]{1,0:T(8,128)(2,1)}, u32[]{:S(2)}) copy-start(bf16[256,512]{1,0:T(8,128)(2,1)} %get-tuple-element.25.refs_0_.refs_1_) | copy-start | bytes 786436
  23.5 14.7 %copy-start.5 = (bf16[64,5376]{1,0:T(8,128)(2,1)S(1)}, bf16[64,5376]{1,0:T(8,128)(2,1)}, u32[]{:S(2)}) copy-start(bf16[64,5376]{1,0:T(8,128)(2,1)} %refs_0_.3) | copy-start | bytes 2064388
  23.6 14.6 %copy-start = (bf16[512,5376]{1,0:T(8,128)(2,1)S(1)}, bf16[512,5376]{1,0:T(8,128)(2,1)}, u32[]{:S(2)}) copy-start(bf16[512,5376]{1,0:T(8,128)(2,1)} %refs_2_.3) | copy-start | bytes 16515076
  23.6 4.5 %collective-permute-start.5 = (bf16[512,512]{1,0:T(8,128)(2,1)S(1)}, bf16[512,512]{1,0:T(8,128)(2,1)S(1)}, u32[]{:S(2)}, u32[]{:S(2)}) collective-permute-start(bf16[512,512]{1,0:T(8,128)(2,1)S(1)} %pair.5), channel_id=1, source_target_pairs={{0,4},{4,0},{8,12},{12,8},{16,20},{20,16},{24,28},{28,24},{1,5},{5... | collective-permute-start | bytes 1572872 | tf_op jit(solution)/shard_map/q_swap/ppermute | solution.py:410
  36.9 19.1 %collective-permute-start.10 = (bf16[64,5376]{1,0:T(8,128)(2,1)S(1)}, bf16[64,5376]{1,0:T(8,128)(2,1)S(1)}, u32[]{:S(2)}, u32[]{:S(2)}) collective-permute-start(bf16[64,5376]{1,0:T(8,128)(2,1)S(1)} %collective-permute-done.7.refs_1_.refs_0_), channel_id=1, source_target_pairs={{1,0},{2,3},{5,4},{6,7},{9,8},{10,11},{13,12},{14,15},{17,16},{18,... | collective-permute-start | bytes 2064392 | tf_op jit(solution)/shard_map/out_third/ppermute | solution.py:414
  38.2 5.6 %copy-start.4 = (bf16[256,512]{1,0:T(8,128)(2,1)S(1)}, bf16[256,512]{1,0:T(8,128)(2,1)}, u32[]{:S(2)}) copy-start(bf16[256,512]{1,0:T(8,128)(2,1)} %get-tuple-element.25.refs_0_.refs_1_) | copy-start | bytes 786436
  40.3 12.8 %collective-permute-start.13 = (bf16[192,640]{1,0:T(8,128)(2,1)S(1)}, bf16[192,640]{1,0:T(8,128)(2,1)S(1)}, u32[]{:S(2)}, u32[]{:S(2)}) collective-permute-start(bf16[192,640]{1,0:T(8,128)(2,1)S(1)} %dout_rows.2.refs_2_.refs_0_.refs_5_), channel_id=1, source_target_pairs={{16,0},{20,4},{24,8},{28,12},{17,1},{21,5},{25,9},{29,13},{18,2},{... | collective-permute-start | bytes 737288 | tf_op jit(solution)/shard_map/early_far/ppermute | solution.py:410
  41.6 11.5 %collective-permute-start.14 = (bf16[192,640]{1,0:T(8,128)(2,1)S(1)}, bf16[192,640]{1,0:T(8,128)(2,1)S(1)}, u32[]{:S(2)}, u32[]{:S(2)}) collective-permute-start(bf16[192,640]{1,0:T(8,128)(2,1)S(1)} %dout_rows.2.refs_2_.refs_0_.refs_5_), channel_id=1, source_target_pairs={{8,0},{12,4},{16,8},{20,12},{24,16},{28,20},{9,1},{13,5},{17,9},{2... | collective-permute-start | bytes 737288 | tf_op jit(solution)/shard_map/early_near/ppermute | solution.py:410
  53.1 9.3 %collective-permute-start.15 = (bf16[384,640]{1,0:T(8,128)(2,1)S(1)}, bf16[384,640]{1,0:T(8,128)(2,1)S(1)}, u32[]{:S(2)}, u32[]{:S(2)}) collective-permute-start(bf16[384,640]{1,0:T(8,128)(2,1)S(1)} %pair.6), channel_id=1, source_target_pairs={{0,4},{4,0},{8,12},{12,8},{16,20},{20,16},{24,28},{28,24},{1,5},{5... | collective-permute-start | bytes 1474568 | tf_op jit(solution)/shard_map/early_swap/ppermute | solution.py:410
  57.8 7.2 %collective-permute-start.11 = (bf16[64,640]{1,0:T(8,128)(2,1)S(1)}, bf16[64,640]{1,0:T(8,128)(2,1)S(1)}, u32[]{:S(2)}, u32[]{:S(2)}) collective-permute-start(bf16[64,640]{1,0:T(8,128)(2,1)S(1)} %dout_rows.3.refs_2_.refs_9_.refs_0_), channel_id=1, source_target_pairs={{16,0},{20,4},{24,8},{28,12},{17,1},{21,5},{25,9},{29,13},{18,2},{... | collective-permute-start | bytes 245768 | tf_op jit(solution)/shard_map/late_far/ppermute | solution.py:410
  59.1 6.1 %collective-permute-start.12 = (bf16[64,640]{1,0:T(8,128)(2,1)S(1)}, bf16[64,640]{1,0:T(8,128)(2,1)S(1)}, u32[]{:S(2)}, u32[]{:S(2)}) collective-permute-start(bf16[64,640]{1,0:T(8,128)(2,1)S(1)} %dout_rows.3.refs_2_.refs_9_.refs_0_), channel_id=1, source_target_pairs={{8,0},{12,4},{16,8},{20,12},{24,16},{28,20},{9,1},{13,5},{17,9},{2... | collective-permute-start | bytes 245768 | tf_op jit(solution)/shard_map/late_near/ppermute | solution.py:410
  65.2 2.9 %collective-permute-start.16 = (bf16[128,640]{1,0:T(8,128)(2,1)S(1)}, bf16[128,640]{1,0:T(8,128)(2,1)S(1)}, u32[]{:S(2)}, u32[]{:S(2)}) collective-permute-start(bf16[128,640]{1,0:T(8,128)(2,1)S(1)} %pair.7), channel_id=1, source_target_pairs={{0,4},{4,0},{8,12},{12,8},{16,20},{20,16},{24,28},{28,24},{1,5},{5... | collective-permute-start | bytes 491528 | tf_op jit(solution)/shard_map/late_swap/ppermute | solution.py:410

commit v10 on v7

--- a/solution.py
+++ b/solution.py
@@ -227,7 +227,8 @@
             part = part + other[...]
         parts.append(part)
         at += n
-    product = dot(jnp.concatenate(parts, axis=0), weight[...], NT)
+    block = parts[0] if len(parts) == 1 else jnp.concatenate(parts, axis=0)
+    product = dot(weight[...], block, NT).T
     for n, slot in enumerate(slots):
         finish_rows(info, slot, product[n * rows : (n + 1) * rows], mixed, stats, pay, n * rows)
 
@@ -447,7 +448,7 @@
         near = along(pay, moved(-2), name + "_near")
         return near, far
 
-    second_came = token_of(token_of(out_second), mid_second, cost=FETCH)
+    second_came = token_of(out_second, mid_second, cost=FETCH)
     mid_second, second_came, stats = lax.optimization_barrier((mid_second, second_came, stats))
     out_third = over(mid_second, outward, "out_third")
     statistics = (out_weight, mixed, stats)

time: 70.8 us -> 70.6 us (level)
  waiting for transfers between devices: 14.2 us -> 19.1 us
  starting transfers between devices: 33.6 us -> 29.3 us
    ppermute x5, waiting for transfers between devices: 2.47 us -> 6.91 us  [over(): return lax.ppermute(x, 'tp', pairs)]
    ppermute x5, starting transfers between devices: 7.84 us -> 5.32 us  [over(): return lax.ppermute(x, 'tp', pairs)]
    ppermute x12, starting transfers between devices: 25.8 us -> 24 us  [along(): return lax.ppermute(x, 'ctx', pairs)]
  transfers between devices with their start and end apart: 17 -> 17, of which waited for: 8 -> 8; matrix products, arithmetic and copies ran while one was open for 0% -> 0% of each run, Pallas kernels for 25% -> 24%
where the time goes in v10:
time: 70.6 us; the launch traced here: 69.8 us
  starting transfers between devices  29.3 us (42%)
  waiting for transfers between devices  19.1 us (27%)
  Pallas kernels  18.4 us (26%)
  local copies, waits for them, and re-layouts  1.92 us (3%)
  between operations  1.08 us (2%)
    ppermute x12, starting transfers between devices, along(): return lax.ppermute(x, 'ctx', pairs)  24 us
    pallas_call x13, Pallas kernels, call(): pl.pallas_call(lambda *refs: kernel(device_info(info), *refs), out_shape=...  16.5 us
    ppermute x12, waiting for transfers between devices, along(): return lax.ppermute(x, 'ctx', pairs)  12.2 us
    ppermute x5, waiting for transfers between devices, over(): return lax.ppermute(x, 'tp', pairs)  6.91 us
    ppermute x5, starting transfers between devices, over(): return lax.ppermute(x, 'tp', pairs)  5.32 us
    unnamed x12, local copies, waits for them, and re-layouts  1.92 us
    pallas_call x1, Pallas kernels, pack(): pl.pallas_call(functools.partial(pack_kernel, places), out_shape=tuple((j...  1.9 us
  transfers between devices with their start and end apart: 17, of which 8 were waited for; matrix products, arithmetic and copies ran while one was open for 0% of the time, Pallas kernels for 24%

profile of v10, /device:TPU:3, one launch (start us, length us, event | category | flops | bytes accessed | tf_op | source)
XLA Modules:
  0.0 69.8 jit_solution(15752546224336257497)
XLA Ops:
  0.6 1.4 %collective-permute-start.6 = (bf16[64,5376]{1,0:T(8,128)(2,1)}, bf16[64,5376]{1,0:T(8,128)(2,1)S(1)}, u32[]{:S(2)}, u32[]{:S(2)}) collective-permute-start(bf16[64,5376]{1,0:T(8,128)(2,1)} %refs_0_.3), channel_id=1, source_target_pairs={{0,1},{1,0},{2,3},{3,2},{4,5},{5,4},{6,7},{7,6},{8,9},{9,8},{10,11... | collective-permute-start | bytes 2064392 | tf_op jit(solution)/shard_map/end_first/ppermute | solution.py:412
  2.0 0.7 collective-permute-start.8
  2.7 1.9 %pack.1 = (bf16[256,512]{1,0:T(8,128)(2,1)}, bf16[256,512]{1,0:T(8,128)(2,1)}) custom-call(bf16[256,256]{1,0:T(8,128)(2,1)} %refs_0_.2, bf16[256,256]{1,0:T(8,128)(2,1)} %refs_1_.1, bf16[256,512]{1,0:T(8,128)(2,1)} %refs_2_.2), custom_call_target="tpu_custom_call" | custom-call | flops 1 | bytes 1 | tf_op jit(solution)/shard_map/pack/pallas_call | solution.py:87
  4.6 3.1 %collective-permute-start = (bf16[256,512]{1,0:T(8,128)(2,1)}, bf16[256,512]{1,0:T(8,128)(2,1)S(1)}, u32[]{:S(2)}, u32[]{:S(2)}) collective-permute-start(bf16[256,512]{1,0:T(8,128)(2,1)} %get-tuple-element.24.refs_0_), channel_id=1, source_target_pairs={{0,8},{4,12},{8,16},{12,20},{16,24},{20,28},{1,9},{5,13},{9,17},{1... | collective-permute-start | bytes 786440 | tf_op jit(solution)/shard_map/kv_near/ppermute | solution.py:408
  7.7 1.3 %collective-permute-start.1 = (bf16[256,512]{1,0:T(8,128)(2,1)}, bf16[256,512]{1,0:T(8,128)(2,1)S(1)}, u32[]{:S(2)}, u32[]{:S(2)}) collective-permute-start(bf16[256,512]{1,0:T(8,128)(2,1)} %get-tuple-element.24.refs_0_), channel_id=1, source_target_pairs={{0,16},{4,20},{8,24},{12,28},{1,17},{5,21},{9,25},{13,29},{2,18},{... | collective-permute-start | bytes 786440 | tf_op jit(solution)/shard_map/kv_far/ppermute | solution.py:408
  9.1 1.3 %collective-permute-start.3 = (bf16[256,512]{1,0:T(8,128)(2,1)}, bf16[256,512]{1,0:T(8,128)(2,1)S(1)}, u32[]{:S(2)}, u32[]{:S(2)}) collective-permute-start(bf16[256,512]{1,0:T(8,128)(2,1)} %get-tuple-element.25.refs_0_.refs_1_), channel_id=1, source_target_pairs={{16,0},{20,4},{24,8},{28,12},{17,1},{21,5},{25,9},{29,13},{18,2},{... | collective-permute-start | bytes 786440 | tf_op jit(solution)/shard_map/q_far/ppermute | solution.py:408
  10.4 3.2 %collective-permute-done.refs_2_ = bf16[256,512]{1,0:T(8,128)(2,1)S(1)} collective-permute-done((bf16[256,512]{1,0:T(8,128)(2,1)}, bf16[256,512]{1,0:T(8,128)(2,1)S(1)}, u32[]{:S(2)}, u32[]{:S(2)}) %collective-permute-start) | collective-permute-done | bytes 262176 | tf_op jit(solution)/shard_map/kv_near/ppermute | solution.py:408
  13.6 1.9 %collective-permute-start.4 = (bf16[256,512]{1,0:T(8,128)(2,1)}, bf16[256,512]{1,0:T(8,128)(2,1)S(1)}, u32[]{:S(2)}, u32[]{:S(2)}) collective-permute-start(bf16[256,512]{1,0:T(8,128)(2,1)} %get-tuple-element.25.refs_0_.refs_1_), channel_id=1, source_target_pairs={{8,0},{12,4},{16,8},{20,12},{24,16},{28,20},{9,1},{13,5},{17,9},{2... | collective-permute-start | bytes 786440 | tf_op jit(solution)/shard_map/q_near/ppermute | solution.py:408
  15.5 1.7 %collective-permute-done.6.refs_1_ = bf16[64,5376]{1,0:T(8,128)(2,1)S(1)} collective-permute-done((bf16[64,5376]{1,0:T(8,128)(2,1)}, bf16[64,5376]{1,0:T(8,128)(2,1)S(1)}, u32[]{:S(2)}, u32[]{:S(2)}) %collective-permute-start.6) | collective-permute-done | bytes 688160 | tf_op jit(solution)/shard_map/end_first/ppermute | solution.py:412
  17.2 0.7 collective-permute-start.7
  17.9 0.0 collective-permute-done.8.refs_2_
  17.9 1.3 %collective-permute-start.9 = (bf16[64,5376]{1,0:T(8,128)(2,1)S(1)}, bf16[64,5376]{1,0:T(8,128)(2,1)S(1)}, u32[]{:S(2)}, u32[]{:S(2)}) collective-permute-start(bf16[64,5376]{1,0:T(8,128)(2,1)S(1)} %collective-permute-done.8.refs_2_), channel_id=1, source_target_pairs={{1,0},{2,3},{5,4},{6,7},{9,8},{10,11},{13,12},{14,15},{17,16},{18,... | collective-permute-start | bytes 2064392 | tf_op jit(solution)/shard_map/out_second/ppermute | solution.py:412
  19.2 0.0 collective-permute-done.1.refs_1_.refs_3_
  19.2 0.0 copy-start.1
  19.2 0.9 %copy-done.1 = bf16[256,512]{1,0:T(8,128)(2,1)S(1)} copy-done((bf16[256,512]{1,0:T(8,128)(2,1)S(1)}, bf16[256,512]{1,0:T(8,128)(2,1)}, u32[]{:S(2)}) %copy-start.1) | copy-done | bytes 262168
  20.2 0.0 copy-start.2
  20.2 1.6 %collective-permute-start.2 = (bf16[512,512]{1,0:T(8,128)(2,1)S(1)}, bf16[512,512]{1,0:T(8,128)(2,1)S(1)}, u32[]{:S(2)}, u32[]{:S(2)}) collective-permute-start(bf16[512,512]{1,0:T(8,128)(2,1)S(1)} %pair.4), channel_id=1, source_target_pairs={{0,4},{4,0},{8,12},{12,8},{16,20},{20,16},{24,28},{28,24},{1,5},{5... | collective-permute-start | bytes 1572872 | tf_op jit(solution)/shard_map/kv_swap/ppermute | solution.py:408
  21.8 0.0 collective-permute-done.3.refs_1_.refs_3_.refs_2_
  21.8 0.7 %collective-permute-done.4.refs_2_.refs_1_ = bf16[256,512]{1,0:T(8,128)(2,1)S(1)} collective-permute-done((bf16[256,512]{1,0:T(8,128)(2,1)}, bf16[256,512]{1,0:T(8,128)(2,1)S(1)}, u32[]{:S(2)}, u32[]{:S(2)}) %collective-permute-start.4) | collective-permute-done | bytes 262176 | tf_op jit(solution)/shard_map/q_near/ppermute | solution.py:408
  22.6 0.0 copy-start.3
  22.6 0.9 %copy-done.3 = bf16[256,512]{1,0:T(8,128)(2,1)S(1)} copy-done((bf16[256,512]{1,0:T(8,128)(2,1)S(1)}, bf16[256,512]{1,0:T(8,128)(2,1)}, u32[]{:S(2)}) %copy-start.3) | copy-done | bytes 262168
  23.5 0.0 copy-start.5
  23.6 0.0 copy-start
  23.6 3.0 %collective-permute-start.5 = (bf16[512,512]{1,0:T(8,128)(2,1)S(1)}, bf16[512,512]{1,0:T(8,128)(2,1)S(1)}, u32[]{:S(2)}, u32[]{:S(2)}) collective-permute-start(bf16[512,512]{1,0:T(8,128)(2,1)S(1)} %pair.5), channel_id=1, source_target_pairs={{0,4},{4,0},{8,12},{12,8},{16,20},{20,16},{24,28},{28,24},{1,5},{5... | collective-permute-start | bytes 1572872 | tf_op jit(solution)/shard_map/q_swap/ppermute | solution.py:408
  26.6 0.0 collective-permute-done.2.refs_4_
  26.6 1.5 %collective-permute-done.5.refs_5_.refs_4_.refs_1_ = bf16[512,512]{1,0:T(8,128)(2,1)S(1)} collective-permute-done((bf16[512,512]{1,0:T(8,128)(2,1)S(1)}, bf16[512,512]{1,0:T(8,128)(2,1)S(1)}, u32[]{:S(2)}, u32[]{:S(2)}) %collective-permute-start.5) | collective-permute-done | bytes 524320 | tf_op jit(solution)/shard_map/q_swap/ppermute | solution.py:408
  28.1 0.0 copy-done.2
  28.1 3.6 %attention_probs.1 = (bf16[4,256,1280]{2,1,0:T(8,128)(2,1)S(1)}, f32[256,512]{1,0:T(8,128)S(1)}, bf16[256,128]{1,0:T(8,128)(2,1)S(1)}, bf16[1280,512]{1,0:T(8,128)(2,1)S(1)}) custom-call(bf16[256,512]{1,0:T(8,128)(2,1)S(1)} %copy-done.2, bf16[256,512]{1,0:T(8,128)(2,1)S(1)} %copy-done.3, bf16[256,512]{1,0:T(8,128)(2,1)S(1)} %collective-permute-done.refs_2_, ...), custom_call_target="tpu_custom_call" | custom-call | flops 1 | bytes 1 | tf_op jit(solution)/shard_map/attention_probs/pallas_call | solution.py:41
  31.7 0.0 collective-permute-done.7.refs_1_.refs_0_
  31.7 5.2 %collective-permute-done.9.refs_0_.refs_3_ = bf16[64,5376]{1,0:T(8,128)(2,1)S(1)} collective-permute-done((bf16[64,5376]{1,0:T(8,128)(2,1)S(1)}, bf16[64,5376]{1,0:T(8,128)(2,1)S(1)}, u32[]{:S(2)}, u32[]{:S(2)}) %collective-permute-start.9) | collective-permute-done | bytes 688160 | tf_op jit(solution)/shard_map/out_second/ppermute | solution.py:412
  36.9 1.3 %collective-permute-start.10 = (bf16[64,5376]{1,0:T(8,128)(2,1)S(1)}, bf16[64,5376]{1,0:T(8,128)(2,1)S(1)}, u32[]{:S(2)}, u32[]{:S(2)}) collective-permute-start(bf16[64,5376]{1,0:T(8,128)(2,1)S(1)} %collective-permute-done.7.refs_1_.refs_0_), channel_id=1, source_target_pairs={{1,0},{2,3},{5,4},{6,7},{9,8},{10,11},{13,12},{14,15},{17,16},{18,... | collective-permute-start | bytes 2064392 | tf_op jit(solution)/shard_map/out_third/ppermute | solution.py:412
  38.2 0.0 copy-done.5
  38.2 0.0 copy-done
  38.2 0.0 copy-start.4
  38.2 1.9 %dout_rows.2.refs_2_.refs_0_.refs_5_ = bf16[192,640]{1,0:T(8,128)(2,1)S(1)} custom-call(bf16[64,5376]{1,0:T(8,128)(2,1)S(1)} %copy-done.5, bf16[64,5376]{1,0:T(8,128)(2,1)S(1)} %collective-permute-done.6.refs_1_, bf16[64,5376]{1,0:T(8,128)(2,1)S(1)} %collective-permute-done.8.refs_2_, bf16[64,5376]{1,0:T(8,128)(2,1)S(1)} %collective-permute-done.9.refs_0_.refs_3_, ...), custom_call_target="tpu_custom_call" | custom-call | flops 1 | bytes 1 | tf_op jit(solution)/shard_map/dout_rows/pallas_call | solution.py:41
  40.1 1.3 %collective-permute-start.13 = (bf16[192,640]{1,0:T(8,128)(2,1)S(1)}, bf16[192,640]{1,0:T(8,128)(2,1)S(1)}, u32[]{:S(2)}, u32[]{:S(2)}) collective-permute-start(bf16[192,640]{1,0:T(8,128)(2,1)S(1)} %dout_rows.2.refs_2_.refs_0_.refs_5_), channel_id=1, source_target_pairs={{16,0},{20,4},{24,8},{28,12},{17,1},{21,5},{25,9},{29,13},{18,2},{... | collective-permute-start | bytes 737288 | tf_op jit(solution)/shard_map/early_far/ppermute | solution.py:408
  41.4 2.2 %collective-permute-start.14 = (bf16[192,640]{1,0:T(8,128)(2,1)S(1)}, bf16[192,640]{1,0:T(8,128)(2,1)S(1)}, u32[]{:S(2)}, u32[]{:S(2)}) collective-permute-start(bf16[192,640]{1,0:T(8,128)(2,1)S(1)} %dout_rows.2.refs_2_.refs_0_.refs_5_), channel_id=1, source_target_pairs={{8,0},{12,4},{16,8},{20,12},{24,16},{28,20},{9,1},{13,5},{17,9},{2... | collective-permute-start | bytes 737288 | tf_op jit(solution)/shard_map/early_near/ppermute | solution.py:408
  43.6 0.0 copy-done.4
  43.6 0.9 %key_grads.4 = (f32[256,256]{1,0:T(8,128)S(1)}, f32[256,256]{1,0:T(8,128)S(1)}) custom-call(bf16[256,512]{1,0:T(8,128)(2,1)S(1)} %copy-done.2, bf16[256,512]{1,0:T(8,128)(2,1)S(1)} %copy-done.4, bf16[192,640]{1,0:T(8,128)(2,1)S(1)} %dout_rows.2.refs_2_.refs_0_.refs_5_), custom_call_target="tpu_custom_call" | custom-call | flops 1 | bytes 1 | tf_op jit(solution)/shard_map/key_grads/pallas_call | solution.py:41
  44.5 2.1 %query_grads.2 = (f32[256,512]{1,0:T(8,128)}, f32[8,128]{1,0:T(8,128)S(1)}) custom-call(bf16[4,256,1280]{2,1,0:T(8,128)(2,1)S(1)} %get-tuple-element.26.refs_0_, bf16[1280,512]{1,0:T(8,128)(2,1)S(1)} %get-tuple-element.27.refs_1_, bf16[192,640]{1,0:T(8,128)(2,1)S(1)} %dout_rows.2.refs_2_.refs_0_.refs_5_), custom_call_target="tpu_custom_call" | custom-call | flops 1 | bytes 1 | tf_op jit(solution)/shard_map/query_grads/pallas_call | solution.py:41
  46.6 6.3 %collective-permute-done.13.refs_1_.refs_6_ = bf16[192,640]{1,0:T(8,128)(2,1)S(1)} collective-permute-done((bf16[192,640]{1,0:T(8,128)(2,1)S(1)}, bf16[192,640]{1,0:T(8,128)(2,1)S(1)}, u32[]{:S(2)}, u32[]{:S(2)}) %collective-permute-start.13) | collective-permute-done | bytes 245792 | tf_op jit(solution)/shard_map/early_far/ppermute | solution.py:408
  52.9 0.0 collective-permute-done.14.refs_2_.refs_7_
  52.9 2.8 %collective-permute-start.15 = (bf16[384,640]{1,0:T(8,128)(2,1)S(1)}, bf16[384,640]{1,0:T(8,128)(2,1)S(1)}, u32[]{:S(2)}, u32[]{:S(2)}) collective-permute-start(bf16[384,640]{1,0:T(8,128)(2,1)S(1)} %pair.6), channel_id=1, source_target_pairs={{0,4},{4,0},{8,12},{12,8},{16,20},{20,16},{24,28},{28,24},{1,5},{5... | collective-permute-start | bytes 1474568 | tf_op jit(solution)/shard_map/early_swap/ppermute | solution.py:408
  55.8 0.0 collective-permute-done.10.refs_1_
  55.8 1.8 %dout_rows.3.refs_2_.refs_9_.refs_0_ = bf16[64,640]{1,0:T(8,128)(2,1)S(1)} custom-call(bf16[64,5376]{1,0:T(8,128)(2,1)S(1)} %collective-permute-done.7.refs_1_.refs_0_, bf16[64,5376]{1,0:T(8,128)(2,1)S(1)} %collective-permute-done.10.refs_1_, bf16[512,5376]{1,0:T(8,128)(2,1)S(1)} %copy-done, f32[256,512]{1,0:T(8,128)S(1)} %get-tuple-element.30.refs_5_.refs_3_, ...), custom_call_target="tpu_custom_call" | custom-call | flops 1 | bytes 1 | tf_op jit(solution)/shard_map/dout_rows/pallas_call | solution.py:41
  57.5 1.3 %collective-permute-start.11 = (bf16[64,640]{1,0:T(8,128)(2,1)S(1)}, bf16[64,640]{1,0:T(8,128)(2,1)S(1)}, u32[]{:S(2)}, u32[]{:S(2)}) collective-permute-start(bf16[64,640]{1,0:T(8,128)(2,1)S(1)} %dout_rows.3.refs_2_.refs_9_.refs_0_), channel_id=1, source_target_pairs={{16,0},{20,4},{24,8},{28,12},{17,1},{21,5},{25,9},{29,13},{18,2},{... | collective-permute-start | bytes 245768 | tf_op jit(solution)/shard_map/late_far/ppermute | solution.py:408
  58.9 2.1 %collective-permute-start.12 = (bf16[64,640]{1,0:T(8,128)(2,1)S(1)}, bf16[64,640]{1,0:T(8,128)(2,1)S(1)}, u32[]{:S(2)}, u32[]{:S(2)}) collective-permute-start(bf16[64,640]{1,0:T(8,128)(2,1)S(1)} %dout_rows.3.refs_2_.refs_9_.refs_0_), channel_id=1, source_target_pairs={{8,0},{12,4},{16,8},{20,12},{24,16},{28,20},{9,1},{13,5},{17,9},{2... | collective-permute-start | bytes 245768 | tf_op jit(solution)/shard_map/late_near/ppermute | solution.py:408
  61.0 1.3 %query_grads.3 = (f32[256,512]{1,0:T(8,128)}, f32[8,128]{1,0:T(8,128)S(1)}) custom-call(bf16[4,256,1280]{2,1,0:T(8,128)(2,1)S(1)} %get-tuple-element.26.refs_0_, bf16[1280,512]{1,0:T(8,128)(2,1)S(1)} %get-tuple-element.27.refs_1_, bf16[64,640]{1,0:T(8,128)(2,1)S(1)} %dout_rows.3.refs_2_.refs_9_.refs_0_, ...), custom_call_target="tpu_custom_call", output_to_operand_aliasing={{0}: (3, {})} | custom-call | flops 1 | bytes 1 | tf_op jit(solution)/shard_map/query_grads/pallas_call | solution.py:41
  62.2 0.0 collective-permute-done.15.refs_8_
  62.2 2.5 %key_grads.5 = (f32[256,256]{1,0:T(8,128)S(1)}, f32[256,256]{1,0:T(8,128)S(1)}) custom-call(bf16[256,512]{1,0:T(8,128)(2,1)S(1)} %copy-done.2, bf16[256,512]{1,0:T(8,128)(2,1)S(1)} %copy-done.4, bf16[256,512]{1,0:T(8,128)(2,1)S(1)} %collective-permute-done.4.refs_2_.refs_1_, bf16[256,512]{1,0:T(8,128)(2,1)S(1)} %collective-permute-done.3.refs_1_.refs_3_.refs_2_, ...), custom_call_target="tpu_custom_call" | custom-call | flops 1 | bytes 1 | tf_op jit(solution)/shard_map/key_grads/pallas_call | solution.py:41
  64.7 0.0 collective-permute-done.11.refs_1_.refs_3_
  64.7 0.2 collective-permute-done.12.refs_2_.refs_4_
  65.0 2.1 %collective-permute-start.16 = (bf16[128,640]{1,0:T(8,128)(2,1)S(1)}, bf16[128,640]{1,0:T(8,128)(2,1)S(1)}, u32[]{:S(2)}, u32[]{:S(2)}) collective-permute-start(bf16[128,640]{1,0:T(8,128)(2,1)S(1)} %pair.7), channel_id=1, source_target_pairs={{0,4},{4,0},{8,12},{12,8},{16,20},{20,16},{24,28},{28,24},{1,5},{5... | collective-permute-start | bytes 491528 | tf_op jit(solution)/shard_map/late_swap/ppermute | solution.py:408
  67.0 0.8 %key_grads.6 = (f32[256,256]{1,0:T(8,128)S(1)}, f32[256,256]{1,0:T(8,128)S(1)}) custom-call(bf16[256,512]{1,0:T(8,128)(2,1)S(1)} %copy-done.2, bf16[256,512]{1,0:T(8,128)(2,1)S(1)} %collective-permute-done.4.refs_2_.refs_1_, bf16[256,512]{1,0:T(8,128)(2,1)S(1)} %collective-permute-done.3.refs_1_.refs_3_.refs_2_, ...), custom_call_target="tpu_custom_call" | custom-call | flops 1 | bytes 1 | tf_op jit(solution)/shard_map/key_grads/pallas_call | solution.py:41
  67.8 0.2 collective-permute-done.16.refs_2_
  68.1 1.5 %key_grads.7 = (f32[256,256]{1,0:T(8,128)}, f32[256,256]{1,0:T(8,128)}) custom-call(bf16[256,512]{1,0:T(8,128)(2,1)S(1)} %copy-done.2, bf16[512,512]{1,0:T(8,128)(2,1)S(1)} %collective-permute-done.5.refs_5_.refs_4_.refs_1_, bf16[128,640]{1,0:T(8,128)(2,1)S(1)} %collective-permute-done.16.refs_2_, f32[256,256]{1,0:T(8,128)S(1)} %get-tuple-element.41.refs_3_, ...), custom_call_target="tpu_custom_call" | custom-call | flops 1 | bytes 1 | tf_op jit(solution)/shard_map/key_grads/pallas_call | solution.py:41
  (5 shorter events, 0.1 us)
Async XLA Ops:
  0.6 16.6 %collective-permute-start.6 = (bf16[64,5376]{1,0:T(8,128)(2,1)}, bf16[64,5376]{1,0:T(8,128)(2,1)S(1)}, u32[]{:S(2)}, u32[]{:S(2)}) collective-permute-start(bf16[64,5376]{1,0:T(8,128)(2,1)} %refs_0_.3), channel_id=1, source_target_pairs={{0,1},{1,0},{2,3},{3,2},{4,5},{5,4},{6,7},{7,6},{8,9},{9,8},{10,11... | collective-permute-start | bytes 2064392 | tf_op jit(solution)/shard_map/end_first/ppermute | solution.py:412
  2.0 15.9 %collective-permute-start.8 = (bf16[64,5376]{1,0:T(8,128)(2,1)}, bf16[64,5376]{1,0:T(8,128)(2,1)S(1)}, u32[]{:S(2)}, u32[]{:S(2)}) collective-permute-start(bf16[64,5376]{1,0:T(8,128)(2,1)} %refs_0_.3), channel_id=1, source_target_pairs={{1,2},{2,1},{5,6},{6,5},{9,10},{10,9},{13,14},{14,13},{17,18},{18,... | collective-permute-start | bytes 2064392 | tf_op jit(solution)/shard_map/mid_first/ppermute | solution.py:412
  4.6 9.0 %collective-permute-start = (bf16[256,512]{1,0:T(8,128)(2,1)}, bf16[256,512]{1,0:T(8,128)(2,1)S(1)}, u32[]{:S(2)}, u32[]{:S(2)}) collective-permute-start(bf16[256,512]{1,0:T(8,128)(2,1)} %get-tuple-element.24.refs_0_), channel_id=1, source_target_pairs={{0,8},{4,12},{8,16},{12,20},{16,24},{20,28},{1,9},{5,13},{9,17},{1... | collective-permute-start | bytes 786440 | tf_op jit(solution)/shard_map/kv_near/ppermute | solution.py:408
  7.7 11.5 %collective-permute-start.1 = (bf16[256,512]{1,0:T(8,128)(2,1)}, bf16[256,512]{1,0:T(8,128)(2,1)S(1)}, u32[]{:S(2)}, u32[]{:S(2)}) collective-permute-start(bf16[256,512]{1,0:T(8,128)(2,1)} %get-tuple-element.24.refs_0_), channel_id=1, source_target_pairs={{0,16},{4,20},{8,24},{12,28},{1,17},{5,21},{9,25},{13,29},{2,18},{... | collective-permute-start | bytes 786440 | tf_op jit(solution)/shard_map/kv_far/ppermute | solution.py:408
  9.1 12.8 %collective-permute-start.3 = (bf16[256,512]{1,0:T(8,128)(2,1)}, bf16[256,512]{1,0:T(8,128)(2,1)S(1)}, u32[]{:S(2)}, u32[]{:S(2)}) collective-permute-start(bf16[256,512]{1,0:T(8,128)(2,1)} %get-tuple-element.25.refs_0_.refs_1_), channel_id=1, source_target_pairs={{16,0},{20,4},{24,8},{28,12},{17,1},{21,5},{25,9},{29,13},{18,2},{... | collective-permute-start | bytes 786440 | tf_op jit(solution)/shard_map/q_far/ppermute | solution.py:408
  13.6 9.0 %collective-permute-start.4 = (bf16[256,512]{1,0:T(8,128)(2,1)}, bf16[256,512]{1,0:T(8,128)(2,1)S(1)}, u32[]{:S(2)}, u32[]{:S(2)}) collective-permute-start(bf16[256,512]{1,0:T(8,128)(2,1)} %get-tuple-element.25.refs_0_.refs_1_), channel_id=1, source_target_pairs={{8,0},{12,4},{16,8},{20,12},{24,16},{28,20},{9,1},{13,5},{17,9},{2... | collective-permute-start | bytes 786440 | tf_op jit(solution)/shard_map/q_near/ppermute | solution.py:408
  17.2 14.5 %collective-permute-start.7 = (bf16[64,5376]{1,0:T(8,128)(2,1)S(1)}, bf16[64,5376]{1,0:T(8,128)(2,1)S(1)}, u32[]{:S(2)}, u32[]{:S(2)}) collective-permute-start(bf16[64,5376]{1,0:T(8,128)(2,1)S(1)} %collective-permute-done.6.refs_1_), channel_id=1, source_target_pairs={{1,2},{2,1},{5,6},{6,5},{9,10},{10,9},{13,14},{14,13},{17,18},{18,... | collective-permute-start | bytes 2064392 | tf_op jit(solution)/shard_map/mid_second/ppermute | solution.py:412
  17.9 19.0 %collective-permute-start.9 = (bf16[64,5376]{1,0:T(8,128)(2,1)S(1)}, bf16[64,5376]{1,0:T(8,128)(2,1)S(1)}, u32[]{:S(2)}, u32[]{:S(2)}) collective-permute-start(bf16[64,5376]{1,0:T(8,128)(2,1)S(1)} %collective-permute-done.8.refs_2_), channel_id=1, source_target_pairs={{1,0},{2,3},{5,4},{6,7},{9,8},{10,11},{13,12},{14,15},{17,16},{18,... | collective-permute-start | bytes 2064392 | tf_op jit(solution)/shard_map/out_second/ppermute | solution.py:412
  19.2 1.0 %copy-start.1 = (bf16[256,512]{1,0:T(8,128)(2,1)S(1)}, bf16[256,512]{1,0:T(8,128)(2,1)}, u32[]{:S(2)}) copy-start(bf16[256,512]{1,0:T(8,128)(2,1)} %get-tuple-element.24.refs_0_) | copy-start | bytes 786436
  20.2 7.9 %copy-start.2 = (bf16[256,512]{1,0:T(8,128)(2,1)S(1)}, bf16[256,512]{1,0:T(8,128)(2,1)}, u32[]{:S(2)}) copy-start(bf16[256,512]{1,0:T(8,128)(2,1)} %get-tuple-element.24.refs_0_) | copy-start | bytes 786436
  20.2 6.4 %collective-permute-start.2 = (bf16[512,512]{1,0:T(8,128)(2,1)S(1)}, bf16[512,512]{1,0:T(8,128)(2,1)S(1)}, u32[]{:S(2)}, u32[]{:S(2)}) collective-permute-start(bf16[512,512]{1,0:T(8,128)(2,1)S(1)} %pair.4), channel_id=1, source_target_pairs={{0,4},{4,0},{8,12},{12,8},{16,20},{20,16},{24,28},{28,24},{1,5},{5... | collective-permute-start | bytes 1572872 | tf_op jit(solution)/shard_map/kv_swap/ppermute | solution.py:408
  22.6 1.0 %copy-start.3 = (bf16[256,512]{1,0:T(8,128)(2,1)S(1)}, bf16[256,512]{1,0:T(8,128)(2,1)}, u32[]{:S(2)}) copy-start(bf16[256,512]{1,0:T(8,128)(2,1)} %get-tuple-element.25.refs_0_.refs_1_) | copy-start | bytes 786436
  23.5 14.7 %copy-start.5 = (bf16[64,5376]{1,0:T(8,128)(2,1)S(1)}, bf16[64,5376]{1,0:T(8,128)(2,1)}, u32[]{:S(2)}) copy-start(bf16[64,5376]{1,0:T(8,128)(2,1)} %refs_0_.3) | copy-start | bytes 2064388
  23.6 14.6 %copy-start = (bf16[512,5376]{1,0:T(8,128)(2,1)S(1)}, bf16[512,5376]{1,0:T(8,128)(2,1)}, u32[]{:S(2)}) copy-start(bf16[512,5376]{1,0:T(8,128)(2,1)} %refs_2_.3) | copy-start | bytes 16515076
  23.6 4.5 %collective-permute-start.5 = (bf16[512,512]{1,0:T(8,128)(2,1)S(1)}, bf16[512,512]{1,0:T(8,128)(2,1)S(1)}, u32[]{:S(2)}, u32[]{:S(2)}) collective-permute-start(bf16[512,512]{1,0:T(8,128)(2,1)S(1)} %pair.5), channel_id=1, source_target_pairs={{0,4},{4,0},{8,12},{12,8},{16,20},{20,16},{24,28},{28,24},{1,5},{5... | collective-permute-start | bytes 1572872 | tf_op jit(solution)/shard_map/q_swap/ppermute | solution.py:408
  36.9 18.9 %collective-permute-start.10 = (bf16[64,5376]{1,0:T(8,128)(2,1)S(1)}, bf16[64,5376]{1,0:T(8,128)(2,1)S(1)}, u32[]{:S(2)}, u32[]{:S(2)}) collective-permute-start(bf16[64,5376]{1,0:T(8,128)(2,1)S(1)} %collective-permute-done.7.refs_1_.refs_0_), channel_id=1, source_target_pairs={{1,0},{2,3},{5,4},{6,7},{9,8},{10,11},{13,12},{14,15},{17,16},{18,... | collective-permute-start | bytes 2064392 | tf_op jit(solution)/shard_map/out_third/ppermute | solution.py:412
  38.2 5.4 %copy-start.4 = (bf16[256,512]{1,0:T(8,128)(2,1)S(1)}, bf16[256,512]{1,0:T(8,128)(2,1)}, u32[]{:S(2)}) copy-start(bf16[256,512]{1,0:T(8,128)(2,1)} %get-tuple-element.25.refs_0_.refs_1_) | copy-start | bytes 786436
  40.1 12.8 %collective-permute-start.13 = (bf16[192,640]{1,0:T(8,128)(2,1)S(1)}, bf16[192,640]{1,0:T(8,128)(2,1)S(1)}, u32[]{:S(2)}, u32[]{:S(2)}) collective-permute-start(bf16[192,640]{1,0:T(8,128)(2,1)S(1)} %dout_rows.2.refs_2_.refs_0_.refs_5_), channel_id=1, source_target_pairs={{16,0},{20,4},{24,8},{28,12},{17,1},{21,5},{25,9},{29,13},{18,2},{... | collective-permute-start | bytes 737288 | tf_op jit(solution)/shard_map/early_far/ppermute | solution.py:408
  41.4 11.5 %collective-permute-start.14 = (bf16[192,640]{1,0:T(8,128)(2,1)S(1)}, bf16[192,640]{1,0:T(8,128)(2,1)S(1)}, u32[]{:S(2)}, u32[]{:S(2)}) collective-permute-start(bf16[192,640]{1,0:T(8,128)(2,1)S(1)} %dout_rows.2.refs_2_.refs_0_.refs_5_), channel_id=1, source_target_pairs={{8,0},{12,4},{16,8},{20,12},{24,16},{28,20},{9,1},{13,5},{17,9},{2... | collective-permute-start | bytes 737288 | tf_op jit(solution)/shard_map/early_near/ppermute | solution.py:408
  52.9 9.3 %collective-permute-start.15 = (bf16[384,640]{1,0:T(8,128)(2,1)S(1)}, bf16[384,640]{1,0:T(8,128)(2,1)S(1)}, u32[]{:S(2)}, u32[]{:S(2)}) collective-permute-start(bf16[384,640]{1,0:T(8,128)(2,1)S(1)} %pair.6), channel_id=1, source_target_pairs={{0,4},{4,0},{8,12},{12,8},{16,20},{20,16},{24,28},{28,24},{1,5},{5... | collective-permute-start | bytes 1474568 | tf_op jit(solution)/shard_map/early_swap/ppermute | solution.py:408
  57.5 7.2 %collective-permute-start.11 = (bf16[64,640]{1,0:T(8,128)(2,1)S(1)}, bf16[64,640]{1,0:T(8,128)(2,1)S(1)}, u32[]{:S(2)}, u32[]{:S(2)}) collective-permute-start(bf16[64,640]{1,0:T(8,128)(2,1)S(1)} %dout_rows.3.refs_2_.refs_9_.refs_0_), channel_id=1, source_target_pairs={{16,0},{20,4},{24,8},{28,12},{17,1},{21,5},{25,9},{29,13},{18,2},{... | collective-permute-start | bytes 245768 | tf_op jit(solution)/shard_map/late_far/ppermute | solution.py:408
  58.9 6.1 %collective-permute-start.12 = (bf16[64,640]{1,0:T(8,128)(2,1)S(1)}, bf16[64,640]{1,0:T(8,128)(2,1)S(1)}, u32[]{:S(2)}, u32[]{:S(2)}) collective-permute-start(bf16[64,640]{1,0:T(8,128)(2,1)S(1)} %dout_rows.3.refs_2_.refs_9_.refs_0_), channel_id=1, source_target_pairs={{8,0},{12,4},{16,8},{20,12},{24,16},{28,20},{9,1},{13,5},{17,9},{2... | collective-permute-start | bytes 245768 | tf_op jit(solution)/shard_map/late_near/ppermute | solution.py:408
  65.0 3.1 %collective-permute-start.16 = (bf16[128,640]{1,0:T(8,128)(2,1)S(1)}, bf16[128,640]{1,0:T(8,128)(2,1)S(1)}, u32[]{:S(2)}, u32[]{:S(2)}) collective-permute-start(bf16[128,640]{1,0:T(8,128)(2,1)S(1)} %pair.7), channel_id=1, source_target_pairs={{0,4},{4,0},{8,12},{12,8},{16,20},{20,16},{24,28},{28,24},{1,5},{5... | collective-permute-start | bytes 491528 | tf_op jit(solution)/shard_map/late_swap/ppermute | solution.py:408

commit v11 on v10

--- a/solution.py
+++ b/solution.py
@@ -240,7 +240,7 @@
     return call(functools.partial(dout_kernel, slots), "dout_rows", shape, info, arrays)
 
 
-def query_kernel(slots, count, info, probs, span, *refs):
+def query_kernel(slots, count, info, probs, span, *refs, then=lambda: None):
     out, done, held, sems = refs[-4:]
     done[...] = jnp.zeros_like(done)
     pay = stacked(refs[:count])
@@ -280,6 +280,7 @@
     ]
     for copy in copies:
         copy.start()
+    then()
     for copy in copies:
         copy.wait()
 
@@ -397,6 +398,40 @@
     )
 
 
+def late_kernel(slots, blocks, counts, info, probs, span, pay, *refs):
+    out, done, grad_k, grad_v, held, sems, q_cat, d_cat = refs[-8:]
+    arrays = refs[: 1 + sum(counts)]
+    query_kernel(
+        slots, 1, info, probs, span, pay, out, done, held, sems,
+        then=lambda: key_kernel(
+            blocks, *counts, False, info, *arrays, grad_k, grad_v, q_cat, d_cat
+        ),
+    )
+
+
+def late_grads(info, slots, pay, probs, span, grad_q, blocks, kv, q_arrays, d_arrays, slot_rows, before):
+    heads, rows, _ = probs.shape
+    lanes = sum(len(block[1]) for block in blocks) * slot_rows
+    width = heads * HD
+    shape = jax.ShapeDtypeStruct((rows, kv.shape[1] // 2), F32)
+    counts = (len(q_arrays), len(d_arrays), len(before))
+    return call(
+        functools.partial(late_kernel, slots, blocks, counts),
+        "late_grads",
+        (jax.ShapeDtypeStruct((rows, width), F32), TOKEN, shape, shape),
+        info,
+        (probs, span, pay, kv, *q_arrays, *d_arrays, *before),
+        [
+            pltpu.VMEM((pay.shape[0], width), F32),
+            pltpu.SemaphoreType.DMA((len(slots),)),
+            pltpu.VMEM((lanes, width), BF16),
+            pltpu.VMEM((lanes, width + HD), BF16),
+        ],
+        outs=(ANY, VMEM, VMEM, VMEM),
+        in_place=(grad_q,),
+    )
+
+
 def on_device(ctx, queries, keys, values, grad_out, out_weight):
     rows, width = queries.shape
     kv_width = 2 * keys.shape[1]
@@ -464,7 +499,6 @@
 
     pay_b = dout_rows(info, late, (mid_second, out_third), *statistics, (queries_done,))
     near_b, far_b = sent(pay_b, "late")
-    grad_q, queries_done = query_grads(info, late, (pay_b,), probs, span, (grad_q,))
     blocks = (
         (2, a, 1, 0, 2, 0),
         (4, a, 2, 0, 1, 0),
@@ -474,7 +508,9 @@
     )
     q_arrays = (query, near_q, far_q, odd_q)
     d_arrays = (pay_a, far_a, near_a, odd_a, pay_b)
-    grads = key_grads(info, blocks, kv, q_arrays, d_arrays, slot_rows, grads)
+    grad_q, queries_done, *grads = late_grads(
+        info, late, pay_b, probs, span, grad_q, blocks, kv, q_arrays, d_arrays, slot_rows, grads
+    )
     after = (queries_done, grads[0])
     pair = pair_for_peer(info, 1, (pay_b,), (near_b,), (far_b,), after)
     odd_b = along(pair, swap, "late_swap")

time: 70.6 us -> 70.6 us (level)
    pallas_call x13 -> x12, Pallas kernels: 16.5 us -> 16.3 us  [call(): pl.pallas_call(lambda *refs: kernel(device_info(info), *refs), out_shape=...]
where the time goes in v11:
time: 70.6 us; the launch traced here: 69.8 us
  starting transfers between devices  29.3 us (42%)
  waiting for transfers between devices  19.3 us (27%)
  Pallas kernels  18.2 us (26%)
  local copies, waits for them, and re-layouts  1.92 us (3%)
  between operations  1.07 us (2%)
    ppermute x12, starting transfers between devices, along(): return lax.ppermute(x, 'ctx', pairs)  24 us
    pallas_call x12, Pallas kernels, call(): pl.pallas_call(lambda *refs: kernel(device_info(info), *refs), out_shape=...  16.3 us
    ppermute x12, waiting for transfers between devices, along(): return lax.ppermute(x, 'ctx', pairs)  12.5 us
    ppermute x5, waiting for transfers between devices, over(): return lax.ppermute(x, 'tp', pairs)  6.82 us
    ppermute x5, starting transfers between devices, over(): return lax.ppermute(x, 'tp', pairs)  5.32 us
    unnamed x12, local copies, waits for them, and re-layouts  1.92 us
    pallas_call x1, Pallas kernels, pack(): pl.pallas_call(functools.partial(pack_kernel, places), out_shape=tuple((j...  1.9 us
  transfers between devices with their start and end apart: 17, of which 8 were waited for; matrix products, arithmetic and copies ran while one was open for 0% of the time, Pallas kernels for 24%

profile of v11, /device:TPU:3, one launch (start us, length us, event | category | flops | bytes accessed | tf_op | source)
XLA Modules:
  0.0 69.8 jit_solution(5415970034637963241)
XLA Ops:
  0.6 1.4 %collective-permute-start.6 = (bf16[64,5376]{1,0:T(8,128)(2,1)}, bf16[64,5376]{1,0:T(8,128)(2,1)S(1)}, u32[]{:S(2)}, u32[]{:S(2)}) collective-permute-start(bf16[64,5376]{1,0:T(8,128)(2,1)} %refs_0_.3), channel_id=1, source_target_pairs={{0,1},{1,0},{2,3},{3,2},{4,5},{5,4},{6,7},{7,6},{8,9},{9,8},{10,11... | collective-permute-start | bytes 2064392 | tf_op jit(solution)/shard_map/end_first/ppermute | solution.py:447
  2.0 0.7 collective-permute-start.8
  2.7 1.9 %pack.1 = (bf16[256,512]{1,0:T(8,128)(2,1)}, bf16[256,512]{1,0:T(8,128)(2,1)}) custom-call(bf16[256,256]{1,0:T(8,128)(2,1)} %refs_0_.2, bf16[256,256]{1,0:T(8,128)(2,1)} %refs_1_.1, bf16[256,512]{1,0:T(8,128)(2,1)} %refs_2_.2), custom_call_target="tpu_custom_call" | custom-call | flops 1 | bytes 1 | tf_op jit(solution)/shard_map/pack/pallas_call | solution.py:87
  4.6 3.1 %collective-permute-start = (bf16[256,512]{1,0:T(8,128)(2,1)}, bf16[256,512]{1,0:T(8,128)(2,1)S(1)}, u32[]{:S(2)}, u32[]{:S(2)}) collective-permute-start(bf16[256,512]{1,0:T(8,128)(2,1)} %get-tuple-element.24.refs_0_.refs_3_), channel_id=1, source_target_pairs={{0,8},{4,12},{8,16},{12,20},{16,24},{20,28},{1,9},{5,13},{9,17},{1... | collective-permute-start | bytes 786440 | tf_op jit(solution)/shard_map/kv_near/ppermute | solution.py:443
  7.7 1.3 %collective-permute-start.1 = (bf16[256,512]{1,0:T(8,128)(2,1)}, bf16[256,512]{1,0:T(8,128)(2,1)S(1)}, u32[]{:S(2)}, u32[]{:S(2)}) collective-permute-start(bf16[256,512]{1,0:T(8,128)(2,1)} %get-tuple-element.24.refs_0_.refs_3_), channel_id=1, source_target_pairs={{0,16},{4,20},{8,24},{12,28},{1,17},{5,21},{9,25},{13,29},{2,18},{... | collective-permute-start | bytes 786440 | tf_op jit(solution)/shard_map/kv_far/ppermute | solution.py:443
  9.1 1.3 %collective-permute-start.3 = (bf16[256,512]{1,0:T(8,128)(2,1)}, bf16[256,512]{1,0:T(8,128)(2,1)S(1)}, u32[]{:S(2)}, u32[]{:S(2)}) collective-permute-start(bf16[256,512]{1,0:T(8,128)(2,1)} %get-tuple-element.25.refs_0_.refs_1_.refs_4_), channel_id=1, source_target_pairs={{16,0},{20,4},{24,8},{28,12},{17,1},{21,5},{25,9},{29,13},{18,2},{... | collective-permute-start | bytes 786440 | tf_op jit(solution)/shard_map/q_far/ppermute | solution.py:443
  10.4 3.2 %collective-permute-done.refs_2_ = bf16[256,512]{1,0:T(8,128)(2,1)S(1)} collective-permute-done((bf16[256,512]{1,0:T(8,128)(2,1)}, bf16[256,512]{1,0:T(8,128)(2,1)S(1)}, u32[]{:S(2)}, u32[]{:S(2)}) %collective-permute-start) | collective-permute-done | bytes 262176 | tf_op jit(solution)/shard_map/kv_near/ppermute | solution.py:443
  13.6 1.9 %collective-permute-start.4 = (bf16[256,512]{1,0:T(8,128)(2,1)}, bf16[256,512]{1,0:T(8,128)(2,1)S(1)}, u32[]{:S(2)}, u32[]{:S(2)}) collective-permute-start(bf16[256,512]{1,0:T(8,128)(2,1)} %get-tuple-element.25.refs_0_.refs_1_.refs_4_), channel_id=1, source_target_pairs={{8,0},{12,4},{16,8},{20,12},{24,16},{28,20},{9,1},{13,5},{17,9},{2... | collective-permute-start | bytes 786440 | tf_op jit(solution)/shard_map/q_near/ppermute | solution.py:443
  15.5 1.7 %collective-permute-done.6.refs_1_ = bf16[64,5376]{1,0:T(8,128)(2,1)S(1)} collective-permute-done((bf16[64,5376]{1,0:T(8,128)(2,1)}, bf16[64,5376]{1,0:T(8,128)(2,1)S(1)}, u32[]{:S(2)}, u32[]{:S(2)}) %collective-permute-start.6) | collective-permute-done | bytes 688160 | tf_op jit(solution)/shard_map/end_first/ppermute | solution.py:447
  17.2 0.7 collective-permute-start.7
  17.9 0.0 collective-permute-done.8.refs_2_
  17.9 1.3 %collective-permute-start.9 = (bf16[64,5376]{1,0:T(8,128)(2,1)S(1)}, bf16[64,5376]{1,0:T(8,128)(2,1)S(1)}, u32[]{:S(2)}, u32[]{:S(2)}) collective-permute-start(bf16[64,5376]{1,0:T(8,128)(2,1)S(1)} %collective-permute-done.8.refs_2_), channel_id=1, source_target_pairs={{1,0},{2,3},{5,4},{6,7},{9,8},{10,11},{13,12},{14,15},{17,16},{18,... | collective-permute-start | bytes 2064392 | tf_op jit(solution)/shard_map/out_second/ppermute | solution.py:447
  19.2 0.0 collective-permute-done.1.refs_1_.refs_3_
  19.2 0.0 copy-start.1
  19.2 0.9 %copy-done.1 = bf16[256,512]{1,0:T(8,128)(2,1)S(1)} copy-done((bf16[256,512]{1,0:T(8,128)(2,1)S(1)}, bf16[256,512]{1,0:T(8,128)(2,1)}, u32[]{:S(2)}) %copy-start.1) | copy-done | bytes 262168
  20.2 0.0 copy-start.2
  20.2 1.6 %collective-permute-start.2 = (bf16[512,512]{1,0:T(8,128)(2,1)S(1)}, bf16[512,512]{1,0:T(8,128)(2,1)S(1)}, u32[]{:S(2)}, u32[]{:S(2)}) collective-permute-start(bf16[512,512]{1,0:T(8,128)(2,1)S(1)} %pair.4), channel_id=1, source_target_pairs={{0,4},{4,0},{8,12},{12,8},{16,20},{20,16},{24,28},{28,24},{1,5},{5... | collective-permute-start | bytes 1572872 | tf_op jit(solution)/shard_map/kv_swap/ppermute | solution.py:443
  21.8 0.0 collective-permute-done.3.refs_1_.refs_6_.refs_2_
  21.8 0.7 %collective-permute-done.4.refs_2_.refs_5_.refs_1_ = bf16[256,512]{1,0:T(8,128)(2,1)S(1)} collective-permute-done((bf16[256,512]{1,0:T(8,128)(2,1)}, bf16[256,512]{1,0:T(8,128)(2,1)S(1)}, u32[]{:S(2)}, u32[]{:S(2)}) %collective-permute-start.4) | collective-permute-done | bytes 262176 | tf_op jit(solution)/shard_map/q_near/ppermute | solution.py:443
  22.6 0.0 copy-start.3
  22.6 0.9 %copy-done.3 = bf16[256,512]{1,0:T(8,128)(2,1)S(1)} copy-done((bf16[256,512]{1,0:T(8,128)(2,1)S(1)}, bf16[256,512]{1,0:T(8,128)(2,1)}, u32[]{:S(2)}) %copy-start.3) | copy-done | bytes 262168
  23.5 0.0 copy-start.5
  23.6 0.0 copy-start
  23.6 3.0 %collective-permute-start.5 = (bf16[512,512]{1,0:T(8,128)(2,1)S(1)}, bf16[512,512]{1,0:T(8,128)(2,1)S(1)}, u32[]{:S(2)}, u32[]{:S(2)}) collective-permute-start(bf16[512,512]{1,0:T(8,128)(2,1)S(1)} %pair.5), channel_id=1, source_target_pairs={{0,4},{4,0},{8,12},{12,8},{16,20},{20,16},{24,28},{28,24},{1,5},{5... | collective-permute-start | bytes 1572872 | tf_op jit(solution)/shard_map/q_swap/ppermute | solution.py:443
  26.6 0.0 collective-permute-done.2.refs_4_
  26.6 1.5 %collective-permute-done.5.refs_5_.refs_7_.refs_1_ = bf16[512,512]{1,0:T(8,128)(2,1)S(1)} collective-permute-done((bf16[512,512]{1,0:T(8,128)(2,1)S(1)}, bf16[512,512]{1,0:T(8,128)(2,1)S(1)}, u32[]{:S(2)}, u32[]{:S(2)}) %collective-permute-start.5) | collective-permute-done | bytes 524320 | tf_op jit(solution)/shard_map/q_swap/ppermute | solution.py:443
  28.1 0.0 copy-done.2
  28.1 3.7 %attention_probs.1 = (bf16[4,256,1280]{2,1,0:T(8,128)(2,1)S(1)}, f32[256,512]{1,0:T(8,128)S(1)}, bf16[256,128]{1,0:T(8,128)(2,1)S(1)}, bf16[1280,512]{1,0:T(8,128)(2,1)S(1)}) custom-call(bf16[256,512]{1,0:T(8,128)(2,1)S(1)} %copy-done.2, bf16[256,512]{1,0:T(8,128)(2,1)S(1)} %copy-done.3, bf16[256,512]{1,0:T(8,128)(2,1)S(1)} %collective-permute-done.refs_2_, ...), custom_call_target="tpu_custom_call" | custom-call | flops 1 | bytes 1 | tf_op jit(solution)/shard_map/attention_probs/pallas_call | solution.py:41
  31.8 0.0 collective-permute-done.7.refs_1_.refs_0_
  31.8 5.1 %collective-permute-done.9.refs_0_.refs_3_ = bf16[64,5376]{1,0:T(8,128)(2,1)S(1)} collective-permute-done((bf16[64,5376]{1,0:T(8,128)(2,1)S(1)}, bf16[64,5376]{1,0:T(8,128)(2,1)S(1)}, u32[]{:S(2)}, u32[]{:S(2)}) %collective-permute-start.9) | collective-permute-done | bytes 688160 | tf_op jit(solution)/shard_map/out_second/ppermute | solution.py:447
  36.9 1.3 %collective-permute-start.10 = (bf16[64,5376]{1,0:T(8,128)(2,1)S(1)}, bf16[64,5376]{1,0:T(8,128)(2,1)S(1)}, u32[]{:S(2)}, u32[]{:S(2)}) collective-permute-start(bf16[64,5376]{1,0:T(8,128)(2,1)S(1)} %collective-permute-done.7.refs_1_.refs_0_), channel_id=1, source_target_pairs={{1,0},{2,3},{5,4},{6,7},{9,8},{10,11},{13,12},{14,15},{17,16},{18,... | collective-permute-start | bytes 2064392 | tf_op jit(solution)/shard_map/out_third/ppermute | solution.py:447
  38.2 0.0 copy-done.5
  38.2 0.0 copy-done
  38.2 0.0 copy-start.4
  38.2 1.9 %dout_rows.2.refs_2_.refs_0_.refs_8_ = bf16[192,640]{1,0:T(8,128)(2,1)S(1)} custom-call(bf16[64,5376]{1,0:T(8,128)(2,1)S(1)} %copy-done.5, bf16[64,5376]{1,0:T(8,128)(2,1)S(1)} %collective-permute-done.6.refs_1_, bf16[64,5376]{1,0:T(8,128)(2,1)S(1)} %collective-permute-done.8.refs_2_, bf16[64,5376]{1,0:T(8,128)(2,1)S(1)} %collective-permute-done.9.refs_0_.refs_3_, ...), custom_call_target="tpu_custom_call" | custom-call | flops 1 | bytes 1 | tf_op jit(solution)/shard_map/dout_rows/pallas_call | solution.py:41
  40.1 1.3 %collective-permute-start.11 = (bf16[192,640]{1,0:T(8,128)(2,1)S(1)}, bf16[192,640]{1,0:T(8,128)(2,1)S(1)}, u32[]{:S(2)}, u32[]{:S(2)}) collective-permute-start(bf16[192,640]{1,0:T(8,128)(2,1)S(1)} %dout_rows.2.refs_2_.refs_0_.refs_8_), channel_id=1, source_target_pairs={{16,0},{20,4},{24,8},{28,12},{17,1},{21,5},{25,9},{29,13},{18,2},{... | collective-permute-start | bytes 737288 | tf_op jit(solution)/shard_map/early_far/ppermute | solution.py:443
  41.4 2.2 %collective-permute-start.12 = (bf16[192,640]{1,0:T(8,128)(2,1)S(1)}, bf16[192,640]{1,0:T(8,128)(2,1)S(1)}, u32[]{:S(2)}, u32[]{:S(2)}) collective-permute-start(bf16[192,640]{1,0:T(8,128)(2,1)S(1)} %dout_rows.2.refs_2_.refs_0_.refs_8_), channel_id=1, source_target_pairs={{8,0},{12,4},{16,8},{20,12},{24,16},{28,20},{9,1},{13,5},{17,9},{2... | collective-permute-start | bytes 737288 | tf_op jit(solution)/shard_map/early_near/ppermute | solution.py:443
  43.6 0.0 copy-done.4
  43.6 0.9 %key_grads.3 = (f32[256,256]{1,0:T(8,128)S(1)}, f32[256,256]{1,0:T(8,128)S(1)}) custom-call(bf16[256,512]{1,0:T(8,128)(2,1)S(1)} %copy-done.2, bf16[256,512]{1,0:T(8,128)(2,1)S(1)} %copy-done.4, bf16[192,640]{1,0:T(8,128)(2,1)S(1)} %dout_rows.2.refs_2_.refs_0_.refs_8_), custom_call_target="tpu_custom_call" | custom-call | flops 1 | bytes 1 | tf_op jit(solution)/shard_map/key_grads/pallas_call | solution.py:41
  44.5 2.1 %query_grads.1 = (f32[256,512]{1,0:T(8,128)}, f32[8,128]{1,0:T(8,128)S(1)}) custom-call(bf16[4,256,1280]{2,1,0:T(8,128)(2,1)S(1)} %get-tuple-element.26.refs_0_, bf16[1280,512]{1,0:T(8,128)(2,1)S(1)} %get-tuple-element.27.refs_1_, bf16[192,640]{1,0:T(8,128)(2,1)S(1)} %dout_rows.2.refs_2_.refs_0_.refs_8_), custom_call_target="tpu_custom_call" | custom-call | flops 1 | bytes 1 | tf_op jit(solution)/shard_map/query_grads/pallas_call | solution.py:41
  46.6 6.3 %collective-permute-done.11.refs_1_.refs_9_ = bf16[192,640]{1,0:T(8,128)(2,1)S(1)} collective-permute-done((bf16[192,640]{1,0:T(8,128)(2,1)S(1)}, bf16[192,640]{1,0:T(8,128)(2,1)S(1)}, u32[]{:S(2)}, u32[]{:S(2)}) %collective-permute-start.11) | collective-permute-done | bytes 245792 | tf_op jit(solution)/shard_map/early_far/ppermute | solution.py:443
  52.9 0.0 collective-permute-done.12.refs_2_.refs_10_
  52.9 2.8 %collective-permute-start.13 = (bf16[384,640]{1,0:T(8,128)(2,1)S(1)}, bf16[384,640]{1,0:T(8,128)(2,1)S(1)}, u32[]{:S(2)}, u32[]{:S(2)}) collective-permute-start(bf16[384,640]{1,0:T(8,128)(2,1)S(1)} %pair.6), channel_id=1, source_target_pairs={{0,4},{4,0},{8,12},{12,8},{16,20},{20,16},{24,28},{28,24},{1,5},{5... | collective-permute-start | bytes 1474568 | tf_op jit(solution)/shard_map/early_swap/ppermute | solution.py:443
  55.8 0.0 collective-permute-done.10.refs_1_
  55.8 1.8 %dout_rows.3.refs_2_.refs_12_.refs_0_ = bf16[64,640]{1,0:T(8,128)(2,1)S(1)} custom-call(bf16[64,5376]{1,0:T(8,128)(2,1)S(1)} %collective-permute-done.7.refs_1_.refs_0_, bf16[64,5376]{1,0:T(8,128)(2,1)S(1)} %collective-permute-done.10.refs_1_, bf16[512,5376]{1,0:T(8,128)(2,1)S(1)} %copy-done, f32[256,512]{1,0:T(8,128)S(1)} %get-tuple-element.30.refs_5_.refs_3_, ...), custom_call_target="tpu_custom_call" | custom-call | flops 1 | bytes 1 | tf_op jit(solution)/shard_map/dout_rows/pallas_call | solution.py:41
  57.5 1.3 %collective-permute-start.14 = (bf16[64,640]{1,0:T(8,128)(2,1)S(1)}, bf16[64,640]{1,0:T(8,128)(2,1)S(1)}, u32[]{:S(2)}, u32[]{:S(2)}) collective-permute-start(bf16[64,640]{1,0:T(8,128)(2,1)S(1)} %dout_rows.3.refs_2_.refs_12_.refs_0_), channel_id=1, source_target_pairs={{16,0},{20,4},{24,8},{28,12},{17,1},{21,5},{25,9},{29,13},{18,2},{... | collective-permute-start | bytes 245768 | tf_op jit(solution)/shard_map/late_far/ppermute | solution.py:443
  58.8 2.1 %collective-permute-start.15 = (bf16[64,640]{1,0:T(8,128)(2,1)S(1)}, bf16[64,640]{1,0:T(8,128)(2,1)S(1)}, u32[]{:S(2)}, u32[]{:S(2)}) collective-permute-start(bf16[64,640]{1,0:T(8,128)(2,1)S(1)} %dout_rows.3.refs_2_.refs_12_.refs_0_), channel_id=1, source_target_pairs={{8,0},{12,4},{16,8},{20,12},{24,16},{28,20},{9,1},{13,5},{17,9},{2... | collective-permute-start | bytes 245768 | tf_op jit(solution)/shard_map/late_near/ppermute | solution.py:443
  61.0 0.0 collective-permute-done.13.refs_11_
  61.0 3.5 %late_grads.1 = (f32[256,512]{1,0:T(8,128)}, f32[8,128]{1,0:T(8,128)S(1)}, f32[256,256]{1,0:T(8,128)S(1)}, f32[256,256]{1,0:T(8,128)S(1)}) custom-call(bf16[4,256,1280]{2,1,0:T(8,128)(2,1)S(1)} %get-tuple-element.26.refs_0_, bf16[1280,512]{1,0:T(8,128)(2,1)S(1)} %get-tuple-element.27.refs_1_, ...), custom_call_target="tpu_custom_call", output_to_operand_aliasing={{0}: (15, {})} | custom-call | flops 1 | bytes 1 | tf_op jit(solution)/shard_map/late_grads/pallas_call | solution.py:41
  64.5 0.0 collective-permute-done.14.refs_1_.refs_3_
  64.5 0.5 collective-permute-done.15.refs_2_.refs_4_
  65.0 2.1 %collective-permute-start.16 = (bf16[128,640]{1,0:T(8,128)(2,1)S(1)}, bf16[128,640]{1,0:T(8,128)(2,1)S(1)}, u32[]{:S(2)}, u32[]{:S(2)}) collective-permute-start(bf16[128,640]{1,0:T(8,128)(2,1)S(1)} %pair.7), channel_id=1, source_target_pairs={{0,4},{4,0},{8,12},{12,8},{16,20},{20,16},{24,28},{28,24},{1,5},{5... | collective-permute-start | bytes 491528 | tf_op jit(solution)/shard_map/late_swap/ppermute | solution.py:443
  67.0 0.8 %key_grads.4 = (f32[256,256]{1,0:T(8,128)S(1)}, f32[256,256]{1,0:T(8,128)S(1)}) custom-call(bf16[256,512]{1,0:T(8,128)(2,1)S(1)} %copy-done.2, bf16[256,512]{1,0:T(8,128)(2,1)S(1)} %collective-permute-done.4.refs_2_.refs_5_.refs_1_, bf16[256,512]{1,0:T(8,128)(2,1)S(1)} %collective-permute-done.3.refs_1_.refs_6_.refs_2_, ...), custom_call_target="tpu_custom_call" | custom-call | flops 1 | bytes 1 | tf_op jit(solution)/shard_map/key_grads/pallas_call | solution.py:41
  67.8 0.2 collective-permute-done.16.refs_2_
  68.1 1.5 %key_grads.5 = (f32[256,256]{1,0:T(8,128)}, f32[256,256]{1,0:T(8,128)}) custom-call(bf16[256,512]{1,0:T(8,128)(2,1)S(1)} %copy-done.2, bf16[512,512]{1,0:T(8,128)(2,1)S(1)} %collective-permute-done.5.refs_5_.refs_7_.refs_1_, bf16[128,640]{1,0:T(8,128)(2,1)S(1)} %collective-permute-done.16.refs_2_, f32[256,256]{1,0:T(8,128)S(1)} %get-tuple-element.41.refs_3_, ...), custom_call_target="tpu_custom_call" | custom-call | flops 1 | bytes 1 | tf_op jit(solution)/shard_map/key_grads/pallas_call | solution.py:41
  (5 shorter events, 0.1 us)
Async XLA Ops:
  0.6 16.6 %collective-permute-start.6 = (bf16[64,5376]{1,0:T(8,128)(2,1)}, bf16[64,5376]{1,0:T(8,128)(2,1)S(1)}, u32[]{:S(2)}, u32[]{:S(2)}) collective-permute-start(bf16[64,5376]{1,0:T(8,128)(2,1)} %refs_0_.3), channel_id=1, source_target_pairs={{0,1},{1,0},{2,3},{3,2},{4,5},{5,4},{6,7},{7,6},{8,9},{9,8},{10,11... | collective-permute-start | bytes 2064392 | tf_op jit(solution)/shard_map/end_first/ppermute | solution.py:447
  2.0 15.9 %collective-permute-start.8 = (bf16[64,5376]{1,0:T(8,128)(2,1)}, bf16[64,5376]{1,0:T(8,128)(2,1)S(1)}, u32[]{:S(2)}, u32[]{:S(2)}) collective-permute-start(bf16[64,5376]{1,0:T(8,128)(2,1)} %refs_0_.3), channel_id=1, source_target_pairs={{1,2},{2,1},{5,6},{6,5},{9,10},{10,9},{13,14},{14,13},{17,18},{18,... | collective-permute-start | bytes 2064392 | tf_op jit(solution)/shard_map/mid_first/ppermute | solution.py:447
  4.6 9.0 %collective-permute-start = (bf16[256,512]{1,0:T(8,128)(2,1)}, bf16[256,512]{1,0:T(8,128)(2,1)S(1)}, u32[]{:S(2)}, u32[]{:S(2)}) collective-permute-start(bf16[256,512]{1,0:T(8,128)(2,1)} %get-tuple-element.24.refs_0_.refs_3_), channel_id=1, source_target_pairs={{0,8},{4,12},{8,16},{12,20},{16,24},{20,28},{1,9},{5,13},{9,17},{1... | collective-permute-start | bytes 786440 | tf_op jit(solution)/shard_map/kv_near/ppermute | solution.py:443
  7.7 11.5 %collective-permute-start.1 = (bf16[256,512]{1,0:T(8,128)(2,1)}, bf16[256,512]{1,0:T(8,128)(2,1)S(1)}, u32[]{:S(2)}, u32[]{:S(2)}) collective-permute-start(bf16[256,512]{1,0:T(8,128)(2,1)} %get-tuple-element.24.refs_0_.refs_3_), channel_id=1, source_target_pairs={{0,16},{4,20},{8,24},{12,28},{1,17},{5,21},{9,25},{13,29},{2,18},{... | collective-permute-start | bytes 786440 | tf_op jit(solution)/shard_map/kv_far/ppermute | solution.py:443
  9.1 12.8 %collective-permute-start.3 = (bf16[256,512]{1,0:T(8,128)(2,1)}, bf16[256,512]{1,0:T(8,128)(2,1)S(1)}, u32[]{:S(2)}, u32[]{:S(2)}) collective-permute-start(bf16[256,512]{1,0:T(8,128)(2,1)} %get-tuple-element.25.refs_0_.refs_1_.refs_4_), channel_id=1, source_target_pairs={{16,0},{20,4},{24,8},{28,12},{17,1},{21,5},{25,9},{29,13},{18,2},{... | collective-permute-start | bytes 786440 | tf_op jit(solution)/shard_map/q_far/ppermute | solution.py:443
  13.6 9.0 %collective-permute-start.4 = (bf16[256,512]{1,0:T(8,128)(2,1)}, bf16[256,512]{1,0:T(8,128)(2,1)S(1)}, u32[]{:S(2)}, u32[]{:S(2)}) collective-permute-start(bf16[256,512]{1,0:T(8,128)(2,1)} %get-tuple-element.25.refs_0_.refs_1_.refs_4_), channel_id=1, source_target_pairs={{8,0},{12,4},{16,8},{20,12},{24,16},{28,20},{9,1},{13,5},{17,9},{2... | collective-permute-start | bytes 786440 | tf_op jit(solution)/shard_map/q_near/ppermute | solution.py:443
  17.2 14.6 %collective-permute-start.7 = (bf16[64,5376]{1,0:T(8,128)(2,1)S(1)}, bf16[64,5376]{1,0:T(8,128)(2,1)S(1)}, u32[]{:S(2)}, u32[]{:S(2)}) collective-permute-start(bf16[64,5376]{1,0:T(8,128)(2,1)S(1)} %collective-permute-done.6.refs_1_), channel_id=1, source_target_pairs={{1,2},{2,1},{5,6},{6,5},{9,10},{10,9},{13,14},{14,13},{17,18},{18,... | collective-permute-start | bytes 2064392 | tf_op jit(solution)/shard_map/mid_second/ppermute | solution.py:447
  17.9 19.0 %collective-permute-start.9 = (bf16[64,5376]{1,0:T(8,128)(2,1)S(1)}, bf16[64,5376]{1,0:T(8,128)(2,1)S(1)}, u32[]{:S(2)}, u32[]{:S(2)}) collective-permute-start(bf16[64,5376]{1,0:T(8,128)(2,1)S(1)} %collective-permute-done.8.refs_2_), channel_id=1, source_target_pairs={{1,0},{2,3},{5,4},{6,7},{9,8},{10,11},{13,12},{14,15},{17,16},{18,... | collective-permute-start | bytes 2064392 | tf_op jit(solution)/shard_map/out_second/ppermute | solution.py:447
  19.2 1.0 %copy-start.1 = (bf16[256,512]{1,0:T(8,128)(2,1)S(1)}, bf16[256,512]{1,0:T(8,128)(2,1)}, u32[]{:S(2)}) copy-start(bf16[256,512]{1,0:T(8,128)(2,1)} %get-tuple-element.24.refs_0_.refs_3_) | copy-start | bytes 786436
  20.2 7.9 %copy-start.2 = (bf16[256,512]{1,0:T(8,128)(2,1)S(1)}, bf16[256,512]{1,0:T(8,128)(2,1)}, u32[]{:S(2)}) copy-start(bf16[256,512]{1,0:T(8,128)(2,1)} %get-tuple-element.24.refs_0_.refs_3_) | copy-start | bytes 786436
  20.2 6.4 %collective-permute-start.2 = (bf16[512,512]{1,0:T(8,128)(2,1)S(1)}, bf16[512,512]{1,0:T(8,128)(2,1)S(1)}, u32[]{:S(2)}, u32[]{:S(2)}) collective-permute-start(bf16[512,512]{1,0:T(8,128)(2,1)S(1)} %pair.4), channel_id=1, source_target_pairs={{0,4},{4,0},{8,12},{12,8},{16,20},{20,16},{24,28},{28,24},{1,5},{5... | collective-permute-start | bytes 1572872 | tf_op jit(solution)/shard_map/kv_swap/ppermute | solution.py:443
  22.6 1.0 %copy-start.3 = (bf16[256,512]{1,0:T(8,128)(2,1)S(1)}, bf16[256,512]{1,0:T(8,128)(2,1)}, u32[]{:S(2)}) copy-start(bf16[256,512]{1,0:T(8,128)(2,1)} %get-tuple-element.25.refs_0_.refs_1_.refs_4_) | copy-start | bytes 786436
  23.5 14.7 %copy-start.5 = (bf16[64,5376]{1,0:T(8,128)(2,1)S(1)}, bf16[64,5376]{1,0:T(8,128)(2,1)}, u32[]{:S(2)}) copy-start(bf16[64,5376]{1,0:T(8,128)(2,1)} %refs_0_.3) | copy-start | bytes 2064388
  23.6 14.6 %copy-start = (bf16[512,5376]{1,0:T(8,128)(2,1)S(1)}, bf16[512,5376]{1,0:T(8,128)(2,1)}, u32[]{:S(2)}) copy-start(bf16[512,5376]{1,0:T(8,128)(2,1)} %refs_2_.3) | copy-start | bytes 16515076
  23.6 4.5 %collective-permute-start.5 = (bf16[512,512]{1,0:T(8,128)(2,1)S(1)}, bf16[512,512]{1,0:T(8,128)(2,1)S(1)}, u32[]{:S(2)}, u32[]{:S(2)}) collective-permute-start(bf16[512,512]{1,0:T(8,128)(2,1)S(1)} %pair.5), channel_id=1, source_target_pairs={{0,4},{4,0},{8,12},{12,8},{16,20},{20,16},{24,28},{28,24},{1,5},{5... | collective-permute-start | bytes 1572872 | tf_op jit(solution)/shard_map/q_swap/ppermute | solution.py:443
  36.9 18.9 %collective-permute-start.10 = (bf16[64,5376]{1,0:T(8,128)(2,1)S(1)}, bf16[64,5376]{1,0:T(8,128)(2,1)S(1)}, u32[]{:S(2)}, u32[]{:S(2)}) collective-permute-start(bf16[64,5376]{1,0:T(8,128)(2,1)S(1)} %collective-permute-done.7.refs_1_.refs_0_), channel_id=1, source_target_pairs={{1,0},{2,3},{5,4},{6,7},{9,8},{10,11},{13,12},{14,15},{17,16},{18,... | collective-permute-start | bytes 2064392 | tf_op jit(solution)/shard_map/out_third/ppermute | solution.py:447
  38.2 5.4 %copy-start.4 = (bf16[256,512]{1,0:T(8,128)(2,1)S(1)}, bf16[256,512]{1,0:T(8,128)(2,1)}, u32[]{:S(2)}) copy-start(bf16[256,512]{1,0:T(8,128)(2,1)} %get-tuple-element.25.refs_0_.refs_1_.refs_4_) | copy-start | bytes 786436
  40.1 12.8 %collective-permute-start.11 = (bf16[192,640]{1,0:T(8,128)(2,1)S(1)}, bf16[192,640]{1,0:T(8,128)(2,1)S(1)}, u32[]{:S(2)}, u32[]{:S(2)}) collective-permute-start(bf16[192,640]{1,0:T(8,128)(2,1)S(1)} %dout_rows.2.refs_2_.refs_0_.refs_8_), channel_id=1, source_target_pairs={{16,0},{20,4},{24,8},{28,12},{17,1},{21,5},{25,9},{29,13},{18,2},{... | collective-permute-start | bytes 737288 | tf_op jit(solution)/shard_map/early_far/ppermute | solution.py:443
  41.4 11.5 %collective-permute-start.12 = (bf16[192,640]{1,0:T(8,128)(2,1)S(1)}, bf16[192,640]{1,0:T(8,128)(2,1)S(1)}, u32[]{:S(2)}, u32[]{:S(2)}) collective-permute-start(bf16[192,640]{1,0:T(8,128)(2,1)S(1)} %dout_rows.2.refs_2_.refs_0_.refs_8_), channel_id=1, source_target_pairs={{8,0},{12,4},{16,8},{20,12},{24,16},{28,20},{9,1},{13,5},{17,9},{2... | collective-permute-start | bytes 737288 | tf_op jit(solution)/shard_map/early_near/ppermute | solution.py:443
  52.9 8.0 %collective-permute-start.13 = (bf16[384,640]{1,0:T(8,128)(2,1)S(1)}, bf16[384,640]{1,0:T(8,128)(2,1)S(1)}, u32[]{:S(2)}, u32[]{:S(2)}) collective-permute-start(bf16[384,640]{1,0:T(8,128)(2,1)S(1)} %pair.6), channel_id=1, source_target_pairs={{0,4},{4,0},{8,12},{12,8},{16,20},{20,16},{24,28},{28,24},{1,5},{5... | collective-permute-start | bytes 1474568 | tf_op jit(solution)/shard_map/early_swap/ppermute | solution.py:443
  57.5 6.9 %collective-permute-start.14 = (bf16[64,640]{1,0:T(8,128)(2,1)S(1)}, bf16[64,640]{1,0:T(8,128)(2,1)S(1)}, u32[]{:S(2)}, u32[]{:S(2)}) collective-permute-start(bf16[64,640]{1,0:T(8,128)(2,1)S(1)} %dout_rows.3.refs_2_.refs_12_.refs_0_), channel_id=1, source_target_pairs={{16,0},{20,4},{24,8},{28,12},{17,1},{21,5},{25,9},{29,13},{18,2},{... | collective-permute-start | bytes 245768 | tf_op jit(solution)/shard_map/late_far/ppermute | solution.py:443
  58.8 6.1 %collective-permute-start.15 = (bf16[64,640]{1,0:T(8,128)(2,1)S(1)}, bf16[64,640]{1,0:T(8,128)(2,1)S(1)}, u32[]{:S(2)}, u32[]{:S(2)}) collective-permute-start(bf16[64,640]{1,0:T(8,128)(2,1)S(1)} %dout_rows.3.refs_2_.refs_12_.refs_0_), channel_id=1, source_target_pairs={{8,0},{12,4},{16,8},{20,12},{24,16},{28,20},{9,1},{13,5},{17,9},{2... | collective-permute-start | bytes 245768 | tf_op jit(solution)/shard_map/late_near/ppermute | solution.py:443
  65.0 3.1 %collective-permute-start.16 = (bf16[128,640]{1,0:T(8,128)(2,1)S(1)}, bf16[128,640]{1,0:T(8,128)(2,1)S(1)}, u32[]{:S(2)}, u32[]{:S(2)}) collective-permute-start(bf16[128,640]{1,0:T(8,128)(2,1)S(1)} %pair.7), channel_id=1, source_target_pairs={{0,4},{4,0},{8,12},{12,8},{16,20},{20,16},{24,28},{28,24},{1,5},{5... | collective-permute-start | bytes 491528 | tf_op jit(solution)/shard_map/late_swap/ppermute | solution.py:443

commit v12 on v10

--- a/solution.py
+++ b/solution.py
@@ -339,7 +339,7 @@
         cols = head_cols(group)
         key = kv[:, cols]
         value = kv[:, kv_width + group * HD : kv_width + (group + 1) * HD]
-        sum_k = None
+        key_pairs = []
         sum_v = None
         for head in (2 * group, 2 * group + 1):
             queries = q_cat[:, head_cols(head)]
@@ -359,19 +359,19 @@
             )
             dscores = (probability * centred).astype(BF16)
             term_v = dot(probability.astype(BF16), dout, NN)
-            term_k = dot(dscores, queries, NN)
+            key_pairs.append((dscores, queries))
             sum_v = term_v if sum_v is None else sum_v + term_v
-            sum_k = term_k if sum_k is None else sum_k + term_k
-        sum_k = sum_k * SCALE
-        if before:
-            sum_k = sum_k + before[0][:, cols]
-            sum_v = sum_v + before[1][:, cols]
-        held_k[:, cols] = sum_k
-        held_v[:, cols] = sum_v
-        for n, (held, out) in enumerate(((held_k, grad_k), (held_v, grad_v)) if last else ()):
-            copy = pltpu.make_async_copy(held.at[:, cols], out.at[:, cols], sems.at[2 * group + n])
-            copy.start()
-            copies.append(copy)
+        sums = ((sum_v, held_v, grad_v if last else None), (None, held_k, grad_k if last else None))
+        for n, (total, held, out) in enumerate(sums):
+            if n == 1:
+                total = sum(dot(ds, q, NN) for ds, q in key_pairs) * SCALE
+            if before:
+                total = total + before[1 - n][:, cols]
+            held[:, cols] = total
+            if last:
+                copy = pltpu.make_async_copy(held.at[:, cols], out.at[:, cols], sems.at[2 * group + n])
+                copy.start()
+                copies.append(copy)
     for copy in copies:
         copy.wait()
 

time: 70.6 us -> 70.6 us (level)
  no operation moved by 1% of the time
where the time goes in v12:
time: 70.6 us; the launch traced here: 69.8 us
  starting transfers between devices  29.3 us (42%)
  waiting for transfers between devices  19.1 us (27%)
  Pallas kernels  18.4 us (26%)
  local copies, waits for them, and re-layouts  1.92 us (3%)
  between operations  1.08 us (2%)
    ppermute x12, starting transfers between devices, along(): return lax.ppermute(x, 'ctx', pairs)  24 us
    pallas_call x13, Pallas kernels, call(): pl.pallas_call(lambda *refs: kernel(device_info(info), *refs), out_shape=...  16.5 us
    ppermute x12, waiting for transfers between devices, along(): return lax.ppermute(x, 'ctx', pairs)  12.2 us
    ppermute x5, waiting for transfers between devices, over(): return lax.ppermute(x, 'tp', pairs)  6.91 us
    ppermute x5, starting transfers between devices, over(): return lax.ppermute(x, 'tp', pairs)  5.32 us
    unnamed x12, local copies, waits for them, and re-layouts  1.92 us
    pallas_call x1, Pallas kernels, pack(): pl.pallas_call(functools.partial(pack_kernel, places), out_shape=tuple((j...  1.9 us
  transfers between devices with their start and end apart: 17, of which 8 were waited for; matrix products, arithmetic and copies ran while one was open for 0% of the time, Pallas kernels for 24%

profile of v12, /device:TPU:3, one launch (start us, length us, event | category | flops | bytes accessed | tf_op | source)
XLA Modules:
  0.0 69.8 jit_solution(8643651260616184273)
XLA Ops:
  0.6 1.4 %collective-permute-start.6 = (bf16[64,5376]{1,0:T(8,128)(2,1)}, bf16[64,5376]{1,0:T(8,128)(2,1)S(1)}, u32[]{:S(2)}, u32[]{:S(2)}) collective-permute-start(bf16[64,5376]{1,0:T(8,128)(2,1)} %refs_0_.3), channel_id=1, source_target_pairs={{0,1},{1,0},{2,3},{3,2},{4,5},{5,4},{6,7},{7,6},{8,9},{9,8},{10,11... | collective-permute-start | bytes 2064392 | tf_op jit(solution)/shard_map/end_first/ppermute | solution.py:412
  2.0 0.7 collective-permute-start.8
  2.7 1.9 %pack.1 = (bf16[256,512]{1,0:T(8,128)(2,1)}, bf16[256,512]{1,0:T(8,128)(2,1)}) custom-call(bf16[256,256]{1,0:T(8,128)(2,1)} %refs_0_.2, bf16[256,256]{1,0:T(8,128)(2,1)} %refs_1_.1, bf16[256,512]{1,0:T(8,128)(2,1)} %refs_2_.2), custom_call_target="tpu_custom_call" | custom-call | flops 1 | bytes 1 | tf_op jit(solution)/shard_map/pack/pallas_call | solution.py:87
  4.6 3.1 %collective-permute-start = (bf16[256,512]{1,0:T(8,128)(2,1)}, bf16[256,512]{1,0:T(8,128)(2,1)S(1)}, u32[]{:S(2)}, u32[]{:S(2)}) collective-permute-start(bf16[256,512]{1,0:T(8,128)(2,1)} %get-tuple-element.24.refs_0_), channel_id=1, source_target_pairs={{0,8},{4,12},{8,16},{12,20},{16,24},{20,28},{1,9},{5,13},{9,17},{1... | collective-permute-start | bytes 786440 | tf_op jit(solution)/shard_map/kv_near/ppermute | solution.py:408
  7.7 1.3 %collective-permute-start.1 = (bf16[256,512]{1,0:T(8,128)(2,1)}, bf16[256,512]{1,0:T(8,128)(2,1)S(1)}, u32[]{:S(2)}, u32[]{:S(2)}) collective-permute-start(bf16[256,512]{1,0:T(8,128)(2,1)} %get-tuple-element.24.refs_0_), channel_id=1, source_target_pairs={{0,16},{4,20},{8,24},{12,28},{1,17},{5,21},{9,25},{13,29},{2,18},{... | collective-permute-start | bytes 786440 | tf_op jit(solution)/shard_map/kv_far/ppermute | solution.py:408
  9.1 1.3 %collective-permute-start.3 = (bf16[256,512]{1,0:T(8,128)(2,1)}, bf16[256,512]{1,0:T(8,128)(2,1)S(1)}, u32[]{:S(2)}, u32[]{:S(2)}) collective-permute-start(bf16[256,512]{1,0:T(8,128)(2,1)} %get-tuple-element.25.refs_0_.refs_1_), channel_id=1, source_target_pairs={{16,0},{20,4},{24,8},{28,12},{17,1},{21,5},{25,9},{29,13},{18,2},{... | collective-permute-start | bytes 786440 | tf_op jit(solution)/shard_map/q_far/ppermute | solution.py:408
  10.4 3.2 %collective-permute-done.refs_2_ = bf16[256,512]{1,0:T(8,128)(2,1)S(1)} collective-permute-done((bf16[256,512]{1,0:T(8,128)(2,1)}, bf16[256,512]{1,0:T(8,128)(2,1)S(1)}, u32[]{:S(2)}, u32[]{:S(2)}) %collective-permute-start) | collective-permute-done | bytes 262176 | tf_op jit(solution)/shard_map/kv_near/ppermute | solution.py:408
  13.6 1.9 %collective-permute-start.4 = (bf16[256,512]{1,0:T(8,128)(2,1)}, bf16[256,512]{1,0:T(8,128)(2,1)S(1)}, u32[]{:S(2)}, u32[]{:S(2)}) collective-permute-start(bf16[256,512]{1,0:T(8,128)(2,1)} %get-tuple-element.25.refs_0_.refs_1_), channel_id=1, source_target_pairs={{8,0},{12,4},{16,8},{20,12},{24,16},{28,20},{9,1},{13,5},{17,9},{2... | collective-permute-start | bytes 786440 | tf_op jit(solution)/shard_map/q_near/ppermute | solution.py:408
  15.5 1.7 %collective-permute-done.6.refs_1_ = bf16[64,5376]{1,0:T(8,128)(2,1)S(1)} collective-permute-done((bf16[64,5376]{1,0:T(8,128)(2,1)}, bf16[64,5376]{1,0:T(8,128)(2,1)S(1)}, u32[]{:S(2)}, u32[]{:S(2)}) %collective-permute-start.6) | collective-permute-done | bytes 688160 | tf_op jit(solution)/shard_map/end_first/ppermute | solution.py:412
  17.2 0.7 collective-permute-start.7
  17.9 0.0 collective-permute-done.8.refs_2_
  17.9 1.3 %collective-permute-start.9 = (bf16[64,5376]{1,0:T(8,128)(2,1)S(1)}, bf16[64,5376]{1,0:T(8,128)(2,1)S(1)}, u32[]{:S(2)}, u32[]{:S(2)}) collective-permute-start(bf16[64,5376]{1,0:T(8,128)(2,1)S(1)} %collective-permute-done.8.refs_2_), channel_id=1, source_target_pairs={{1,0},{2,3},{5,4},{6,7},{9,8},{10,11},{13,12},{14,15},{17,16},{18,... | collective-permute-start | bytes 2064392 | tf_op jit(solution)/shard_map/out_second/ppermute | solution.py:412
  19.2 0.0 collective-permute-done.1.refs_1_.refs_3_
  19.2 0.0 copy-start.1
  19.2 0.9 %copy-done.1 = bf16[256,512]{1,0:T(8,128)(2,1)S(1)} copy-done((bf16[256,512]{1,0:T(8,128)(2,1)S(1)}, bf16[256,512]{1,0:T(8,128)(2,1)}, u32[]{:S(2)}) %copy-start.1) | copy-done | bytes 262168
  20.2 0.0 copy-start.2
  20.2 1.6 %collective-permute-start.2 = (bf16[512,512]{1,0:T(8,128)(2,1)S(1)}, bf16[512,512]{1,0:T(8,128)(2,1)S(1)}, u32[]{:S(2)}, u32[]{:S(2)}) collective-permute-start(bf16[512,512]{1,0:T(8,128)(2,1)S(1)} %pair.4), channel_id=1, source_target_pairs={{0,4},{4,0},{8,12},{12,8},{16,20},{20,16},{24,28},{28,24},{1,5},{5... | collective-permute-start | bytes 1572872 | tf_op jit(solution)/shard_map/kv_swap/ppermute | solution.py:408
  21.8 0.0 collective-permute-done.3.refs_1_.refs_3_.refs_2_
  21.8 0.7 %collective-permute-done.4.refs_2_.refs_1_ = bf16[256,512]{1,0:T(8,128)(2,1)S(1)} collective-permute-done((bf16[256,512]{1,0:T(8,128)(2,1)}, bf16[256,512]{1,0:T(8,128)(2,1)S(1)}, u32[]{:S(2)}, u32[]{:S(2)}) %collective-permute-start.4) | collective-permute-done | bytes 262176 | tf_op jit(solution)/shard_map/q_near/ppermute | solution.py:408
  22.6 0.0 copy-start.3
  22.6 0.9 %copy-done.3 = bf16[256,512]{1,0:T(8,128)(2,1)S(1)} copy-done((bf16[256,512]{1,0:T(8,128)(2,1)S(1)}, bf16[256,512]{1,0:T(8,128)(2,1)}, u32[]{:S(2)}) %copy-start.3) | copy-done | bytes 262168
  23.5 0.0 copy-start.5
  23.6 0.0 copy-start
  23.6 3.0 %collective-permute-start.5 = (bf16[512,512]{1,0:T(8,128)(2,1)S(1)}, bf16[512,512]{1,0:T(8,128)(2,1)S(1)}, u32[]{:S(2)}, u32[]{:S(2)}) collective-permute-start(bf16[512,512]{1,0:T(8,128)(2,1)S(1)} %pair.5), channel_id=1, source_target_pairs={{0,4},{4,0},{8,12},{12,8},{16,20},{20,16},{24,28},{28,24},{1,5},{5... | collective-permute-start | bytes 1572872 | tf_op jit(solution)/shard_map/q_swap/ppermute | solution.py:408
  26.6 0.0 collective-permute-done.2.refs_4_
  26.6 1.5 %collective-permute-done.5.refs_5_.refs_4_.refs_1_ = bf16[512,512]{1,0:T(8,128)(2,1)S(1)} collective-permute-done((bf16[512,512]{1,0:T(8,128)(2,1)S(1)}, bf16[512,512]{1,0:T(8,128)(2,1)S(1)}, u32[]{:S(2)}, u32[]{:S(2)}) %collective-permute-start.5) | collective-permute-done | bytes 524320 | tf_op jit(solution)/shard_map/q_swap/ppermute | solution.py:408
  28.1 0.0 copy-done.2
  28.1 3.6 %attention_probs.1 = (bf16[4,256,1280]{2,1,0:T(8,128)(2,1)S(1)}, f32[256,512]{1,0:T(8,128)S(1)}, bf16[256,128]{1,0:T(8,128)(2,1)S(1)}, bf16[1280,512]{1,0:T(8,128)(2,1)S(1)}) custom-call(bf16[256,512]{1,0:T(8,128)(2,1)S(1)} %copy-done.2, bf16[256,512]{1,0:T(8,128)(2,1)S(1)} %copy-done.3, bf16[256,512]{1,0:T(8,128)(2,1)S(1)} %collective-permute-done.refs_2_, ...), custom_call_target="tpu_custom_call" | custom-call | flops 1 | bytes 1 | tf_op jit(solution)/shard_map/attention_probs/pallas_call | solution.py:41
  31.7 0.0 collective-permute-done.7.refs_1_.refs_0_
  31.7 5.2 %collective-permute-done.9.refs_0_.refs_3_ = bf16[64,5376]{1,0:T(8,128)(2,1)S(1)} collective-permute-done((bf16[64,5376]{1,0:T(8,128)(2,1)S(1)}, bf16[64,5376]{1,0:T(8,128)(2,1)S(1)}, u32[]{:S(2)}, u32[]{:S(2)}) %collective-permute-start.9) | collective-permute-done | bytes 688160 | tf_op jit(solution)/shard_map/out_second/ppermute | solution.py:412
  36.9 1.3 %collective-permute-start.10 = (bf16[64,5376]{1,0:T(8,128)(2,1)S(1)}, bf16[64,5376]{1,0:T(8,128)(2,1)S(1)}, u32[]{:S(2)}, u32[]{:S(2)}) collective-permute-start(bf16[64,5376]{1,0:T(8,128)(2,1)S(1)} %collective-permute-done.7.refs_1_.refs_0_), channel_id=1, source_target_pairs={{1,0},{2,3},{5,4},{6,7},{9,8},{10,11},{13,12},{14,15},{17,16},{18,... | collective-permute-start | bytes 2064392 | tf_op jit(solution)/shard_map/out_third/ppermute | solution.py:412
  38.2 0.0 copy-done.5
  38.2 0.0 copy-done
  38.2 0.0 copy-start.4
  38.2 1.9 %dout_rows.2.refs_2_.refs_0_.refs_5_ = bf16[192,640]{1,0:T(8,128)(2,1)S(1)} custom-call(bf16[64,5376]{1,0:T(8,128)(2,1)S(1)} %copy-done.5, bf16[64,5376]{1,0:T(8,128)(2,1)S(1)} %collective-permute-done.6.refs_1_, bf16[64,5376]{1,0:T(8,128)(2,1)S(1)} %collective-permute-done.8.refs_2_, bf16[64,5376]{1,0:T(8,128)(2,1)S(1)} %collective-permute-done.9.refs_0_.refs_3_, ...), custom_call_target="tpu_custom_call" | custom-call | flops 1 | bytes 1 | tf_op jit(solution)/shard_map/dout_rows/pallas_call | solution.py:41
  40.1 1.3 %collective-permute-start.13 = (bf16[192,640]{1,0:T(8,128)(2,1)S(1)}, bf16[192,640]{1,0:T(8,128)(2,1)S(1)}, u32[]{:S(2)}, u32[]{:S(2)}) collective-permute-start(bf16[192,640]{1,0:T(8,128)(2,1)S(1)} %dout_rows.2.refs_2_.refs_0_.refs_5_), channel_id=1, source_target_pairs={{16,0},{20,4},{24,8},{28,12},{17,1},{21,5},{25,9},{29,13},{18,2},{... | collective-permute-start | bytes 737288 | tf_op jit(solution)/shard_map/early_far/ppermute | solution.py:408
  41.4 2.2 %collective-permute-start.14 = (bf16[192,640]{1,0:T(8,128)(2,1)S(1)}, bf16[192,640]{1,0:T(8,128)(2,1)S(1)}, u32[]{:S(2)}, u32[]{:S(2)}) collective-permute-start(bf16[192,640]{1,0:T(8,128)(2,1)S(1)} %dout_rows.2.refs_2_.refs_0_.refs_5_), channel_id=1, source_target_pairs={{8,0},{12,4},{16,8},{20,12},{24,16},{28,20},{9,1},{13,5},{17,9},{2... | collective-permute-start | bytes 737288 | tf_op jit(solution)/shard_map/early_near/ppermute | solution.py:408
  43.6 0.0 copy-done.4
  43.6 0.9 %key_grads.4 = (f32[256,256]{1,0:T(8,128)S(1)}, f32[256,256]{1,0:T(8,128)S(1)}) custom-call(bf16[256,512]{1,0:T(8,128)(2,1)S(1)} %copy-done.2, bf16[256,512]{1,0:T(8,128)(2,1)S(1)} %copy-done.4, bf16[192,640]{1,0:T(8,128)(2,1)S(1)} %dout_rows.2.refs_2_.refs_0_.refs_5_), custom_call_target="tpu_custom_call" | custom-call | flops 1 | bytes 1 | tf_op jit(solution)/shard_map/key_grads/pallas_call | solution.py:41
  44.5 2.1 %query_grads.2 = (f32[256,512]{1,0:T(8,128)}, f32[8,128]{1,0:T(8,128)S(1)}) custom-call(bf16[4,256,1280]{2,1,0:T(8,128)(2,1)S(1)} %get-tuple-element.26.refs_0_, bf16[1280,512]{1,0:T(8,128)(2,1)S(1)} %get-tuple-element.27.refs_1_, bf16[192,640]{1,0:T(8,128)(2,1)S(1)} %dout_rows.2.refs_2_.refs_0_.refs_5_), custom_call_target="tpu_custom_call" | custom-call | flops 1 | bytes 1 | tf_op jit(solution)/shard_map/query_grads/pallas_call | solution.py:41
  46.6 6.3 %collective-permute-done.13.refs_1_.refs_6_ = bf16[192,640]{1,0:T(8,128)(2,1)S(1)} collective-permute-done((bf16[192,640]{1,0:T(8,128)(2,1)S(1)}, bf16[192,640]{1,0:T(8,128)(2,1)S(1)}, u32[]{:S(2)}, u32[]{:S(2)}) %collective-permute-start.13) | collective-permute-done | bytes 245792 | tf_op jit(solution)/shard_map/early_far/ppermute | solution.py:408
  52.9 0.0 collective-permute-done.14.refs_2_.refs_7_
  52.9 2.8 %collective-permute-start.15 = (bf16[384,640]{1,0:T(8,128)(2,1)S(1)}, bf16[384,640]{1,0:T(8,128)(2,1)S(1)}, u32[]{:S(2)}, u32[]{:S(2)}) collective-permute-start(bf16[384,640]{1,0:T(8,128)(2,1)S(1)} %pair.6), channel_id=1, source_target_pairs={{0,4},{4,0},{8,12},{12,8},{16,20},{20,16},{24,28},{28,24},{1,5},{5... | collective-permute-start | bytes 1474568 | tf_op jit(solution)/shard_map/early_swap/ppermute | solution.py:408
  55.8 0.0 collective-permute-done.10.refs_1_
  55.8 1.8 %dout_rows.3.refs_2_.refs_9_.refs_0_ = bf16[64,640]{1,0:T(8,128)(2,1)S(1)} custom-call(bf16[64,5376]{1,0:T(8,128)(2,1)S(1)} %collective-permute-done.7.refs_1_.refs_0_, bf16[64,5376]{1,0:T(8,128)(2,1)S(1)} %collective-permute-done.10.refs_1_, bf16[512,5376]{1,0:T(8,128)(2,1)S(1)} %copy-done, f32[256,512]{1,0:T(8,128)S(1)} %get-tuple-element.30.refs_5_.refs_3_, ...), custom_call_target="tpu_custom_call" | custom-call | flops 1 | bytes 1 | tf_op jit(solution)/shard_map/dout_rows/pallas_call | solution.py:41
  57.5 1.3 %collective-permute-start.11 = (bf16[64,640]{1,0:T(8,128)(2,1)S(1)}, bf16[64,640]{1,0:T(8,128)(2,1)S(1)}, u32[]{:S(2)}, u32[]{:S(2)}) collective-permute-start(bf16[64,640]{1,0:T(8,128)(2,1)S(1)} %dout_rows.3.refs_2_.refs_9_.refs_0_), channel_id=1, source_target_pairs={{16,0},{20,4},{24,8},{28,12},{17,1},{21,5},{25,9},{29,13},{18,2},{... | collective-permute-start | bytes 245768 | tf_op jit(solution)/shard_map/late_far/ppermute | solution.py:408
  58.9 2.1 %collective-permute-start.12 = (bf16[64,640]{1,0:T(8,128)(2,1)S(1)}, bf16[64,640]{1,0:T(8,128)(2,1)S(1)}, u32[]{:S(2)}, u32[]{:S(2)}) collective-permute-start(bf16[64,640]{1,0:T(8,128)(2,1)S(1)} %dout_rows.3.refs_2_.refs_9_.refs_0_), channel_id=1, source_target_pairs={{8,0},{12,4},{16,8},{20,12},{24,16},{28,20},{9,1},{13,5},{17,9},{2... | collective-permute-start | bytes 245768 | tf_op jit(solution)/shard_map/late_near/ppermute | solution.py:408
  61.0 1.3 %query_grads.3 = (f32[256,512]{1,0:T(8,128)}, f32[8,128]{1,0:T(8,128)S(1)}) custom-call(bf16[4,256,1280]{2,1,0:T(8,128)(2,1)S(1)} %get-tuple-element.26.refs_0_, bf16[1280,512]{1,0:T(8,128)(2,1)S(1)} %get-tuple-element.27.refs_1_, bf16[64,640]{1,0:T(8,128)(2,1)S(1)} %dout_rows.3.refs_2_.refs_9_.refs_0_, ...), custom_call_target="tpu_custom_call", output_to_operand_aliasing={{0}: (3, {})} | custom-call | flops 1 | bytes 1 | tf_op jit(solution)/shard_map/query_grads/pallas_call | solution.py:41
  62.2 0.0 collective-permute-done.15.refs_8_
  62.2 2.5 %key_grads.5 = (f32[256,256]{1,0:T(8,128)S(1)}, f32[256,256]{1,0:T(8,128)S(1)}) custom-call(bf16[256,512]{1,0:T(8,128)(2,1)S(1)} %copy-done.2, bf16[256,512]{1,0:T(8,128)(2,1)S(1)} %copy-done.4, bf16[256,512]{1,0:T(8,128)(2,1)S(1)} %collective-permute-done.4.refs_2_.refs_1_, bf16[256,512]{1,0:T(8,128)(2,1)S(1)} %collective-permute-done.3.refs_1_.refs_3_.refs_2_, ...), custom_call_target="tpu_custom_call" | custom-call | flops 1 | bytes 1 | tf_op jit(solution)/shard_map/key_grads/pallas_call | solution.py:41
  64.7 0.0 collective-permute-done.11.refs_1_.refs_3_
  64.8 0.2 collective-permute-done.12.refs_2_.refs_4_
  65.0 2.1 %collective-permute-start.16 = (bf16[128,640]{1,0:T(8,128)(2,1)S(1)}, bf16[128,640]{1,0:T(8,128)(2,1)S(1)}, u32[]{:S(2)}, u32[]{:S(2)}) collective-permute-start(bf16[128,640]{1,0:T(8,128)(2,1)S(1)} %pair.7), channel_id=1, source_target_pairs={{0,4},{4,0},{8,12},{12,8},{16,20},{20,16},{24,28},{28,24},{1,5},{5... | collective-permute-start | bytes 491528 | tf_op jit(solution)/shard_map/late_swap/ppermute | solution.py:408
  67.0 0.8 %key_grads.6 = (f32[256,256]{1,0:T(8,128)S(1)}, f32[256,256]{1,0:T(8,128)S(1)}) custom-call(bf16[256,512]{1,0:T(8,128)(2,1)S(1)} %copy-done.2, bf16[256,512]{1,0:T(8,128)(2,1)S(1)} %collective-permute-done.4.refs_2_.refs_1_, bf16[256,512]{1,0:T(8,128)(2,1)S(1)} %collective-permute-done.3.refs_1_.refs_3_.refs_2_, ...), custom_call_target="tpu_custom_call" | custom-call | flops 1 | bytes 1 | tf_op jit(solution)/shard_map/key_grads/pallas_call | solution.py:41
  67.8 0.2 collective-permute-done.16.refs_2_
  68.1 1.5 %key_grads.7 = (f32[256,256]{1,0:T(8,128)}, f32[256,256]{1,0:T(8,128)}) custom-call(bf16[256,512]{1,0:T(8,128)(2,1)S(1)} %copy-done.2, bf16[512,512]{1,0:T(8,128)(2,1)S(1)} %collective-permute-done.5.refs_5_.refs_4_.refs_1_, bf16[128,640]{1,0:T(8,128)(2,1)S(1)} %collective-permute-done.16.refs_2_, f32[256,256]{1,0:T(8,128)S(1)} %get-tuple-element.41.refs_3_, ...), custom_call_target="tpu_custom_call" | custom-call | flops 1 | bytes 1 | tf_op jit(solution)/shard_map/key_grads/pallas_call | solution.py:41
  (5 shorter events, 0.1 us)
Async XLA Ops:
  0.6 16.6 %collective-permute-start.6 = (bf16[64,5376]{1,0:T(8,128)(2,1)}, bf16[64,5376]{1,0:T(8,128)(2,1)S(1)}, u32[]{:S(2)}, u32[]{:S(2)}) collective-permute-start(bf16[64,5376]{1,0:T(8,128)(2,1)} %refs_0_.3), channel_id=1, source_target_pairs={{0,1},{1,0},{2,3},{3,2},{4,5},{5,4},{6,7},{7,6},{8,9},{9,8},{10,11... | collective-permute-start | bytes 2064392 | tf_op jit(solution)/shard_map/end_first/ppermute | solution.py:412
  2.0 15.9 %collective-permute-start.8 = (bf16[64,5376]{1,0:T(8,128)(2,1)}, bf16[64,5376]{1,0:T(8,128)(2,1)S(1)}, u32[]{:S(2)}, u32[]{:S(2)}) collective-permute-start(bf16[64,5376]{1,0:T(8,128)(2,1)} %refs_0_.3), channel_id=1, source_target_pairs={{1,2},{2,1},{5,6},{6,5},{9,10},{10,9},{13,14},{14,13},{17,18},{18,... | collective-permute-start | bytes 2064392 | tf_op jit(solution)/shard_map/mid_first/ppermute | solution.py:412
  4.6 9.0 %collective-permute-start = (bf16[256,512]{1,0:T(8,128)(2,1)}, bf16[256,512]{1,0:T(8,128)(2,1)S(1)}, u32[]{:S(2)}, u32[]{:S(2)}) collective-permute-start(bf16[256,512]{1,0:T(8,128)(2,1)} %get-tuple-element.24.refs_0_), channel_id=1, source_target_pairs={{0,8},{4,12},{8,16},{12,20},{16,24},{20,28},{1,9},{5,13},{9,17},{1... | collective-permute-start | bytes 786440 | tf_op jit(solution)/shard_map/kv_near/ppermute | solution.py:408
  7.7 11.5 %collective-permute-start.1 = (bf16[256,512]{1,0:T(8,128)(2,1)}, bf16[256,512]{1,0:T(8,128)(2,1)S(1)}, u32[]{:S(2)}, u32[]{:S(2)}) collective-permute-start(bf16[256,512]{1,0:T(8,128)(2,1)} %get-tuple-element.24.refs_0_), channel_id=1, source_target_pairs={{0,16},{4,20},{8,24},{12,28},{1,17},{5,21},{9,25},{13,29},{2,18},{... | collective-permute-start | bytes 786440 | tf_op jit(solution)/shard_map/kv_far/ppermute | solution.py:408
  9.1 12.8 %collective-permute-start.3 = (bf16[256,512]{1,0:T(8,128)(2,1)}, bf16[256,512]{1,0:T(8,128)(2,1)S(1)}, u32[]{:S(2)}, u32[]{:S(2)}) collective-permute-start(bf16[256,512]{1,0:T(8,128)(2,1)} %get-tuple-element.25.refs_0_.refs_1_), channel_id=1, source_target_pairs={{16,0},{20,4},{24,8},{28,12},{17,1},{21,5},{25,9},{29,13},{18,2},{... | collective-permute-start | bytes 786440 | tf_op jit(solution)/shard_map/q_far/ppermute | solution.py:408
  13.6 9.0 %collective-permute-start.4 = (bf16[256,512]{1,0:T(8,128)(2,1)}, bf16[256,512]{1,0:T(8,128)(2,1)S(1)}, u32[]{:S(2)}, u32[]{:S(2)}) collective-permute-start(bf16[256,512]{1,0:T(8,128)(2,1)} %get-tuple-element.25.refs_0_.refs_1_), channel_id=1, source_target_pairs={{8,0},{12,4},{16,8},{20,12},{24,16},{28,20},{9,1},{13,5},{17,9},{2... | collective-permute-start | bytes 786440 | tf_op jit(solution)/shard_map/q_near/ppermute | solution.py:408
  17.2 14.5 %collective-permute-start.7 = (bf16[64,5376]{1,0:T(8,128)(2,1)S(1)}, bf16[64,5376]{1,0:T(8,128)(2,1)S(1)}, u32[]{:S(2)}, u32[]{:S(2)}) collective-permute-start(bf16[64,5376]{1,0:T(8,128)(2,1)S(1)} %collective-permute-done.6.refs_1_), channel_id=1, source_target_pairs={{1,2},{2,1},{5,6},{6,5},{9,10},{10,9},{13,14},{14,13},{17,18},{18,... | collective-permute-start | bytes 2064392 | tf_op jit(solution)/shard_map/mid_second/ppermute | solution.py:412
  17.9 19.0 %collective-permute-start.9 = (bf16[64,5376]{1,0:T(8,128)(2,1)S(1)}, bf16[64,5376]{1,0:T(8,128)(2,1)S(1)}, u32[]{:S(2)}, u32[]{:S(2)}) collective-permute-start(bf16[64,5376]{1,0:T(8,128)(2,1)S(1)} %collective-permute-done.8.refs_2_), channel_id=1, source_target_pairs={{1,0},{2,3},{5,4},{6,7},{9,8},{10,11},{13,12},{14,15},{17,16},{18,... | collective-permute-start | bytes 2064392 | tf_op jit(solution)/shard_map/out_second/ppermute | solution.py:412
  19.2 1.0 %copy-start.1 = (bf16[256,512]{1,0:T(8,128)(2,1)S(1)}, bf16[256,512]{1,0:T(8,128)(2,1)}, u32[]{:S(2)}) copy-start(bf16[256,512]{1,0:T(8,128)(2,1)} %get-tuple-element.24.refs_0_) | copy-start | bytes 786436
  20.2 7.9 %copy-start.2 = (bf16[256,512]{1,0:T(8,128)(2,1)S(1)}, bf16[256,512]{1,0:T(8,128)(2,1)}, u32[]{:S(2)}) copy-start(bf16[256,512]{1,0:T(8,128)(2,1)} %get-tuple-element.24.refs_0_) | copy-start | bytes 786436
  20.2 6.4 %collective-permute-start.2 = (bf16[512,512]{1,0:T(8,128)(2,1)S(1)}, bf16[512,512]{1,0:T(8,128)(2,1)S(1)}, u32[]{:S(2)}, u32[]{:S(2)}) collective-permute-start(bf16[512,512]{1,0:T(8,128)(2,1)S(1)} %pair.4), channel_id=1, source_target_pairs={{0,4},{4,0},{8,12},{12,8},{16,20},{20,16},{24,28},{28,24},{1,5},{5... | collective-permute-start | bytes 1572872 | tf_op jit(solution)/shard_map/kv_swap/ppermute | solution.py:408
  22.6 1.0 %copy-start.3 = (bf16[256,512]{1,0:T(8,128)(2,1)S(1)}, bf16[256,512]{1,0:T(8,128)(2,1)}, u32[]{:S(2)}) copy-start(bf16[256,512]{1,0:T(8,128)(2,1)} %get-tuple-element.25.refs_0_.refs_1_) | copy-start | bytes 786436
  23.5 14.7 %copy-start.5 = (bf16[64,5376]{1,0:T(8,128)(2,1)S(1)}, bf16[64,5376]{1,0:T(8,128)(2,1)}, u32[]{:S(2)}) copy-start(bf16[64,5376]{1,0:T(8,128)(2,1)} %refs_0_.3) | copy-start | bytes 2064388
  23.6 14.6 %copy-start = (bf16[512,5376]{1,0:T(8,128)(2,1)S(1)}, bf16[512,5376]{1,0:T(8,128)(2,1)}, u32[]{:S(2)}) copy-start(bf16[512,5376]{1,0:T(8,128)(2,1)} %refs_2_.3) | copy-start | bytes 16515076
  23.6 4.5 %collective-permute-start.5 = (bf16[512,512]{1,0:T(8,128)(2,1)S(1)}, bf16[512,512]{1,0:T(8,128)(2,1)S(1)}, u32[]{:S(2)}, u32[]{:S(2)}) collective-permute-start(bf16[512,512]{1,0:T(8,128)(2,1)S(1)} %pair.5), channel_id=1, source_target_pairs={{0,4},{4,0},{8,12},{12,8},{16,20},{20,16},{24,28},{28,24},{1,5},{5... | collective-permute-start | bytes 1572872 | tf_op jit(solution)/shard_map/q_swap/ppermute | solution.py:408
  36.9 18.9 %collective-permute-start.10 = (bf16[64,5376]{1,0:T(8,128)(2,1)S(1)}, bf16[64,5376]{1,0:T(8,128)(2,1)S(1)}, u32[]{:S(2)}, u32[]{:S(2)}) collective-permute-start(bf16[64,5376]{1,0:T(8,128)(2,1)S(1)} %collective-permute-done.7.refs_1_.refs_0_), channel_id=1, source_target_pairs={{1,0},{2,3},{5,4},{6,7},{9,8},{10,11},{13,12},{14,15},{17,16},{18,... | collective-permute-start | bytes 2064392 | tf_op jit(solution)/shard_map/out_third/ppermute | solution.py:412
  38.2 5.4 %copy-start.4 = (bf16[256,512]{1,0:T(8,128)(2,1)S(1)}, bf16[256,512]{1,0:T(8,128)(2,1)}, u32[]{:S(2)}) copy-start(bf16[256,512]{1,0:T(8,128)(2,1)} %get-tuple-element.25.refs_0_.refs_1_) | copy-start | bytes 786436
  40.1 12.8 %collective-permute-start.13 = (bf16[192,640]{1,0:T(8,128)(2,1)S(1)}, bf16[192,640]{1,0:T(8,128)(2,1)S(1)}, u32[]{:S(2)}, u32[]{:S(2)}) collective-permute-start(bf16[192,640]{1,0:T(8,128)(2,1)S(1)} %dout_rows.2.refs_2_.refs_0_.refs_5_), channel_id=1, source_target_pairs={{16,0},{20,4},{24,8},{28,12},{17,1},{21,5},{25,9},{29,13},{18,2},{... | collective-permute-start | bytes 737288 | tf_op jit(solution)/shard_map/early_far/ppermute | solution.py:408
  41.4 11.5 %collective-permute-start.14 = (bf16[192,640]{1,0:T(8,128)(2,1)S(1)}, bf16[192,640]{1,0:T(8,128)(2,1)S(1)}, u32[]{:S(2)}, u32[]{:S(2)}) collective-permute-start(bf16[192,640]{1,0:T(8,128)(2,1)S(1)} %dout_rows.2.refs_2_.refs_0_.refs_5_), channel_id=1, source_target_pairs={{8,0},{12,4},{16,8},{20,12},{24,16},{28,20},{9,1},{13,5},{17,9},{2... | collective-permute-start | bytes 737288 | tf_op jit(solution)/shard_map/early_near/ppermute | solution.py:408
  52.9 9.3 %collective-permute-start.15 = (bf16[384,640]{1,0:T(8,128)(2,1)S(1)}, bf16[384,640]{1,0:T(8,128)(2,1)S(1)}, u32[]{:S(2)}, u32[]{:S(2)}) collective-permute-start(bf16[384,640]{1,0:T(8,128)(2,1)S(1)} %pair.6), channel_id=1, source_target_pairs={{0,4},{4,0},{8,12},{12,8},{16,20},{20,16},{24,28},{28,24},{1,5},{5... | collective-permute-start | bytes 1474568 | tf_op jit(solution)/shard_map/early_swap/ppermute | solution.py:408
  57.5 7.2 %collective-permute-start.11 = (bf16[64,640]{1,0:T(8,128)(2,1)S(1)}, bf16[64,640]{1,0:T(8,128)(2,1)S(1)}, u32[]{:S(2)}, u32[]{:S(2)}) collective-permute-start(bf16[64,640]{1,0:T(8,128)(2,1)S(1)} %dout_rows.3.refs_2_.refs_9_.refs_0_), channel_id=1, source_target_pairs={{16,0},{20,4},{24,8},{28,12},{17,1},{21,5},{25,9},{29,13},{18,2},{... | collective-permute-start | bytes 245768 | tf_op jit(solution)/shard_map/late_far/ppermute | solution.py:408
  58.9 6.1 %collective-permute-start.12 = (bf16[64,640]{1,0:T(8,128)(2,1)S(1)}, bf16[64,640]{1,0:T(8,128)(2,1)S(1)}, u32[]{:S(2)}, u32[]{:S(2)}) collective-permute-start(bf16[64,640]{1,0:T(8,128)(2,1)S(1)} %dout_rows.3.refs_2_.refs_9_.refs_0_), channel_id=1, source_target_pairs={{8,0},{12,4},{16,8},{20,12},{24,16},{28,20},{9,1},{13,5},{17,9},{2... | collective-permute-start | bytes 245768 | tf_op jit(solution)/shard_map/late_near/ppermute | solution.py:408
  65.0 3.1 %collective-permute-start.16 = (bf16[128,640]{1,0:T(8,128)(2,1)S(1)}, bf16[128,640]{1,0:T(8,128)(2,1)S(1)}, u32[]{:S(2)}, u32[]{:S(2)}) collective-permute-start(bf16[128,640]{1,0:T(8,128)(2,1)S(1)} %pair.7), channel_id=1, source_target_pairs={{0,4},{4,0},{8,12},{12,8},{16,20},{20,16},{24,28},{28,24},{1,5},{5... | collective-permute-start | bytes 491528 | tf_op jit(solution)/shard_map/late_swap/ppermute | solution.py:408
